TPU v7x, 128 devices: a whole 4x4x4 slice. The times are simulated.
128 devices in a mesh: ctx: 8 (over y_hi, z), fsdp: 16 (over x, y_lo, core).
Axes of the slice: x: 4, y: 4 (y_hi: 2, y_lo: 2; y = y_hi * 2 + y_lo), z: 4, core: 2. Of those that a mesh axis runs over, the one named last changes fastest.
Arguments:
- hidden_in: bfloat16 [16384, 2048], P(('ctx', 'fsdp')), may hold values from -6 to 6
- teacher: bfloat16 [16384, 2048], P(('ctx', 'fsdp')), may hold values from -6 to 6
- doc_ids: int32 [16, 1024], P('fsdp'), may hold values from 0 to 3, as said below
- valid_mask: int32 [16384], P(('ctx', 'fsdp')), may hold values from 0 to 1
- norm1_gain: bfloat16 [2048], P('fsdp'), may hold values from 0.5 to 1.5
- w_query: bfloat16 [2048, 2048], P('fsdp'), may hold values from -0.125 to 0.125
- w_key: bfloat16 [2048, 256], P('fsdp'), may hold values from -0.125 to 0.125
- w_value: bfloat16 [2048, 256], P('fsdp'), may hold values from -0.125 to 0.125
- w_out: bfloat16 [2048, 2048], P('fsdp'), may hold values from -0.75 to 0.75
- norm2_gain: bfloat16 [2048], P('fsdp'), may hold values from 0.5 to 1.5
- w_gate: bfloat16 [2048, 5632], P('fsdp'), may hold values from -0.125 to 0.125
- w_up: bfloat16 [2048, 5632], P('fsdp'), may hold values from -0.125 to 0.125
- w_down: bfloat16 [5632, 2048], P('fsdp'), may hold values from -0.078125 to 0.078125
Outputs:
- layer_out: bfloat16 [16384, 2048], P(('ctx', 'fsdp'))
- mean_loss: float32 [], replicated
- input_grad: float32 [16384, 2048], P(('ctx', 'fsdp'))
- grad_norm1_gain: float32 [2048], P('fsdp')
- grad_w_query: float32 [2048, 2048], P('fsdp')
- grad_w_key: float32 [2048, 256], P('fsdp')
- grad_w_value: float32 [2048, 256], P('fsdp')
- grad_w_out: float32 [2048, 2048], P('fsdp')
- grad_norm2_gain: float32 [2048], P('fsdp')
- grad_w_gate: float32 [2048, 5632], P('fsdp')
- grad_w_up: float32 [2048, 5632], P('fsdp')
- grad_w_down: float32 [5632, 2048], P('fsdp')
Inputs may be any that keep to these rules, and one draw needn't show every extreme that they name: `doc_ids`: document numbers never fall along a sequence; every sequence holds exactly four documents; its first or its last document has 512 positions or more, the others 1024 // 10 or more.
All inputs are finite; a program needn't handle non-finite values.
Results may differ from a plain program's by a relative error of at most 0.023.
Values may be sent and summed in bfloat16 or wider, within the bound.
A program may use at most 320 MiB of HBM per device.

v0:
```python
from functools import partial
import math

import jax
import jax.numpy as jnp
from jax import lax
from jax.sharding import PartitionSpec as P

D = 2048
HEADS = 32
KV_HEADS = 4
HEAD_DIM = 64
FF = 5632
QD = 2048
KVD = 256


EPSILON = 1e-05
THETA = 10000.0
NEGATIVE = -1e30


def tables(positions, head_dim):
    indices = jnp.arange(head_dim // 2, dtype=jnp.int32).astype(jnp.float32)
    frequency = THETA ** (-(indices * 2.0 / head_dim))
    angles = positions.astype(jnp.float32)[:, None] * frequency[None, :]
    angles = jnp.concatenate([angles, angles], axis=1)
    return (jnp.cos(angles), jnp.sin(angles))


def rotate(values, cosines, sines):
    half_dim = values.shape[-1] // 2
    turned = jnp.concatenate([-values[..., half_dim:], values[..., :half_dim]], axis=-1)
    return values * cosines[:, None, None, :] + turned * sines[:, None, None, :]


def unrotate(gradients, cosines, sines):
    half_dim = gradients.shape[-1] // 2
    scaled = gradients * sines[:, None, None, :]
    turned = jnp.concatenate([scaled[..., half_dim:], -scaled[..., :half_dim]], axis=-1)
    return gradients * cosines[:, None, None, :] + turned


def place_rows(row_ids, block_len, ctx_count):
    owners = row_ids // (2 * block_len)
    within = row_ids % (2 * block_len)
    blocks = jnp.where(within < block_len, owners, 2 * ctx_count - 1 - owners)
    return blocks * block_len + within % block_len


def split_groups(values, groups):
    layout = values.shape
    folded = values.reshape((layout[0], groups, layout[1] // groups) + layout[2:])
    return jnp.moveaxis(folded, 1, 0)


def merge_groups(values):
    moved = jnp.moveaxis(values, 0, 1)
    layout = moved.shape
    return moved.reshape((layout[0], layout[1] * layout[2]) + layout[3:])


def times_transposed(left, right):
    return lax.dot_general(
        left, right, (((1,), (1,)), ((), ())), preferred_element_type=jnp.float32
    )


def inner_rows(left, right):
    return lax.dot_general(
        left, right, (((0,), (0,)), ((), ())), preferred_element_type=jnp.float32
    )


def attend(entries, factor):
    queries, key_rows, value_rows, allowed = entries
    raw_scores = jnp.einsum(
        "rgkhd,sgkd->gkhrs", queries, key_rows, preferred_element_type=jnp.float32
    )
    masked = jnp.where(allowed[:, None, None], raw_scores * factor, NEGATIVE)
    highest = jnp.max(masked, axis=-1, keepdims=True)
    exponent = jnp.exp(masked - highest)
    totals = jnp.sum(exponent, axis=-1, keepdims=True)
    weights_soft = (exponent / totals).astype(jnp.bfloat16)
    mixed_out = jnp.einsum(
        "gkhrs,sgkd->rgkhd", weights_soft, value_rows, preferred_element_type=jnp.float32
    )
    return (mixed_out, highest + jnp.log(totals))


def attend_back(entries, factor):
    queries, key_rows, value_rows, allowed, log_total, grad_mixed = entries
    raw_scores = jnp.einsum(
        "rgkhd,sgkd->gkhrs", queries, key_rows, preferred_element_type=jnp.float32
    )
    masked = jnp.where(allowed[:, None, None], raw_scores * factor, NEGATIVE)
    weights_soft = jnp.exp(masked - log_total)
    grad_values = jnp.einsum(
        "gkhrs,rgkhd->sgkd",
        weights_soft.astype(jnp.bfloat16),
        grad_mixed,
        preferred_element_type=jnp.float32,
    )
    grad_weights = jnp.einsum(
        "rgkhd,sgkd->gkhrs", grad_mixed, value_rows, preferred_element_type=jnp.float32
    )
    centre = jnp.sum(weights_soft * grad_weights, axis=-1, keepdims=True)
    grad_scores = (weights_soft * (grad_weights - centre)).astype(jnp.bfloat16)
    grad_queries = (
        jnp.einsum("gkhrs,sgkd->rgkhd", grad_scores, key_rows, preferred_element_type=jnp.float32)
        * factor
    )
    grad_keys = (
        jnp.einsum("gkhrs,rgkhd->sgkd", grad_scores, queries, preferred_element_type=jnp.float32)
        * factor
    )
    return (grad_queries, grad_keys, grad_values)


def local(
    hidden_in,
    teacher,
    doc_ids,
    valid_mask,
    norm1_gain,
    w_query,
    w_key,
    w_value,
    w_out,
    norm2_gain,
    w_gate,
    w_up,
    w_down,
):
    tokens_here = hidden_in.shape[0]
    seq_here = doc_ids.shape[0]
    pair_rows = tokens_here // seq_here
    block_len = pair_rows // 2
    ctx_count = lax.axis_size("ctx")
    ctx_here = lax.axis_index("ctx")
    group_heads = HEADS // KV_HEADS
    factor = 1.0 / math.sqrt(HEAD_DIM)
    together = math.gcd(seq_here, max(1, 512 // pair_rows))
    set_count = seq_here // together
    local_rows = ctx_here * pair_rows + jnp.arange(pair_rows, dtype=jnp.int32)
    query_pos = place_rows(local_rows, block_len, ctx_count)
    key_pos = place_rows(jnp.arange(ctx_count * pair_rows, dtype=jnp.int32), block_len, ctx_count)
    query_doc = jnp.take(doc_ids, query_pos, axis=1)
    key_doc = jnp.take(doc_ids, key_pos, axis=1)
    allowed = (query_pos[:, None] >= key_pos[None, :])[None] & (
        query_doc[:, :, None] == key_doc[:, None, :]
    )
    allowed = allowed.reshape((set_count, together) + allowed.shape[1:])
    cosines, sines = tables(query_pos, HEAD_DIM)
    inputs = hidden_in.astype(jnp.float32)
    inverse1 = lax.rsqrt(jnp.mean(inputs * inputs, axis=1, keepdims=True) + EPSILON)
    normed1 = inputs * inverse1
    gain1, query_all, key_all, value_all, out_all = (
        lax.all_gather(norm1_gain, "fsdp", axis=0, tiled=True),
        lax.all_gather(w_query, "fsdp", axis=0, tiled=True),
        lax.all_gather(w_key, "fsdp", axis=0, tiled=True),
        lax.all_gather(w_value, "fsdp", axis=0, tiled=True),
        lax.all_gather(w_out, "fsdp", axis=0, tiled=True),
    )
    gain1 = gain1.astype(jnp.float32)
    hidden1 = (normed1 * gain1).astype(jnp.bfloat16)
    query_proj = jnp.dot(hidden1, query_all, preferred_element_type=jnp.float32)
    key_proj = jnp.dot(hidden1, key_all, preferred_element_type=jnp.float32)
    value_low = (
        jnp.dot(hidden1, value_all, preferred_element_type=jnp.float32)
        .astype(jnp.bfloat16)
        .reshape(pair_rows, seq_here, KVD)
    )
    query_rot = rotate(
        query_proj.reshape(pair_rows, seq_here, HEADS, HEAD_DIM), cosines, sines
    ).astype(jnp.bfloat16)
    key_rot = rotate(
        key_proj.reshape(pair_rows, seq_here, KV_HEADS, HEAD_DIM), cosines, sines
    ).astype(jnp.bfloat16)
    key_rot = key_rot.reshape(pair_rows, seq_here, KVD)
    keys_whole, values_whole = (
        lax.all_gather(key_rot, "ctx", axis=0, tiled=True),
        lax.all_gather(value_low, "ctx", axis=0, tiled=True),
    )
    query_sets = split_groups(
        query_rot.reshape(pair_rows, seq_here, KV_HEADS, group_heads, HEAD_DIM), set_count
    )
    key_sets = split_groups(keys_whole.reshape(-1, seq_here, KV_HEADS, HEAD_DIM), set_count)
    value_sets = split_groups(values_whole.reshape(-1, seq_here, KV_HEADS, HEAD_DIM), set_count)
    attended, log_total = lax.map(
        partial(attend, factor=factor), (query_sets, key_sets, value_sets, allowed)
    )
    mixed_low = merge_groups(attended).reshape(tokens_here, QD).astype(jnp.bfloat16)
    resid1 = inputs + jnp.dot(mixed_low, out_all, preferred_element_type=jnp.float32)
    inverse2 = lax.rsqrt(jnp.mean(resid1 * resid1, axis=1, keepdims=True) + EPSILON)
    normed2 = resid1 * inverse2
    gain_piece = lax.all_gather(norm2_gain, "fsdp", axis=0, tiled=True)
    gate_piece = lax.all_gather(w_gate, "fsdp", axis=0, tiled=True)
    up_piece = lax.all_gather(w_up, "fsdp", axis=0, tiled=True)
    gain_piece = gain_piece.astype(jnp.float32)
    hidden_piece = (normed2 * gain_piece).astype(jnp.bfloat16)
    gate_sum = jnp.dot(hidden_piece, gate_piece, preferred_element_type=jnp.float32)
    up_sum = jnp.dot(hidden_piece, up_piece, preferred_element_type=jnp.float32)
    sigmoid_gate = jax.nn.sigmoid(gate_sum)
    activated = gate_sum * sigmoid_gate
    product = (activated * up_sum).astype(jnp.bfloat16)
    columns = product
    down_proj = jnp.dot(
        columns,
        lax.all_gather(w_down, "fsdp", axis=0, tiled=True),
        preferred_element_type=jnp.float32,
    )
    result = resid1 + down_proj
    weights_valid = valid_mask.astype(jnp.float32)
    mismatch = result - teacher.astype(jnp.float32)
    squares_here = jnp.sum(weights_valid * jnp.mean(mismatch * mismatch, axis=1))
    count_here = jnp.sum(weights_valid)
    squares_all, count_all = lax.psum((squares_here, count_here), ("ctx", "fsdp"))
    loss_value = squares_all / count_all
    grad_result = weights_valid[:, None] * 2.0 * mismatch / (D * count_all)
    grad_low = grad_result.astype(jnp.bfloat16)
    columns = product
    down_grad = lax.psum_scatter(
        inner_rows(columns, grad_low).astype(jnp.bfloat16), "fsdp", scatter_dimension=0, tiled=True
    ).astype(jnp.float32)
    grad_product = times_transposed(grad_low, lax.all_gather(w_down, "fsdp", axis=0, tiled=True))
    grad_gate = (
        grad_product * up_sum * sigmoid_gate * (1.0 + gate_sum * (1.0 - sigmoid_gate))
    ).astype(jnp.bfloat16)
    grad_up = (grad_product * activated).astype(jnp.bfloat16)
    both_grads = jnp.concatenate([grad_gate, grad_up], axis=1)
    columns = hidden_piece
    gate_up_grad = lax.psum_scatter(
        inner_rows(columns, both_grads).astype(jnp.bfloat16),
        "fsdp",
        scatter_dimension=0,
        tiled=True,
    ).astype(jnp.float32)
    gate_piece = lax.all_gather(w_gate, "fsdp", axis=0, tiled=True)
    up_piece = lax.all_gather(w_up, "fsdp", axis=0, tiled=True)
    columns = times_transposed(grad_gate, gate_piece) + times_transposed(grad_up, up_piece)
    gain2_here = jnp.sum(columns * normed2, axis=0)
    scaled2 = columns * gain_piece
    grad_resid1 = grad_result + inverse2 * (
        scaled2 - normed2 * jnp.mean(scaled2 * normed2, axis=1, keepdims=True)
    )
    grad_out_low = grad_resid1.astype(jnp.bfloat16)
    grad_mixed = times_transposed(grad_out_low, out_all).astype(jnp.bfloat16)
    grad_sets = split_groups(
        grad_mixed.reshape(pair_rows, seq_here, KV_HEADS, group_heads, HEAD_DIM), set_count
    )
    grad_queries, grad_keys, grad_values = lax.map(
        partial(attend_back, factor=factor),
        (query_sets, key_sets, value_sets, allowed, log_total, grad_sets),
    )
    grad_keys = merge_groups(grad_keys).reshape(-1, seq_here, KVD)
    grad_values = merge_groups(grad_values).reshape(-1, seq_here, KVD)
    key_grad_here, value_grad_here = (
        lax.psum_scatter(
            grad_keys.astype(jnp.bfloat16), "ctx", scatter_dimension=0, tiled=True
        ).astype(jnp.float32),
        lax.psum_scatter(
            grad_values.astype(jnp.bfloat16), "ctx", scatter_dimension=0, tiled=True
        ).astype(jnp.float32),
    )
    grad_query_low = unrotate(
        merge_groups(grad_queries).reshape(pair_rows, seq_here, HEADS, HEAD_DIM), cosines, sines
    )
    grad_query_low = grad_query_low.astype(jnp.bfloat16).reshape(tokens_here, QD)
    grad_key_low = unrotate(
        key_grad_here.reshape(pair_rows, seq_here, KV_HEADS, HEAD_DIM), cosines, sines
    )
    grad_key_low = grad_key_low.astype(jnp.bfloat16).reshape(tokens_here, KVD)
    grad_value_low = value_grad_here.astype(jnp.bfloat16).reshape(tokens_here, KVD)
    projection_grads = jnp.concatenate([grad_query_low, grad_key_low, grad_value_low], axis=1)
    attn_grad = lax.psum_scatter(
        jnp.concatenate(
            [inner_rows(hidden1, projection_grads), inner_rows(mixed_low, grad_out_low)], axis=1
        ).astype(jnp.bfloat16),
        "fsdp",
        scatter_dimension=0,
        tiled=True,
    ).astype(jnp.float32)
    grad_hidden1 = (
        times_transposed(grad_query_low, query_all)
        + times_transposed(grad_key_low, key_all)
        + times_transposed(grad_value_low, value_all)
    )
    gain1_here = jnp.sum(grad_hidden1 * normed1, axis=0)
    scaled1 = grad_hidden1 * gain1
    grad_inputs = grad_resid1 + inverse1 * (
        scaled1 - normed1 * jnp.mean(scaled1 * normed1, axis=1, keepdims=True)
    )
    gain1_all, gain2_all = lax.psum((gain1_here, gain2_here), ("ctx", "fsdp"))
    gain_rows = norm1_gain.shape[0]
    fsdp_here = lax.axis_index("fsdp")
    gain1_grad = lax.dynamic_slice_in_dim(gain1_all, fsdp_here * gain_rows, gain_rows, 0)
    gain2_grad = lax.dynamic_slice_in_dim(gain2_all, fsdp_here * gain_rows, gain_rows, 0)
    query_grad = attn_grad[:, :QD]
    key_grad = attn_grad[:, QD : QD + KVD]
    value_grad = attn_grad[:, QD + KVD : QD + 2 * KVD]
    out_grad = attn_grad[:, QD + 2 * KVD :]
    gate_grad = gate_up_grad[:, :FF]
    up_grad = gate_up_grad[:, FF:]
    query_grad, key_grad, value_grad, out_grad, gate_grad, up_grad, down_grad = (
        lax.psum(query_grad.astype(jnp.bfloat16), "ctx").astype(jnp.float32),
        lax.psum(key_grad.astype(jnp.bfloat16), "ctx").astype(jnp.float32),
        lax.psum(value_grad.astype(jnp.bfloat16), "ctx").astype(jnp.float32),
        lax.psum(out_grad.astype(jnp.bfloat16), "ctx").astype(jnp.float32),
        lax.psum(gate_grad.astype(jnp.bfloat16), "ctx").astype(jnp.float32),
        lax.psum(up_grad.astype(jnp.bfloat16), "ctx").astype(jnp.float32),
        lax.psum(down_grad.astype(jnp.bfloat16), "ctx").astype(jnp.float32),
    )
    return (
        result.astype(jnp.bfloat16),
        loss_value,
        grad_inputs,
        gain1_grad,
        query_grad,
        key_grad,
        value_grad,
        out_grad,
        gain2_grad,
        gate_grad,
        up_grad,
        down_grad,
    )


def solution(mesh):
    placed = (
        P(("ctx", "fsdp"), None),
        P(("ctx", "fsdp"), None),
        P("fsdp", None),
        P(("ctx", "fsdp")),
        P("fsdp"),
        P("fsdp", None),
        P("fsdp", None),
        P("fsdp", None),
        P("fsdp", None),
        P("fsdp"),
        P("fsdp", None),
        P("fsdp", None),
        P("fsdp", None),
    )
    return jax.shard_map(
        local,
        mesh=mesh,
        in_specs=placed,
        out_specs=(
            P(("ctx", "fsdp"), None),
            P(),
            P(("ctx", "fsdp"), None),
            P("fsdp"),
            P("fsdp", None),
            P("fsdp", None),
            P("fsdp", None),
            P("fsdp", None),
            P("fsdp"),
            P("fsdp", None),
            P("fsdp", None),
            P("fsdp", None),
        ),
        check_vma=False,
    )
```

profile of v0, /device:TPU:1, one launch (start us, length us, event | category | flops | bytes accessed | tf_op | source)
XLA Modules:
  0.0 2013.1 jit_solution(1407754395076970668)
XLA Ops:
  17.6 20.9 %all-gather.2 = bf16[16,1,128]{2,1,0:T(2,128)(2,1)S(1)} all-gather(bf16[1,1,128]{2,1,0:T(2,128)(2,1)S(1)} %bitcast.192), channel_id=1, replica_groups=mesh['ctx'=8,'fsdp'=16] {'fsdp'}, dimensions={0}, use_global_device_ids=true | all-gather | bytes 4352 | tf_op jit(solution)/shard_map/all_gather | solution.py:159
  38.5 16.1 all-gather.3
  57.7 30.9 %all-gather.1 = bf16[1024,256]{1,0:T(8,128)(2,1)S(1)} all-gather(bf16[128,256]{1,0:T(8,128)(2,1)S(1)} %add_convert_fusion), channel_id=3, replica_groups=mesh['ctx'=8,'fsdp'=16] {'ctx'}, dimensions={0}, use_global_device_ids=true | all-gather | bytes 589824 | tf_op jit(solution)/shard_map/all_gather | solution.py:182
  90.5 31.6 %all-gather = bf16[1024,256]{1,0:T(8,128)(2,1)S(1)} all-gather(bf16[128,256]{1,0:T(8,128)(2,1)S(1)} %convolution_convert_fusion.5), channel_id=2, replica_groups=mesh['ctx'=8,'fsdp'=16] {'ctx'}, dimensions={0}, use_global_device_ids=true | all-gather | bytes 589824 | tf_op jit(solution)/shard_map/all_gather | solution.py:183
  122.3 17.3 all-gather.16.cloned.1.call-done
  139.6 6.9 fusion.78
  146.9 7.3 fusion.88
  154.2 8.7 fusion.3
  163.0 8.0 fusion.28
  170.9 22.1 %all-gather.18.cloned.1.call-done = bf16[2048,2048]{1,0:T(8,128)(2,1)} async-done(((bf16[128,2048]{1,0:T(8,128)(2,1)}), bf16[2048,2048]{1,0:T(8,128)(2,1)}) %all-gather.18.cloned.1.call-update) | async-done | bytes 8388624 | tf_op jit(solution)/shard_map/all_gather | solution.py:163
  198.6 118.1 %all-gather.20.cloned.1.call-done = bf16[2048,5632]{1,0:T(8,128)(2,1)} async-done(((bf16[128,5632]{1,0:T(8,128)(2,1)}), bf16[2048,5632]{1,0:T(8,128)(2,1)}) %all-gather.20.cloned.1.call-update) | async-done | bytes 23068688 | tf_op jit(solution)/shard_map/all_gather | solution.py:198
  316.7 12.4 fusion.89
  329.2 111.1 %all-gather.22.cloned.1.call-done = bf16[2048,5632]{1,0:T(8,128)(2,1)} async-done(((bf16[128,5632]{1,0:T(8,128)(2,1)}), bf16[2048,5632]{1,0:T(8,128)(2,1)}) %all-gather.22.cloned.1.call-update) | async-done | bytes 23068688 | tf_op jit(solution)/shard_map/all_gather | solution.py:199
  440.3 14.0 multiply_convert_fusion.2
  454.3 109.6 %all-gather.24.cloned.1.call-done = bf16[5632,2048]{1,0:T(8,128)(2,1)} async-done(((bf16[352,2048]{1,0:T(8,128)(2,1)}), bf16[5632,2048]{1,0:T(8,128)(2,1)}) %all-gather.24.cloned.1.call-update) | async-done | bytes 23068688 | tf_op jit(solution)/shard_map/all_gather | solution.py:210
  563.9 12.4 multiply_reduce_fusion.2
  577.0 66.2 %psum.78 = f32[]{:T(128)} all-reduce(f32[]{:T(128)} %get-tuple-element.57), channel_id=1, replica_groups=mesh['ctx'=8,'fsdp'=16] {'ctx','fsdp'}, use_global_device_ids=true, to_apply=%region_8.9 | all-reduce | flops 1 | bytes 8 | tf_op jit(solution)/shard_map/psum | solution.py:218
  643.8 14.9 multiply_convert_fusion
  658.7 13.4 fusion.90
  672.2 14.3 multiply_reduce_fusion
  695.7 9.3 fusion.24
  705.0 10.8 fusion
  717.9 11.8 fusion.8
  749.8 54.2 %reduce-scatter.16.cloned.1.call-done = bf16[128,256]{1,0:T(8,128)(2,1)} async-done(((bf16[1024,256]{1,0:T(8,128)(2,1)}), bf16[128,256]{1,0:T(8,128)(2,1)}) %reduce-scatter.16.cloned.1.call-update) | async-done | bytes 65552
  805.1 72.4 %reduce-scatter.18.cloned.1.call-done = bf16[128,256]{1,0:T(8,128)(2,1)} async-done(((bf16[1024,256]{1,0:T(8,128)(2,1)}), bf16[128,256]{1,0:T(8,128)(2,1)}) %reduce-scatter.18.cloned.1.call-update) | async-done | bytes 65552 | tf_op jit(solution)/shard_map/reshape | solution.py:274
  882.8 13.6 pad_maximum_fusion
  897.4 20.7 %convolution_convert_fusion = bf16[2048,11264]{1,0:T(8,128)(2,1)} fusion(bf16[128,2048]{1,0:T(8,128)(2,1)S(1)} %copy-done.9, bf16[128,5632]{1,0:T(8,128)(2,1)} %copy-done.4, bf16[128,5632]{1,0:T(8,128)(2,1)} %get-tuple-element.80), kind=kOutput, calls=%fused_computation.2 | convolution fusion | flops 5934415872 | bytes 49545216 | tf_op jit(solution)/shard_map/dot_general | solution.py:70
  919.5 12.5 convolution_convert_fusion.1
  932.3 167.0 %reduce-scatter.10.cloned.1.call-done = bf16[128,4608]{1,0:T(8,128)(2,1)} async-done(((bf16[2048,4608]{1,0:T(8,128)(2,1)}), bf16[128,4608]{1,0:T(8,128)(2,1)}) %reduce-scatter.10.cloned.1.call-update) | async-done | bytes 1179664 | tf_op jit(solution)/shard_map/reduce_scatter | solution.py:276
  1103.1 474.7 %reduce-scatter.12.cloned.1.call-done = bf16[128,11264]{1,0:T(8,128)(2,1)} async-done(((bf16[2048,11264]{1,0:T(8,128)(2,1)}), bf16[128,11264]{1,0:T(8,128)(2,1)}) %reduce-scatter.12.cloned.1.call-update) | async-done | bytes 2883600 | tf_op jit(solution)/shard_map/reduce_scatter | solution.py:233
  1581.3 243.0 %reduce-scatter.14.cloned.1.call-done = bf16[352,2048]{1,0:T(8,128)(2,1)} async-done(((bf16[5632,2048]{1,0:T(8,128)(2,1)}), bf16[352,2048]{1,0:T(8,128)(2,1)}) %reduce-scatter.14.cloned.1.call-update) | async-done | bytes 1441808 | tf_op jit(solution)/shard_map/reduce_scatter | solution.py:223
  1834.3 152.6 %all-reduce = (f32[]{:T(128)}, f32[2048]{0:T(1024)S(1)}, f32[2048]{0:T(1024)S(1)}) all-reduce(f32[]{:T(128)} %get-tuple-element.68, f32[2048]{0:T(1024)S(1)} %get-tuple-element.55, f32[2048]{0:T(1024)S(1)} %copy-done.30), channel_id=1, replica_groups=mesh['ctx'=8,'fsdp'=16] {'ctx','fsdp'}, use_global_device_ids=true, to_apply=%region_6.7 | all-reduce | flops 4097 | bytes 32776 | tf_op jit(solution)/shard_map/psum | solution.py:218
  (180 shorter events, 96.1 us)
Async XLA Ops:
  7.2 31.3 %copy-start.36 = (bf16[128]{0:T(256)(128)(2,1)S(1)}, bf16[128]{0:T(256)(128)(2,1)}, u32[]{:S(2)}) copy-start(bf16[128]{0:T(256)(128)(2,1)} %param.22) | copy-start | bytes 772
  7.2 47.9 %copy-start.3 = (bf16[128,2048]{1,0:T(8,128)(2,1)S(1)}, bf16[128,2048]{1,0:T(8,128)(2,1)}, u32[]{:S(2)}) copy-start(bf16[128,2048]{1,0:T(8,128)(2,1)} %param.13) | copy-start | bytes 1572868
  7.2 48.5 %all-gather.14.cloned.1.call-start = ((), (), s32[]{:S(2)}) async-start(), calls=%async_computation.6 | async-start | bytes 1114112 | tf_op jit(solution)/shard_map/all_gather | solution.py:161
  8.0 80.8 %all-gather.12.cloned.1.call-start = ((), (), s32[]{:S(2)}) async-start(), calls=%async_computation.5 | async-start | bytes 1114112 | tf_op jit(solution)/shard_map/all_gather | solution.py:162
  8.7 130.9 %all-gather.16.cloned.1.call-start = ((), (), s32[]{:S(2)}) async-start(), calls=%async_computation.7 | async-start | bytes 8912896 | tf_op jit(solution)/shard_map/all_gather | solution.py:160
  9.4 183.6 %all-gather.18.cloned.1.call-start = ((), (), s32[]{:S(2)}) async-start(), calls=%async_computation.8 | async-start | bytes 8912896 | tf_op jit(solution)/shard_map/all_gather | solution.py:163
  10.0 306.7 %all-gather.20.cloned.1.call-start = ((), (), s32[]{:S(2)}) async-start(), calls=%async_computation.9 | async-start | bytes 24510464 | tf_op jit(solution)/shard_map/all_gather | solution.py:198
  10.6 429.6 %all-gather.22.cloned.1.call-start = ((), (), s32[]{:S(2)}) async-start(), calls=%async_computation.10 | async-start | bytes 24510464 | tf_op jit(solution)/shard_map/all_gather | solution.py:199
  11.2 552.7 %all-gather.24.cloned.1.call-start = ((), (), s32[]{:S(2)}) async-start(), calls=%async_computation.11 | async-start | bytes 24510464 | tf_op jit(solution)/shard_map/all_gather | solution.py:210
  11.9 792.1 %reduce-scatter.16.cloned.1.call-start = ((), (), s32[]{:S(2)}) async-start(), calls=%async_computation.15 | async-start | bytes 589824
  38.5 108.0 %copy-start.26 = (f32[16,1,128]{2,1,0:T(1,128)}, f32[16,1,128]{2,1,0:T(1,128)S(1)}, u32[]{:S(2)}) copy-start(f32[16,1,128]{2,1,0:T(1,128)S(1)} %convert_element_type.242) | copy-start | bytes 24580
  54.8 91.8 %copy-start.22 = (f32[128,64]{0,1:T(8,128)}, f32[128,64]{0,1:T(8,128)S(1)}, u32[]{:S(2)}) copy-start(f32[128,64]{0,1:T(8,128)S(1)} %get-tuple-element.98) | copy-start | bytes 98308
  54.8 91.8 %copy-start.24 = (f32[128,64]{0,1:T(8,128)}, f32[128,64]{0,1:T(8,128)S(1)}, u32[]{:S(2)}) copy-start(f32[128,64]{0,1:T(8,128)S(1)} %get-tuple-element.97) | copy-start | bytes 98308
  55.3 91.2 %copy-start.31 = (f32[128]{0:T(128)}, f32[128]{0:T(128)S(1)}, u32[]{:S(2)}) copy-start(f32[128]{0:T(128)S(1)} %add_rsqrt_fusion.1) | copy-start | bytes 1540
  88.7 58.1 %copy-start.12 = (bf16[1024,256]{0,1:T(8,128)(2,1)}, bf16[1024,256]{0,1:T(8,128)(2,1)S(1)}, u32[]{:S(2)}) copy-start(bf16[1024,256]{0,1:T(8,128)(2,1)S(1)} %copy.63) | copy-start | bytes 1572868
  122.3 40.6 %copy-start.18 = (bf16[1024,256]{0,1:T(8,128)(2,1)}, bf16[1024,256]{0,1:T(8,128)(2,1)S(1)}, u32[]{:S(2)}) copy-start(bf16[1024,256]{0,1:T(8,128)(2,1)S(1)} %copy.58) | copy-start | bytes 1572868
  198.6 130.6 %copy-start.8 = (bf16[128,2048]{1,0:T(8,128)(2,1)}, bf16[128,2048]{1,0:T(8,128)(2,1)S(1)}, u32[]{:S(2)}) copy-start(bf16[128,2048]{1,0:T(8,128)(2,1)S(1)} %multiply_convert_fusion.3) | copy-start | bytes 1572868
  454.3 122.1 %copy-start.7 = (bf16[128,5632]{1,0:T(8,128)(2,1)}, bf16[128,5632]{1,0:T(8,128)(2,1)S(1)}, u32[]{:S(2)}) copy-start(bf16[128,5632]{1,0:T(8,128)(2,1)S(1)} %get-tuple-element.104) | copy-start | bytes 4325380
  577.0 109.6 %copy-start.33 = (f32[128]{0:T(128)}, f32[128]{0:T(128)S(1)}, u32[]{:S(2)}) copy-start(f32[128]{0:T(128)S(1)} %get-tuple-element.99) | copy-start | bytes 1540
  672.2 14.4 copy-start.5
  672.2 14.4 copy-start.10
  717.9 15.0 copy-start.17
  738.4 139.1 %reduce-scatter.18.cloned.1.call-start = ((), (), s32[]{:S(2)}) async-start(), calls=%async_computation.16 | async-start | bytes 589824 | tf_op jit(solution)/shard_map/reshape | solution.py:274
  743.9 138.8 %copy-start.14 = (bf16[128,2048]{0,1:T(8,128)(2,1)}, bf16[128,2048]{0,1:T(8,128)(2,1)S(1)}, u32[]{:S(2)}) copy-start(bf16[128,2048]{0,1:T(8,128)(2,1)S(1)} %fusion.41) | copy-start | bytes 1572868
  744.0 134.5 %copy-start.27 = (f32[16,1,128]{2,1,0:T(1,128)S(1)}, f32[16,1,128]{2,1,0:T(1,128)}, u32[]{:S(2)}) copy-start(f32[16,1,128]{2,1,0:T(1,128)} %copy-done.26) | copy-start | bytes 24580
  744.0 134.5 %copy-start.32 = (f32[128]{0:T(128)S(1)}, f32[128]{0:T(128)}, u32[]{:S(2)}) copy-start(f32[128]{0:T(128)} %copy-done.31) | copy-start | bytes 1540
  744.0 355.3 %reduce-scatter.10.cloned.1.call-start = ((), (), s32[]{:S(2)}) async-start(), calls=%async_computation.12 | async-start | bytes 20054016 | tf_op jit(solution)/shard_map/reduce_scatter | solution.py:276
  896.4 681.3 %reduce-scatter.12.cloned.1.call-start = ((), (), s32[]{:S(2)}) async-start(), calls=%async_computation.13 | async-start | bytes 49020928 | tf_op jit(solution)/shard_map/reduce_scatter | solution.py:233
  918.1 906.1 %reduce-scatter.14.cloned.1.call-start = ((), (), s32[]{:S(2)}) async-start(), calls=%async_computation.14 | async-start | bytes 24510464 | tf_op jit(solution)/shard_map/reduce_scatter | solution.py:223
  932.0 892.3 %copy-start.15 = (bf16[128,2048]{0,1:T(8,128)(2,1)S(1)}, bf16[128,2048]{0,1:T(8,128)(2,1)}, u32[]{:S(2)}) copy-start(bf16[128,2048]{0,1:T(8,128)(2,1)} %copy-done.14) | copy-start | bytes 1572868
  932.0 1058.7 %all-reduce.4.cloned.1.call-start = ((), (), s32[]{:S(2)}) async-start(), calls=%async_computation.17 | async-start | bytes 11010048 | tf_op jit(solution)/shard_map/psum | solution.py:306
  1989.4 15.8 copy-start.1
  (19 other events, 137.8 us)
Sparse Core Ops, SparseCore 0:
  9.8 35.9 all-gather.13
  47.5 32.5 all-gather.11
  81.8 57.7 all-gather.15
  141.2 51.7 all-gather.17
  194.6 122.1 all-gather.19
  318.3 121.9 all-gather.21
  442.0 121.9 all-gather.23
  738.6 65.4 reduce-scatter.15
  808.0 69.4 reduce-scatter.17
  896.5 202.6 reduce-scatter.9
  1101.7 475.9 reduce-scatter.11
  1580.0 244.2 reduce-scatter.13
  1828.5 134.8 all-reduce.3
where the time goes:
time: 2020 us; the launch traced here: 2010 us
  waiting for transfers between devices  1390 us (69%)
  blocking collectives  318 us (16%)
  matrix products  200 us (10%)
  other arithmetic  55.5 us (3%)
  local copies, waits for them, and re-layouts  26.7 us (1%)
    reduce_scatter x1, waiting for transfers between devices, local(): lax.psum_scatter(inner_rows(columns, both_grads).astype(jnp.bfloat16), 'f...  475 us
    reduce_scatter x1, waiting for transfers between devices, local(): lax.psum_scatter(inner_rows(columns, grad_low).astype(jnp.bfloat16), 'fsd...  243 us
    psum x2, blocking collectives, local(): lax.psum((squares_here, count_here), ('ctx', 'fsdp'))  219 us
    reduce_scatter x1, waiting for transfers between devices, local(): lax.psum_scatter(jnp.concatenate([inner_rows(hidden1, projection_grads),...  167 us
    all_gather x1, waiting for transfers between devices, local(): gate_piece = lax.all_gather(w_gate, 'fsdp', axis=0, tiled=True)  118 us
    all_gather x1, waiting for transfers between devices, local(): up_piece = lax.all_gather(w_up, 'fsdp', axis=0, tiled=True)  111 us
    all_gather x1, waiting for transfers between devices, local(): lax.all_gather(w_down, 'fsdp', axis=0, tiled=True)  110 us
    reshape x1, waiting for transfers between devices, local(): value_grad_here.astype(jnp.bfloat16).reshape(tokens_here, KVD)  72.4 us
  transfers between devices with their start and end apart: 13, of which 10 were waited for; matrix products, arithmetic and copies ran while one was open for 7% of the time, Pallas kernels for 0%

commit v1 on v0

v1 whole, which is shorter than its diff:
```python
import math

import jax
import jax.numpy as jnp
from jax import lax
from jax.sharding import Mesh, PartitionSpec as P

D = 2048
HEADS = 32
KV_HEADS = 4
HD = 64
FF = 5632
KVD = 256
EPSILON = 1e-05
THETA = 10000.0
NEGATIVE = -1e30
AXES = ("y_hi", "z", "x", "y_lo", "core")
TP = ("x", "core")
CTX = ("y_hi", "z")
BF = jnp.bfloat16
F32 = jnp.float32


def dot(a, b, ca, cb):
    return lax.dot_general(a, b, (((ca,), (cb,)), ((), ())), preferred_element_type=F32)


def tables(positions):
    indices = jnp.arange(HD // 2, dtype=jnp.int32).astype(F32)
    frequency = THETA ** (-(indices * 2.0 / HD))
    angles = positions.astype(F32)[:, None] * frequency[None, :]
    angles = jnp.concatenate([angles, angles], axis=1)
    return jnp.cos(angles), jnp.sin(angles)


def positions_of(c):
    t = jnp.arange(64, dtype=jnp.int32)
    return jnp.concatenate([c * 64 + t, (15 - c) * 64 + t])


def rotate(u, cos, sin):
    turned = jnp.concatenate([-u[..., HD // 2 :], u[..., : HD // 2]], axis=-1)
    return u * cos + turned * sin


def unrotate(w, cos, sin):
    s = w * sin
    turned = jnp.concatenate([s[..., HD // 2 :], -s[..., : HD // 2]], axis=-1)
    return w * cos + turned


def ag_tp(v):
    return lax.all_gather(v, TP, axis=0, tiled=True)


def rs_tp(v):
    return lax.psum_scatter(v.astype(BF), TP, scatter_dimension=0, tiled=True).astype(F32)


def spread_columns(w):
    n = w.shape[1] // 16
    parts = w.reshape(128, 4, 2, 2, n).transpose(1, 3, 0, 2, 4).reshape(8, 128, 2 * n)
    got = lax.all_to_all(parts, TP, 0, 0)
    got = lax.all_gather(got, "y_lo", axis=0)
    got = got.reshape(2, 4, 2, 128, 2 * n).transpose(1, 0, 2, 3, 4)
    return got.reshape(D, 2 * n)


def spread_kv(w):
    parts = w.reshape(128, 4, 1, 64).transpose(1, 2, 0, 3)
    parts = jnp.broadcast_to(parts, (4, 2, 128, 64)).reshape(8, 128, 64)
    got = lax.all_to_all(parts, TP, 0, 0)
    got = lax.all_gather(got, "y_lo", axis=0)
    return got.reshape(2, 4, 2, 128, 64).transpose(1, 0, 2, 3, 4).reshape(D, 64)


def return_rows(g):
    n = g.shape[1]
    g = g.astype(BF).reshape(4, 2, 2, 8, 16, n).transpose(1, 3, 0, 2, 4, 5)
    g = lax.psum_scatter(g.reshape(16, 8 * 16, n), ("y_lo", "y_hi", "z"), scatter_dimension=0, tiled=True)
    g = lax.all_to_all(g.reshape(8, 16, n), TP, 0, 0)
    g = lax.all_gather(g, CTX, axis=0)
    return g.transpose(0, 2, 1, 3).reshape(128, 8, n).astype(F32)


def return_columns(g):
    r = g.shape[0] // 2
    g = g.astype(BF).reshape(2, r, 8, 256).transpose(0, 2, 1, 3).reshape(16, r, 256)
    g = lax.psum_scatter(g, ("y_lo", "y_hi", "z"), scatter_dimension=0, tiled=True)
    g = lax.all_gather(g.reshape(r, 256), CTX, axis=1, tiled=True)
    return g.astype(F32)


def local(hidden_in, teacher, doc_ids, valid_mask, norm1_gain, w_query, w_key, w_value, w_out, norm2_gain, w_gate, w_up, w_down):
    c = lax.axis_index(CTX)
    factor = 1.0 / math.sqrt(HD)
    g1 = norm1_gain.astype(F32)
    g2 = norm2_gain.astype(F32)
    valid = valid_mask.astype(F32)
    count = lax.psum(jnp.sum(valid), AXES)

    def fold(g, w):
        return (g[:, None] * w.astype(F32)).astype(BF)

    wqkv = jnp.concatenate([spread_columns(fold(g1, w_query)), spread_kv(fold(g1, w_key)), spread_kv(fold(g1, w_value))], axis=1)
    wgu = jnp.concatenate([spread_columns(fold(g2, w_gate)), spread_columns(fold(g2, w_up))], axis=1)
    wo = lax.all_gather(w_out, "y_lo", axis=0, tiled=True)
    wd = lax.all_gather(w_down, "y_lo", axis=0, tiled=True)
    docs = ag_tp(doc_ids)

    qpos = positions_of(c)
    kpos = jax.vmap(positions_of)(jnp.arange(8, dtype=jnp.int32)).reshape(1024)
    cos, sin = tables(qpos)
    qdoc = jnp.take(docs, qpos, axis=1)
    kdoc = jnp.take(docs, kpos, axis=1)
    allowed = (qpos[:, None] >= kpos[None, :])[None] & (qdoc[:, :, None] == kdoc[:, None, :])

    x = hidden_in.astype(F32)
    r1 = lax.rsqrt(jnp.mean(x * x, axis=1, keepdims=True) + EPSILON)
    n1 = x * r1
    n1_all = ag_tp(n1.astype(BF))
    qkv = dot(n1_all, wqkv, 1, 0)
    q = rotate(qkv[:, :256].reshape(8, 128, 4, HD), cos[None, :, None], sin[None, :, None]).astype(BF)
    k = rotate(qkv[:, 256:320].reshape(8, 128, HD), cos[None], sin[None]).astype(BF)
    v = qkv[:, 320:].reshape(8, 128, HD).astype(BF)
    kv = lax.all_gather(jnp.concatenate([k, v], axis=2), CTX, axis=1, tiled=True)
    k_all, v_all = kv[..., :HD], kv[..., HD:]

    s = jnp.einsum("sqhd,skd->shqk", q, k_all, preferred_element_type=F32) * factor
    s = jnp.where(allowed[:, None], s, NEGATIVE)
    top = jnp.max(s, axis=-1, keepdims=True)
    e = jnp.exp(s - top)
    total = jnp.sum(e, axis=-1, keepdims=True)
    lse = top + jnp.log(total)
    a = jnp.einsum("shqk,skd->sqhd", (e / total).astype(BF), v_all, preferred_element_type=F32)
    a = a.astype(BF).reshape(1024, 256)

    y1 = x + rs_tp(dot(a, wo, 1, 0))
    r2 = lax.rsqrt(jnp.mean(y1 * y1, axis=1, keepdims=True) + EPSILON)
    n2 = y1 * r2
    n2_all = ag_tp(n2.astype(BF))
    gu = dot(n2_all, wgu, 1, 0)
    gate, up = gu[:, :704], gu[:, 704:]
    sg = jax.nn.sigmoid(gate)
    act = gate * sg
    mid = (act * up).astype(BF)
    y = y1 + rs_tp(dot(mid, wd, 1, 0))
    miss = y - teacher.astype(F32)
    loss_here = jnp.sum(valid * jnp.mean(miss * miss, axis=1))
    dy = valid[:, None] * miss
    dy_all = ag_tp(dy.astype(BF))

    grad_down = dot(mid, dy_all, 0, 0)
    dmid = dot(dy_all, wd, 1, 1)
    dgate = (dmid * up * sg * (1.0 + gate * (1.0 - sg))).astype(BF)
    dup = (dmid * act).astype(BF)
    dgu = jnp.concatenate([dgate, dup], axis=1)
    grad_gu = dot(n2_all, dgu, 0, 0)
    u2 = rs_tp(dot(dgu, wgu, 1, 1))
    dy1 = dy + r2 * (u2 - n2 * jnp.mean(u2 * n2, axis=1, keepdims=True))
    da_all = ag_tp(dy1.astype(BF))
    grad_out = dot(a, da_all, 0, 0)
    da = dot(da_all, wo, 1, 1).astype(BF).reshape(8, 128, 4, HD)

    s = jnp.einsum("sqhd,skd->shqk", q, k_all, preferred_element_type=F32) * factor
    probs = jnp.exp(jnp.where(allowed[:, None], s, NEGATIVE) - lse)
    dv = jnp.einsum("shqk,sqhd->skd", probs.astype(BF), da, preferred_element_type=F32)
    dp = jnp.einsum("sqhd,skd->shqk", da, v_all, preferred_element_type=F32)
    ds = (probs * (dp - jnp.sum(probs * dp, axis=-1, keepdims=True))).astype(BF)
    dq = jnp.einsum("shqk,skd->sqhd", ds, k_all, preferred_element_type=F32) * factor
    dk = jnp.einsum("shqk,sqhd->skd", ds, q, preferred_element_type=F32) * factor
    dkv = jnp.concatenate([dk, dv], axis=2).astype(BF)
    dkv = lax.psum_scatter(dkv, CTX, scatter_dimension=1, tiled=True).astype(F32)
    dq = unrotate(dq, cos[None, :, None], sin[None, :, None]).astype(BF).reshape(1024, 256)
    dk = unrotate(dkv[..., :HD], cos[None], sin[None]).astype(BF).reshape(1024, HD)
    dv = dkv[..., HD:].astype(BF).reshape(1024, HD)
    dqkv = jnp.concatenate([dq, dk, dv], axis=1)
    grad_qkv = dot(n1_all, dqkv, 0, 0)
    u1 = rs_tp(dot(dqkv, wqkv, 1, 1))
    loss = lax.psum(loss_here, AXES) / count
    scale = 2.0 / (D * count)
    input_grad = (dy1 + r1 * (u1 - n1 * jnp.mean(u1 * n1, axis=1, keepdims=True))) * scale

    ga = return_rows(jnp.concatenate([grad_qkv, grad_gu], axis=1))
    gb = return_columns(jnp.concatenate([grad_out.reshape(2, 128, D), grad_down.reshape(2, 352, D)], axis=1).reshape(960, D))

    def columns(part):
        n = part.shape[2] // 2
        return part.reshape(128, 4, 2, 2, n).transpose(0, 1, 3, 2, 4).reshape(128, 16 * n)

    gq = columns(ga[:, :, :256])
    gk = ga[:, :, 256:320].reshape(128, 4, 2, HD).sum(2).reshape(128, KVD)
    gv = ga[:, :, 320:384].reshape(128, 4, 2, HD).sum(2).reshape(128, KVD)
    gg = columns(ga[:, :, 384 : 384 + 704])
    gp = columns(ga[:, :, 384 + 704 :])

    def rowsum(w, g):
        return jnp.sum(w.astype(F32) * g, axis=1)

    gain1 = (rowsum(w_query, gq) + rowsum(w_key, gk) + rowsum(w_value, gv)) * scale
    gain2 = (rowsum(w_gate, gg) + rowsum(w_up, gp)) * scale
    s1 = (g1 * scale)[:, None]
    s2 = (g2 * scale)[:, None]
    return (
        y.astype(BF), loss, input_grad, gain1, gq * s1, gk * s1, gv * s1, gb[:128] * scale,
        gain2, gg * s2, gp * s2, gb[128:] * scale,
    )


def solution(mesh):
    fine = Mesh(mesh.devices.reshape(2, 4, 4, 2, 2), AXES)
    rows = ("y_hi", "z", "x", "y_lo", "core")
    fs = ("x", "y_lo", "core")
    token, shard = P(rows, None), P(fs, None)
    return jax.shard_map(
        local,
        mesh=fine,
        in_specs=(token, token, shard, P(rows), P(fs), shard, shard, shard, shard, P(fs), shard, shard, shard),
        out_specs=(token, P(), token, P(fs), shard, shard, shard, shard, P(fs), shard, shard, shard),
        check_vma=False,
    )
```

time: 2020 us -> 1110 us (0.55)
  waiting for transfers between devices: 1390 us -> 591 us
  blocking collectives: 318 us -> 188 us
  local copies, waits for them, and re-layouts: 26.7 us -> 109 us
  matrix products: 200 us -> 126 us
    reduce_scatter x3 -> x6, waiting for transfers between devices: 885 us -> 229 us  [the longest x1 93.8 us: return_rows(): lax.psum_scatter(g.reshape(16, 8 * 16, n), ('y_lo', 'y_hi', 'z'), scatter...]
    psum x2 -> x1, blocking collectives: 219 us -> 67.3 us  [local(): loss = lax.psum(loss_here, AXES) / count]
    all_to_all x0 -> x4, blocking collectives: none -> 94.5 us  [the longest x3 72.7 us: spread_columns(): got = lax.all_to_all(parts, TP, 0, 0)]
    dot_general x24 -> x18, matrix products: 200 us -> 126 us  [the longest x12 81.4 us: dot(): lax.dot_general(a, b, (((ca,), (cb,)), ((), ())), preferred_element_type=...]
    all_gather x4 -> x3, blocking collectives: 99.4 us -> 26.4 us  [the longest x2 13.4 us: spread_kv(): got = lax.all_gather(got, 'y_lo', axis=0)]
    reshape x1 -> x0, waiting for transfers between devices: 72.4 us -> none  [local(): value_grad_here.astype(jnp.bfloat16).reshape(tokens_here, KVD)]
    all_gather x7 -> x12, waiting for transfers between devices: 378 us -> 322 us  [the longest x4 115 us: ag_tp(): return lax.all_gather(v, TP, axis=0, tiled=True)]
    unnamed x79 -> x126, local copies, waits for them, and re-layouts: 10.7 us -> 36 us
  transfers between devices with their start and end apart: 13 -> 21, of which waited for: 10 -> 16; matrix products, arithmetic and copies ran while one was open for 7% -> 14% of each run, Pallas kernels for 0% -> 0%
where the time goes in v1:
time: 1110 us; the launch traced here: 1100 us
  waiting for transfers between devices  591 us (53%)
  blocking collectives  188 us (17%)
  matrix products  126 us (11%)
  local copies, waits for them, and re-layouts  109 us (10%)
  other arithmetic  62.1 us (6%)
  between operations  18.5 us (2%)
    all_gather x4, waiting for transfers between devices, ag_tp(): return lax.all_gather(v, TP, axis=0, tiled=True)  115 us
    reduce_scatter x1, waiting for transfers between devices, return_rows(): lax.psum_scatter(g.reshape(16, 8 * 16, n), ('y_lo', 'y_hi', 'z'), scatter...  93.8 us
    dot_general x12, matrix products, dot(): lax.dot_general(a, b, (((ca,), (cb,)), ((), ())), preferred_element_type=...  81.4 us
    all_gather x3, waiting for transfers between devices, spread_columns(): got = lax.all_gather(got, 'y_lo', axis=0)  75.5 us
    all_to_all x3, blocking collectives, spread_columns(): got = lax.all_to_all(parts, TP, 0, 0)  72.7 us
    reduce_scatter x4, waiting for transfers between devices, rs_tp(): lax.psum_scatter(v.astype(BF), TP, scatter_dimension=0, tiled=True)  72.2 us
    psum x1, blocking collectives, local(): loss = lax.psum(loss_here, AXES) / count  67.3 us
    all_gather x1, waiting for transfers between devices, return_rows(): g = lax.all_gather(g, CTX, axis=0)  67.3 us
  transfers between devices with their start and end apart: 21, of which 16 were waited for; matrix products, arithmetic and copies ran while one was open for 14% of the time, Pallas kernels for 0%

profile of v1, /device:TPU:1, one launch (start us, length us, event | category | flops | bytes accessed | tf_op | source)
XLA Modules:
  0.0 1104.6 jit_solution(16665262432504130767)
XLA Ops:
  9.5 15.1 %all_to_all.30 = bf16[8,128,256]{1,2,0:T(8,128)(2,1)S(1)} all-to-all(bf16[8,128,256]{1,2,0:T(8,128)(2,1)S(1)} %bitcast.271), channel_id=1, replica_groups=mesh['y_hi'=2,'z'=4,'x'=4,'y_lo'=2,'core'=2] {'x','core'}, dimensions={0} | all-to-all | bytes 1048576 | tf_op jit(solution)/shard_map/all_to_all | solution.py:63
  43.0 8.9 all-gather.2
  60.0 28.8 %all-gather.21.cloned.1.call-done = bf16[1024,2048]{1,0:T(8,128)(2,1)} async-done(((bf16[128,2048]{1,0:T(8,128)(2,1)}), bf16[1024,2048]{1,0:T(8,128)(2,1)}) %all-gather.21.cloned.1.call-update) | async-done | bytes 4194320 | tf_op jit(solution)/shard_map/all_gather | solution.py:53
  95.2 13.1 %all-gather.7 = s32[8,1,1024]{2,1,0:T(1,128)S(1)} all-gather(s32[1,1,1024]{2,1,0:T(1,128)S(1)} %bitcast.302), channel_id=1, replica_groups=mesh['y_hi'=2,'z'=4,'x'=4,'y_lo'=2,'core'=2] {'x','core'}, dimensions={0}, use_global_device_ids=true | all-gather | bytes 36864 | tf_op jit(solution)/shard_map/all_gather | solution.py:53
  116.0 32.1 %all-gather.23.cloned.1.call-done = bf16[8,1024,128]{1,2,0:T(8,128)(2,1)} async-done(((bf16[8,128,128]{1,2,0:T(8,128)(2,1)}), bf16[8,1024,128]{1,2,0:T(8,128)(2,1)}) %all-gather.23.cloned.1.call-update) | async-done | bytes 2097168 | tf_op jit(solution)/shard_map/all_gather | solution.py:126
  148.2 8.8 fusion.68
  157.0 8.7 fusion.3
  165.7 7.4 fusion.22
  184.4 32.4 %all_to_all.31 = bf16[8,128,704]{1,2,0:T(8,128)(2,1)} all-to-all(bf16[8,128,704]{1,2,0:T(8,128)(2,1)S(1)} %bitcast.259), channel_id=1, replica_groups=mesh['y_hi'=2,'z'=4,'x'=4,'y_lo'=2,'core'=2] {'x','core'}, dimensions={0} | all-to-all | bytes 2883584 | tf_op jit(solution)/shard_map/all_to_all | solution.py:63
  217.0 25.2 %all_to_all.32 = bf16[8,128,704]{1,2,0:T(8,128)(2,1)} all-to-all(bf16[8,128,704]{1,2,0:T(8,128)(2,1)S(1)} %bitcast.260), channel_id=1, replica_groups=mesh['y_hi'=2,'z'=4,'x'=4,'y_lo'=2,'core'=2] {'x','core'}, dimensions={0} | all-to-all | bytes 2883584 | tf_op jit(solution)/shard_map/all_to_all | solution.py:63
  246.9 41.0 %all-gather.37.cloned.1.call-done = bf16[16,128,704]{1,2,0:T(8,128)(2,1)} async-done(((bf16[8,128,704]{1,2,0:T(8,128)(2,1)}), bf16[16,128,704]{1,2,0:T(8,128)(2,1)}) %all-gather.37.cloned.1.call-update) | async-done | bytes 2883600 | tf_op jit(solution)/shard_map/all_gather | solution.py:64
  300.7 34.4 %all-gather.39.cloned.1.call-done = bf16[16,128,704]{1,2,0:T(8,128)(2,1)} async-done(((bf16[8,128,704]{1,2,0:T(8,128)(2,1)}), bf16[16,128,704]{1,2,0:T(8,128)(2,1)}) %all-gather.39.cloned.1.call-update) | async-done | bytes 2883600 | tf_op jit(solution)/shard_map/all_gather | solution.py:64
  341.5 7.4 reshape.519
  353.6 17.3 %all-gather.27.cloned.1.call-done = bf16[1024,2048]{1,0:T(8,128)(2,1)} async-done(((bf16[128,2048]{1,0:T(8,128)(2,1)}), bf16[1024,2048]{1,0:T(8,128)(2,1)}) %all-gather.27.cloned.1.call-update) | async-done | bytes 4194320 | tf_op jit(solution)/shard_map/all_gather | solution.py:53
  370.9 10.6 fusion.69
  385.0 31.7 %all-gather.29.cloned.1.call-done = bf16[704,2048]{1,0:T(8,128)(2,1)} async-done(((bf16[352,2048]{1,0:T(8,128)(2,1)}), bf16[704,2048]{1,0:T(8,128)(2,1)}) %all-gather.29.cloned.1.call-update) | async-done | bytes 2883600 | tf_op jit(solution)/shard_map/all_gather | solution.py:108
  424.3 35.4 %reduce-scatter.12.cloned.1.call-done = bf16[128,2048]{1,0:T(8,128)(2,1)} async-done(((bf16[1024,2048]{1,0:T(8,128)(2,1)}), bf16[128,2048]{1,0:T(8,128)(2,1)}) %reduce-scatter.12.cloned.1.call-update) | async-done | bytes 524304 | tf_op jit(solution)/shard_map/reduce_scatter | solution.py:57
  461.9 34.6 %all-gather.31.cloned.1.call-done = bf16[1024,2048]{1,0:T(8,128)(2,1)} async-done(((bf16[128,2048]{1,0:T(8,128)(2,1)}), bf16[1024,2048]{1,0:T(8,128)(2,1)}) %all-gather.31.cloned.1.call-update) | async-done | bytes 4194320 | tf_op jit(solution)/shard_map/all_gather | solution.py:53
  496.5 9.2 multiply_convert_fusion.1
  507.3 11.0 convolution_convert_fusion.2
  518.4 34.6 %reduce-scatter.14.cloned.1.call-done = bf16[128,2048]{1,0:T(8,128)(2,1)} async-done(((bf16[1024,2048]{1,0:T(8,128)(2,1)}), bf16[128,2048]{1,0:T(8,128)(2,1)}) %reduce-scatter.14.cloned.1.call-update) | async-done | bytes 524304 | tf_op jit(solution)/shard_map/reduce_scatter | solution.py:57
  557.7 34.4 %all-gather.33.cloned.1.call-done = bf16[1024,2048]{1,0:T(8,128)(2,1)} async-done(((bf16[128,2048]{1,0:T(8,128)(2,1)}), bf16[1024,2048]{1,0:T(8,128)(2,1)}) %all-gather.33.cloned.1.call-update) | async-done | bytes 4194320 | tf_op jit(solution)/shard_map/all_gather | solution.py:53
  596.9 9.5 bitcast_convert_fusion
  606.4 8.0 fusion
  614.4 10.2 fusion.2
  658.7 11.8 %convolution_convert_fusion = bf16[2048,1408]{1,0:T(8,128)(2,1)} fusion(bf16[1024,2048]{1,0:T(8,128)(2,1)} %all-gather.27.cloned.1.call-done, bf16[1024,704]{1,0:T(8,128)(2,1)} %copy-done.52, bf16[1024,704]{1,0:T(8,128)(2,1)} %copy-done.51), kind=kOutput, calls=%fused_computation.16 | convolution fusion | flops 5914230784 | bytes 12845056 | tf_op jit(solution)/shard_map/dot_general | solution.py:25
  676.9 34.0 %reduce-scatter.22.cloned.1.call-done = bf16[128,1024]{1,0:T(8,128)(2,1)} async-done(((bf16[1024,1024]{1,0:T(8,128)(2,1)}), bf16[128,1024]{1,0:T(8,128)(2,1)}) %reduce-scatter.22.cloned.1.call-update) | async-done | bytes 262160
  726.0 62.9 %reduce-scatter.20.cloned.1.call-done = bf16[1,480,256]{2,1,0:T(8,128)(2,1)} async-done(((bf16[16,480,256]{2,1,0:T(8,128)(2,1)}), bf16[1,480,256]{2,1,0:T(8,128)(2,1)}) %reduce-scatter.20.cloned.1.call-update) | async-done | bytes 245776 | tf_op jit(solution)/shard_map/reduce_scatter | solution.py:89
  794.8 93.8 %reduce-scatter.18.cloned.1.call-done = bf16[1,128,1792]{2,1,0:T(8,128)(2,1)} async-done(((bf16[16,128,1792]{2,1,0:T(8,128)(2,1)}), bf16[1,128,1792]{2,1,0:T(8,128)(2,1)}) %reduce-scatter.18.cloned.1.call-update) | async-done | bytes 458768 | tf_op jit(solution)/shard_map/reduce_scatter | solution.py:80
  888.7 21.8 %all_to_all.33 = bf16[8,16,1792]{2,1,0:T(8,128)(2,1)} all-to-all(bf16[8,16,1792]{2,1,0:T(8,128)(2,1)} %bitcast.290), channel_id=1, replica_groups=mesh['y_hi'=2,'z'=4,'x'=4,'y_lo'=2,'core'=2] {'x','core'}, dimensions={0} | all-to-all | bytes 917504 | tf_op jit(solution)/shard_map/all_to_all | solution.py:81
  911.1 67.3 %all-reduce = (f32[]{:T(128)}, f32[]{:T(128)}) all-reduce(f32[]{:T(128)} %get-tuple-element.63, f32[]{:T(128)} %get-tuple-element.62), channel_id=1, replica_groups=mesh['y_hi'=2,'z'=4,'x'=4,'y_lo'=2,'core'=2] {'y_hi','z','x','y_lo','core'}, use_global_device_ids=true, to_apply=%region_8.9 | all-reduce | flops 2 | bytes 16 | tf_op jit(solution)/shard_map/psum | solution.py:180
  991.4 67.3 %all-gather.41.cloned.1.call-done = bf16[64,16,1792]{2,1,0:T(8,128)(2,1)} async-done(((bf16[8,16,1792]{2,1,0:T(8,128)(2,1)}), bf16[64,16,1792]{2,1,0:T(8,128)(2,1)}) %all-gather.41.cloned.1.call-update) | async-done | bytes 3670032 | tf_op jit(solution)/shard_map/all_gather | solution.py:82
  (295 shorter events, 217.6 us)
Async XLA Ops:
  7.2 50.5 %all-gather.35.cloned.1.call-start = ((), (), s32[]{:S(2)}) async-start(), calls=%async_computation.26 | async-start | bytes 1572864 | tf_op jit(solution)/shard_map/all_gather | solution.py:64
  25.6 63.3 %all-gather.21.cloned.1.call-start = ((), (), s32[]{:S(2)}) async-start(), calls=%async_computation.13 | async-start | bytes 4718592 | tf_op jit(solution)/shard_map/all_gather | solution.py:53
  27.8 9.6 all-to-all-start.2
  38.1 14.1 %all-to-all-start.1 = ((bf16[8,128,64]{1,2,0:T(8,128)(2,1)}), bf16[8,128,64]{1,2,0:T(8,128)(2,1)S(1)}, u32[]{:S(2)}, u32[]{:S(2)}) async-start(bf16[8,128,64]{1,2,0:T(8,128)(2,1)} %bitcast.9), calls=%async_computation.1 | async-start | bytes 262144 | tf_op jit(solution)/shard_map/all_to_all | solution.py:72
  42.2 105.9 %all-gather.23.cloned.1.call-start = ((), (), s32[]{:S(2)}) async-start(), calls=%async_computation.14 | async-start | bytes 2359296 | tf_op jit(solution)/shard_map/all_gather | solution.py:126
  43.0 72.7 %copy-start.31 = (f32[128,64]{0,1:T(8,128)}, f32[128,64]{0,1:T(8,128)S(1)}, u32[]{:S(2)}) copy-start(f32[128,64]{0,1:T(8,128)S(1)} %get-tuple-element.102) | copy-start | bytes 98308
  43.0 72.7 %copy-start.33 = (f32[128,64]{0,1:T(8,128)}, f32[128,64]{0,1:T(8,128)S(1)}, u32[]{:S(2)}) copy-start(f32[128,64]{0,1:T(8,128)S(1)} %get-tuple-element.101) | copy-start | bytes 98308
  52.1 41.2 %copy-start.35 = (bf16[4,2,2,128,64]{4,3,2,1,0:T(8,128)(2,1)}, bf16[4,2,2,128,64]{4,3,2,1,0:T(8,128)(2,1)S(1)}, u32[]{:S(2)}) copy-start(bf16[4,2,2,128,64]{4,3,2,1,0:T(8,128)(2,1)S(1)} %copy.210) | copy-start | bytes 786436
  94.2 79.2 %all-gather.25.cloned.1.call-start = ((), (), s32[]{:S(2)}) async-start(), calls=%async_computation.15 | async-start | bytes 1572864 | tf_op jit(solution)/shard_map/all_gather | solution.py:107
  94.8 148.0 %reduce-scatter.10.cloned.1.call-start = ((), (), s32[]{:S(2)}) async-start(), calls=%async_computation.16 | async-start | bytes 4718592 | tf_op jit(solution)/shard_map/reduce_scatter | solution.py:57
  116.0 40.9 %copy-start.38 = (bf16[8,128,4,64]{1,3,2,0:T(8,128)(2,1)}, bf16[8,128,4,64]{1,3,2,0:T(8,128)(2,1)S(1)}, u32[]{:S(2)}) copy-start(bf16[8,128,4,64]{1,3,2,0:T(8,128)(2,1)S(1)} %fusion.35) | copy-start | bytes 1572868
  178.1 109.8 %all-gather.37.cloned.1.call-start = ((), (), s32[]{:S(2)}) async-start(), calls=%async_computation.27 | async-start | bytes 4325376 | tf_op jit(solution)/shard_map/all_gather | solution.py:64
  216.9 118.3 %all-gather.39.cloned.1.call-start = ((), (), s32[]{:S(2)}) async-start(), calls=%async_computation.28 | async-start | bytes 4325376 | tf_op jit(solution)/shard_map/all_gather | solution.py:64
  242.3 128.6 %all-gather.27.cloned.1.call-start = ((), (), s32[]{:S(2)}) async-start(), calls=%async_computation.17 | async-start | bytes 4718592 | tf_op jit(solution)/shard_map/all_gather | solution.py:53
  246.1 170.5 %all-gather.29.cloned.1.call-start = ((), (), s32[]{:S(2)}) async-start(), calls=%async_computation.18 | async-start | bytes 4325376 | tf_op jit(solution)/shard_map/all_gather | solution.py:108
  246.9 212.8 %reduce-scatter.12.cloned.1.call-start = ((), (), s32[]{:S(2)}) async-start(), calls=%async_computation.19 | async-start | bytes 4718592 | tf_op jit(solution)/shard_map/reduce_scatter | solution.py:57
  423.7 72.8 %all-gather.31.cloned.1.call-start = ((), (), s32[]{:S(2)}) async-start(), calls=%async_computation.20 | async-start | bytes 4718592 | tf_op jit(solution)/shard_map/all_gather | solution.py:53
  461.9 91.1 %reduce-scatter.14.cloned.1.call-start = ((), (), s32[]{:S(2)}) async-start(), calls=%async_computation.21 | async-start | bytes 4718592 | tf_op jit(solution)/shard_map/reduce_scatter | solution.py:57
  518.3 73.7 %all-gather.33.cloned.1.call-start = ((), (), s32[]{:S(2)}) async-start(), calls=%async_computation.22 | async-start | bytes 4718592 | tf_op jit(solution)/shard_map/all_gather | solution.py:53
  554.6 37.5 %copy-start.26 = (bf16[256,2048]{1,0:T(8,128)(2,1)S(1)}, bf16[256,2048]{1,0:T(8,128)(2,1)}, u32[]{:S(2)}) copy-start(bf16[256,2048]{1,0:T(8,128)(2,1)} %all-gather.25.cloned.1.call-done) | copy-start | bytes 3145732
  557.6 153.4 %reduce-scatter.22.cloned.1.call-start = ((), (), s32[]{:S(2)}) async-start(), calls=%async_computation.31 | async-start | bytes 2359296
  637.5 151.4 %reduce-scatter.20.cloned.1.call-start = ((), (), s32[]{:S(2)}) async-start(), calls=%async_computation.25 | async-start | bytes 4177920 | tf_op jit(solution)/shard_map/reduce_scatter | solution.py:89
  658.7 230.0 %reduce-scatter.18.cloned.1.call-start = ((), (), s32[]{:S(2)}) async-start(), calls=%async_computation.24 | async-start | bytes 7798784 | tf_op jit(solution)/shard_map/reduce_scatter | solution.py:80
  675.5 37.0 %copy-start.34 = (f32[128,64]{0,1:T(8,128)S(1)}, f32[128,64]{0,1:T(8,128)}, u32[]{:S(2)}) copy-start(f32[128,64]{0,1:T(8,128)} %copy-done.33) | copy-start | bytes 98308
  725.9 63.0 %copy-start.25 = (bf16[4,2,2,128,256]{4,3,2,1,0:T(8,128)(2,1)S(1)}, bf16[4,2,2,128,256]{4,3,2,1,0:T(8,128)(2,1)}, u32[]{:S(2)}) copy-start(bf16[4,2,2,128,256]{4,3,2,1,0:T(8,128)(2,1)} %copy.206) | copy-start | bytes 3145732
  725.9 63.0 %copy-start.36 = (bf16[4,2,2,128,64]{4,3,2,1,0:T(8,128)(2,1)S(1)}, bf16[4,2,2,128,64]{4,3,2,1,0:T(8,128)(2,1)}, u32[]{:S(2)}) copy-start(bf16[4,2,2,128,64]{4,3,2,1,0:T(8,128)(2,1)} %copy-done.35) | copy-start | bytes 786436
  725.9 63.0 %copy-start.37 = (bf16[4,2,2,128,64]{4,3,2,1,0:T(8,128)(2,1)S(1)}, bf16[4,2,2,128,64]{4,3,2,1,0:T(8,128)(2,1)}, u32[]{:S(2)}) copy-start(bf16[4,2,2,128,64]{4,3,2,1,0:T(8,128)(2,1)} %copy.208) | copy-start | bytes 786436
  725.9 254.6 %all-gather.43.cloned.1.call-start = ((), (), s32[]{:S(2)}) async-start(), calls=%async_computation.30 | async-start | bytes 2211840 | tf_op jit(solution)/shard_map/all_gather | solution.py:90
  788.9 198.7 %reduce-scatter.16.cloned.1.call-start = ((), (), s32[]{:S(2)}) async-start(), calls=%async_computation.23 | async-start | bytes 4718592 | tf_op jit(solution)/shard_map/reduce_scatter | solution.py:57
  794.5 185.9 %copy-start.48 = (bf16[128]{0:T(256)(128)(2,1)S(1)}, bf16[128]{0:T(256)(128)(2,1)}, u32[]{:S(2)}) copy-start(bf16[128]{0:T(256)(128)(2,1)} %param.17) | copy-start | bytes 772
  794.5 185.9 %copy-start.50 = (bf16[128]{0:T(256)(128)(2,1)S(1)}, bf16[128]{0:T(256)(128)(2,1)}, u32[]{:S(2)}) copy-start(bf16[128]{0:T(256)(128)(2,1)} %param.22) | copy-start | bytes 772
  794.6 264.0 %all-gather.41.cloned.1.call-start = ((), (), s32[]{:S(2)}) async-start(), calls=%async_computation.29 | async-start | bytes 4128768 | tf_op jit(solution)/shard_map/all_gather | solution.py:82
  (42 other events, 490.7 us)
Sparse Core Ops, SparseCore 0:
  25.7 27.5 all-gather.34
  55.5 33.2 all-gather.20
  94.4 53.7 all-gather.22
  149.7 21.9 all-gather.24
  178.2 49.0 reduce-scatter.9
  228.9 59.0 all-gather.36
  289.6 45.4 all-gather.38
  337.4 33.4 all-gather.26
  372.6 44.0 all-gather.28
  423.8 35.8 reduce-scatter.11
  462.0 34.4 all-gather.30
  518.5 34.4 reduce-scatter.13
  557.7 34.3 all-gather.32
  637.6 73.3 reduce-scatter.21
  713.3 75.5 reduce-scatter.19
  791.2 97.3 reduce-scatter.17
  890.9 60.8 all-gather.42
  954.2 33.3 reduce-scatter.15
  990.1 68.4 all-gather.40

commit v2 on v1

--- a/solution.py
+++ b/solution.py
@@ -1,8 +1,11 @@
+import functools
 import math
 
 import jax
 import jax.numpy as jnp
 from jax import lax
+from jax.experimental import pallas as pl
+from jax.experimental.pallas import tpu as pltpu
 from jax.sharding import Mesh, PartitionSpec as P
 
 D = 2048
@@ -49,6 +52,262 @@
     return w * cos + turned
 
 
+MESH = pl.DeviceIdType.MESH
+HALVES = (pl.ds(0, 64), pl.ds(64, 64))
+VM = pl.BlockSpec(memory_space=pltpu.VMEM)
+HB = pl.BlockSpec(memory_space=pl.ANY)
+
+
+def params(number):
+    return pltpu.CompilerParams(collective_id=number, has_side_effects=True, vmem_limit_bytes=56 * 2**20)
+
+
+def send(src, dst, sems, i, device):
+    copy = pltpu.make_async_remote_copy(
+        src_ref=src, dst_ref=dst, send_sem=sems[0].at[i], recv_sem=sems[1].at[i], device_id=device, device_id_type=MESH
+    )
+    copy.start()
+    return copy
+
+
+def meet(devices):
+    barrier = pltpu.get_barrier_semaphore()
+    for device in devices:
+        pl.semaphore_signal(barrier, inc=1, device_id=device, device_id_type=MESH)
+    pl.semaphore_wait(barrier, len(devices))
+
+
+class Ring:
+    def __init__(self):
+        x, core = lax.axis_index("x"), lax.axis_index("core")
+        self.x, self.core = x, core
+        self.right_x, self.left_x, self.far_x = lax.rem(x + 1, 4), lax.rem(x + 3, 4), lax.rem(x + 2, 4)
+        self.right, self.left, self.sibling = {"x": self.right_x}, {"x": self.left_x}, {"core": 1 - core}
+
+
+class Gather:
+    def __init__(self, ring, own, out, sems, local_sem):
+        self.r, self.own, self.out, self.sems, self.local_sem = ring, own, out, sems, local_sem
+        self.c = {}
+
+    def slot(self, x, half):
+        return self.out.at[x * 2 + self.r.core, HALVES[half]]
+
+    def start(self, half):
+        r, src, dst = self.r, self.own.at[HALVES[half]], self.slot(self.r.x, half)
+        first, second = (r.right, r.left) if half == 0 else (r.left, r.right)
+        i, j = (0, 3) if half == 0 else (2, 1)
+        self.c[i] = send(src, dst, self.sems, i, first)
+        self.c[j] = send(src, dst, self.sems, j, second)
+        self.c[6 + half] = send(src, dst, self.sems, 6 + half, r.sibling)
+        copy = pltpu.make_async_copy(src, dst, self.local_sem.at[half])
+        copy.start()
+        self.c[14 + half] = copy
+
+    def finish(self):
+        r, c = self.r, self.c
+        for got, x, half, onward, core_i in (
+            (0, r.left_x, 0, (4, r.right), 8),
+            (2, r.right_x, 1, (5, r.left), 11),
+            (1, r.left_x, 1, None, 9),
+            (3, r.right_x, 0, None, 10),
+            (4, r.far_x, 0, None, 12),
+            (5, r.far_x, 1, None, 13),
+        ):
+            c[got].wait_recv()
+            block = self.slot(x, half)
+            if onward is not None:
+                c[onward[0]] = send(block, block, self.sems, onward[0], onward[1])
+            c[core_i] = send(block, block, self.sems, core_i, r.sibling)
+        for i in range(6, 14):
+            c[i].wait_recv()
+        for i in range(14):
+            c[i].wait_send()
+        c[14].wait()
+        c[15].wait()
+
+
+class Scatter:
+    def __init__(self, ring, parts, held, got, sems):
+        self.r, self.parts, self.held, self.got, self.sems = ring, parts, held, got, sems
+        self.c = {}
+
+    def pair(self, i, half):
+        r = self.r
+        x = (r.far_x, r.right_x, r.left_x, r.x)[i]
+
+        def body(k, _):
+            rows = pl.ds(half * 64 + k * 16, 16)
+            total = self.parts[x * 2 + r.core, rows, :].astype(F32) + self.got[i, rows, :].astype(F32)
+            self.held[i, rows, :] = total.astype(BF)
+            return 0
+
+        lax.fori_loop(0, 4, body, 0)
+
+    def onward(self, i, half, slot):
+        def body(k, _):
+            rows = pl.ds(half * 64 + k * 16, 16)
+            total = self.held[i, rows, :].astype(F32) + self.got[slot, rows, :].astype(F32)
+            self.held[i, rows, :] = total.astype(BF)
+            return 0
+
+        lax.fori_loop(0, 4, body, 0)
+
+    def run(self):
+        r, c, held, got, sems = self.r, self.c, self.held, self.got, self.sems
+        blocks = (r.far_x, r.right_x, r.left_x, r.x)
+        for i in range(4):
+            c[i] = send(self.parts.at[blocks[i] * 2 + (1 - r.core)], got.at[i], sems, i, r.sibling)
+        a, b = HALVES
+        c[0].wait_recv()
+        self.pair(0, 0)
+        c[4] = send(held.at[0, a], got.at[4, a], sems, 4, r.right)
+        self.pair(0, 1)
+        c[5] = send(held.at[0, b], got.at[4, b], sems, 5, r.left)
+        c[1].wait_recv()
+        self.pair(1, 1)
+        c[6] = send(held.at[1, b], got.at[5, b], sems, 6, r.right)
+        c[2].wait_recv()
+        self.pair(2, 0)
+        c[7] = send(held.at[2, a], got.at[5, a], sems, 7, r.left)
+        self.pair(1, 0)
+        self.pair(2, 1)
+        c[4].wait_recv()
+        self.onward(1, 0, 4)
+        c[8] = send(held.at[1, a], got.at[6, a], sems, 8, r.right)
+        c[5].wait_recv()
+        self.onward(2, 1, 4)
+        c[9] = send(held.at[2, b], got.at[6, b], sems, 9, r.left)
+        c[3].wait_recv()
+
+    def ready(self, half):
+        c = self.c
+        if half == 0:
+            c[7].wait_recv()
+            c[8].wait_recv()
+        else:
+            c[6].wait_recv()
+            c[9].wait_recv()
+
+    def total(self, rows):
+        r = self.r
+        return (
+            self.parts[r.x * 2 + r.core, rows, :].astype(F32)
+            + self.got[3, rows, :].astype(F32)
+            + self.got[5, rows, :].astype(F32)
+            + self.got[6, rows, :].astype(F32)
+        )
+
+    def finish(self):
+        for i in range(10):
+            self.c[i].wait_send()
+
+
+def norm_scale(v):
+    return lax.rsqrt(jnp.mean(v * v, axis=1, keepdims=True) + EPSILON)
+
+
+def exchange(number, op, parts, inputs, outs, gather=True):
+    n_in, n_out = len(inputs), len(outs)
+
+    def kernel(*refs):
+        parts_ref, ins = refs[0], refs[1 : 1 + n_in]
+        out_refs = refs[1 + n_in : 1 + n_in + n_out]
+        rest = refs[1 + n_in + n_out :]
+        if gather:
+            all_ref, rest = rest[0], rest[1:]
+        held, got, rs_s, rs_r = rest[:4]
+        ring = Ring()
+        meet((ring.right, ring.left, ring.sibling))
+        scatter = Scatter(ring, parts_ref, held, got, (rs_s, rs_r))
+        if gather:
+            own, ag_s, ag_r, loc = rest[4:]
+            gath = Gather(ring, own, all_ref, (ag_s, ag_r), loc)
+        scatter.run()
+        for half in range(2):
+            scatter.ready(half)
+
+            def body(k, _, half=half):
+                rows = pl.ds(half * 64 + k * 16, 16)
+                last = op(rows, scatter.total(rows), ins, out_refs)
+                if gather:
+                    own[rows, :] = last.astype(BF)
+                return 0
+
+            lax.fori_loop(0, 4, body, 0)
+            if gather:
+                gath.start(half)
+        if gather:
+            gath.finish()
+        scatter.finish()
+
+    shapes = list(outs)
+    scratch = [
+        pltpu.VMEM((4, 128, D), BF),
+        pltpu.VMEM((7, 128, D), BF),
+        pltpu.SemaphoreType.DMA((10,)),
+        pltpu.SemaphoreType.DMA((10,)),
+    ]
+    specs = [VM] * n_out
+    if gather:
+        shapes.append(jax.ShapeDtypeStruct((8, 128, D), BF))
+        specs.append(HB)
+        scratch += [
+            pltpu.VMEM((128, D), BF),
+            pltpu.SemaphoreType.DMA((14,)),
+            pltpu.SemaphoreType.DMA((14,)),
+            pltpu.SemaphoreType.DMA((2,)),
+        ]
+    return pl.pallas_call(
+        kernel,
+        out_shape=shapes,
+        in_specs=[VM] * (1 + n_in),
+        out_specs=specs,
+        scratch_shapes=scratch,
+        compiler_params=params(number),
+        name="exchange%d" % number,
+    )(parts, *inputs)
+
+
+def op_mid(rows, total, ins, outs):
+    (x_ref,), (y1_ref,) = ins, outs
+    y1 = x_ref[rows, :].astype(F32) + total
+    y1_ref[rows, :] = y1
+    return y1 * norm_scale(y1)
+
+
+def op_loss(rows, total, ins, outs):
+    y1_ref, teacher_ref, valid_ref = ins
+    out_ref, dy_ref, loss_ref = outs
+    y = y1_ref[rows, :] + total
+    out_ref[rows, :] = y.astype(BF)
+    miss = y - teacher_ref[rows, :].astype(F32)
+    valid = valid_ref[rows, :]
+    loss_ref[rows, :] = valid * jnp.mean(miss * miss, axis=1, keepdims=True)
+    dy = valid * miss
+    dy_ref[rows, :] = dy
+    return dy
+
+
+def back_norm(v, grad, u):
+    r = norm_scale(v)
+    n = v * r
+    return grad + r * (u - n * jnp.mean(u * n, axis=1, keepdims=True))
+
+
+def op_back(rows, total, ins, outs):
+    (y1_ref, dy_ref), (dy1_ref,) = ins, outs
+    dy1 = back_norm(y1_ref[rows, :], dy_ref[rows, :], total)
+    dy1_ref[rows, :] = dy1
+    return dy1
+
+
+def op_input(rows, total, ins, outs):
+    (x_ref, dy1_ref), (grad_ref,) = ins, outs
+    grad_ref[rows, :] = back_norm(x_ref[rows, :].astype(F32), dy1_ref[rows, :], total)
+    return None
+
+
 def ag_tp(v):
     return lax.all_gather(v, TP, axis=0, tiled=True)
 
@@ -135,20 +394,25 @@
     a = jnp.einsum("shqk,skd->sqhd", (e / total).astype(BF), v_all, preferred_element_type=F32)
     a = a.astype(BF).reshape(1024, 256)
 
-    y1 = x + rs_tp(dot(a, wo, 1, 0))
-    r2 = lax.rsqrt(jnp.mean(y1 * y1, axis=1, keepdims=True) + EPSILON)
-    n2 = y1 * r2
-    n2_all = ag_tp(n2.astype(BF))
+    def parts(v):
+        return v.astype(BF).reshape(8, 128, D)
+
+    wide = jax.ShapeDtypeStruct((128, D), F32)
+    y1, n2_all = exchange(1, op_mid, parts(dot(a, wo, 1, 0)), (hidden_in,), (wide,))
+    n2_all = n2_all.reshape(1024, D)
     gu = dot(n2_all, wgu, 1, 0)
     gate, up = gu[:, :704], gu[:, 704:]
     sg = jax.nn.sigmoid(gate)
     act = gate * sg
     mid = (act * up).astype(BF)
-    y = y1 + rs_tp(dot(mid, wd, 1, 0))
-    miss = y - teacher.astype(F32)
-    loss_here = jnp.sum(valid * jnp.mean(miss * miss, axis=1))
-    dy = valid[:, None] * miss
-    dy_all = ag_tp(dy.astype(BF))
+    layer_out, dy, loss_rows, dy_all = exchange(
+        2,
+        op_loss,
+        parts(dot(mid, wd, 1, 0)),
+        (y1, teacher, valid[:, None]),
+        (jax.ShapeDtypeStruct((128, D), BF), wide, jax.ShapeDtypeStruct((128, 1), F32)),
+    )
+    dy_all = dy_all.reshape(1024, D)
 
     grad_down = dot(mid, dy_all, 0, 0)
     dmid = dot(dy_all, wd, 1, 1)
@@ -156,9 +420,8 @@
     dup = (dmid * act).astype(BF)
     dgu = jnp.concatenate([dgate, dup], axis=1)
     grad_gu = dot(n2_all, dgu, 0, 0)
-    u2 = rs_tp(dot(dgu, wgu, 1, 1))
-    dy1 = dy + r2 * (u2 - n2 * jnp.mean(u2 * n2, axis=1, keepdims=True))
-    da_all = ag_tp(dy1.astype(BF))
+    dy1, da_all = exchange(3, op_back, parts(dot(dgu, wgu, 1, 1)), (y1, dy), (wide,))
+    da_all = da_all.reshape(1024, D)
     grad_out = dot(a, da_all, 0, 0)
     da = dot(da_all, wo, 1, 1).astype(BF).reshape(8, 128, 4, HD)
 
@@ -176,10 +439,10 @@
     dv = dkv[..., HD:].astype(BF).reshape(1024, HD)
     dqkv = jnp.concatenate([dq, dk, dv], axis=1)
     grad_qkv = dot(n1_all, dqkv, 0, 0)
-    u1 = rs_tp(dot(dqkv, wqkv, 1, 1))
-    loss = lax.psum(loss_here, AXES) / count
+    (grad_in,) = exchange(4, op_input, parts(dot(dqkv, wqkv, 1, 1)), (hidden_in, dy1), (wide,), gather=False)
+    loss = lax.psum(jnp.sum(loss_rows), AXES) / count
     scale = 2.0 / (D * count)
-    input_grad = (dy1 + r1 * (u1 - n1 * jnp.mean(u1 * n1, axis=1, keepdims=True))) * scale
+    input_grad = grad_in * scale
 
     ga = return_rows(jnp.concatenate([grad_qkv, grad_gu], axis=1))
     gb = return_columns(jnp.concatenate([grad_out.reshape(2, 128, D), grad_down.reshape(2, 352, D)], axis=1).reshape(960, D))
@@ -202,7 +465,7 @@
     s1 = (g1 * scale)[:, None]
     s2 = (g2 * scale)[:, None]
     return (
-        y.astype(BF), loss, input_grad, gain1, gq * s1, gk * s1, gv * s1, gb[:128] * scale,
+        layer_out, loss, input_grad, gain1, gq * s1, gk * s1, gv * s1, gb[:128] * scale,
         gain2, gg * s2, gp * s2, gb[128:] * scale,
     )
 

time: 1110 us -> 975 us (0.88)
  waiting for transfers between devices: 591 us -> 267 us
  Pallas kernels: 0 us -> 179 us
    pallas_call x0 -> x4, Pallas kernels: none -> 179 us  [exchange(): pl.pallas_call(kernel, out_shape=shapes, in_specs=[VM] * (1 + n_in), out_...]
    all_gather x4 -> x1, waiting for transfers between devices: 115 us -> 0.02 us  [ag_tp(): return lax.all_gather(v, TP, axis=0, tiled=True)]
    reduce_scatter x4 -> x0, waiting for transfers between devices: 72.2 us -> none  [rs_tp(): lax.psum_scatter(v.astype(BF), TP, scatter_dimension=0, tiled=True)]
    all_gather x1, waiting for transfers between devices: 67.3 us -> 0.01 us  [return_rows(): g = lax.all_gather(g, CTX, axis=0)]
    all_gather x3, waiting for transfers between devices: 75.5 us -> 26.7 us  [spread_columns(): got = lax.all_gather(got, 'y_lo', axis=0)]
    all_gather x1, waiting for transfers between devices: 31.7 us -> 0.02 us  [local(): wd = lax.all_gather(w_down, 'y_lo', axis=0, tiled=True)]
    unnamed x20 -> x13, waiting for transfers between devices: 35.5 us -> 32.8 us
    unnamed x126 -> x123, local copies, waits for them, and re-layouts: 36 us -> 35.1 us
  transfers between devices with their start and end apart: 21 -> 14, of which waited for: 16 -> 6; matrix products, arithmetic and copies ran while one was open for 14% -> 17% of each run, Pallas kernels for 0% -> 8%
where the time goes in v2:
time: 975 us; the launch traced here: 967 us
  waiting for transfers between devices  267 us (27%)
  blocking collectives  195 us (20%)
  Pallas kernels  179 us (18%)
  matrix products  123 us (13%)
  local copies, waits for them, and re-layouts  117 us (12%)
  other arithmetic  58.3 us (6%)
  between operations  18.7 us (2%)
    pallas_call x4, Pallas kernels, exchange(): pl.pallas_call(kernel, out_shape=shapes, in_specs=[VM] * (1 + n_in), out_...  179 us
    reduce_scatter x1, waiting for transfers between devices, return_rows(): lax.psum_scatter(g.reshape(16, 8 * 16, n), ('y_lo', 'y_hi', 'z'), scatter...  99.5 us
    dot_general x12, matrix products, dot(): lax.dot_general(a, b, (((ca,), (cb,)), ((), ())), preferred_element_type=...  77.9 us
    all_to_all x3, blocking collectives, spread_columns(): got = lax.all_to_all(parts, TP, 0, 0)  74.8 us
    psum x1, blocking collectives, local(): loss = lax.psum(jnp.sum(loss_rows), AXES) / count  67.5 us
    reduce_scatter x1, waiting for transfers between devices, return_columns(): lax.psum_scatter(g, ('y_lo', 'y_hi', 'z'), scatter_dimension=0, tiled=True)  64.7 us
    all_gather x1, waiting for transfers between devices, local(): lax.all_gather(jnp.concatenate([k, v], axis=2), CTX, axis=1, tiled=True)  37.8 us
    unnamed x123, local copies, waits for them, and re-layouts  35.1 us
  transfers between devices with their start and end apart: 14, of which 6 were waited for; matrix products, arithmetic and copies ran while one was open for 17% of the time, Pallas kernels for 8%

profile of v2, /device:TPU:1, one launch (start us, length us, event | category | flops | bytes accessed | tf_op | source)
XLA Modules:
  0.0 967.1 jit_solution(10796206279226825636)
XLA Ops:
  9.4 15.0 %all_to_all.30 = bf16[8,128,256]{1,2,0:T(8,128)(2,1)S(1)} all-to-all(bf16[8,128,256]{1,2,0:T(8,128)(2,1)S(1)} %bitcast.293), channel_id=1, replica_groups=mesh['y_hi'=2,'z'=4,'x'=4,'y_lo'=2,'core'=2] {'x','core'}, dimensions={0} | all-to-all | bytes 1048576 | tf_op jit(solution)/shard_map/all_to_all | solution.py:322
  32.7 23.8 %all_to_all.31 = bf16[8,128,704]{1,2,0:T(8,128)(2,1)} all-to-all(bf16[8,128,704]{1,2,0:T(8,128)(2,1)S(1)} %bitcast.278), channel_id=1, replica_groups=mesh['y_hi'=2,'z'=4,'x'=4,'y_lo'=2,'core'=2] {'x','core'}, dimensions={0} | all-to-all | bytes 2883584 | tf_op jit(solution)/shard_map/all_to_all | solution.py:322
  56.8 36.1 %all_to_all.32 = bf16[8,128,704]{1,2,0:T(8,128)(2,1)} all-to-all(bf16[8,128,704]{1,2,0:T(8,128)(2,1)S(1)} %bitcast.279), channel_id=1, replica_groups=mesh['y_hi'=2,'z'=4,'x'=4,'y_lo'=2,'core'=2] {'x','core'}, dimensions={0} | all-to-all | bytes 2883584 | tf_op jit(solution)/shard_map/all_to_all | solution.py:322
  109.2 6.4 all-gather.2
  115.9 9.2 all-gather.1
  135.0 15.5 %all-gather.7 = s32[8,1,1024]{2,1,0:T(1,128)S(1)} all-gather(s32[1,1,1024]{2,1,0:T(1,128)S(1)} %bitcast.325), channel_id=1, replica_groups=mesh['y_hi'=2,'z'=4,'x'=4,'y_lo'=2,'core'=2] {'x','core'}, dimensions={0}, use_global_device_ids=true | all-gather | bytes 36864 | tf_op jit(solution)/shard_map/all_gather | solution.py:312
  158.5 6.4 copy.299
  164.8 6.4 reshape.518
  171.2 26.7 %all-gather.30.cloned.1.call-done = bf16[16,128,704]{1,2,0:T(8,128)(2,1)} async-done(((bf16[8,128,704]{1,2,0:T(8,128)(2,1)}), bf16[16,128,704]{1,2,0:T(8,128)(2,1)}) %all-gather.30.cloned.1.call-update) | async-done | bytes 2883600 | tf_op jit(solution)/shard_map/all_gather | solution.py:323
  204.3 7.4 reshape.522
  217.9 37.8 %all-gather.20.cloned.1.call-done = bf16[8,1024,128]{1,2,0:T(8,128)(2,1)} async-done(((bf16[8,128,128]{1,2,0:T(8,128)(2,1)}), bf16[8,1024,128]{1,2,0:T(8,128)(2,1)}) %all-gather.20.cloned.1.call-update) | async-done | bytes 2097168 | tf_op jit(solution)/shard_map/all_gather | solution.py:385
  255.8 9.3 fusion.55
  265.1 8.8 fusion.3
  273.9 7.4 fusion.20
  286.2 49.9 %exchange1.1 = (f32[128,2048]{1,0:T(8,128)}, bf16[8,128,2048]{2,1,0:T(8,128)(2,1)}) custom-call(bf16[8,128,2048]{2,1,0:T(8,128)(2,1)} %bitcast.265, bf16[128,2048]{1,0:T(8,128)(2,1)} %refs_1_.3), custom_call_target="tpu_custom_call" | custom-call | tf_op jit(solution)/shard_map/exchange1/pallas_call | solution.py:261
  336.1 11.9 %fusion.56 = f32[1024,1408]{1,0:T(8,128)} fusion(bf16[1024,2048]{1,0:T(8,128)(2,1)} %bitcast.283, bf16[2048,1408]{0,1:T(8,128)(2,1)} %copy-done.16), kind=kOutput, calls=%fused_computation.163 | convolution fusion | flops 5905580032 | bytes 15728640 | tf_op jit(solution)/shard_map/dot_general | solution.py:28
  348.1 9.3 convolution_convert_fusion.3
  357.4 49.3 %exchange2.1 = (bf16[128,2048]{1,0:T(8,128)(2,1)}, f32[128,2048]{1,0:T(8,128)}, f32[128,1]{1,0:T(8,128)}, bf16[8,128,2048]{2,1,0:T(8,128)(2,1)}) custom-call(bf16[8,128,2048]{2,1,0:T(8,128)(2,1)} %bitcast.286, f32[128,2048]{1,0:T(8,128)} %get-tuple-element.21.refs_1_, bf16[128,2048]{1,0:T(8,128)(2,1)} %refs_2_.1, f32[128,1]{1,0:T(8,128)} %copy.230.refs_3_), custom_call_target="tpu_custom_call" | custom-call | tf_op jit(solution)/shard_map/exchange2/pallas_call | solution.py:261
  406.7 7.4 multiply_convert_fusion.1
  414.1 12.1 %convolution_convert_fusion.2 = bf16[1024,2048]{1,0:T(8,128)(2,1)} fusion(bf16[2048,1408]{0,1:T(8,128)(2,1)} %copy-done.16, bf16[1024,704]{1,0:T(8,128)(2,1)S(1)} %get-tuple-element.83, bf16[1024,704]{1,0:T(8,128)(2,1)S(1)} %get-tuple-element.82), kind=kOutput, calls=%fused_computation.23 | convolution fusion | flops 5913444352 | bytes 12845056 | tf_op jit(solution)/shard_map/dot_general | solution.py:28
  426.2 49.9 %exchange3.1 = (f32[128,2048]{1,0:T(8,128)}, bf16[8,128,2048]{2,1,0:T(8,128)(2,1)}) custom-call(bf16[8,128,2048]{2,1,0:T(8,128)(2,1)} %bitcast.282, f32[128,2048]{1,0:T(8,128)} %get-tuple-element.21.refs_1_, f32[128,2048]{1,0:T(8,128)} %get-tuple-element.25.refs_2_), custom_call_target="tpu_custom_call" | custom-call | tf_op jit(solution)/shard_map/exchange3/pallas_call | solution.py:261
  482.7 9.5 bitcast_convert_fusion
  492.2 8.0 fusion
  500.1 10.2 %fusion.2 = bf16[8,4,128,1024]{2,3,1,0:T(8,128)(2,1)} fusion(f32[8,1024,128,4]{2,1,3,0:T(8,128)S(1)} %get-tuple-element.123, f32[8,4,128,1024]{2,3,1,0:T(8,128)} %get-tuple-element.121, f32[8,4,128]{2,1,0:T(4,128)S(1)} %get-tuple-element.122, f32[8,4,128]{2,1,0:T(4,128)S(1)} %bitcast.316), kind=kLoop, calls=%fused_computation.6 | loop fusion | flops 16777216 | bytes 41975808 | tf_op jit(solution)/shard_map/convert_element_type | solution.py:432
  540.0 7.1 copy.242
  555.1 8.7 convolution_convert_fusion
  563.8 31.4 %reduce-scatter.10.cloned.1.call-done = bf16[128,1024]{1,0:T(8,128)(2,1)} async-done(((bf16[1024,1024]{1,0:T(8,128)(2,1)}), bf16[128,1024]{1,0:T(8,128)(2,1)}) %reduce-scatter.10.cloned.1.call-update) | async-done | bytes 262160
  608.8 64.7 %reduce-scatter.8.cloned.1.call-done = bf16[1,480,256]{2,1,0:T(8,128)(2,1)} async-done(((bf16[16,480,256]{2,1,0:T(8,128)(2,1)}), bf16[1,480,256]{2,1,0:T(8,128)(2,1)}) %reduce-scatter.8.cloned.1.call-update) | async-done | bytes 245776 | tf_op jit(solution)/shard_map/reduce_scatter | solution.py:348
  673.5 99.5 %reduce-scatter.6.cloned.1.call-done = bf16[1,128,1792]{2,1,0:T(8,128)(2,1)} async-done(((bf16[16,128,1792]{2,1,0:T(8,128)(2,1)}), bf16[1,128,1792]{2,1,0:T(8,128)(2,1)}) %reduce-scatter.6.cloned.1.call-update) | async-done | bytes 458768 | tf_op jit(solution)/shard_map/reduce_scatter | solution.py:339
  773.0 21.9 %all_to_all.33 = bf16[8,16,1792]{2,1,0:T(8,128)(2,1)} all-to-all(bf16[8,16,1792]{2,1,0:T(8,128)(2,1)} %bitcast.313), channel_id=1, replica_groups=mesh['y_hi'=2,'z'=4,'x'=4,'y_lo'=2,'core'=2] {'x','core'}, dimensions={0} | all-to-all | bytes 917504 | tf_op jit(solution)/shard_map/all_to_all | solution.py:340
  796.1 67.5 %all-reduce = (f32[]{:T(128)}, f32[]{:T(128)}) all-reduce(f32[]{:T(128)} %reduce_sum.110, f32[]{:T(128)} %convert_reduce_fusion), channel_id=1, replica_groups=mesh['y_hi'=2,'z'=4,'x'=4,'y_lo'=2,'core'=2] {'y_hi','z','x','y_lo','core'}, use_global_device_ids=true, to_apply=%region_4.5 | all-reduce | flops 2 | bytes 16 | tf_op jit(solution)/shard_map/psum | solution.py:443
  870.7 29.9 %exchange4.1 = f32[128,2048]{1,0:T(8,128)} custom-call(bf16[8,128,2048]{2,1,0:T(8,128)(2,1)} %bitcast.288, bf16[128,2048]{1,0:T(8,128)(2,1)} %refs_1_.3, f32[128,2048]{1,0:T(8,128)} %get-tuple-element.27.refs_2_), custom_call_target="tpu_custom_call" | custom-call | tf_op jit(solution)/shard_map/exchange4/pallas_call | solution.py:261
  (269 shorter events, 184.1 us)
Async XLA Ops:
  7.2 18.3 %copy-start.6 = (bf16[128,2048]{1,0:T(8,128)(2,1)S(1)}, bf16[128,2048]{1,0:T(8,128)(2,1)}, u32[]{:S(2)}) copy-start(bf16[128,2048]{1,0:T(8,128)(2,1)} %refs_1_.3) | copy-start | bytes 1572868
  7.2 118.2 %all-gather.26.cloned.1.call-start = ((), (), s32[]{:S(2)}) async-start(), calls=%async_computation.15 | async-start | bytes 1572864 | tf_op jit(solution)/shard_map/all_gather | solution.py:323
  25.4 101.5 %all-gather.18.cloned.1.call-start = ((), (), s32[]{:S(2)}) async-start(), calls=%async_computation.9 | async-start | bytes 4718592 | tf_op jit(solution)/shard_map/all_gather | solution.py:312
  26.7 131.8 %all-gather.28.cloned.1.call-start = ((), (), s32[]{:S(2)}) async-start(), calls=%async_computation.16 | async-start | bytes 4325376 | tf_op jit(solution)/shard_map/all_gather | solution.py:323
  32.6 24.0 %copy-start.8 = (bf16[128,5632]{0,1:T(8,128)(2,1)S(1)}, bf16[128,5632]{0,1:T(8,128)(2,1)}, u32[]{:S(2)}) copy-start(bf16[128,5632]{0,1:T(8,128)(2,1)} %get-tuple-element.116) | copy-start | bytes 4325380
  56.6 141.4 %all-gather.30.cloned.1.call-start = ((), (), s32[]{:S(2)}) async-start(), calls=%async_computation.17 | async-start | bytes 4325376 | tf_op jit(solution)/shard_map/all_gather | solution.py:323
  56.6 36.2 %copy-start.36 = (bf16[128,256]{1,0:T(8,128)(2,1)S(1)}, bf16[128,256]{1,0:T(8,128)(2,1)}, u32[]{:S(2)}) copy-start(bf16[128,256]{1,0:T(8,128)(2,1)} %param.19) | copy-start | bytes 196612
  56.6 36.3 %copy-start.37 = (bf16[128,256]{1,0:T(8,128)(2,1)S(1)}, bf16[128,256]{1,0:T(8,128)(2,1)}, u32[]{:S(2)}) copy-start(bf16[128,256]{1,0:T(8,128)(2,1)} %param.20) | copy-start | bytes 196612
  93.8 9.8 %all-to-all-start.2 = ((bf16[8,128,64]{1,2,0:T(8,128)(2,1)}), bf16[8,128,64]{1,2,0:T(8,128)(2,1)S(1)}, u32[]{:S(2)}, u32[]{:S(2)}) async-start(bf16[8,128,64]{1,2,0:T(8,128)(2,1)} %bitcast.16), calls=%async_computation.2 | async-start | bytes 262144 | tf_op jit(solution)/shard_map/all_to_all | solution.py:331
  104.3 11.6 %all-to-all-start.1 = ((bf16[8,128,64]{1,2,0:T(8,128)(2,1)}), bf16[8,128,64]{1,2,0:T(8,128)(2,1)S(1)}, u32[]{:S(2)}, u32[]{:S(2)}) async-start(bf16[8,128,64]{1,2,0:T(8,128)(2,1)} %bitcast.9), calls=%async_computation.1 | async-start | bytes 262144 | tf_op jit(solution)/shard_map/all_to_all | solution.py:331
  108.4 147.3 %all-gather.20.cloned.1.call-start = ((), (), s32[]{:S(2)}) async-start(), calls=%async_computation.10 | async-start | bytes 2359296 | tf_op jit(solution)/shard_map/all_gather | solution.py:385
  109.1 108.5 %copy-start.25 = (f32[128,64]{0,1:T(8,128)}, f32[128,64]{0,1:T(8,128)S(1)}, u32[]{:S(2)}) copy-start(f32[128,64]{0,1:T(8,128)S(1)} %get-tuple-element.111) | copy-start | bytes 98308
  109.2 108.5 %copy-start.27 = (f32[128,64]{0,1:T(8,128)}, f32[128,64]{0,1:T(8,128)S(1)}, u32[]{:S(2)}) copy-start(f32[128,64]{0,1:T(8,128)S(1)} %get-tuple-element.110) | copy-start | bytes 98308
  133.3 148.3 %all-gather.22.cloned.1.call-start = ((), (), s32[]{:S(2)}) async-start(), calls=%async_computation.11 | async-start | bytes 1572864 | tf_op jit(solution)/shard_map/all_gather | solution.py:366
  133.9 214.2 %all-gather.24.cloned.1.call-start = ((), (), s32[]{:S(2)}) async-start(), calls=%async_computation.12 | async-start | bytes 4325376 | tf_op jit(solution)/shard_map/all_gather | solution.py:367
  134.6 460.6 %reduce-scatter.10.cloned.1.call-start = ((), (), s32[]{:S(2)}) async-start(), calls=%async_computation.20 | async-start | bytes 2359296
  215.4 40.4 %copy-start.17 = (pred[8,128,1024]{1,2,0:T(8,128)(4,1)S(1)}, pred[8,128,1024]{1,2,0:T(8,128)(4,1)}, u32[]{:S(2)}) copy-start(pred[8,128,1024]{1,2,0:T(8,128)(4,1)} %compare_and_fusion) | copy-start | bytes 3145732
  357.4 49.3 %copy-start.7 = (f32[1024,1408]{1,0:T(8,128)S(1)}, f32[1024,1408]{1,0:T(8,128)}, u32[]{:S(2)}) copy-start(f32[1024,1408]{1,0:T(8,128)} %fusion.56) | copy-start | bytes 17301508
  426.2 49.9 %copy-start.20 = (bf16[256,2048]{1,0:T(8,128)(2,1)S(1)}, bf16[256,2048]{1,0:T(8,128)(2,1)}, u32[]{:S(2)}) copy-start(bf16[256,2048]{1,0:T(8,128)(2,1)} %all-gather.22.cloned.1.call-done) | copy-start | bytes 3145732
  523.1 150.4 %reduce-scatter.8.cloned.1.call-start = ((), (), s32[]{:S(2)}) async-start(), calls=%async_computation.14 | async-start | bytes 4177920 | tf_op jit(solution)/shard_map/reduce_scatter | solution.py:348
  539.9 233.0 %reduce-scatter.6.cloned.1.call-start = ((), (), s32[]{:S(2)}) async-start(), calls=%async_computation.13 | async-start | bytes 7798784 | tf_op jit(solution)/shard_map/reduce_scatter | solution.py:339
  555.1 41.7 %copy-start.28 = (f32[128,64]{0,1:T(8,128)S(1)}, f32[128,64]{0,1:T(8,128)}, u32[]{:S(2)}) copy-start(f32[128,64]{0,1:T(8,128)} %copy-done.27) | copy-start | bytes 98308
  563.8 33.0 %copy-start.26 = (f32[128,64]{0,1:T(8,128)S(1)}, f32[128,64]{0,1:T(8,128)}, u32[]{:S(2)}) copy-start(f32[128,64]{0,1:T(8,128)} %copy-done.25) | copy-start | bytes 98308
  608.6 186.2 %copy-start.43 = (s32[128]{0:T(128)S(1)}, s32[128]{0:T(128)}, u32[]{:S(2)}) copy-start(s32[128]{0:T(128)} %param.16) | copy-start | bytes 1540
  608.6 186.9 %copy-start.38 = (f32[128,1]{1,0:T(8,128)S(1)}, f32[128,1]{1,0:T(8,128)}, u32[]{:S(2)}) copy-start(f32[128,1]{1,0:T(8,128)} %get-tuple-element.23) | copy-start | bytes 1540
  608.6 257.0 %copy-start.44 = (bf16[128]{0:T(256)(128)(2,1)S(1)}, bf16[128]{0:T(256)(128)(2,1)}, u32[]{:S(2)}) copy-start(bf16[128]{0:T(256)(128)(2,1)} %param.17) | copy-start | bytes 772
  608.6 257.1 %copy-start.46 = (bf16[128]{0:T(256)(128)(2,1)S(1)}, bf16[128]{0:T(256)(128)(2,1)}, u32[]{:S(2)}) copy-start(bf16[128]{0:T(256)(128)(2,1)} %param.22) | copy-start | bytes 772
  608.6 257.6 %copy-start.19 = (bf16[4,2,2,128,256]{4,3,2,1,0:T(8,128)(2,1)S(1)}, bf16[4,2,2,128,256]{4,3,2,1,0:T(8,128)(2,1)}, u32[]{:S(2)}) copy-start(bf16[4,2,2,128,256]{4,3,2,1,0:T(8,128)(2,1)} %copy-done.18) | copy-start | bytes 3145732
  608.7 257.6 %copy-start.30 = (bf16[4,2,2,128,64]{4,3,2,1,0:T(8,128)(2,1)S(1)}, bf16[4,2,2,128,64]{4,3,2,1,0:T(8,128)(2,1)}, u32[]{:S(2)}) copy-start(bf16[4,2,2,128,64]{4,3,2,1,0:T(8,128)(2,1)} %copy-done.29) | copy-start | bytes 786436
  608.7 257.6 %copy-start.32 = (bf16[4,2,2,128,64]{4,3,2,1,0:T(8,128)(2,1)S(1)}, bf16[4,2,2,128,64]{4,3,2,1,0:T(8,128)(2,1)}, u32[]{:S(2)}) copy-start(bf16[4,2,2,128,64]{4,3,2,1,0:T(8,128)(2,1)} %copy-done.31) | copy-start | bytes 786436
  608.7 294.2 %all-gather.34.cloned.1.call-start = ((), (), s32[]{:S(2)}) async-start(), calls=%async_computation.19 | async-start | bytes 2211840 | tf_op jit(solution)/shard_map/all_gather | solution.py:349
  673.5 234.3 %all-gather.32.cloned.1.call-start = ((), (), s32[]{:S(2)}) async-start(), calls=%async_computation.18 | async-start | bytes 4128768 | tf_op jit(solution)/shard_map/all_gather | solution.py:341
  (33 other events, 216.9 us)
Sparse Core Ops, SparseCore 0:
  25.6 24.7 all-gather.25
  52.6 46.1 all-gather.17
  100.5 48.7 all-gather.27
  150.7 47.1 all-gather.29
  200.6 55.1 all-gather.19
  257.3 21.9 all-gather.21
  281.0 45.4 all-gather.23
  523.2 71.9 reduce-scatter.9
  597.7 75.7 reduce-scatter.7
  675.8 97.0 reduce-scatter.5
  775.4 61.1 all-gather.33
  839.0 65.0 all-gather.31

commit v3 on v2

v3 whole, which is shorter than its diff:
```python
import functools

import jax
import jax.numpy as jnp
from jax import lax
from jax.experimental import pallas as pl
from jax.experimental.pallas import tpu as pltpu
from jax.sharding import Mesh, PartitionSpec as P

D = 2048
HEADS = 32
KV_HEADS = 4
HD = 64
FF = 5632
KVD = 256
EPSILON = 1e-05
THETA = 10000.0
NEGATIVE = -1e30
AXES = ("y_hi", "z", "x", "y_lo", "core")
BF = jnp.bfloat16
F32 = jnp.float32


def dot(a, b, ca, cb):
    return lax.dot_general(a, b, (((ca,), (cb,)), ((), ())), preferred_element_type=F32)


def tables(positions):
    indices = jnp.arange(HD // 2, dtype=jnp.int32).astype(F32)
    frequency = THETA ** (-(indices * 2.0 / HD))
    angles = positions.astype(F32)[:, None] * frequency[None, :]
    angles = jnp.concatenate([angles, angles], axis=1)
    return jnp.cos(angles), jnp.sin(angles)


def positions_of(c):
    t = jnp.arange(64, dtype=jnp.int32)
    return jnp.concatenate([c * 64 + t, (15 - c) * 64 + t])


MESH = pl.DeviceIdType.MESH
HALVES = (pl.ds(0, 64), pl.ds(64, 64))
VM = pl.BlockSpec(memory_space=pltpu.VMEM)
HB = pl.BlockSpec(memory_space=pl.ANY)


def params(number):
    return pltpu.CompilerParams(collective_id=number, has_side_effects=True, vmem_limit_bytes=56 * 2**20)


def send(src, dst, sems, i, device):
    copy = pltpu.make_async_remote_copy(
        src_ref=src, dst_ref=dst, send_sem=sems[0].at[i], recv_sem=sems[1].at[i], device_id=device, device_id_type=MESH
    )
    copy.start()
    return copy


def meet(devices):
    barrier = pltpu.get_barrier_semaphore()
    for device in devices:
        pl.semaphore_signal(barrier, inc=1, device_id=device, device_id_type=MESH)
    pl.semaphore_wait(barrier, len(devices))


class Ring:
    def __init__(self):
        x, core = lax.axis_index("x"), lax.axis_index("core")
        self.x, self.core = x, core
        self.right_x, self.left_x, self.far_x = lax.rem(x + 1, 4), lax.rem(x + 3, 4), lax.rem(x + 2, 4)
        self.right, self.left, self.sibling = {"x": self.right_x}, {"x": self.left_x}, {"core": 1 - core}


class Gather:
    def __init__(self, ring, own, out, sems, local_sem):
        self.r, self.own, self.out, self.sems, self.local_sem = ring, own, out, sems, local_sem
        self.c = {}

    def slot(self, x, half):
        return self.out.at[x * 2 + self.r.core, HALVES[half]]

    def start(self, half):
        r, src, dst = self.r, self.own.at[HALVES[half]], self.slot(self.r.x, half)
        first, second = (r.right, r.left) if half == 0 else (r.left, r.right)
        i, j = (0, 3) if half == 0 else (2, 1)
        self.c[i] = send(src, dst, self.sems, i, first)
        self.c[j] = send(src, dst, self.sems, j, second)
        self.c[6 + half] = send(src, dst, self.sems, 6 + half, r.sibling)
        copy = pltpu.make_async_copy(src, dst, self.local_sem.at[half])
        copy.start()
        self.c[14 + half] = copy

    def forward(self):
        r, c = self.r, self.c
        for got, x, half, onward, core_i in (
            (0, r.left_x, 0, (4, r.right), 8),
            (2, r.right_x, 1, (5, r.left), 11),
            (1, r.left_x, 1, None, 9),
            (3, r.right_x, 0, None, 10),
            (4, r.far_x, 0, None, 12),
            (5, r.far_x, 1, None, 13),
        ):
            c[got].wait_recv()
            block = self.slot(x, half)
            if onward is not None:
                c[onward[0]] = send(block, block, self.sems, onward[0], onward[1])
            c[core_i] = send(block, block, self.sems, core_i, r.sibling)

    def finish(self):
        c = self.c
        for i in range(6, 14):
            c[i].wait_recv()
        for i in range(14):
            c[i].wait_send()
        c[14].wait()
        c[15].wait()


class Scatter:
    def __init__(self, ring, parts, held, got, sems):
        self.r, self.parts, self.held, self.got, self.sems = ring, parts, held, got, sems
        self.c = {}

    def pair(self, i, half):
        r = self.r
        x = (r.far_x, r.right_x, r.left_x, r.x)[i]

        def body(k, _):
            rows = pl.ds(half * 64 + k * 16, 16)
            total = self.parts[x * 2 + r.core, rows, :].astype(F32) + self.got[i, rows, :].astype(F32)
            self.held[i, rows, :] = total.astype(BF)
            return 0

        lax.fori_loop(0, 4, body, 0)

    def onward(self, i, half, slot):
        def body(k, _):
            rows = pl.ds(half * 64 + k * 16, 16)
            total = self.held[i, rows, :].astype(F32) + self.got[slot, rows, :].astype(F32)
            self.held[i, rows, :] = total.astype(BF)
            return 0

        lax.fori_loop(0, 4, body, 0)

    def begin(self):
        r = self.r
        for i, x in enumerate((r.far_x, r.right_x, r.left_x, r.x)):
            self.c[i] = send(self.parts.at[x * 2 + (1 - r.core)], self.got.at[i], self.sems, i, r.sibling)

    def run(self):
        r, c, held, got, sems = self.r, self.c, self.held, self.got, self.sems
        a, b = HALVES
        c[0].wait_recv()
        self.pair(0, 0)
        c[4] = send(held.at[0, a], got.at[4, a], sems, 4, r.right)
        self.pair(0, 1)
        c[5] = send(held.at[0, b], got.at[4, b], sems, 5, r.left)
        c[1].wait_recv()
        self.pair(1, 1)
        c[6] = send(held.at[1, b], got.at[5, b], sems, 6, r.right)
        c[2].wait_recv()
        self.pair(2, 0)
        c[7] = send(held.at[2, a], got.at[5, a], sems, 7, r.left)
        self.pair(1, 0)
        self.pair(2, 1)
        c[4].wait_recv()
        self.onward(1, 0, 4)
        c[8] = send(held.at[1, a], got.at[6, a], sems, 8, r.right)
        c[5].wait_recv()
        self.onward(2, 1, 4)
        c[9] = send(held.at[2, b], got.at[6, b], sems, 9, r.left)
        c[3].wait_recv()

    def ready(self, half):
        c = self.c
        if half == 0:
            c[7].wait_recv()
            c[8].wait_recv()
        else:
            c[6].wait_recv()
            c[9].wait_recv()

    def total(self, rows):
        r = self.r
        return (
            self.parts[r.x * 2 + r.core, rows, :].astype(F32)
            + self.got[3, rows, :].astype(F32)
            + self.got[5, rows, :].astype(F32)
            + self.got[6, rows, :].astype(F32)
        )

    def finish(self):
        for i in range(10):
            self.c[i].wait_send()


def norm_scale(v):
    return lax.rsqrt(jnp.mean(v * v, axis=1, keepdims=True) + EPSILON)


def exchange(number, op, parts, inputs, outs, gather=True, sides=()):
    n_in, n_out = len(inputs), len(outs)
    dma = pltpu.SemaphoreType.DMA

    def kernel(*refs):
        refs = list(refs)

        def take(n):
            taken = refs[:n]
            del refs[:n]
            return taken

        parts_ref, ins = take(1)[0], take(n_in)
        side_ins = [take(len(s.operands)) for s in sides]
        out_refs = take(n_out)
        all_ref = take(1)[0] if gather else None
        side_outs = [take(len(s.shapes)) for s in sides]
        held, got, rs_s, rs_r = take(4)
        if gather:
            own, ag_s, ag_r, loc = take(4)
        ring = Ring()
        peers = [ring.right, ring.left, ring.sibling]
        for s, i, o in zip(sides, side_ins, side_outs):
            s.bind(ring, i, o, take(len(s.scratch)))
            peers += s.peers
        meet(peers)
        scatter = Scatter(ring, parts_ref, held, got, (rs_s, rs_r))
        if gather:
            gath = Gather(ring, own, all_ref, (ag_s, ag_r), loc)
        scatter.begin()
        for s in sides:
            s.start()
        scatter.run()
        for half in range(2):
            scatter.ready(half)

            def body(k, _, half=half):
                rows = pl.ds(half * 64 + k * 16, 16)
                last = op(rows, scatter.total(rows), ins, out_refs)
                if gather:
                    own[rows, :] = last.astype(BF)
                return 0

            lax.fori_loop(0, 4, body, 0)
            if gather:
                gath.start(half)
        if gather:
            gath.forward()
        for s in sides:
            s.middle()
        if gather:
            gath.finish()
        scatter.finish()
        for s in sides:
            s.finish()

    shapes, specs, in_specs, operands, aliases = list(outs), [VM] * n_out, [VM] * (1 + n_in), [parts, *inputs], {}
    scratch = [pltpu.VMEM((4, 128, D), BF), pltpu.VMEM((7, 128, D), BF), dma((10,)), dma((10,))]
    if gather:
        shapes.append(jax.ShapeDtypeStruct((8, 128, D), BF))
        specs.append(HB)
        scratch += [pltpu.VMEM((128, D), BF), dma((14,)), dma((14,)), dma((2,))]
    for s in sides:
        if s.in_place:
            aliases[len(operands)] = len(shapes)
        operands += s.operands
        in_specs += [HB] * len(s.operands)
        shapes += s.shapes
        specs += [HB if s.in_place else VM] * len(s.shapes)
        scratch += s.scratch
    return pl.pallas_call(
        kernel,
        out_shape=shapes,
        in_specs=in_specs,
        out_specs=specs,
        scratch_shapes=scratch,
        input_output_aliases=aliases,
        compiler_params=params(number),
        name="exchange%d" % number,
    )(*operands)


class Side:
    in_place = False

    def middle(self):
        pass


class YSwap(Side):
    in_place = True

    def __init__(self, weights):
        self.operands = [weights]
        self.shapes = [jax.ShapeDtypeStruct(weights.shape, weights.dtype)]
        self.scratch = [pltpu.SemaphoreType.DMA((4,)), pltpu.SemaphoreType.DMA((4,))]

    def bind(self, ring, ins, outs, scratch):
        self.r, self.w, self.sems = ring, outs[0], scratch
        self.peers = list(y_partners())

    def start(self):
        self.c = []
        for dx in range(4):
            x = lax.rem(self.r.x + 4 - dx, 4)
            block = self.w.at[:, :, :, group_lanes(x, lax.axis_index("y_lo"))]
            self.c.append(send(block, block, self.sems, dx, self.peers[dx // 2]))

    def finish(self):
        for c in self.c:
            c.wait()


class Torus:
    def __init__(self):
        self.y_hi, self.y_lo, self.z = lax.axis_index("y_hi"), lax.axis_index("y_lo"), lax.axis_index("z")
        self.y = self.y_hi * 2 + self.y_lo
        self.ys = [(dy, lax.rem(self.y + dy, 4)) for dy in (1, 3, 2)]
        self.zs = [(dz, lax.rem(self.z + dz, 4)) for dz in (1, 3, 2)]
        self.peers = [self.y_device(y) for _, y in self.ys] + [{"z": z} for _, z in self.zs]

    def y_device(self, y):
        return {"y_hi": y // 2, "y_lo": lax.rem(y, 2)}


def lanes_at(start, size):
    return pl.ds(pl.multiple_of(start, 128), size)


def add_up(out, terms, lead, rows):
    steps = rows // 16

    def body(k, _):
        i, r = k // steps, pl.ds(pl.multiple_of(lax.rem(k, steps) * 16, 16), 16)
        total = None
        for at in terms:
            term = at(i, r).astype(F32)
            total = term if total is None else total + term
        out(i, r, total.astype(BF))
        return 0

    lax.fori_loop(0, lead * steps, body, 0)


class SumColumns(Side):
    def __init__(self, grads):
        r = self.rows = grads.shape[2]
        dma = pltpu.SemaphoreType.DMA
        self.operands = [grads]
        self.shapes = [jax.ShapeDtypeStruct((r, 1024), BF)]
        self.scratch = [
            pltpu.VMEM((4, 4, r, 512), BF), pltpu.VMEM((4, 2, 2, r, 512), BF),
            pltpu.VMEM((3, r, 512), BF), pltpu.VMEM((3, r, 512), BF),
            dma((9,)), dma((9,)), dma((6,)), dma((6,)), dma((3,)),
        ]

    def bind(self, ring, ins, outs, scratch):
        (self.g,), (self.out,) = ins, outs
        self.by, self.bz, self.by2, self.bz2, s1, r1, s2, r2, self.loc = scratch
        self.one, self.two = (s1, r1), (s2, r2)
        self.t = Torus()
        self.peers = self.t.peers

    def start(self):
        t, g = self.t, self.g
        self.c = []
        for i, (dy, y) in enumerate(t.ys):
            src = g.at[y // 2, :, :, lanes_at(lax.rem(y, 2) * 1024, 512)]
            self.c.append(send(src, self.by.at[dy], self.one, i, t.y_device(y)))
        for i, (dz, z) in enumerate(t.zs):
            for yl in range(2):
                src = g.at[:, z, :, pl.ds(yl * 1024 + 512, 512)]
                self.c.append(send(src, self.bz.at[dz, yl], self.one, 3 + 2 * i + yl, {"z": z}))
        self.l = [pltpu.make_async_copy(g.at[t.y_hi, :, :, lanes_at(t.y_lo * 1024, 512)], self.by.at[0], self.loc.at[0])]
        for yl in range(2):
            self.l.append(
                pltpu.make_async_copy(g.at[:, t.z, :, pl.ds(yl * 1024 + 512, 512)], self.bz.at[0, yl], self.loc.at[1 + yl])
            )
        for copy in self.l:
            copy.start()

    def middle(self):
        t, by, bz = self.t, self.by, self.bz
        for copy in self.l:
            copy.wait()
        for copy in self.c:
            copy.wait_recv()

        def put_y(i, r, v):
            by[0, i, r, :] = v

        def put_z(i, r, v):
            bz[0, i // 2, lax.rem(i, 2), r, :] = v

        add_up(put_y, [lambda i, r, k=k: by[k, i, r, :] for k in range(4)], 4, self.rows)
        add_up(put_z, [lambda i, r, k=k: bz[k, i // 2, lax.rem(i, 2), r, :] for k in range(4)], 4, self.rows)
        self.c2 = []
        for i, (dz, z) in enumerate(t.zs):
            self.c2.append(send(by.at[0, z], self.by2.at[dz - 1], self.two, i, {"z": z}))
        for i, (dy, y) in enumerate(t.ys):
            self.c2.append(send(bz.at[0, lax.rem(y, 2), y // 2], self.bz2.at[dy - 1], self.two, 3 + i, t.y_device(y)))

    def finish(self):
        t, by, bz, by2, bz2, out = self.t, self.by, self.bz, self.by2, self.bz2, self.out
        for copy in self.c2:
            copy.wait_recv()

        def put_a(i, r, v):
            out[r, 0:512] = v

        def put_b(i, r, v):
            out[r, 512:1024] = v

        add_up(put_a, [lambda i, r: by[0, t.z, r, :]] + [lambda i, r, k=k: by2[k, r, :] for k in range(3)], 1, self.rows)
        add_up(put_b, [lambda i, r: bz[0, t.y_lo, t.y_hi, r, :]] + [lambda i, r, k=k: bz2[k, r, :] for k in range(3)], 1, self.rows)
        for copy in self.c + self.c2:
            copy.wait_send()


class SumRows(Side):
    def __init__(self, grads):
        r = self.rows = grads.shape[1]
        dma = pltpu.SemaphoreType.DMA
        self.operands = [grads]
        self.shapes = [jax.ShapeDtypeStruct((2, r, 128), BF)]
        self.scratch = [
            pltpu.VMEM((4, r, 512), BF), pltpu.VMEM((4, 2, 2, r, 128), BF),
            pltpu.VMEM((3, r, 128), BF), pltpu.VMEM((3, r, 128), BF),
            dma((9,)), dma((9,)), dma((6,)), dma((6,)), dma((3,)),
        ]

    def bind(self, ring, ins, outs, scratch):
        (self.g,), (self.out,) = ins, outs
        self.by, self.bz, self.by2, self.bz2, s1, r1, s2, r2, self.loc = scratch
        self.one, self.two = (s1, r1), (s2, r2)
        self.t = Torus()
        self.peers = self.t.peers

    def start(self):
        t, g = self.t, self.g
        self.c = []
        for i, (dy, y) in enumerate(t.ys):
            src = g.at[lax.rem(y, 2), :, lanes_at((y // 2) * 1024, 512)]
            self.c.append(send(src, self.by.at[dy], self.one, i, t.y_device(y)))
        for i, (dz, z) in enumerate(t.zs):
            for yh in range(2):
                src = g.at[:, :, lanes_at(yh * 1024 + 512 + z * 128, 128)]
                self.c.append(send(src, self.bz.at[dz, yh], self.one, 3 + 2 * i + yh, {"z": z}))
        self.l = [pltpu.make_async_copy(g.at[t.y_lo, :, lanes_at(t.y_hi * 1024, 512)], self.by.at[0], self.loc.at[0])]
        for yh in range(2):
            self.l.append(
                pltpu.make_async_copy(g.at[:, :, lanes_at(yh * 1024 + 512 + t.z * 128, 128)], self.bz.at[0, yh], self.loc.at[1 + yh])
            )
        for copy in self.l:
            copy.start()

    def middle(self):
        t, by, bz = self.t, self.by, self.bz
        for copy in self.l:
            copy.wait()
        for copy in self.c:
            copy.wait_recv()

        def put_y(i, r, v):
            by[0, r, :] = v

        def put_z(i, r, v):
            bz[0, i // 2, lax.rem(i, 2), r, :] = v

        add_up(put_y, [lambda i, r, k=k: by[k, r, :] for k in range(4)], 1, self.rows)
        add_up(put_z, [lambda i, r, k=k: bz[k, i // 2, lax.rem(i, 2), r, :] for k in range(4)], 4, self.rows)
        self.c2 = []
        for i, (dz, z) in enumerate(t.zs):
            self.c2.append(send(by.at[0, :, lanes_at(z * 128, 128)], self.by2.at[dz - 1], self.two, i, {"z": z}))
        for i, (dy, y) in enumerate(t.ys):
            self.c2.append(send(bz.at[0, y // 2, lax.rem(y, 2)], self.bz2.at[dy - 1], self.two, 3 + i, t.y_device(y)))

    def finish(self):
        t, by, bz, by2, bz2, out = self.t, self.by, self.bz, self.by2, self.bz2, self.out
        for copy in self.c2:
            copy.wait_recv()

        def put_a(i, r, v):
            out[0, r, :] = v

        def put_b(i, r, v):
            out[1, r, :] = v

        own = lanes_at(t.z * 128, 128)
        add_up(put_a, [lambda i, r: by[0, r, own]] + [lambda i, r, k=k: by2[k, r, :] for k in range(3)], 1, self.rows)
        add_up(put_b, [lambda i, r: bz[0, t.y_hi, t.y_lo, r, :]] + [lambda i, r, k=k: bz2[k, r, :] for k in range(3)], 1, self.rows)
        for copy in self.c + self.c2:
            copy.wait_send()


def piece_lanes(c, part):
    return lanes_at((c // 4) * 1024 + part * 512 + lax.rem(c, 4) * 128, 128)


class SpreadRows(Side):
    def __init__(self, pieces):
        r = pieces.shape[1]
        dma = pltpu.SemaphoreType.DMA
        self.operands = [pieces]
        self.shapes = [jax.ShapeDtypeStruct((r, D), BF)]
        self.scratch = [dma((14,)), dma((14,)), dma((2,))]

    def bind(self, ring, ins, outs, scratch):
        (self.p,), (self.out,) = ins, outs
        self.sems, self.loc = scratch[:2], scratch[2]
        self.here = lax.axis_index("y_hi") * 4 + lax.axis_index("z")
        self.peers = [ctx_peer(self.here, k) for k in range(1, 8)]

    def start(self):
        self.c = []
        for part in range(2):
            dst = self.out.at[:, piece_lanes(self.here, part)]
            for k in range(1, 8):
                self.c.append(send(self.p.at[part], dst, self.sems, part * 7 + k - 1, self.peers[k - 1]))
            copy = pltpu.make_async_copy(self.p.at[part], dst, self.loc.at[part])
            copy.start()
            self.c.append(copy)

    def finish(self):
        for copy in self.c:
            copy.wait()


def op_mid(rows, total, ins, outs):
    (x_ref,), (y1_ref,) = ins, outs
    y1 = x_ref[rows, :].astype(F32) + total
    y1_ref[rows, :] = y1
    return y1 * norm_scale(y1)


def op_loss(rows, total, ins, outs):
    y1_ref, teacher_ref, valid_ref = ins
    out_ref, dy_ref, loss_ref = outs
    y = y1_ref[rows, :] + total
    out_ref[rows, :] = y.astype(BF)
    miss = y - teacher_ref[rows, :].astype(F32)
    valid = valid_ref[rows, :]
    loss_ref[rows, :] = valid * jnp.mean(miss * miss, axis=1, keepdims=True)
    dy = valid * miss
    dy_ref[rows, :] = dy
    return dy


def back_norm(v, grad, u):
    r = norm_scale(v)
    n = v * r
    return grad + r * (u - n * jnp.mean(u * n, axis=1, keepdims=True))


def op_back(rows, total, ins, outs):
    (y1_ref, dy_ref), (dy1_ref,) = ins, outs
    dy1 = back_norm(y1_ref[rows, :], dy_ref[rows, :], total)
    dy1_ref[rows, :] = dy1
    return dy1


def op_input(rows, total, ins, outs):
    (x_ref, dy1_ref), (grad_ref,) = ins, outs
    grad_ref[rows, :] = back_norm(x_ref[rows, :].astype(F32), dy1_ref[rows, :], total)
    return None


def y_partners():
    y_hi, y_lo = lax.axis_index("y_hi"), lax.axis_index("y_lo")
    return {"y_lo": 1 - y_lo}, {"y_hi": 1 - y_hi, "y_lo": 1 - y_lo}


def group_lanes(x, y_lo):
    return pl.ds(pl.multiple_of(x * 512 + y_lo * 256, 256), 256)


def tp_peers(ring):
    found = []
    for k in range(1, 8):
        dx, dc = k // 2, k % 2
        core = 1 - ring.core if dc else ring.core
        found.append((k, lax.rem(ring.x + dx, 4), core))
    return found


def enter_kernel(
    x_ref, meta_ref, g1_ref, g2_ref, wq_ref, wk_ref, wv_ref, wg_ref, wu_ref, wo_ref,
    n1_ref, metas_ref, wqkv_ref, wos_ref, wt_ref,
    own, w, ag_s, ag_r, loc, meta_s, meta_r, w_s, w_r, y_s, y_r, loc2,
):
    ring = Ring()
    y_lo = lax.axis_index("y_lo")
    near, other = y_partners()
    peers = tp_peers(ring)
    meet([{"x": x, "core": core} for _, x, core in peers] + [near, other])
    here = ring.x * 2 + ring.core
    copies = []
    for k, x, core in peers:
        copies.append(send(meta_ref, metas_ref.at[here], (meta_s, meta_r), k, {"x": x, "core": core}))
    local = [pltpu.make_async_copy(meta_ref, metas_ref.at[here], loc2.at[0])]
    local.append(pltpu.make_async_copy(wo_ref, wos_ref.at[y_lo], loc2.at[1]))
    for c in local:
        c.start()
    for half, device in enumerate((near, other)):
        copies.append(send(wo_ref.at[HALVES[half]], wos_ref.at[y_lo, HALVES[half]], (y_s, y_r), 4 + half, device))

    gath = Gather(ring, own, n1_ref, (ag_s, ag_r), loc)
    for half in range(2):

        def body(k, _, half=half):
            rows = pl.ds(half * 64 + k * 16, 16)
            v = x_ref[rows, :].astype(F32)
            own[rows, :] = (v * norm_scale(v)).astype(BF)
            return 0

        lax.fori_loop(0, 4, body, 0)
        gath.start(half)

    def turned(ref, gain, k):
        tile = ref[:, pl.ds(pl.multiple_of(k * 128, 128), 128)].astype(F32) * gain
        return tile.T.astype(BF)

    g1, g2 = g1_ref[...], g2_ref[...]
    for f in range(16):
        w[(f // 4) * 2 + f % 2, pl.ds((f // 2 % 2) * 128, 128), :] = turned(wq_ref, g1, f)
    for ref, at in ((wk_ref, 256), (wv_ref, 320)):
        for k in range(2):
            tile = turned(ref, g1, k)
            for x in (2 * k, 2 * k + 1):
                part = tile[(x % 2) * 64 : (x % 2) * 64 + 64]
                w[2 * x, pl.ds(at, 64), :] = part
                w[2 * x + 1, pl.ds(at, 64), :] = part
    lanes = pl.ds(pl.multiple_of((ring.x * 4 + y_lo * 2 + ring.core) * 128, 128), 128)
    wcopies = {}
    for k, x, core in peers:
        wcopies[k] = send(w.at[x * 2 + core], wqkv_ref.at[:, lanes], (w_s, w_r), k, {"x": x, "core": core})
    wcopies[0] = pltpu.make_async_copy(w.at[here], wqkv_ref.at[:, lanes], loc2.at[2])
    wcopies[0].start()

    def turn_all(ref, i):
        def body(k, _):
            wt_ref[i, pl.ds(pl.multiple_of(k * 128, 128), 128), :] = turned(ref, g2, k)
            return 0

        lax.fori_loop(0, FF // 128, body, 0)

    turn_all(wg_ref, 0)
    gath.forward()
    turn_all(wu_ref, 1)
    for dx in range(4):
        x = lax.rem(ring.x + 4 - dx, 4)
        if dx == 0:
            wcopies[0].wait()
        else:
            wcopies[2 * dx].wait_recv()
        wcopies[2 * dx + 1].wait_recv()
        block = wqkv_ref.at[:, group_lanes(x, y_lo)]
        copies.append(send(block, block, (y_s, y_r), dx, (near, other)[dx // 2]))
    gath.finish()
    for k in range(1, 8):
        wcopies[k].wait_send()
    for c in copies:
        c.wait()
    for c in local:
        c.wait()


def enter(hidden_in, meta, g1, g2, w_query, w_key, w_value, w_gate, w_up, w_out):
    dma = pltpu.SemaphoreType.DMA
    return pl.pallas_call(
        enter_kernel,
        out_shape=[
            jax.ShapeDtypeStruct((8, 128, D), BF),
            jax.ShapeDtypeStruct((8, 16, 128), jnp.int32),
            jax.ShapeDtypeStruct((384, D), BF),
            jax.ShapeDtypeStruct((2, 128, D), BF),
            jax.ShapeDtypeStruct((2, FF, 128), BF),
        ],
        in_specs=[VM] * 9 + [HB],
        out_specs=[HB, VM, HB, HB, VM],
        scratch_shapes=[
            pltpu.VMEM((128, D), BF), pltpu.VMEM((8, 384, 128), BF),
            dma((14,)), dma((14,)), dma((2,)), dma((8,)), dma((8,)), dma((8,)), dma((8,)), dma((6,)), dma((6,)), dma((3,)),
        ],
        compiler_params=params(5),
        name="enter",
    )(hidden_in, meta, g1, g2, w_query, w_key, w_value, w_gate, w_up, w_out)


def ctx_peer(c, k):
    other = lax.rem(c + k, 8)
    return {"y_hi": other // 4, "z": lax.rem(other, 4)}


def nt(a, b):
    return dot(a, b, 1, 1)


def nn(a, b):
    return dot(a, b, 1, 0)


def key_bias(meta_ref, d, c, bias):
    docs = meta_ref[d].astype(F32)
    query_docs = meta_ref[d, pl.ds(c, 1), :].astype(F32)
    lane = lax.broadcasted_iota(jnp.int32, (128, 128), 1)
    row = lax.broadcasted_iota(jnp.int32, (128, 128), 0)

    def position(owner, i):
        return jnp.where(i < 64, owner * 64 + i, (15 - owner) * 64 + i - 64)

    query_pos = position(c, lane)
    for b in range(8):
        key_docs = jnp.broadcast_to(docs[b : b + 1, :], (128, 128)).T
        good = (query_pos >= position(b, row)) & (key_docs == query_docs)
        bias[pl.ds(b * 128, 128), :] = jnp.where(good, 0.0, NEGATIVE)


def attend_kernel(
    qkv_ref, meta_ref, tab_ref, wt_ref, wdn_ref,
    a_ref, qp_ref, kv_ref, lse_ref, wgu_ref, wd_ref,
    bias, probs, kv_s, kv_r, fw_s, fw_r, w_s, w_r, y_s, y_r, loc,
):
    ring = Ring()
    y_lo = lax.axis_index("y_lo")
    c = lax.axis_index("y_hi") * 4 + lax.axis_index("z")
    near, other = y_partners()
    peers = tp_peers(ring)
    meet([ctx_peer(c, k) for k in range(1, 8)] + [{"x": x, "core": core} for _, x, core in peers] + [near, other])

    lane = lax.broadcasted_iota(jnp.int32, (128, 128), 1)

    def rope(u, i):
        return u * tab_ref[i] + pltpu.roll(u, 96, 1) * tab_ref[i + 1] + pltpu.roll(u, 32, 1) * tab_ref[i + 2]

    for d in range(8):
        kv_ref[d % 2, d // 2, c] = rope(qkv_ref[pl.ds(d * 128, 128), 256:384], 3).astype(BF)
    kv_copies = []
    for k in range(1, 8):
        block = kv_ref.at[ring.core, :, c]
        kv_copies.append(send(block, block, (kv_s, kv_r), k - 1, ctx_peer(c, k)))

    copies, local = [], []
    here = pl.ds(pl.multiple_of((ring.x * 4 + y_lo * 2 + ring.core) * 128, 128), 128)
    for j in range(2):
        rows = pl.ds(pl.multiple_of((ring.x * 4 + 2 * j + ring.core) * 352, 32), 352)
        local.append(pltpu.make_async_copy(wt_ref.at[:, rows], wgu_ref.at[:, j, :, here], loc.at[j]))
    rows = pl.ds(pl.multiple_of(y_lo * 352, 32), 352)
    local.append(pltpu.make_async_copy(wdn_ref, wd_ref.at[rows], loc.at[2]))
    for copy in local:
        copy.start()
    for k, x, core in peers:
        for j in range(2):
            rows = pl.ds(pl.multiple_of((x * 4 + 2 * j + core) * 352, 32), 352)
            copies.append(
                send(wt_ref.at[:, rows], wgu_ref.at[:, j, :, here], (w_s, w_r), k * 2 + j, {"x": x, "core": core})
            )
    for half, device in enumerate((near, other)):
        rows = pl.ds(pl.multiple_of(y_lo * 352 + half * 176, 16), 176)
        copies.append(send(wdn_ref.at[pl.ds(half * 176, 176)], wd_ref.at[rows], (y_s, y_r), half, device))

    def turn_queries(d, _):
        for j in range(2):
            u = rope(qkv_ref[pl.ds(pl.multiple_of(d * 128, 128), 128), pl.ds(j * 128, 128)], 0) * 0.125
            qp_ref[d, pl.ds(j * 256, 128), :] = jnp.where(lane < 64, u, 0.0).astype(BF)
            qp_ref[d, pl.ds(j * 256 + 128, 128), :] = jnp.where(lane < 64, pltpu.roll(u, 64, 1), 0.0).astype(BF)
        return 0

    lax.fori_loop(0, 8, turn_queries, 0)

    forwards = []
    for k in range(1, 8):
        kv_copies[k - 1].wait_recv()
        block = kv_ref.at[ring.core, :, lax.rem(c + 8 - k, 8)]
        forwards.append(send(block, block, (fw_s, fw_r), k - 1, ring.sibling))
    for copy in forwards:
        copy.wait_recv()

    def one(d, _):
        key_bias(meta_ref, d, c, bias)
        kv = kv_ref[lax.rem(d, 2), d // 2].reshape(1024, 128)
        scores = nt(kv, qp_ref[d])
        for h in range(4):
            s = scores[:, h * 128 : (h + 1) * 128] + bias[...]
            top = jnp.max(s, axis=0, keepdims=True)
            e = jnp.exp(s - top)
            total = jnp.sum(e, axis=0, keepdims=True)
            probs[:, h * 128 : (h + 1) * 128] = (e * (1.0 / total)).astype(BF)
            lse_ref[d, :, h * 128 : (h + 1) * 128] = jnp.broadcast_to(top + jnp.log(total), (8, 128))
        mixed = nn(kv.T, probs[...])
        for j in range(2):
            two = jnp.concatenate([mixed[64:, (2 * j) * 128 : (2 * j + 1) * 128], mixed[64:, (2 * j + 1) * 128 : (2 * j + 2) * 128]], axis=0)
            a_ref[pl.ds(pl.multiple_of(d * 128, 128), 128), pl.ds(j * 128, 128)] = two.T.astype(BF)
        return 0

    lax.fori_loop(0, 8, one, 0)
    for copy in kv_copies + forwards:
        copy.wait_send()
    for copy in copies:
        copy.wait()
    for copy in local:
        copy.wait()


def attend(qkv, metas, tabs, wt, w_down):
    dma = pltpu.SemaphoreType.DMA
    return pl.pallas_call(
        attend_kernel,
        out_shape=[
            jax.ShapeDtypeStruct((1024, 256), BF),
            jax.ShapeDtypeStruct((8, 512, 128), BF),
            jax.ShapeDtypeStruct((2, 4, 8, 128, 128), BF),
            jax.ShapeDtypeStruct((8, 8, 512), F32),
            jax.ShapeDtypeStruct((2, 2, 352, D), BF),
            jax.ShapeDtypeStruct((704, D), BF),
        ],
        in_specs=[VM, VM, VM, HB, HB],
        out_specs=[VM, VM, VM, VM, HB, HB],
        scratch_shapes=[
            pltpu.VMEM((1024, 128), F32), pltpu.VMEM((1024, 512), BF),
            dma((7,)), dma((7,)), dma((7,)), dma((7,)), dma((16,)), dma((16,)), dma((2,)), dma((2,)), dma((3,)),
        ],
        compiler_params=params(6),
        name="attend",
    )(qkv, metas, tabs, wt, w_down)


def attend_back_kernel(
    side, qp_ref, kv_ref, lse_ref, meta_ref, tab_ref, da_ref, side_in,
    dqkv_ref, side_out,
    bias, dap, ds, pb, mine, theirs, stage, back, co_s, co_r, kv_s, kv_r, *side_scratch,
):
    ring = Ring()
    c = lax.axis_index("y_hi") * 4 + lax.axis_index("z")
    side.bind(ring, (side_in,), (side_out,), side_scratch)
    meet([ctx_peer(c, k) for k in range(1, 8)] + [ring.sibling] + side.peers)
    side.start()
    lane = lax.broadcasted_iota(jnp.int32, (128, 128), 1)

    def unrope(u, i):
        return u * tab_ref[i] - pltpu.roll(u, 96, 1) * tab_ref[i + 1] - pltpu.roll(u, 32, 1) * tab_ref[i + 2]

    def one(x, core):
        d = x * 2 + core
        rows = pl.ds(pl.multiple_of(d * 128, 128), 128)
        key_bias(meta_ref, d, c, bias)
        for j in range(2):
            tile = da_ref[rows, pl.ds(j * 128, 128)].astype(F32)
            dap[pl.ds(j * 256, 128), :] = jnp.where(lane >= 64, pltpu.roll(tile, 64, 1), 0.0).astype(BF)
            dap[pl.ds(j * 256 + 128, 128), :] = jnp.where(lane >= 64, tile, 0.0).astype(BF)
        kv = kv_ref[core, x].reshape(1024, 128)
        scores = nt(kv, qp_ref[d])
        dprobs = nt(kv, dap[...])
        for h in range(4):
            cols = slice(h * 128, (h + 1) * 128)
            p = jnp.exp(scores[:, cols] + bias[...] - lse_ref[d, 0:1, cols])
            pb[:, cols] = p.astype(BF)
            dp = dprobs[:, cols]
            centre = jnp.sum(p * dp, axis=0, keepdims=True)
            ds[:, cols] = (p * (dp - centre)).astype(BF)
        dkv = nn(ds[...], qp_ref[d]) + nn(pb[...], dap[...])
        dq = nn(kv.T, ds[...]) * 0.125
        for j in range(2):
            two = jnp.concatenate([dq[:64, (2 * j) * 128 : (2 * j + 1) * 128], dq[:64, (2 * j + 1) * 128 : (2 * j + 2) * 128]], axis=0)
            dqkv_ref[rows, pl.ds(j * 128, 128)] = unrope(two.T, 0).astype(BF)
        return dkv

    def to_sibling(x, _):
        mine[x] = one(x, 1 - ring.core).astype(BF).reshape(8, 128, 128)
        send(mine.at[x], theirs.at[x], (co_s, co_r), x, ring.sibling)
        dqkv_ref[pl.ds(pl.multiple_of((x * 2 + 1 - ring.core) * 128, 128), 128), 256:384] = jnp.zeros((128, 128), BF)
        return 0

    lax.fori_loop(0, 4, to_sibling, 0)

    def core_copy(x):
        return pltpu.make_async_remote_copy(
            src_ref=mine.at[x], dst_ref=theirs.at[x], send_sem=co_s.at[x], recv_sem=co_r.at[x],
            device_id=ring.sibling, device_id_type=MESH,
        )

    def kv_copy(x, k):
        return pltpu.make_async_remote_copy(
            src_ref=stage.at[x, lax.rem(c + k, 8)], dst_ref=back.at[x, k - 1], send_sem=kv_s.at[x * 7 + k - 1],
            recv_sem=kv_r.at[x * 7 + k - 1], device_id=ctx_peer(c, k), device_id_type=MESH,
        )

    def to_owners(x, _):
        dkv = one(x, ring.core)
        core_copy(x).wait_recv()
        stage[x] = (dkv + theirs[x].reshape(1024, 128).astype(F32)).astype(BF).reshape(8, 128, 128)
        for k in range(1, 8):
            kv_copy(x, k).start()
        return 0

    side.middle()
    lax.fori_loop(0, 4, to_owners, 0)

    def gather_up(x, _):
        total = stage[x, c].astype(F32)
        for k in range(1, 8):
            kv_copy(x, k).wait_recv()
            total += back[x, k - 1].astype(F32)
        rows = pl.ds(pl.multiple_of((x * 2 + ring.core) * 128, 128), 128)
        dqkv_ref[rows, 256:384] = unrope(total, 3).astype(BF)
        return 0

    lax.fori_loop(0, 4, gather_up, 0)

    def drain(x, _):
        core_copy(x).wait_send()
        for k in range(1, 8):
            kv_copy(x, k).wait_send()
        return 0

    lax.fori_loop(0, 4, drain, 0)
    side.finish()


def attend_back(qp, kv, lse, metas, tabs, da, side):
    dma = pltpu.SemaphoreType.DMA
    return pl.pallas_call(
        functools.partial(attend_back_kernel, side),
        out_shape=[jax.ShapeDtypeStruct((1024, 384), BF)] + side.shapes,
        in_specs=[VM] * 6 + [HB],
        out_specs=[VM, VM],
        scratch_shapes=[
            pltpu.VMEM((1024, 128), F32), pltpu.VMEM((512, 128), BF),
            pltpu.VMEM((1024, 512), BF), pltpu.VMEM((1024, 512), BF),
            pltpu.VMEM((4, 8, 128, 128), BF), pltpu.VMEM((4, 8, 128, 128), BF),
            pltpu.VMEM((4, 8, 128, 128), BF), pltpu.VMEM((4, 7, 128, 128), BF),
            dma((4,)), dma((4,)), dma((28,)), dma((28,)), *side.scratch,
        ],
        compiler_params=params(7),
        name="attend_back",
    )(qp, kv, lse, metas, tabs, da, *side.operands)


def rope_tables(c):
    cos, sin = tables(positions_of(c))
    low = jnp.arange(HD) < HD // 2
    to_low, to_high = jnp.where(low, -sin, 0.0), jnp.where(low, 0.0, sin)
    one, zero = jnp.ones_like(cos), jnp.zeros_like(cos)
    pairs = [(cos, cos), (to_low, to_low), (to_high, to_high), (cos, one), (to_low, zero), (to_high, zero)]
    return jnp.stack([jnp.concatenate(p, axis=1) for p in pairs])


def group_peers():
    x, y_lo, core = lax.axis_index("x"), lax.axis_index("y_lo"), lax.axis_index("core")
    found = []
    for k in range(1, 16):
        dx, dy, dc = k // 4, k // 2 % 2, k % 2
        found.append((k, {"x": lax.rem(x + dx, 4), "y_lo": 1 - y_lo if dy else y_lo, "core": 1 - core if dc else core}))
    return found


def return_kernel(
    stats_ref, gu_ref, qkv_ref, out_ref, dn_ref, g1_ref, g2_ref, wq_ref, wk_ref, wv_ref, wg_ref, wu_ref,
    info_ref, q_ref, k_ref, v_ref, o_ref, gate_ref, up_ref, down_ref, gains_ref,
    st1, st2, mid, got_gu, got_qkv, all_gu, all_qkv, all_out,
    st_s, st_r, st2_s, st2_r, gu_s, gu_r, qkv_s, qkv_r, agu_s, agu_r, aqkv_s, aqkv_r, ao_s, ao_r, loc,
):
    x, y_lo, core = lax.axis_index("x"), lax.axis_index("y_lo"), lax.axis_index("core")
    c = lax.axis_index("y_hi") * 4 + lax.axis_index("z")
    group = group_peers()
    ctx = [(k, ctx_peer(c, k)) for k in range(1, 8)]
    meet([device for _, device in group] + [device for _, device in ctx])
    here16, here8 = x * 4 + y_lo * 2 + core, x * 2 + core

    def same(j):
        return here16 == y_lo * 8 + j

    def owner(j):
        return {"x": y_lo * 2 + j // 4, "y_lo": j // 2 % 2, "core": j % 2}

    moves = ((gu_ref, got_gu, (gu_s, gu_r)), (qkv_ref, got_qkv, (qkv_s, qkv_r)))

    def move(src, dst, sems, j):
        return pltpu.make_async_remote_copy(
            src_ref=src.at[:, pl.ds(j * 128, 128)], dst_ref=dst.at[here8], send_sem=sems[0].at[j], recv_sem=sems[1].at[here8],
            device_id=owner(j), device_id_type=MESH,
        )

    def move_here(src, dst, sems, j):
        return pltpu.make_async_copy(src.at[:, pl.ds(j * 128, 128)], dst.at[here8], sems[1].at[here8])

    for src, dst, sems in moves:
        for j in range(8):

            @pl.when(same(j))
            def _():
                move_here(src, dst, sems, j).start()

            @pl.when(jnp.logical_not(same(j)))
            def _():
                move(src, dst, sems, j).start()

    copies = [send(stats_ref, st1.at[here16], (st_s, st_r), k, device) for k, device in group]
    st1[here16] = stats_ref[...]
    for part in range(2):
        dst = all_out.at[:, piece_lanes(c, part)]
        for k, device in ctx:
            copies.append(send(out_ref.at[part], dst, (ao_s, ao_r), part * 7 + k - 1, device))
        copy = pltpu.make_async_copy(out_ref.at[part], dst, loc.at[part])
        copy.start()
        copies.append(copy)

    for copy in copies[:15]:
        copy.wait_recv()
    total = st1[0]
    for i in range(1, 16):
        total += st1[i]
    mid[...] = total
    st2[c] = total
    copies2 = [send(mid, st2.at[c], (st2_s, st2_r), k - 1, device) for k, device in ctx]

    def from_source(dst, sems, s):
        return pltpu.make_async_copy(dst.at[s], dst.at[s], sems[1].at[s])

    for _, dst, sems in moves:
        for s in range(8):
            from_source(dst, sems, s).wait()

    def gu_rows(s):
        return pl.ds(pl.multiple_of(((s // 2) * 4 + lax.rem(c // 2, 2) * 2 + s % 2) * 352 + lax.rem(c, 2) * 176, 16), 176)

    for s in range(8):
        dst = all_gu.at[c // 4, gu_rows(s)]
        copy = pltpu.make_async_copy(got_gu.at[s], dst, loc.at[2 + s])
        copy.start()
        copies2.append(copy)
        for k, device in ctx:
            copies2.append(send(got_gu.at[s], dst, (agu_s, agu_r), s * 7 + k - 1, device))
    dst = all_qkv.at[:, c]
    copy = pltpu.make_async_copy(got_qkv, dst, loc.at[10])
    copy.start()
    copies2.append(copy)
    for k, device in ctx:
        copies2.append(send(got_qkv, dst, (aqkv_s, aqkv_r), k - 1, device))

    for copy in copies2[:7]:
        copy.wait_recv()
    total = st2[0]
    for i in range(1, 8):
        total += st2[i]
    sums = jnp.sum(total, axis=1, keepdims=True)
    squares, count = sums[0:1], sums[1:2]
    scale = 2.0 / (D * count)
    info_ref[...] = jnp.concatenate([squares / count, scale, jnp.zeros((6, 1), F32)], axis=0) + jnp.zeros((8, 128), F32)

    down_scale = jnp.broadcast_to(scale, (16, 1))

    def scaled(src, dst, rows):
        def body(i, _):
            r = pl.ds(pl.multiple_of(i * 16, 16), 16)
            dst[r, :] = src[r, :].astype(F32) * down_scale
            return 0

        lax.fori_loop(0, rows // 16, body, 0)

    scaled(dn_ref, down_ref, 352)
    for copy in copies[15:]:
        copy.wait()
    scaled(all_out, o_ref, 128)

    for copy in copies2[7:]:
        copy.wait()
    g1, g2 = g1_ref[...], g2_ref[...]
    s1, s2 = g1 * scale, g2 * scale

    sum1 = jnp.zeros((128, 128), F32)
    for s in range(8):
        for j in range(2):
            f = (s // 2) * 4 + j * 2 + s % 2
            part = all_qkv[s].reshape(384, 128)[j * 128 : (j + 1) * 128].astype(F32).T
            sum1 += part * wq_ref[:, f * 128 : (f + 1) * 128].astype(F32)
            q_ref[:, f * 128 : (f + 1) * 128] = part * s1
    for i in range(2):
        both = []
        for xs in (2 * i, 2 * i + 1):
            both.append(
                all_qkv[2 * xs].reshape(384, 128)[256:].astype(F32) + all_qkv[2 * xs + 1].reshape(384, 128)[256:].astype(F32)
            )
        for at, w_ref, g_ref in ((0, wk_ref, k_ref), (64, wv_ref, v_ref)):
            part = jnp.concatenate([both[0][at : at + 64], both[1][at : at + 64]], axis=0).T
            sum1 += part * w_ref[:, i * 128 : (i + 1) * 128].astype(F32)
            g_ref[:, i * 128 : (i + 1) * 128] = part * s1

    def body(k, total):
        at = lanes_at(k * 128, 128)
        rows = pl.ds(pl.multiple_of(k * 128, 128), 128)
        for i, w_ref, g_ref in ((0, wg_ref, gate_ref), (1, wu_ref, up_ref)):
            part = all_gu[i, rows, :].astype(F32).T
            total += part * w_ref[:, at].astype(F32)
            g_ref[:, at] = part * s2
        return total

    sum2 = lax.fori_loop(0, FF // 128, body, jnp.zeros((128, 128), F32))
    gains_ref[0] = jnp.sum(sum1, axis=1, keepdims=True) * scale
    gains_ref[1] = jnp.sum(sum2, axis=1, keepdims=True) * scale
    for copy in copies[:15] + copies2[:7]:
        copy.wait_send()
    for src, dst, sems in moves:
        for j in range(8):

            @pl.when(jnp.logical_not(same(j)))
            def _():
                move(src, dst, sems, j).wait_send()


def return_grads(stats, gu, qkv, out, down, g1, g2, w_query, w_key, w_value, w_gate, w_up):
    dma = pltpu.SemaphoreType.DMA
    f32 = lambda *shape: jax.ShapeDtypeStruct(shape, F32)
    pair = lambda n: [dma((n,)), dma((n,))]
    return pl.pallas_call(
        return_kernel,
        out_shape=[
            f32(8, 128), f32(128, D), f32(128, KVD), f32(128, KVD), f32(128, D), f32(128, FF), f32(128, FF), f32(352, D), f32(2, 128, 1),
        ],
        in_specs=[VM] * 12,
        out_specs=[VM] * 9,
        scratch_shapes=[
            pltpu.VMEM((16, 8, 128), F32), pltpu.VMEM((8, 8, 128), F32), pltpu.VMEM((8, 128), F32),
            pltpu.VMEM((8, 176, 128), BF), pltpu.VMEM((8, 48, 128), BF),
            pltpu.VMEM((2, FF, 128), BF), pltpu.VMEM((8, 8, 48, 128), BF), pltpu.VMEM((128, D), BF),
            *pair(16), *pair(7), *pair(8), *pair(8), *pair(56), *pair(7), *pair(14), dma((11,)),
        ],
        compiler_params=params(8),
        name="return_grads",
    )(stats, gu, qkv, out, down, g1, g2, w_query, w_key, w_value, w_gate, w_up)


def local(hidden_in, teacher, doc_ids, valid_mask, norm1_gain, w_query, w_key, w_value, w_out, norm2_gain, w_gate, w_up, w_down):
    c = lax.axis_index(("y_hi", "z"))
    g1 = norm1_gain.astype(F32)
    g2 = norm2_gain.astype(F32)
    valid = valid_mask.astype(F32)
    tabs = rope_tables(c)
    blocks = doc_ids.reshape(16, 64)
    key_docs = jnp.concatenate([blocks[:8], blocks[:7:-1]], axis=1)
    meta = jnp.concatenate([key_docs, valid_mask[None], jnp.zeros((7, 128), jnp.int32)], axis=0)

    n1_all, metas, wqkv, wo, wt = enter(
        hidden_in, meta, g1[:, None], g2[:, None], w_query, w_key, w_value, w_gate, w_up, w_out
    )
    n1_all = n1_all.reshape(1024, D)
    wo = wo.reshape(256, D)
    qkv = dot(n1_all, wqkv, 1, 1)
    a, qp, kv, lse, wgu, wd = attend(qkv, metas, tabs, wt, w_down)

    def parts(v):
        return v.astype(BF).reshape(8, 128, D)

    wide = jax.ShapeDtypeStruct((128, D), F32)
    y1, n2_all, wgu = exchange(1, op_mid, parts(dot(a, wo, 1, 0)), (hidden_in,), (wide,), sides=[YSwap(wgu)])
    n2_all = n2_all.reshape(1024, D)
    wgu = wgu.reshape(1408, D)
    gate = dot(n2_all, wgu[:704], 1, 1)
    up = dot(n2_all, wgu[704:], 1, 1)
    sg = jax.nn.sigmoid(gate)
    act = gate * sg
    mid = (act * up).astype(BF)
    layer_out, dy, loss_rows, dy_all = exchange(
        2,
        op_loss,
        parts(dot(mid, wd, 1, 0)),
        (y1, teacher, valid[:, None]),
        (jax.ShapeDtypeStruct((128, D), BF), wide, jax.ShapeDtypeStruct((128, 1), F32)),
    )
    dy_all = dy_all.reshape(1024, D)

    grad_down = dot(mid, dy_all, 0, 0).astype(BF)
    dmid = dot(dy_all, wd, 1, 1)
    dgate = (dmid * up * sg * (1.0 + gate * (1.0 - sg))).astype(BF)
    dup = (dmid * act).astype(BF)
    dgu = jnp.concatenate([dgate, dup], axis=1)
    grad_gu = dot(dgu, n2_all, 0, 0).astype(BF)
    dy1, da_all, piece_gu = exchange(
        3, op_back, parts(dot(dgu, wgu, 1, 0)), (y1, dy), (wide,), sides=[SumColumns(grad_gu.reshape(2, 4, 176, D))]
    )
    da_all = da_all.reshape(1024, D)
    da = dot(da_all, wo, 1, 1).astype(BF)
    dqkv, piece_down = attend_back(qp, kv, lse, metas, tabs, da, SumRows(grad_down.reshape(2, 352, D)))
    grad_out = dot(a, da_all, 0, 0).astype(BF)
    grad_qkv = dot(dqkv, n1_all, 0, 0).astype(BF)
    grad_in, piece_qkv, piece_out, all_down = exchange(
        4,
        op_input,
        parts(dot(dqkv, wqkv, 1, 0)),
        (hidden_in, dy1),
        (wide,),
        gather=False,
        sides=[SumColumns(grad_qkv.reshape(2, 4, 48, D)), SumRows(grad_out.reshape(2, 128, D)), SpreadRows(piece_down)],
    )
    stats = jnp.concatenate([loss_rows.reshape(1, 128), valid[None], jnp.zeros((6, 128), F32)], axis=0)
    info, gq, gk, gv, go, gg, gp, gd, gains = return_grads(
        stats, piece_gu, piece_qkv, piece_out, all_down, g1[:, None], g2[:, None], w_query, w_key, w_value, w_gate, w_up
    )
    return (
        layer_out, info[0, 0], grad_in * info[1, 0], gains[0, :, 0], gq, gk, gv, go, gains[1, :, 0], gg, gp, gd,
    )


def solution(mesh):
    fine = Mesh(mesh.devices.reshape(2, 4, 4, 2, 2), AXES)
    rows = ("y_hi", "z", "x", "y_lo", "core")
    fs = ("x", "y_lo", "core")
    token, shard = P(rows, None), P(fs, None)
    return jax.shard_map(
        local,
        mesh=fine,
        in_specs=(token, token, shard, P(rows), P(fs), shard, shard, shard, shard, P(fs), shard, shard, shard),
        out_specs=(token, P(), token, P(fs), shard, shard, shard, shard, P(fs), shard, shard, shard),
        check_vma=False,
    )
```

time: 975 us -> 545 us (0.56)
  waiting for transfers between devices: 267 us -> 0 us
  Pallas kernels: 179 us -> 442 us
  blocking collectives: 195 us -> 0 us
  local copies, waits for them, and re-layouts: 117 us -> 21.5 us
  matrix products: 123 us -> 68.6 us
  other arithmetic: 58.3 us -> 5.96 us
  between operations: 18.7 us -> 1.46 us
    pallas_call x4 -> x8, Pallas kernels: 179 us -> 442 us  [the longest x4 204 us: exchange(): pl.pallas_call(kernel, out_shape=shapes, in_specs=in_specs, out_specs=spe...]
    reduce_scatter x2 -> x0, waiting for transfers between devices: 164 us -> none  [the longest x1 99.5 us: return_rows(): lax.psum_scatter(g.reshape(16, 8 * 16, n), ('y_lo', 'y_hi', 'z'), scatter...]
    all_to_all x4 -> x0, blocking collectives: 96.7 us -> none  [the longest x3 74.8 us: spread_columns(): got = lax.all_to_all(parts, TP, 0, 0)]
    psum x1 -> x0, blocking collectives: 67.5 us -> none  [local(): loss = lax.psum(jnp.sum(loss_rows), AXES) / count]
    all_gather x9 -> x0, waiting for transfers between devices: 64.6 us -> none  [the longest x1 37.8 us: local(): lax.all_gather(jnp.concatenate([k, v], axis=2), CTX, axis=1, tiled=True)]
    dot_general x6 -> x0, matrix products: 45.4 us -> none  [the longest x1 9.48 us: local(): jnp.einsum('shqk,sqhd->skd', probs.astype(BF), da, preferred_element_type...]
    unnamed x13 -> x0, waiting for transfers between devices: 32.8 us -> none
    all_gather x3 -> x0, blocking collectives: 31.2 us -> none  [the longest x2 15.6 us: spread_kv(): got = lax.all_gather(got, 'y_lo', axis=0)]
  transfers between devices with their start and end apart: 14 -> 0, of which waited for: 6 -> 0; matrix products, arithmetic and copies ran while one was open for 17% -> 0% of each run, Pallas kernels for 8% -> 0%
where the time goes in v3:
time: 545 us; the launch traced here: 539 us
  Pallas kernels  442 us (81%)
  matrix products  68.6 us (13%)
  local copies, waits for them, and re-layouts  21.5 us (4%)
  other arithmetic  5.96 us (1%)
    pallas_call x4, Pallas kernels, exchange(): pl.pallas_call(kernel, out_shape=shapes, in_specs=in_specs, out_specs=spe...  204 us
    pallas_call x1, Pallas kernels, return_grads(): pl.pallas_call(return_kernel, out_shape=[f32(8, 128), f32(128, D), f32(12...  74.6 us
    dot_general x13, matrix products, dot(): lax.dot_general(a, b, (((ca,), (cb,)), ((), ())), preferred_element_type=...  68.6 us
    pallas_call x1, Pallas kernels, attend(): pl.pallas_call(attend_kernel, out_shape=[jax.ShapeDtypeStruct((1024, 256)...  64.7 us
    pallas_call x1, Pallas kernels, enter(): pl.pallas_call(enter_kernel, out_shape=[jax.ShapeDtypeStruct((8, 128, D),...  56.1 us
    pallas_call x1, Pallas kernels, attend_back(): pl.pallas_call(functools.partial(attend_back_kernel, side), out_shape=[ja...  42.2 us
    unnamed x62, local copies, waits for them, and re-layouts  11.5 us

profile of v3, /device:TPU:1, one launch (start us, length us, event | category | flops | bytes accessed | tf_op | source)
XLA Modules:
  0.0 539.5 jit_solution(14199938402680918280)
XLA Ops:
  2.5 1.3 add_add_fusion.meta_ref
  6.7 56.1 %enter.1 = (bf16[8,128,2048]{2,1,0:T(8,128)(2,1)}, s32[8,16,128]{2,1,0:T(8,128)}, bf16[384,2048]{1,0:T(8,128)(2,1)}, bf16[2,128,2048]{2,1,0:T(8,128)(2,1)}, bf16[2,5632,128]{2,1,0:T(8,128)(2,1)}) custom-call(bf16[128,2048]{1,0:T(8,128)(2,1)} %refs_1_.3, s32[16,128]{1,0:T(8,128)} %add_add_fusion.meta_ref, f32[128,1]{1,0:T(8,128)} %copy.31.g1_ref, ...), custom_call_target="tpu_custom_call" | custom-call | tf_op jit(solution)/shard_map/enter/pallas_call | solution.py:670
  62.8 6.2 %fusion.11.qkv_ref = f32[1024,384]{1,0:T(8,128)} fusion(bf16[1024,2048]{1,0:T(8,128)(2,1)} %bitcast.89, bf16[384,2048]{1,0:T(8,128)(2,1)} %get-tuple-element.49), kind=kOutput, calls=%fused_computation.50 | convolution fusion | flops 1610612736 | bytes 7340032 | tf_op jit(solution)/shard_map/dot_general | solution.py:25
  69.0 64.7 %attend.1 = (bf16[1024,256]{1,0:T(8,128)(2,1)}, bf16[8,512,128]{2,1,0:T(8,128)(2,1)}, bf16[2,4,8,128,128]{4,3,2,1,0:T(8,128)(2,1)}, f32[8,8,512]{2,1,0:T(8,128)}...) custom-call(f32[1024,384]{1,0:T(8,128)} %fusion.11.qkv_ref, s32[8,16,128]{2,1,0:T(8,128)} %get-tuple-element.50.meta_ref, ...), custom_call_target="tpu_custom_call" | custom-call | tf_op jit(solution)/shard_map/attend/pallas_call | solution.py:807
  133.8 4.2 convolution_convert_fusion.4
  138.0 49.7 %exchange1.1 = (f32[128,2048]{1,0:T(8,128)}, bf16[8,128,2048]{2,1,0:T(8,128)(2,1)}, bf16[2,2,352,2048]{3,2,1,0:T(8,128)(2,1)}) custom-call(bf16[8,128,2048]{2,1,0:T(8,128)(2,1)} %bitcast.72, bf16[128,2048]{1,0:T(8,128)(2,1)} %refs_1_.3, bf16[2,2,352,2048]{3,2,1,0:T(8,128)(2,1)} %get-tuple-element.54.refs_2_), custom_call_target="tpu_custom_call", output_to_operand_aliasing={{2}: (2, {})} | custom-call | tf_op jit(solution)/shard_map/exchange1/pallas_call | solution.py:271
  187.7 3.8 fusion.9
  191.6 3.2 fusion.12
  194.8 4.9 multiply_convert_fusion.2
  199.6 5.1 convolution_convert_fusion.3
  205.5 50.1 %exchange2.1 = (bf16[128,2048]{1,0:T(8,128)(2,1)}, f32[128,2048]{1,0:T(8,128)}, f32[128,1]{1,0:T(8,128)}, bf16[8,128,2048]{2,1,0:T(8,128)(2,1)}) custom-call(bf16[8,128,2048]{2,1,0:T(8,128)(2,1)} %bitcast.79, f32[128,2048]{1,0:T(8,128)} %get-tuple-element.58.refs_1_, bf16[128,2048]{1,0:T(8,128)(2,1)} %refs_2_.1, f32[128,1]{1,0:T(8,128)} %copy.33.refs_3_), custom_call_target="tpu_custom_call" | custom-call | tf_op jit(solution)/shard_map/exchange2/pallas_call | solution.py:271
  255.6 7.3 %multiply_convert_fusion.1 = (bf16[1024,704]{0,1:T(8,128)(2,1)S(1)}, bf16[1024,704]{0,1:T(8,128)(2,1)S(1)}) fusion(f32[1024,704]{0,1:T(8,128)} %copy-done.23, f32[1024,704]{0,1:T(8,128)} %get-tuple-element.100, bf16[1024,2048]{1,0:T(8,128)(2,1)} %bitcast.94, bf16[704,2048]{1,0:T(8,128)(2,1)S(1)} %copy-done.20), kind=kOutput, calls=%fused_computation.8 | convolution fusion | flops 2962161664 | bytes 15728640 | tf_op jit(solution)/shard_map/dot_general | solution.py:25
  263.0 9.4 %convolution_convert_fusion = bf16[1408,2048]{1,0:T(8,128)(2,1)} fusion(bf16[1024,2048]{1,0:T(8,128)(2,1)S(1)} %bitcast.93, bf16[1024,704]{0,1:T(8,128)(2,1)S(1)} %get-tuple-element.89, bf16[1024,704]{0,1:T(8,128)(2,1)S(1)} %get-tuple-element.88), kind=kOutput, calls=%fused_computation | convolution fusion | flops 5914230784 | bytes 12845056 | tf_op jit(solution)/shard_map/dot_general | solution.py:25
  272.4 8.6 %convolution_convert_fusion.2 = bf16[1024,2048]{1,0:T(8,128)(2,1)} fusion(bf16[1408,2048]{1,0:T(8,128)(2,1)S(1)} %bitcast.75, bf16[1024,704]{0,1:T(8,128)(2,1)S(1)} %get-tuple-element.89, bf16[1024,704]{0,1:T(8,128)(2,1)S(1)} %get-tuple-element.88), kind=kOutput, calls=%fused_computation.2 | convolution fusion | flops 5913444352 | bytes 12845056 | tf_op jit(solution)/shard_map/dot_general | solution.py:25
  281.0 59.5 %exchange3.1 = (f32[128,2048]{1,0:T(8,128)}, bf16[8,128,2048]{2,1,0:T(8,128)(2,1)}, bf16[176,1024]{1,0:T(8,128)(2,1)}) custom-call(bf16[8,128,2048]{2,1,0:T(8,128)(2,1)} %bitcast.77, f32[128,2048]{1,0:T(8,128)} %get-tuple-element.58.refs_1_, f32[128,2048]{1,0:T(8,128)} %get-tuple-element.62.refs_2_, bf16[2,4,176,2048]{3,2,1,0:T(8,128)(2,1)} %bitcast.76), custom_call_target="tpu_custom_call" | custom-call | tf_op jit(solution)/shard_map/exchange3/pallas_call | solution.py:271
  340.5 4.6 convolution_convert_fusion.7
  345.1 4.4 convolution_convert_fusion.5
  349.5 2.2 convolution_convert_fusion.8.da_ref
  351.7 42.2 %attend_back.1 = (bf16[1024,384]{1,0:T(8,128)(2,1)}, bf16[2,352,128]{2,1,0:T(8,128)(2,1)}) custom-call(bf16[8,512,128]{2,1,0:T(8,128)(2,1)} %get-tuple-element.64.qp_ref, bf16[2,4,8,128,128]{4,3,2,1,0:T(8,128)(2,1)} %get-tuple-element.65.kv_ref, f32[8,8,512]{2,1,0:T(8,128)} %get-tuple-element.66.lse_ref, s32[8,16,128]{2,1,0:T(8,128)} %get-tuple-element.50.meta_ref, ...), custom_call_target="tpu_custom_call" | custom-call | tf_op jit(solution)/shard_map/attend_back/pallas_call | solution.py:922
  393.9 4.3 convolution_convert_fusion.6
  398.2 4.3 convolution_convert_fusion.1
  402.5 45.1 %exchange4.1 = (f32[128,2048]{1,0:T(8,128)}, bf16[48,1024]{1,0:T(8,128)(2,1)}, bf16[2,128,128]{2,1,0:T(8,128)(2,1)}, bf16[352,2048]{1,0:T(8,128)(2,1)}) custom-call(bf16[8,128,2048]{2,1,0:T(8,128)(2,1)} %bitcast.78, bf16[128,2048]{1,0:T(8,128)(2,1)} %refs_1_.3, f32[128,2048]{1,0:T(8,128)} %get-tuple-element.69.refs_2_, bf16[2,4,48,2048]{3,2,1,0:T(8,128)(2,1)} %bitcast.83, ...), custom_call_target="tpu_custom_call" | custom-call | tf_op jit(solution)/shard_map/exchange4/pallas_call | solution.py:271
  448.5 74.6 %return_grads.1 = (f32[8,128]{1,0:T(8,128)}, f32[128,2048]{1,0:T(8,128)}, f32[128,256]{1,0:T(8,128)}, f32[128,256]{1,0:T(8,128)}, f32[128,2048]{1,0:T(8,128)}, /...) custom-call(f32[8,128]{1,0:T(8,128)} %maximum_maximum_fusion.stats_ref, ...), custom_call_target="tpu_custom_call" | custom-call | tf_op jit(solution)/shard_map/return_grads/pallas_call | solution.py:1115
  523.1 1.3 fusion.10
  524.4 1.8 broadcast_multiply_fusion
  526.2 1.5 slice_reduce_fusion
  528.5 1.0 copy.51
  531.7 1.6 copy.55
  533.3 1.3 copy-done.1
  534.6 1.6 copy.56
  536.2 1.3 copy-done
  537.4 1.6 copy.57
  (83 shorter events, 9.4 us)
Async XLA Ops:
  1.5 67.5 %copy-start.3 = (f32[6,128,128]{2,1,0:T(8,128)}, f32[6,128,128]{2,1,0:T(8,128)S(1)}, u32[]{:S(2)}) copy-start(f32[6,128,128]{2,1,0:T(8,128)S(1)} %bitcast_dynamic-update-slice_fusion.tab_ref) | copy-start | bytes 1179652
  69.0 64.7 %copy-start.8 = (bf16[2,128,2048]{2,1,0:T(8,128)(2,1)S(1)}, bf16[2,128,2048]{2,1,0:T(8,128)(2,1)}, u32[]{:S(2)}) copy-start(bf16[2,128,2048]{2,1,0:T(8,128)(2,1)} %get-tuple-element.53) | copy-start | bytes 3145732
  187.7 3.9 copy-start.15
  194.7 4.9 copy-start.23
  194.7 4.9 copy-start.19
  199.6 5.1 copy-start.13
  205.5 50.2 %copy-start.20 = (bf16[704,2048]{1,0:T(8,128)(2,1)S(1)}, bf16[704,2048]{1,0:T(8,128)(2,1)}, u32[]{:S(2)}) copy-start(bf16[704,2048]{1,0:T(8,128)(2,1)} %get-tuple-element.57) | copy-start | bytes 8650756
  255.6 7.4 %copy-start.16 = (bf16[8,128,2048]{2,1,0:T(8,128)(2,1)S(1)}, bf16[8,128,2048]{2,1,0:T(8,128)(2,1)}, u32[]{:S(2)}) copy-start(bf16[8,128,2048]{2,1,0:T(8,128)(2,1)} %get-tuple-element.55) | copy-start | bytes 12582916
  255.6 16.8 %slice-start = ((s8[5767168]{0:T(1024)(128)(4,1)}), s8[4194304]{0:T(1024)(128)(4,1)S(1)}, s32[]{:S(2)}) async-start(s8[5767168]{0:T(1024)(128)(4,1)} %bitcast.73), calls=%async_computation | async-start | bytes 8388608
  263.0 9.4 %slice-start.1 = ((s8[5767168]{0:T(1024)(128)(4,1)}), s8[1572864]{0:T(1024)(128)(4,1)S(1)}, s32[]{:S(2)}) async-start(s8[5767168]{0:T(1024)(128)(4,1)} %bitcast.73), calls=%async_computation.1 | async-start | bytes 3145728
  281.0 59.5 %copy-start.4 = (bf16[1024,256]{1,0:T(8,128)(2,1)S(1)}, bf16[1024,256]{1,0:T(8,128)(2,1)}, u32[]{:S(2)}) copy-start(bf16[1024,256]{1,0:T(8,128)(2,1)} %get-tuple-element.52) | copy-start | bytes 1572868
  340.5 4.6 copy-start.17
  345.1 4.5 copy-start.18
  351.7 42.2 %copy-start.14 = (bf16[8,128,2048]{2,1,0:T(8,128)(2,1)S(1)}, bf16[8,128,2048]{2,1,0:T(8,128)(2,1)}, u32[]{:S(2)}) copy-start(bf16[8,128,2048]{2,1,0:T(8,128)(2,1)} %get-tuple-element.48) | copy-start | bytes 12582916
  393.9 4.3 copy-start.21
  393.9 4.3 copy-start.22
  402.5 45.1 %copy-start.12 = (f32[128,1]{1,0:T(8,128)S(1)}, f32[128,1]{1,0:T(8,128)}, u32[]{:S(2)}) copy-start(f32[128,1]{1,0:T(8,128)} %get-tuple-element.60) | copy-start | bytes 1540
  447.6 76.8 %copy-start.5 = (f32[128,2048]{1,0:T(8,128)S(1)}, f32[128,2048]{1,0:T(8,128)}, u32[]{:S(2)}) copy-start(f32[128,2048]{1,0:T(8,128)} %get-tuple-element.75) | copy-start | bytes 3145732
  448.5 79.2 %copy-start.9 = (bf16[128,2048]{1,0:T(8,128)(2,1)S(1)}, bf16[128,2048]{1,0:T(8,128)(2,1)}, u32[]{:S(2)}) copy-start(bf16[128,2048]{1,0:T(8,128)(2,1)} %get-tuple-element.115) | copy-start | bytes 1572868
  523.0 5.4 %copy-start.7 = (f32[128,2048]{1,0:T(8,128)S(1)}, f32[128,2048]{1,0:T(8,128)}, u32[]{:S(2)}) copy-start(f32[128,2048]{1,0:T(8,128)} %get-tuple-element.119) | copy-start | bytes 3145732
  523.1 6.4 %copy-start.11 = (f32[128,256]{1,0:T(8,128)S(1)}, f32[128,256]{1,0:T(8,128)}, u32[]{:S(2)}) copy-start(f32[128,256]{1,0:T(8,128)} %get-tuple-element.120) | copy-start | bytes 393220
  523.1 7.0 %copy-start.10 = (f32[128,256]{1,0:T(8,128)S(1)}, f32[128,256]{1,0:T(8,128)}, u32[]{:S(2)}) copy-start(f32[128,256]{1,0:T(8,128)} %get-tuple-element.121) | copy-start | bytes 393220
  524.4 6.4 %copy-start.6 = (f32[128,2048]{1,0:T(8,128)S(1)}, f32[128,2048]{1,0:T(8,128)}, u32[]{:S(2)}) copy-start(f32[128,2048]{1,0:T(8,128)} %get-tuple-element.122) | copy-start | bytes 3145732
  527.7 4.1 copy-start.2
  531.7 2.9 copy-start.1
  534.6 2.9 copy-start

commit v4 on v3

--- a/solution.py
+++ b/solution.py
@@ -90,16 +90,18 @@
         copy.start()
         self.c[14 + half] = copy
 
-    def forward(self):
+    def forward(self, between=lambda: None):
         r, c = self.r, self.c
-        for got, x, half, onward, core_i in (
+        for step, (got, x, half, onward, core_i) in enumerate((
             (0, r.left_x, 0, (4, r.right), 8),
             (2, r.right_x, 1, (5, r.left), 11),
             (1, r.left_x, 1, None, 9),
             (3, r.right_x, 0, None, 10),
             (4, r.far_x, 0, None, 12),
             (5, r.far_x, 1, None, 13),
-        ):
+        )):
+            if step == 2:
+                between()
             c[got].wait_recv()
             block = self.slot(x, half)
             if onward is not None:
@@ -116,69 +118,170 @@
         c[15].wait()
 
 
-class Scatter:
+def norm_scale(v):
+    return lax.rsqrt(jnp.mean(v * v, axis=1, keepdims=True) + EPSILON)
+
+
+class Side:
+    in_place = False
+
+    def middle(self):
+        pass
+
+
+class Torus:
+    def __init__(self):
+        self.y_hi, self.y_lo, self.z = lax.axis_index("y_hi"), lax.axis_index("y_lo"), lax.axis_index("z")
+        self.y = self.y_hi * 2 + self.y_lo
+        self.ys = [(dy, lax.rem(self.y + dy, 4)) for dy in (1, 3, 2)]
+        self.zs = [(dz, lax.rem(self.z + dz, 4)) for dz in (1, 3, 2)]
+        self.peers = [self.y_device(y) for _, y in self.ys] + [{"z": z} for _, z in self.zs]
+
+    def y_device(self, y):
+        return {"y_hi": y // 2, "y_lo": lax.rem(y, 2)}
+
+
+def lanes_at(start, size):
+    return pl.ds(pl.multiple_of(start, 128), size)
+
+
+def add_up(out, terms, lead, rows):
+    steps = rows // 16
+
+    def body(k, _):
+        i, r = k // steps, pl.ds(pl.multiple_of(lax.rem(k, steps) * 16, 16), 16)
+        total = None
+        for at in terms:
+            term = at(i, r).astype(F32)
+            total = term if total is None else total + term
+        out(i, r, total.astype(BF))
+        return 0
+
+    lax.fori_loop(0, lead * steps, body, 0)
+
+
+class Ag:
+    def __init__(self, ring, buf, sems):
+        r = self.r = ring
+        self.buf, self.sems = buf, sems
+        self.plan = (
+            (r.x, 0, r.right), (r.x, 1, r.right), (r.x, 1, r.left), (r.x, 0, r.left),
+            (r.left_x, 0, r.right), (r.right_x, 1, r.left),
+            (r.x, 0, r.sibling), (r.x, 1, r.sibling),
+            (r.left_x, 0, r.sibling), (r.left_x, 1, r.sibling), (r.right_x, 0, r.sibling), (r.right_x, 1, r.sibling),
+            (r.far_x, 0, r.sibling), (r.far_x, 1, r.sibling),
+        )
+
+    def copy(self, i):
+        x, half, device = self.plan[i]
+        block = self.buf.at[x * 2 + self.r.core, HALVES[half]]
+        return pltpu.make_async_remote_copy(
+            src_ref=block, dst_ref=block, send_sem=self.sems[0].at[i], recv_sem=self.sems[1].at[i],
+            device_id=device, device_id_type=MESH,
+        )
+
+    def begin(self, half):
+        for i in ((0, 3, 6), (2, 1, 7))[half]:
+            self.copy(i).start()
+
+    def near(self):
+        for got, onward in ((0, (4, 8)), (2, (5, 11)), (1, (9,)), (3, (10,))):
+            self.copy(got).wait_recv()
+            for i in onward:
+                self.copy(i).start()
+
+    def far(self):
+        for got, onward in ((4, 12), (5, 13)):
+            self.copy(got).wait_recv()
+            self.copy(onward).start()
+
+    def have(self, *which):
+        for i in which:
+            self.copy(i).wait_recv()
+
+    def drain(self):
+        for i in range(14):
+            self.copy(i).wait_send()
+
+
+class Rs:
     def __init__(self, ring, parts, held, got, sems):
-        self.r, self.parts, self.held, self.got, self.sems = ring, parts, held, got, sems
-        self.c = {}
+        r = self.r = ring
+        self.parts, self.held, self.got, self.sems = parts, held, got, sems
+        self.blocks = (r.far_x, r.right_x, r.left_x, r.x)
+        a, b = HALVES
+        self.plan = {
+            4: (held.at[0, a], got.at[4, a], r.right), 5: (held.at[0, b], got.at[4, b], r.left),
+            6: (held.at[1, b], got.at[5, b], r.right), 7: (held.at[2, a], got.at[5, a], r.left),
+            8: (held.at[1, a], got.at[6, a], r.right), 9: (held.at[2, b], got.at[6, b], r.left),
+        }
+
+    def swap(self, i, x):
+        return pltpu.make_async_remote_copy(
+            src_ref=self.parts.at[x * 2 + 1 - self.r.core], dst_ref=self.got.at[i], send_sem=self.sems[0].at[i],
+            recv_sem=self.sems[1].at[i], device_id=self.r.sibling, device_id_type=MESH,
+        )
+
+    def copy(self, i):
+        if i < 4:
+            return self.swap(i, self.blocks[i])
+        src, dst, device = self.plan[i]
+        return pltpu.make_async_remote_copy(
+            src_ref=src, dst_ref=dst, send_sem=self.sems[0].at[i], recv_sem=self.sems[1].at[i],
+            device_id=device, device_id_type=MESH,
+        )
 
     def pair(self, i, half):
-        r = self.r
-        x = (r.far_x, r.right_x, r.left_x, r.x)[i]
+        x = self.blocks[i]
 
         def body(k, _):
             rows = pl.ds(half * 64 + k * 16, 16)
-            total = self.parts[x * 2 + r.core, rows, :].astype(F32) + self.got[i, rows, :].astype(F32)
+            total = self.parts[x * 2 + self.r.core, rows, :].astype(F32) + self.got[i, rows, :].astype(F32)
             self.held[i, rows, :] = total.astype(BF)
             return 0
 
         lax.fori_loop(0, 4, body, 0)
 
-    def onward(self, i, half, slot):
+    def onward(self, i, half):
         def body(k, _):
             rows = pl.ds(half * 64 + k * 16, 16)
-            total = self.held[i, rows, :].astype(F32) + self.got[slot, rows, :].astype(F32)
+            total = self.held[i, rows, :].astype(F32) + self.got[4, rows, :].astype(F32)
             self.held[i, rows, :] = total.astype(BF)
             return 0
 
         lax.fori_loop(0, 4, body, 0)
 
-    def begin(self):
-        r = self.r
-        for i, x in enumerate((r.far_x, r.right_x, r.left_x, r.x)):
-            self.c[i] = send(self.parts.at[x * 2 + (1 - r.core)], self.got.at[i], self.sems, i, r.sibling)
-
-    def run(self):
-        r, c, held, got, sems = self.r, self.c, self.held, self.got, self.sems
-        a, b = HALVES
-        c[0].wait_recv()
+    def send_left(self):
+        self.copy(2).wait_recv()
+        self.pair(2, 0)
+        self.copy(7).start()
+
+    def send_right(self):
+        self.copy(1).wait_recv()
+        self.pair(1, 1)
+        self.copy(6).start()
+
+    def send_far(self):
+        self.copy(0).wait_recv()
         self.pair(0, 0)
-        c[4] = send(held.at[0, a], got.at[4, a], sems, 4, r.right)
+        self.copy(4).start()
         self.pair(0, 1)
-        c[5] = send(held.at[0, b], got.at[4, b], sems, 5, r.left)
-        c[1].wait_recv()
-        self.pair(1, 1)
-        c[6] = send(held.at[1, b], got.at[5, b], sems, 6, r.right)
-        c[2].wait_recv()
-        self.pair(2, 0)
-        c[7] = send(held.at[2, a], got.at[5, a], sems, 7, r.left)
+        self.copy(5).start()
+
+    def relay(self):
         self.pair(1, 0)
         self.pair(2, 1)
-        c[4].wait_recv()
-        self.onward(1, 0, 4)
-        c[8] = send(held.at[1, a], got.at[6, a], sems, 8, r.right)
-        c[5].wait_recv()
-        self.onward(2, 1, 4)
-        c[9] = send(held.at[2, b], got.at[6, b], sems, 9, r.left)
-        c[3].wait_recv()
+        self.copy(4).wait_recv()
+        self.onward(1, 0)
+        self.copy(8).start()
+        self.copy(5).wait_recv()
+        self.onward(2, 1)
+        self.copy(9).start()
+        self.copy(3).wait_recv()
 
     def ready(self, half):
-        c = self.c
-        if half == 0:
-            c[7].wait_recv()
-            c[8].wait_recv()
-        else:
-            c[6].wait_recv()
-            c[9].wait_recv()
+        for i in ((7, 8), (6, 9))[half]:
+            self.copy(i).wait_recv()
 
     def total(self, rows):
         r = self.r
@@ -189,157 +292,244 @@
             + self.got[6, rows, :].astype(F32)
         )
 
-    def finish(self):
+    def drain(self):
         for i in range(10):
-            self.c[i].wait_send()
-
-
-def norm_scale(v):
-    return lax.rsqrt(jnp.mean(v * v, axis=1, keepdims=True) + EPSILON)
-
-
-def exchange(number, op, parts, inputs, outs, gather=True, sides=()):
-    n_in, n_out = len(inputs), len(outs)
-    dma = pltpu.SemaphoreType.DMA
-
-    def kernel(*refs):
-        refs = list(refs)
-
-        def take(n):
-            taken = refs[:n]
-            del refs[:n]
-            return taken
-
-        parts_ref, ins = take(1)[0], take(n_in)
-        side_ins = [take(len(s.operands)) for s in sides]
-        out_refs = take(n_out)
-        all_ref = take(1)[0] if gather else None
-        side_outs = [take(len(s.shapes)) for s in sides]
-        held, got, rs_s, rs_r = take(4)
-        if gather:
-            own, ag_s, ag_r, loc = take(4)
-        ring = Ring()
-        peers = [ring.right, ring.left, ring.sibling]
-        for s, i, o in zip(sides, side_ins, side_outs):
-            s.bind(ring, i, o, take(len(s.scratch)))
-            peers += s.peers
-        meet(peers)
-        scatter = Scatter(ring, parts_ref, held, got, (rs_s, rs_r))
-        if gather:
-            gath = Gather(ring, own, all_ref, (ag_s, ag_r), loc)
-        scatter.begin()
-        for s in sides:
-            s.start()
-        scatter.run()
+            self.copy(i).wait_send()
+
+
+def middle_kernel(
+    side, a_ref, wo_ref, x_ref, teacher_ref, valid_ref, half_w_ref, wd_ref,
+    out_ref, loss_ref, dy1_ref, da_ref, dag_out, ggu_ref, piece_ref,
+    w, n2, dyg, dag, parts, held, got, y1, dy, gate, up, mid, mid_t, dgate, dup, dg_t, du_t, gd, stage,
+    rs1_s, rs1_r, ag1_s, ag1_r, rs2_s, rs2_r, ag2_s, ag2_r, rs3_s, rs3_r, ag3_s, ag3_r, w_s, w_r, loc, *side_scratch,
+):
+    ring = Ring()
+    y_lo = lax.axis_index("y_lo")
+    near, other = y_partners()
+    side.bind(ring, (gd,), (piece_ref,), side_scratch)
+    meet([ring.right, ring.left, ring.sibling, near, other] + side.peers)
+    here = ring.x * 2 + ring.core
+
+    wcopies = []
+    for dx in range(4):
+        lanes = group_lanes(lax.rem(ring.x + 4 - dx, 4), y_lo)
+        src, dst = half_w_ref.at[:, :, :, lanes], w.at[:, :, :, lanes]
+        wcopies.append(send(src, dst, (w_s, w_r), dx, (near, other)[dx // 2]))
+        copy = pltpu.make_async_copy(src, dst, loc.at[dx])
+        copy.start()
+        wcopies.append(copy)
+
+    def rows_of(x):
+        return pl.ds(pl.multiple_of(x * 256, 256), 256)
+
+    def block(buf, x):
+        return buf[pl.ds(x * 2, 2)].reshape(256, D)
+
+    def put(x, product):
+        def body(k, _):
+            lanes = lanes_at(k * 512, 512)
+            parts[pl.ds(x * 2, 2), :, lanes] = product(lanes).astype(BF).reshape(2, 128, 512)
+            return 0
+
+        lax.fori_loop(0, 4, body, 0)
+
+    def reduced(rs, op, ag, buf):
         for half in range(2):
-            scatter.ready(half)
+            rs.ready(half)
 
             def body(k, _, half=half):
                 rows = pl.ds(half * 64 + k * 16, 16)
-                last = op(rows, scatter.total(rows), ins, out_refs)
-                if gather:
-                    own[rows, :] = last.astype(BF)
+                buf[here, rows, :] = op(rows, rs.total(rows)).astype(BF)
                 return 0
 
             lax.fori_loop(0, 4, body, 0)
-            if gather:
-                gath.start(half)
-        if gather:
-            gath.forward()
-        for s in sides:
-            s.middle()
-        if gather:
-            gath.finish()
-        scatter.finish()
-        for s in sides:
-            s.finish()
-
-    shapes, specs, in_specs, operands, aliases = list(outs), [VM] * n_out, [VM] * (1 + n_in), [parts, *inputs], {}
-    scratch = [pltpu.VMEM((4, 128, D), BF), pltpu.VMEM((7, 128, D), BF), dma((10,)), dma((10,))]
-    if gather:
-        shapes.append(jax.ShapeDtypeStruct((8, 128, D), BF))
-        specs.append(HB)
-        scratch += [pltpu.VMEM((128, D), BF), dma((14,)), dma((14,)), dma((2,))]
-    for s in sides:
-        if s.in_place:
-            aliases[len(operands)] = len(shapes)
-        operands += s.operands
-        in_specs += [HB] * len(s.operands)
-        shapes += s.shapes
-        specs += [HB if s.in_place else VM] * len(s.shapes)
-        scratch += s.scratch
+            ag.begin(half)
+
+    def over_blocks(ag, rs, work):
+        def step(i, _):
+            at = functools.partial(jnp.equal, i)
+
+            @pl.when(at(0))
+            def _():
+                ag.have(6, 7)
+
+            @pl.when(at(1))
+            def _():
+                ag.near()
+                ag.have(8, 9)
+
+            @pl.when(at(2))
+            def _():
+                ag.have(10, 11)
+                if rs is not None:
+                    rs.send_left()
+
+            @pl.when(at(3))
+            def _():
+                if rs is not None:
+                    rs.send_right()
+                ag.far()
+                ag.have(12, 13)
+
+            x = lax.rem(ring.x + jnp.where(at(1), 3, jnp.where(at(2), 1, jnp.where(at(3), 2, 0))), 4)
+            work(x)
+            if rs is not None:
+                rs.swap(3 - i, x).start()
+            return 0
+
+        lax.fori_loop(0, 4, step, 0)
+
+    rs = Rs(ring, parts, held, got, (rs1_s, rs1_r))
+    ag = Ag(ring, n2, (ag1_s, ag1_r))
+    for i in range(4):
+        x = rs.blocks[i]
+        put(x, lambda lanes, x=x: nn(a_ref[rows_of(x), :], wo_ref[:, lanes]))
+        rs.copy(i).start()
+        if i == 1:
+            rs.send_far()
+        elif i == 2:
+            rs.send_right()
+        elif i == 3:
+            rs.send_left()
+    rs.relay()
+
+    def op1(rows, total):
+        v = x_ref[rows, :].astype(F32) + total
+        y1[rows, :] = v
+        return v * norm_scale(v)
+
+    reduced(rs, op1, ag, n2)
+    rs.drain()
+    for copy in wcopies:
+        copy.wait()
+
+    rs = Rs(ring, parts, held, got, (rs2_s, rs2_r))
+
+    def forward(x):
+        rows = rows_of(x)
+        gate[rows, :] = nt(block(n2, x), w[0].reshape(704, D))
+        up[rows, :] = nt(block(n2, x), w[1].reshape(704, D))
+
+        def body(k, _):
+            r = pl.ds(pl.multiple_of(x * 256 + k * 32, 32), 32)
+            g = gate[r, :]
+            mid[pl.ds(pl.multiple_of(k * 32, 32), 32), :] = (g * jax.nn.sigmoid(g) * up[r, :]).astype(BF)
+            return 0
+
+        lax.fori_loop(0, 8, body, 0)
+        put(x, lambda lanes: nn(mid[...], wd_ref[:, lanes]))
+        mid_t[:, rows] = mid[...].T
+
+    over_blocks(ag, rs, forward)
+    rs.send_far()
+    rs.relay()
+    ag.drain()
+
+    def op2(rows, total):
+        v = y1[rows, :] + total
+        out_ref[rows, :] = v.astype(BF)
+        miss = v - teacher_ref[rows, :].astype(F32)
+        valid = valid_ref[rows, :]
+        loss_ref[rows, :] = valid * jnp.mean(miss * miss, axis=1, keepdims=True)
+        dy[rows, :] = valid * miss
+        return valid * miss
+
+    ag = Ag(ring, dyg, (ag2_s, ag2_r))
+    reduced(rs, op2, ag, dyg)
+    rs.drain()
+
+    rs = Rs(ring, parts, held, got, (rs3_s, rs3_r))
+
+    def backward(x):
+        rows = rows_of(x)
+        dgate_mid = nt(block(dyg, x), wd_ref[...])
+        dmid[...] = dgate_mid
+
+        def body(k, _):
+            r = pl.ds(pl.multiple_of(x * 256 + k * 32, 32), 32)
+            q = pl.ds(pl.multiple_of(k * 32, 32), 32)
+            g, dm = gate[r, :], dmid[q, :]
+            sg = jax.nn.sigmoid(g)
+            dgate[q, :] = (dm * up[r, :] * sg * (1.0 + g * (1.0 - sg))).astype(BF)
+            dup[q, :] = (dm * (g * sg)).astype(BF)
+            return 0
+
+        lax.fori_loop(0, 8, body, 0)
+        put(x, lambda lanes: nn(dgate[...], w[0, :, :, lanes].reshape(704, 512)) + nn(dup[...], w[1, :, :, lanes].reshape(704, 512)))
+        dg_t[:, rows] = dgate[...].T
+        du_t[:, rows] = dup[...].T
+
+    dmid = stage
+    over_blocks(ag, rs, backward)
+    rs.send_far()
+
+    def grad_down(k, _):
+        lanes = lanes_at(k * 512, 512)
+        gd[:, :, lanes] = nn(mid_t[...], dyg[:, :, lanes].reshape(1024, 512)).astype(BF).reshape(2, 352, 512)
+        return 0
+
+    lax.fori_loop(0, 4, grad_down, 0)
+    side.start()
+    rs.relay()
+    ag.drain()
+
+    def op3(rows, total):
+        v = back_norm(y1[rows, :], dy[rows, :], total)
+        dy1_ref[rows, :] = v
+        return v
+
+    ag = Ag(ring, dag, (ag3_s, ag3_r))
+    reduced(rs, op3, ag, dag)
+    rs.drain()
+
+    def grad_gu(first, last):
+        def body(k, _):
+            lanes = lanes_at(k * 256, 256)
+            tokens = n2[:, :, lanes].reshape(1024, 256)
+            ggu_ref[0, :, lanes] = nn(dg_t[...], tokens).astype(BF)
+            ggu_ref[1, :, lanes] = nn(du_t[...], tokens).astype(BF)
+            return 0
+
+        lax.fori_loop(first, last, body, 0)
+
+    def to_attention(x):
+        da_ref[rows_of(x), :] = nt(block(dag, x), wo_ref[...]).astype(BF)
+        grad_gu(2 * x, 2 * x + 2)
+
+    over_blocks(ag, None, to_attention)
+    side.middle()
+    copy = pltpu.make_async_copy(dag, dag_out, loc.at[0])
+    copy.start()
+    ag.drain()
+    side.finish()
+    copy.wait()
+
+
+def middle(a, wo, x, teacher, valid, half_w, wd):
+    dma = pltpu.SemaphoreType.DMA
+    pair = lambda n: [dma((n,)), dma((n,))]
+    big = pltpu.VMEM((8, 128, D), BF)
+    side = SumRows(jax.ShapeDtypeStruct((2, 352, D), BF))
     return pl.pallas_call(
-        kernel,
-        out_shape=shapes,
-        in_specs=in_specs,
-        out_specs=specs,
-        scratch_shapes=scratch,
-        input_output_aliases=aliases,
-        compiler_params=params(number),
-        name="exchange%d" % number,
-    )(*operands)
-
-
-class Side:
-    in_place = False
-
-    def middle(self):
-        pass
-
-
-class YSwap(Side):
-    in_place = True
-
-    def __init__(self, weights):
-        self.operands = [weights]
-        self.shapes = [jax.ShapeDtypeStruct(weights.shape, weights.dtype)]
-        self.scratch = [pltpu.SemaphoreType.DMA((4,)), pltpu.SemaphoreType.DMA((4,))]
-
-    def bind(self, ring, ins, outs, scratch):
-        self.r, self.w, self.sems = ring, outs[0], scratch
-        self.peers = list(y_partners())
-
-    def start(self):
-        self.c = []
-        for dx in range(4):
-            x = lax.rem(self.r.x + 4 - dx, 4)
-            block = self.w.at[:, :, :, group_lanes(x, lax.axis_index("y_lo"))]
-            self.c.append(send(block, block, self.sems, dx, self.peers[dx // 2]))
-
-    def finish(self):
-        for c in self.c:
-            c.wait()
-
-
-class Torus:
-    def __init__(self):
-        self.y_hi, self.y_lo, self.z = lax.axis_index("y_hi"), lax.axis_index("y_lo"), lax.axis_index("z")
-        self.y = self.y_hi * 2 + self.y_lo
-        self.ys = [(dy, lax.rem(self.y + dy, 4)) for dy in (1, 3, 2)]
-        self.zs = [(dz, lax.rem(self.z + dz, 4)) for dz in (1, 3, 2)]
-        self.peers = [self.y_device(y) for _, y in self.ys] + [{"z": z} for _, z in self.zs]
-
-    def y_device(self, y):
-        return {"y_hi": y // 2, "y_lo": lax.rem(y, 2)}
-
-
-def lanes_at(start, size):
-    return pl.ds(pl.multiple_of(start, 128), size)
-
-
-def add_up(out, terms, lead, rows):
-    steps = rows // 16
-
-    def body(k, _):
-        i, r = k // steps, pl.ds(pl.multiple_of(lax.rem(k, steps) * 16, 16), 16)
-        total = None
-        for at in terms:
-            term = at(i, r).astype(F32)
-            total = term if total is None else total + term
-        out(i, r, total.astype(BF))
-        return 0
-
-    lax.fori_loop(0, lead * steps, body, 0)
+        functools.partial(middle_kernel, side),
+        out_shape=[
+            jax.ShapeDtypeStruct((128, D), BF), jax.ShapeDtypeStruct((128, 1), F32), jax.ShapeDtypeStruct((128, D), F32),
+            jax.ShapeDtypeStruct((1024, 256), BF), jax.ShapeDtypeStruct((8, 128, D), BF), jax.ShapeDtypeStruct((2, 704, D), BF),
+            *side.shapes,
+        ],
+        in_specs=[VM] * 5 + [HB, VM],
+        out_specs=[VM, VM, VM, VM, HB, VM, VM],
+        scratch_shapes=[
+            pltpu.VMEM((2, 2, 352, D), BF), big, big, big, big, pltpu.VMEM((4, 128, D), BF), pltpu.VMEM((7, 128, D), BF),
+            pltpu.VMEM((128, D), F32), pltpu.VMEM((128, D), F32),
+            pltpu.VMEM((1024, 704), F32), pltpu.VMEM((1024, 704), F32),
+            pltpu.VMEM((256, 704), BF), pltpu.VMEM((704, 1024), BF), pltpu.VMEM((256, 704), BF), pltpu.VMEM((256, 704), BF),
+            pltpu.VMEM((704, 1024), BF), pltpu.VMEM((704, 1024), BF), pltpu.VMEM((2, 352, D), BF), pltpu.VMEM((256, 704), F32),
+            *pair(10), *pair(14), *pair(10), *pair(14), *pair(10), *pair(14), *pair(4), dma((4,)), *side.scratch,
+        ],
+        compiler_params=pltpu.CompilerParams(collective_id=1, has_side_effects=True, vmem_limit_bytes=63 * 2**20),
+        name="middle",
+    )(a, wo, x, teacher, valid, half_w, wd)
 
 
 class SumColumns(Side):
@@ -497,6 +687,65 @@
     return lanes_at((c // 4) * 1024 + part * 512 + lax.rem(c, 4) * 128, 128)
 
 
+def ctx_at(k):
+    y_hi, z = lax.axis_index("y_hi"), lax.axis_index("z")
+    y, zz = (1 - y_hi if k // 4 else y_hi), lax.rem(z + k % 4, 4)
+    return y * 4 + zz, {"y_hi": y, "z": zz}
+
+
+class Spread:
+    def __init__(self, piece, slot, sems, base, y_first, local):
+        self.piece, self.slot, self.sems, self.base, self.y_first, self.local = piece, slot, sems, base, y_first, local
+
+    def copy(self, k, src, c, device):
+        return pltpu.make_async_remote_copy(
+            src_ref=src, dst_ref=self.slot(c), send_sem=self.sems[0].at[self.base + k - 1],
+            recv_sem=self.sems[1].at[self.base + k - 1], device_id=device, device_id_type=MESH,
+        )
+
+    def first(self, k):
+        here, _ = ctx_at(0)
+        return self.copy(k, self.piece, here, ctx_at(k)[1])
+
+    def second(self, dz):
+        if self.y_first:
+            c, _ = ctx_at(4)
+            return self.copy(4 + dz, self.slot(c), c, ctx_at(dz)[1])
+        c, _ = ctx_at(4 - dz)
+        return self.copy(4 + dz, self.slot(c), c, ctx_at(4)[1])
+
+    def own(self):
+        return pltpu.make_async_copy(self.piece, self.slot(ctx_at(0)[0]), self.local)
+
+    def start(self):
+        for k in (4, 1, 3, 2) if self.y_first else (1, 3, 2, 4):
+            self.first(k).start()
+        self.own().start()
+
+    def relay(self):
+        if self.y_first:
+            self.first(4).wait_recv()
+            for dz in (1, 3, 2):
+                self.second(dz).start()
+        else:
+            for dz in (1, 3, 2):
+                self.first(dz).wait_recv()
+                self.second(dz).start()
+
+    def finish(self):
+        if self.y_first:
+            for dz in (1, 3, 2):
+                self.first(dz).wait_recv()
+        else:
+            self.first(4).wait_recv()
+        for dz in (1, 3, 2):
+            self.second(dz).wait_recv()
+            self.second(dz).wait_send()
+        for k in (1, 2, 3, 4):
+            self.first(k).wait_send()
+        self.own().wait()
+
+
 class SpreadRows(Side):
     def __init__(self, pieces):
         r = pieces.shape[1]
@@ -506,63 +755,190 @@
         self.scratch = [dma((14,)), dma((14,)), dma((2,))]
 
     def bind(self, ring, ins, outs, scratch):
-        (self.p,), (self.out,) = ins, outs
-        self.sems, self.loc = scratch[:2], scratch[2]
-        self.here = lax.axis_index("y_hi") * 4 + lax.axis_index("z")
-        self.peers = [ctx_peer(self.here, k) for k in range(1, 8)]
+        (p,), (out,) = ins, outs
+        self.peers = [ctx_at(k)[1] for k in range(1, 8)]
+        self.s = [
+            Spread(
+                p.at[part], lambda c, part=part: out.at[:, piece_lanes(c, part)], scratch[:2], part * 7, part == 0,
+                scratch[2].at[part],
+            )
+            for part in range(2)
+        ]
 
     def start(self):
-        self.c = []
-        for part in range(2):
-            dst = self.out.at[:, piece_lanes(self.here, part)]
-            for k in range(1, 8):
-                self.c.append(send(self.p.at[part], dst, self.sems, part * 7 + k - 1, self.peers[k - 1]))
-            copy = pltpu.make_async_copy(self.p.at[part], dst, self.loc.at[part])
-            copy.start()
-            self.c.append(copy)
+        for s in self.s:
+            s.start()
+
+    def middle(self):
+        for s in self.s:
+            s.relay()
 
     def finish(self):
-        for copy in self.c:
-            copy.wait()
-
-
-def op_mid(rows, total, ins, outs):
-    (x_ref,), (y1_ref,) = ins, outs
-    y1 = x_ref[rows, :].astype(F32) + total
-    y1_ref[rows, :] = y1
-    return y1 * norm_scale(y1)
-
-
-def op_loss(rows, total, ins, outs):
-    y1_ref, teacher_ref, valid_ref = ins
-    out_ref, dy_ref, loss_ref = outs
-    y = y1_ref[rows, :] + total
-    out_ref[rows, :] = y.astype(BF)
-    miss = y - teacher_ref[rows, :].astype(F32)
-    valid = valid_ref[rows, :]
-    loss_ref[rows, :] = valid * jnp.mean(miss * miss, axis=1, keepdims=True)
-    dy = valid * miss
-    dy_ref[rows, :] = dy
-    return dy
+        for s in self.s:
+            s.finish()
+
+
+class Move(Side):
+    def __init__(self, pieces):
+        dma = pltpu.SemaphoreType.DMA
+        self.operands = [pieces]
+        self.shapes = [jax.ShapeDtypeStruct((8, pieces.shape[0], 128), BF)]
+        self.scratch = [dma((8,)), dma((8,))]
+
+    def bind(self, ring, ins, outs, scratch):
+        (self.p,), (self.out,), self.sems = ins, outs, scratch
+        x, self.y_lo, core = lax.axis_index("x"), lax.axis_index("y_lo"), lax.axis_index("core")
+        self.here16, self.here8 = x * 4 + self.y_lo * 2 + core, x * 2 + core
+        self.peers = [device for _, device in group_peers()]
+
+    def same(self, j):
+        return self.here16 == self.y_lo * 8 + j
+
+    def away(self, j):
+        return pltpu.make_async_remote_copy(
+            src_ref=self.p.at[:, pl.ds(j * 128, 128)], dst_ref=self.out.at[self.here8], send_sem=self.sems[0].at[j],
+            recv_sem=self.sems[1].at[self.here8], device_id={"x": self.y_lo * 2 + j // 4, "y_lo": j // 2 % 2, "core": j % 2},
+            device_id_type=MESH,
+        )
+
+    def stay(self, j):
+        return pltpu.make_async_copy(self.p.at[:, pl.ds(j * 128, 128)], self.out.at[self.here8], self.sems[1].at[self.here8])
+
+    def start(self):
+        for j in range(8):
+
+            @pl.when(self.same(j))
+            def _():
+                self.stay(j).start()
+
+            @pl.when(jnp.logical_not(self.same(j)))
+            def _():
+                self.away(j).start()
+
+    def arrive(self, s):
+        pltpu.make_async_copy(self.out.at[s], self.out.at[s], self.sems[1].at[s]).wait()
+
+    def drain(self):
+        for j in range(8):
+
+            @pl.when(jnp.logical_not(self.same(j)))
+            def _():
+                self.away(j).wait_send()
+
+    def finish(self):
+        for s in range(8):
+            self.arrive(s)
+        self.drain()
+
+
+def group_peers():
+    x, y_lo, core = lax.axis_index("x"), lax.axis_index("y_lo"), lax.axis_index("core")
+    found = []
+    for k in range(1, 16):
+        dx, dy, dc = k // 4, k // 2 % 2, k % 2
+        found.append((k, {"x": lax.rem(x + dx, 4), "y_lo": 1 - y_lo if dy else y_lo, "core": 1 - core if dc else core}))
+    return found
+
+
+def last_kernel(
+    down, move, cols, rows_side, dqkv_ref, wqkv_ref, n1_ref, a_ref, dag_ref, x_ref, dy1_ref, piece_down_ref, piece_gu_ref,
+    grad_ref, down_ref, got_gu_ref, piece_qkv_ref, piece_out_ref,
+    parts, held, got, gq, go, dqkv_t, a_t, rs_s, rs_r, *side_scratch,
+):
+    ring = Ring()
+    scratch = list(side_scratch)
+
+    def take(side):
+        taken = scratch[: len(side.scratch)]
+        del scratch[: len(side.scratch)]
+        return taken
+
+    down.bind(ring, (piece_down_ref,), (down_ref,), take(down))
+    move.bind(ring, (piece_gu_ref,), (got_gu_ref,), take(move))
+    cols.bind(ring, (gq,), (piece_qkv_ref,), take(cols))
+    rows_side.bind(ring, (go,), (piece_out_ref,), take(rows_side))
+    meet([ring.right, ring.left, ring.sibling] + down.peers + move.peers + cols.peers + rows_side.peers)
+    down.start()
+
+    rs = Rs(ring, parts, held, got, (rs_s, rs_r))
+    for i in range(4):
+        x = rs.blocks[i]
+
+        def body(k, _, x=x):
+            lanes = lanes_at(k * 512, 512)
+            block = nn(dqkv_ref[pl.ds(pl.multiple_of(x * 256, 256), 256), :], wqkv_ref[:, lanes])
+            parts[pl.ds(x * 2, 2), :, lanes] = block.astype(BF).reshape(2, 128, 512)
+            return 0
+
+        lax.fori_loop(0, 4, body, 0)
+        rs.copy(i).start()
+        if i == 1:
+            rs.send_far()
+        elif i == 2:
+            rs.send_right()
+        elif i == 3:
+            rs.send_left()
+    move.start()
+
+    dqkv_t[...] = dqkv_ref[...].T
+    a_t[...] = a_ref[...].T
+
+    def grads(k, _):
+        lanes = lanes_at(k * 512, 512)
+        product = nn(dqkv_t[...], n1_ref[:, :, lanes].reshape(1024, 512))
+        gq[:, :, :, lanes] = product.astype(BF).reshape(2, 4, 48, 512)
+        product = nn(a_t[...], dag_ref[:, :, lanes].reshape(1024, 512))
+        go[:, :, lanes] = product.astype(BF).reshape(2, 128, 512)
+        return 0
+
+    lax.fori_loop(0, 4, grads, 0)
+    cols.start()
+    rows_side.start()
+    down.middle()
+    rs.relay()
+    for half in range(2):
+        rs.ready(half)
+
+        def body(k, _, half=half):
+            rows = pl.ds(half * 64 + k * 16, 16)
+            grad_ref[rows, :] = back_norm(x_ref[rows, :].astype(F32), dy1_ref[rows, :], rs.total(rows))
+            return 0
+
+        lax.fori_loop(0, 4, body, 0)
+    cols.middle()
+    rows_side.middle()
+    rs.drain()
+    down.finish()
+    move.finish()
+    cols.finish()
+    rows_side.finish()
+
+
+def last(dqkv, wqkv, n1, a, dag, hidden_in, dy1, piece_down, piece_gu):
+    dma = pltpu.SemaphoreType.DMA
+    sides = [
+        SpreadRows(piece_down), Move(piece_gu),
+        SumColumns(jax.ShapeDtypeStruct((2, 4, 48, D), BF)), SumRows(jax.ShapeDtypeStruct((2, 128, D), BF)),
+    ]
+    return pl.pallas_call(
+        functools.partial(last_kernel, *sides),
+        out_shape=[jax.ShapeDtypeStruct((128, D), F32)] + [s for side in sides for s in side.shapes],
+        in_specs=[VM] * 9,
+        out_specs=[VM] * 5,
+        scratch_shapes=[
+            pltpu.VMEM((8, 128, D), BF), pltpu.VMEM((4, 128, D), BF), pltpu.VMEM((7, 128, D), BF),
+            pltpu.VMEM((2, 4, 48, D), BF), pltpu.VMEM((2, 128, D), BF), pltpu.VMEM((384, 1024), BF), pltpu.VMEM((256, 1024), BF),
+            dma((10,)), dma((10,)), *[s for side in sides for s in side.scratch],
+        ],
+        compiler_params=params(4),
+        name="last",
+    )(dqkv, wqkv, n1, a, dag, hidden_in, dy1, piece_down, piece_gu)
 
 
 def back_norm(v, grad, u):
     r = norm_scale(v)
     n = v * r
     return grad + r * (u - n * jnp.mean(u * n, axis=1, keepdims=True))
-
-
-def op_back(rows, total, ins, outs):
-    (y1_ref, dy_ref), (dy1_ref,) = ins, outs
-    dy1 = back_norm(y1_ref[rows, :], dy_ref[rows, :], total)
-    dy1_ref[rows, :] = dy1
-    return dy1
-
-
-def op_input(rows, total, ins, outs):
-    (x_ref, dy1_ref), (grad_ref,) = ins, outs
-    grad_ref[rows, :] = back_norm(x_ref[rows, :].astype(F32), dy1_ref[rows, :], total)
-    return None
 
 
 def y_partners():
@@ -605,20 +981,18 @@
         copies.append(send(wo_ref.at[HALVES[half]], wos_ref.at[y_lo, HALVES[half]], (y_s, y_r), 4 + half, device))
 
     gath = Gather(ring, own, n1_ref, (ag_s, ag_r), loc)
-    for half in range(2):
-
-        def body(k, _, half=half):
-            rows = pl.ds(half * 64 + k * 16, 16)
-            v = x_ref[rows, :].astype(F32)
-            own[rows, :] = (v * norm_scale(v)).astype(BF)
-            return 0
-
-        lax.fori_loop(0, 4, body, 0)
-        gath.start(half)
+
+    def normed(k, _):
+        rows = pl.ds(pl.multiple_of(k * 16, 16), 16)
+        v = x_ref[rows, :].astype(F32)
+        own[rows, :] = (v * norm_scale(v)).astype(BF)
+        return 0
+
+    lax.fori_loop(0, 4, normed, 0)
+    gath.start(0)
 
     def turned(ref, gain, k):
-        tile = ref[:, pl.ds(pl.multiple_of(k * 128, 128), 128)].astype(F32) * gain
-        return tile.T.astype(BF)
+        return (ref[:, pl.ds(pl.multiple_of(k * 128, 128), 128)].T.astype(F32) * gain).astype(BF)
 
     g1, g2 = g1_ref[...], g2_ref[...]
     for f in range(16):
@@ -637,16 +1011,17 @@
     wcopies[0] = pltpu.make_async_copy(w.at[here], wqkv_ref.at[:, lanes], loc2.at[2])
     wcopies[0].start()
 
-    def turn_all(ref, i):
+    lax.fori_loop(4, 8, normed, 0)
+    gath.start(1)
+
+    def turn_some(ref, i, first, last):
         def body(k, _):
             wt_ref[i, pl.ds(pl.multiple_of(k * 128, 128), 128), :] = turned(ref, g2, k)
             return 0
 
-        lax.fori_loop(0, FF // 128, body, 0)
-
-    turn_all(wg_ref, 0)
-    gath.forward()
-    turn_all(wu_ref, 1)
+        lax.fori_loop(first, last, body, 0)
+
+    turn_some(wg_ref, 0, 0, 44)
     for dx in range(4):
         x = lax.rem(ring.x + 4 - dx, 4)
         if dx == 0:
@@ -656,6 +1031,8 @@
         wcopies[2 * dx + 1].wait_recv()
         block = wqkv_ref.at[:, group_lanes(x, y_lo)]
         copies.append(send(block, block, (y_s, y_r), dx, (near, other)[dx // 2]))
+    turn_some(wu_ref, 1, 0, 22)
+    gath.forward(lambda: turn_some(wu_ref, 1, 22, 44))
     gath.finish()
     for k in range(1, 8):
         wcopies[k].wait_send()
@@ -676,7 +1053,7 @@
             jax.ShapeDtypeStruct((2, 128, D), BF),
             jax.ShapeDtypeStruct((2, FF, 128), BF),
         ],
-        in_specs=[VM] * 9 + [HB],
+        in_specs=[VM] * 10,
         out_specs=[HB, VM, HB, HB, VM],
         scratch_shapes=[
             pltpu.VMEM((128, D), BF), pltpu.VMEM((8, 384, 128), BF),
@@ -717,9 +1094,9 @@
 
 
 def attend_kernel(
-    qkv_ref, meta_ref, tab_ref, wt_ref, wdn_ref,
+    n1_ref, wqkv_ref, meta_ref, tab_ref, wt_ref, wdn_ref,
     a_ref, qp_ref, kv_ref, lse_ref, wgu_ref, wd_ref,
-    bias, probs, kv_s, kv_r, fw_s, fw_r, w_s, w_r, y_s, y_r, loc,
+    qkv_ref, bias, probs, kv_s, kv_r, fw_s, fw_r, w_s, w_r, y_s, y_r, loc,
 ):
     ring = Ring()
     y_lo = lax.axis_index("y_lo")
@@ -732,13 +1109,6 @@
 
     def rope(u, i):
         return u * tab_ref[i] + pltpu.roll(u, 96, 1) * tab_ref[i + 1] + pltpu.roll(u, 32, 1) * tab_ref[i + 2]
-
-    for d in range(8):
-        kv_ref[d % 2, d // 2, c] = rope(qkv_ref[pl.ds(d * 128, 128), 256:384], 3).astype(BF)
-    kv_copies = []
-    for k in range(1, 8):
-        block = kv_ref.at[ring.core, :, c]
-        kv_copies.append(send(block, block, (kv_s, kv_r), k - 1, ctx_peer(c, k)))
 
     copies, local = [], []
     here = pl.ds(pl.multiple_of((ring.x * 4 + y_lo * 2 + ring.core) * 128, 128), 128)
@@ -759,6 +1129,14 @@
         rows = pl.ds(pl.multiple_of(y_lo * 352 + half * 176, 16), 176)
         copies.append(send(wdn_ref.at[pl.ds(half * 176, 176)], wd_ref.at[rows], (y_s, y_r), half, device))
 
+    kv_copies = []
+    qkv_ref[...] = nt(n1_ref[...], wqkv_ref[...])
+    for d in range(8):
+        kv_ref[d % 2, d // 2, c] = rope(qkv_ref[pl.ds(d * 128, 128), 256:384], 3).astype(BF)
+    for k in range(1, 8):
+        block = kv_ref.at[ring.core, :, c]
+        kv_copies.append(send(block, block, (kv_s, kv_r), k - 1, ctx_peer(c, k)))
+
     def turn_queries(d, _):
         for j in range(2):
             u = rope(qkv_ref[pl.ds(pl.multiple_of(d * 128, 128), 128), pl.ds(j * 128, 128)], 0) * 0.125
@@ -802,7 +1180,7 @@
         copy.wait()
 
 
-def attend(qkv, metas, tabs, wt, w_down):
+def attend(n1, wqkv, metas, tabs, wt, w_down):
     dma = pltpu.SemaphoreType.DMA
     return pl.pallas_call(
         attend_kernel,
@@ -814,15 +1192,16 @@
             jax.ShapeDtypeStruct((2, 2, 352, D), BF),
             jax.ShapeDtypeStruct((704, D), BF),
         ],
-        in_specs=[VM, VM, VM, HB, HB],
-        out_specs=[VM, VM, VM, VM, HB, HB],
+        in_specs=[VM] * 4 + [HB] * 2,
+        out_specs=[VM, VM, VM, VM, HB, VM],
         scratch_shapes=[
+            pltpu.VMEM((1024, 384), F32),
             pltpu.VMEM((1024, 128), F32), pltpu.VMEM((1024, 512), BF),
             dma((7,)), dma((7,)), dma((7,)), dma((7,)), dma((16,)), dma((16,)), dma((2,)), dma((2,)), dma((3,)),
         ],
         compiler_params=params(6),
         name="attend",
-    )(qkv, metas, tabs, wt, w_down)
+    )(n1, wqkv, metas, tabs, wt, w_down)
 
 
 def attend_back_kernel(
@@ -893,8 +1272,8 @@
             kv_copy(x, k).start()
         return 0
 
+    lax.fori_loop(0, 4, to_owners, 0)
     side.middle()
-    lax.fori_loop(0, 4, to_owners, 0)
 
     def gather_up(x, _):
         total = stage[x, c].astype(F32)
@@ -945,67 +1324,47 @@
     return jnp.stack([jnp.concatenate(p, axis=1) for p in pairs])
 
 
-def group_peers():
-    x, y_lo, core = lax.axis_index("x"), lax.axis_index("y_lo"), lax.axis_index("core")
-    found = []
-    for k in range(1, 16):
-        dx, dy, dc = k // 4, k // 2 % 2, k % 2
-        found.append((k, {"x": lax.rem(x + dx, 4), "y_lo": 1 - y_lo if dy else y_lo, "core": 1 - core if dc else core}))
-    return found
-
-
 def return_kernel(
-    stats_ref, gu_ref, qkv_ref, out_ref, dn_ref, g1_ref, g2_ref, wq_ref, wk_ref, wv_ref, wg_ref, wu_ref,
-    info_ref, q_ref, k_ref, v_ref, o_ref, gate_ref, up_ref, down_ref, gains_ref,
-    st1, st2, mid, got_gu, got_qkv, all_gu, all_qkv, all_out,
-    st_s, st_r, st2_s, st2_r, gu_s, gu_r, qkv_s, qkv_r, agu_s, agu_r, aqkv_s, aqkv_r, ao_s, ao_r, loc,
+    move, stats_ref, got_gu, qkv_ref, out_ref,
+    info_ref, all_gu, all_qkv, all_out,
+    st1, st2, mid, got_qkv,
+    st_s, st_r, st2_s, st2_r, agu_s, agu_r, aqkv_s, aqkv_r, ao_s, ao_r, loc, *move_scratch,
 ):
     x, y_lo, core = lax.axis_index("x"), lax.axis_index("y_lo"), lax.axis_index("core")
-    c = lax.axis_index("y_hi") * 4 + lax.axis_index("z")
+    ring = Ring()
+    move.bind(ring, (qkv_ref,), (got_qkv,), move_scratch)
     group = group_peers()
-    ctx = [(k, ctx_peer(c, k)) for k in range(1, 8)]
+    ctx = [(k, ctx_at(k)[1]) for k in range(1, 8)]
     meet([device for _, device in group] + [device for _, device in ctx])
-    here16, here8 = x * 4 + y_lo * 2 + core, x * 2 + core
-
-    def same(j):
-        return here16 == y_lo * 8 + j
-
-    def owner(j):
-        return {"x": y_lo * 2 + j // 4, "y_lo": j // 2 % 2, "core": j % 2}
-
-    moves = ((gu_ref, got_gu, (gu_s, gu_r)), (qkv_ref, got_qkv, (qkv_s, qkv_r)))
-
-    def move(src, dst, sems, j):
-        return pltpu.make_async_remote_copy(
-            src_ref=src.at[:, pl.ds(j * 128, 128)], dst_ref=dst.at[here8], send_sem=sems[0].at[j], recv_sem=sems[1].at[here8],
-            device_id=owner(j), device_id_type=MESH,
-        )
-
-    def move_here(src, dst, sems, j):
-        return pltpu.make_async_copy(src.at[:, pl.ds(j * 128, 128)], dst.at[here8], sems[1].at[here8])
-
-    for src, dst, sems in moves:
-        for j in range(8):
-
-            @pl.when(same(j))
-            def _():
-                move_here(src, dst, sems, j).start()
-
-            @pl.when(jnp.logical_not(same(j)))
-            def _():
-                move(src, dst, sems, j).start()
-
+    c, _ = ctx_at(0)
+    here16 = x * 4 + y_lo * 2 + core
+    move.start()
     copies = [send(stats_ref, st1.at[here16], (st_s, st_r), k, device) for k, device in group]
     st1[here16] = stats_ref[...]
+
+    spreads = []
+    for s in range(8):
+
+        def slot(c, s=s):
+            rows = ((s // 2) * 4 + lax.rem(c // 2, 2) * 2 + s % 2) * 352 + lax.rem(c, 2) * 176
+            return all_gu.at[c // 4, pl.ds(pl.multiple_of(rows, 16), 176)]
+
+        spreads.append(Spread(got_gu.at[s], slot, (agu_s, agu_r), s * 7, s % 3 == 0, loc.at[s]))
     for part in range(2):
-        dst = all_out.at[:, piece_lanes(c, part)]
-        for k, device in ctx:
-            copies.append(send(out_ref.at[part], dst, (ao_s, ao_r), part * 7 + k - 1, device))
-        copy = pltpu.make_async_copy(out_ref.at[part], dst, loc.at[part])
-        copy.start()
-        copies.append(copy)
-
-    for copy in copies[:15]:
+        spreads.append(
+            Spread(
+                out_ref.at[part], lambda c, part=part: all_out.at[:, piece_lanes(c, part)], (ao_s, ao_r), part * 7, part == 0,
+                loc.at[8 + part],
+            )
+        )
+    for s in spreads:
+        s.start()
+    for s in range(8):
+        move.arrive(s)
+    last_spread = Spread(got_qkv, lambda c: all_qkv.at[:, c], (aqkv_s, aqkv_r), 0, False, loc.at[10])
+    last_spread.start()
+
+    for copy in copies:
         copy.wait_recv()
     total = st1[0]
     for i in range(1, 16):
@@ -1014,31 +1373,15 @@
     st2[c] = total
     copies2 = [send(mid, st2.at[c], (st2_s, st2_r), k - 1, device) for k, device in ctx]
 
-    def from_source(dst, sems, s):
-        return pltpu.make_async_copy(dst.at[s], dst.at[s], sems[1].at[s])
-
-    for _, dst, sems in moves:
-        for s in range(8):
-            from_source(dst, sems, s).wait()
-
-    def gu_rows(s):
-        return pl.ds(pl.multiple_of(((s // 2) * 4 + lax.rem(c // 2, 2) * 2 + s % 2) * 352 + lax.rem(c, 2) * 176, 16), 176)
-
-    for s in range(8):
-        dst = all_gu.at[c // 4, gu_rows(s)]
-        copy = pltpu.make_async_copy(got_gu.at[s], dst, loc.at[2 + s])
-        copy.start()
-        copies2.append(copy)
-        for k, device in ctx:
-            copies2.append(send(got_gu.at[s], dst, (agu_s, agu_r), s * 7 + k - 1, device))
-    dst = all_qkv.at[:, c]
-    copy = pltpu.make_async_copy(got_qkv, dst, loc.at[10])
-    copy.start()
-    copies2.append(copy)
-    for k, device in ctx:
-        copies2.append(send(got_qkv, dst, (aqkv_s, aqkv_r), k - 1, device))
-
-    for copy in copies2[:7]:
+    for s in spreads:
+        if s.y_first:
+            s.relay()
+    for s in spreads:
+        if not s.y_first:
+            s.relay()
+    last_spread.relay()
+
+    for copy in copies2:
         copy.wait_recv()
     total = st2[0]
     for i in range(1, 8):
@@ -1048,86 +1391,100 @@
     scale = 2.0 / (D * count)
     info_ref[...] = jnp.concatenate([squares / count, scale, jnp.zeros((6, 1), F32)], axis=0) + jnp.zeros((8, 128), F32)
 
-    down_scale = jnp.broadcast_to(scale, (16, 1))
-
-    def scaled(src, dst, rows):
-        def body(i, _):
-            r = pl.ds(pl.multiple_of(i * 16, 16), 16)
-            dst[r, :] = src[r, :].astype(F32) * down_scale
-            return 0
-
-        lax.fori_loop(0, rows // 16, body, 0)
-
-    scaled(dn_ref, down_ref, 352)
-    for copy in copies[15:]:
-        copy.wait()
-    scaled(all_out, o_ref, 128)
-
-    for copy in copies2[7:]:
-        copy.wait()
-    g1, g2 = g1_ref[...], g2_ref[...]
-    s1, s2 = g1 * scale, g2 * scale
-
-    sum1 = jnp.zeros((128, 128), F32)
+    for s in spreads + [last_spread]:
+        s.finish()
+    for copy in copies + copies2:
+        copy.wait_send()
+    move.drain()
+
+
+def return_grads(stats, got_gu, qkv, out):
+    dma = pltpu.SemaphoreType.DMA
+    pair = lambda n: [dma((n,)), dma((n,))]
+    move = Move(qkv)
+    return pl.pallas_call(
+        functools.partial(return_kernel, move),
+        out_shape=[
+            jax.ShapeDtypeStruct((8, 128), F32),
+            jax.ShapeDtypeStruct((2, FF, 128), BF),
+            jax.ShapeDtypeStruct((8, 8, 48, 128), BF),
+            jax.ShapeDtypeStruct((128, D), BF),
+        ],
+        in_specs=[VM] * 4,
+        out_specs=[VM] * 4,
+        scratch_shapes=[
+            pltpu.VMEM((16, 8, 128), F32), pltpu.VMEM((8, 8, 128), F32), pltpu.VMEM((8, 128), F32), pltpu.VMEM((8, 48, 128), BF),
+            *pair(16), *pair(7), *pair(56), *pair(7), *pair(14), dma((11,)), *move.scratch,
+        ],
+        compiler_params=params(8),
+        name="return_grads",
+    )(stats, got_gu, qkv, out)
+
+
+def turn_back_kernel(info_ref, all_ref, gain_ref, wg_ref, wu_ref, down_ref, gate_ref, up_ref, down_out, sum_ref):
+    scale = info_ref[1:2, 0:1]
+    s = gain_ref[...] * scale
+
+    @pl.when(pl.program_id(0) == 0)
+    def _():
+        sum_ref[...] = jnp.zeros_like(sum_ref)
+
+    total = jnp.zeros((128, 128), F32)
+    for k in range(4):
+        at = slice(k * 128, (k + 1) * 128)
+        for i, w_ref, g_ref in ((0, wg_ref, gate_ref), (1, wu_ref, up_ref)):
+            part = all_ref[i, at, :].T.astype(F32)
+            total += part * w_ref[:, at].astype(F32)
+            g_ref[:, at] = part * s
+    sum_ref[...] += jnp.sum(total, axis=1, keepdims=True) * scale
+    down_out[...] = down_ref[...].astype(F32) * scale
+
+
+def turn_back(info, all_gu, gain, w_gate, w_up, down):
+    wide = pl.BlockSpec((128, 512), lambda i: (0, i))
+    rows = pl.BlockSpec((32, D), lambda i: (i, 0))
+    whole = lambda *shape: pl.BlockSpec(shape, lambda i: (0,) * len(shape))
+    f32 = lambda *shape: jax.ShapeDtypeStruct(shape, F32)
+    return pl.pallas_call(
+        turn_back_kernel,
+        grid=(11,),
+        out_shape=[f32(128, FF), f32(128, FF), f32(352, D), f32(128, 1)],
+        in_specs=[whole(8, 128), pl.BlockSpec((2, 512, 128), lambda i: (0, i, 0)), whole(128, 1), wide, wide, rows],
+        out_specs=[wide, wide, rows, whole(128, 1)],
+        name="turn_back",
+    )(info, all_gu, gain, w_gate, w_up, down)
+
+
+def turn_back_qkv_kernel(
+    info_ref, all_ref, gain_ref, wq_ref, wk_ref, wv_ref, out_ref, gin_ref, q_ref, k_ref, v_ref, sum_ref, o_ref, input_ref
+):
+    scale = info_ref[1:2, 0:1]
+    s1 = gain_ref[...] * scale
+    total = jnp.zeros((128, 128), F32)
     for s in range(8):
         for j in range(2):
             f = (s // 2) * 4 + j * 2 + s % 2
-            part = all_qkv[s].reshape(384, 128)[j * 128 : (j + 1) * 128].astype(F32).T
-            sum1 += part * wq_ref[:, f * 128 : (f + 1) * 128].astype(F32)
+            part = all_ref[s, j * 128 : (j + 1) * 128].T.astype(F32)
+            total += part * wq_ref[:, f * 128 : (f + 1) * 128].astype(F32)
             q_ref[:, f * 128 : (f + 1) * 128] = part * s1
     for i in range(2):
-        both = []
-        for xs in (2 * i, 2 * i + 1):
-            both.append(
-                all_qkv[2 * xs].reshape(384, 128)[256:].astype(F32) + all_qkv[2 * xs + 1].reshape(384, 128)[256:].astype(F32)
-            )
+        both = [all_ref[2 * x, 256:].astype(F32) + all_ref[2 * x + 1, 256:].astype(F32) for x in (2 * i, 2 * i + 1)]
         for at, w_ref, g_ref in ((0, wk_ref, k_ref), (64, wv_ref, v_ref)):
             part = jnp.concatenate([both[0][at : at + 64], both[1][at : at + 64]], axis=0).T
-            sum1 += part * w_ref[:, i * 128 : (i + 1) * 128].astype(F32)
+            total += part * w_ref[:, i * 128 : (i + 1) * 128].astype(F32)
             g_ref[:, i * 128 : (i + 1) * 128] = part * s1
-
-    def body(k, total):
-        at = lanes_at(k * 128, 128)
-        rows = pl.ds(pl.multiple_of(k * 128, 128), 128)
-        for i, w_ref, g_ref in ((0, wg_ref, gate_ref), (1, wu_ref, up_ref)):
-            part = all_gu[i, rows, :].astype(F32).T
-            total += part * w_ref[:, at].astype(F32)
-            g_ref[:, at] = part * s2
-        return total
-
-    sum2 = lax.fori_loop(0, FF // 128, body, jnp.zeros((128, 128), F32))
-    gains_ref[0] = jnp.sum(sum1, axis=1, keepdims=True) * scale
-    gains_ref[1] = jnp.sum(sum2, axis=1, keepdims=True) * scale
-    for copy in copies[:15] + copies2[:7]:
-        copy.wait_send()
-    for src, dst, sems in moves:
-        for j in range(8):
-
-            @pl.when(jnp.logical_not(same(j)))
-            def _():
-                move(src, dst, sems, j).wait_send()
-
-
-def return_grads(stats, gu, qkv, out, down, g1, g2, w_query, w_key, w_value, w_gate, w_up):
-    dma = pltpu.SemaphoreType.DMA
+    sum_ref[...] = jnp.sum(total, axis=1, keepdims=True) * scale
+    o_ref[...] = out_ref[...].astype(F32) * scale
+    input_ref[...] = gin_ref[...] * scale
+
+
+def turn_back_qkv(info, all_qkv, gain, w_query, w_key, w_value, out, grad_in):
     f32 = lambda *shape: jax.ShapeDtypeStruct(shape, F32)
-    pair = lambda n: [dma((n,)), dma((n,))]
     return pl.pallas_call(
-        return_kernel,
-        out_shape=[
-            f32(8, 128), f32(128, D), f32(128, KVD), f32(128, KVD), f32(128, D), f32(128, FF), f32(128, FF), f32(352, D), f32(2, 128, 1),
-        ],
-        in_specs=[VM] * 12,
-        out_specs=[VM] * 9,
-        scratch_shapes=[
-            pltpu.VMEM((16, 8, 128), F32), pltpu.VMEM((8, 8, 128), F32), pltpu.VMEM((8, 128), F32),
-            pltpu.VMEM((8, 176, 128), BF), pltpu.VMEM((8, 48, 128), BF),
-            pltpu.VMEM((2, FF, 128), BF), pltpu.VMEM((8, 8, 48, 128), BF), pltpu.VMEM((128, D), BF),
-            *pair(16), *pair(7), *pair(8), *pair(8), *pair(56), *pair(7), *pair(14), dma((11,)),
-        ],
-        compiler_params=params(8),
-        name="return_grads",
-    )(stats, gu, qkv, out, down, g1, g2, w_query, w_key, w_value, w_gate, w_up)
+        turn_back_qkv_kernel,
+        out_shape=[f32(128, D), f32(128, KVD), f32(128, KVD), f32(128, 1), f32(128, D), f32(128, D)],
+        name="turn_back_qkv",
+    )(info, all_qkv, gain, w_query, w_key, w_value, out, grad_in)
 
 
 def local(hidden_in, teacher, doc_ids, valid_mask, norm1_gain, w_query, w_key, w_value, w_out, norm2_gain, w_gate, w_up, w_down):
@@ -1141,64 +1498,24 @@
     meta = jnp.concatenate([key_docs, valid_mask[None], jnp.zeros((7, 128), jnp.int32)], axis=0)
 
     n1_all, metas, wqkv, wo, wt = enter(
-        hidden_in, meta, g1[:, None], g2[:, None], w_query, w_key, w_value, w_gate, w_up, w_out
+        hidden_in, meta, g1[None], g2[None], w_query, w_key, w_value, w_gate, w_up, w_out
     )
     n1_all = n1_all.reshape(1024, D)
     wo = wo.reshape(256, D)
-    qkv = dot(n1_all, wqkv, 1, 1)
-    a, qp, kv, lse, wgu, wd = attend(qkv, metas, tabs, wt, w_down)
-
-    def parts(v):
-        return v.astype(BF).reshape(8, 128, D)
-
-    wide = jax.ShapeDtypeStruct((128, D), F32)
-    y1, n2_all, wgu = exchange(1, op_mid, parts(dot(a, wo, 1, 0)), (hidden_in,), (wide,), sides=[YSwap(wgu)])
-    n2_all = n2_all.reshape(1024, D)
-    wgu = wgu.reshape(1408, D)
-    gate = dot(n2_all, wgu[:704], 1, 1)
-    up = dot(n2_all, wgu[704:], 1, 1)
-    sg = jax.nn.sigmoid(gate)
-    act = gate * sg
-    mid = (act * up).astype(BF)
-    layer_out, dy, loss_rows, dy_all = exchange(
-        2,
-        op_loss,
-        parts(dot(mid, wd, 1, 0)),
-        (y1, teacher, valid[:, None]),
-        (jax.ShapeDtypeStruct((128, D), BF), wide, jax.ShapeDtypeStruct((128, 1), F32)),
-    )
-    dy_all = dy_all.reshape(1024, D)
-
-    grad_down = dot(mid, dy_all, 0, 0).astype(BF)
-    dmid = dot(dy_all, wd, 1, 1)
-    dgate = (dmid * up * sg * (1.0 + gate * (1.0 - sg))).astype(BF)
-    dup = (dmid * act).astype(BF)
-    dgu = jnp.concatenate([dgate, dup], axis=1)
-    grad_gu = dot(dgu, n2_all, 0, 0).astype(BF)
-    dy1, da_all, piece_gu = exchange(
-        3, op_back, parts(dot(dgu, wgu, 1, 0)), (y1, dy), (wide,), sides=[SumColumns(grad_gu.reshape(2, 4, 176, D))]
-    )
-    da_all = da_all.reshape(1024, D)
-    da = dot(da_all, wo, 1, 1).astype(BF)
-    dqkv, piece_down = attend_back(qp, kv, lse, metas, tabs, da, SumRows(grad_down.reshape(2, 352, D)))
-    grad_out = dot(a, da_all, 0, 0).astype(BF)
-    grad_qkv = dot(dqkv, n1_all, 0, 0).astype(BF)
-    grad_in, piece_qkv, piece_out, all_down = exchange(
-        4,
-        op_input,
-        parts(dot(dqkv, wqkv, 1, 0)),
-        (hidden_in, dy1),
-        (wide,),
-        gather=False,
-        sides=[SumColumns(grad_qkv.reshape(2, 4, 48, D)), SumRows(grad_out.reshape(2, 128, D)), SpreadRows(piece_down)],
+    a, qp, kv, lse, wgu, wd = attend(n1_all, wqkv, metas, tabs, wt, w_down)
+
+    layer_out, loss_rows, dy1, da, da_all, grad_gu, piece_down = middle(a, wo, hidden_in, teacher, valid[:, None], wgu, wd)
+    dqkv, piece_gu = attend_back(qp, kv, lse, metas, tabs, da, SumColumns(grad_gu.reshape(2, 4, 176, D)))
+    grad_in, all_down, got_gu, piece_qkv, piece_out = last(
+        dqkv, wqkv, n1_all.reshape(8, 128, D), a, da_all, hidden_in, dy1, piece_down, piece_gu
     )
     stats = jnp.concatenate([loss_rows.reshape(1, 128), valid[None], jnp.zeros((6, 128), F32)], axis=0)
-    info, gq, gk, gv, go, gg, gp, gd, gains = return_grads(
-        stats, piece_gu, piece_qkv, piece_out, all_down, g1[:, None], g2[:, None], w_query, w_key, w_value, w_gate, w_up
+    info, all_gu, all_qkv, all_out = return_grads(stats, got_gu, piece_qkv, piece_out)
+    gg, gp, gd, gain2 = turn_back(info, all_gu, g2[:, None], w_gate, w_up, all_down)
+    gq, gk, gv, gain1, go, input_grad = turn_back_qkv(
+        info, all_qkv.reshape(8, 384, 128), g1[:, None], w_query, w_key, w_value, all_out, grad_in
     )
-    return (
-        layer_out, info[0, 0], grad_in * info[1, 0], gains[0, :, 0], gq, gk, gv, go, gains[1, :, 0], gg, gp, gd,
-    )
+    return (layer_out, info[0, 0], input_grad, gain1[:, 0], gq, gk, gv, go, gain2[:, 0], gg, gp, gd)
 
 
 def solution(mesh):

time: 545 us -> 458 us (0.84)
  matrix products: 68.6 us -> 0 us
  local copies, waits for them, and re-layouts: 21.5 us -> 5.29 us
    dot_general x13 -> x0, matrix products: 68.6 us -> none  [dot(): lax.dot_general(a, b, (((ca,), (cb,)), ((), ())), preferred_element_type=...]
    pallas_call x1, Pallas kernels: 42.2 us -> 60.1 us  [attend_back(): pl.pallas_call(functools.partial(attend_back_kernel, side), out_shape=[ja...]
    pallas_call x1, Pallas kernels: 56.1 us -> 40.8 us  [enter(): pl.pallas_call(enter_kernel, out_shape=[jax.ShapeDtypeStruct((8, 128, D),...]
    pallas_call x1, Pallas kernels: 64.7 us -> 51.1 us  [attend(): pl.pallas_call(attend_kernel, out_shape=[jax.ShapeDtypeStruct((1024, 256)...]
    pallas_call x5, Pallas kernels: 279 us -> 292 us  [the longest x1 172 us: middle(): pl.pallas_call(functools.partial(middle_kernel, side), out_shape=[jax.Sha...]
    unnamed x62 -> x11, local copies, waits for them, and re-layouts: 11.5 us -> 0.83 us
where the time goes in v4:
time: 458 us; the launch traced here: 457 us
  Pallas kernels  444 us (97%)
  other arithmetic  7.1 us (2%)
  local copies, waits for them, and re-layouts  5.29 us (1%)
    pallas_call x1, Pallas kernels, middle(): pl.pallas_call(functools.partial(middle_kernel, side), out_shape=[jax.Sha...  172 us
    pallas_call x1, Pallas kernels, attend_back(): pl.pallas_call(functools.partial(attend_back_kernel, side), out_shape=[ja...  60.1 us
    pallas_call x1, Pallas kernels, last(): pl.pallas_call(functools.partial(last_kernel, *sides), out_shape=[jax.Sha...  54.7 us
    pallas_call x1, Pallas kernels, attend(): pl.pallas_call(attend_kernel, out_shape=[jax.ShapeDtypeStruct((1024, 256)...  51.1 us
    pallas_call x1, Pallas kernels, return_grads(): pl.pallas_call(functools.partial(return_kernel, move), out_shape=[jax.Sha...  49.2 us
    pallas_call x1, Pallas kernels, enter(): pl.pallas_call(enter_kernel, out_shape=[jax.ShapeDtypeStruct((8, 128, D),...  40.8 us
    pallas_call x1, Pallas kernels, turn_back(): pl.pallas_call(turn_back_kernel, grid=(11,), out_shape=[f32(128, FF), f32...  11.6 us

profile of v4, /device:TPU:1, one launch (start us, length us, event | category | flops | bytes accessed | tf_op | source)
XLA Modules:
  0.0 457.1 jit_solution(17826899594072662351)
XLA Ops:
  0.7 0.1 add_convert_fusion
  0.7 0.1 broadcast_multiply_fusion
  0.9 0.3 fusion.5
  1.2 0.1 fusion
  1.3 0.1 fusion.1
  1.4 0.1 fusion.2
  1.5 0.0 copy-start
  1.5 1.3 convert_bitcast_fusion.2
  2.8 0.7 slice_reduce_fusion.1
  3.5 0.1 slice.18
  3.6 0.1 slice.16
  3.7 0.1 pad.19.clone
  3.7 1.3 add_add_fusion.meta_ref
  5.1 40.8 %enter.1 = (bf16[8,128,2048]{2,1,0:T(8,128)(2,1)}, s32[8,16,128]{2,1,0:T(8,128)}, bf16[384,2048]{1,0:T(8,128)(2,1)}, bf16[2,128,2048]{2,1,0:T(8,128)(2,1)}, bf16[2,5632,128]{2,1,0:T(8,128)(2,1)}) custom-call(bf16[128,2048]{1,0:T(8,128)(2,1)} %x_ref.5, s32[16,128]{1,0:T(8,128)} %add_add_fusion.meta_ref, f32[1,128]{1,0:T(1,128)} %get-tuple-element.101.g1_ref, ...), custom_call_target="tpu_custom_call" | custom-call | tf_op jit(solution)/shard_map/enter/pallas_call | solution.py:1047
  45.9 0.0 copy-start.3
  45.9 51.1 %attend.1 = (bf16[1024,256]{1,0:T(8,128)(2,1)}, bf16[8,512,128]{2,1,0:T(8,128)(2,1)}, bf16[2,4,8,128,128]{4,3,2,1,0:T(8,128)(2,1)}, f32[8,8,512]{2,1,0:T(8,128)}...) custom-call(bf16[1024,2048]{1,0:T(8,128)(2,1)} %bitcast.37, bf16[384,2048]{1,0:T(8,128)(2,1)} %get-tuple-element.52.wqkv_ref, ...), custom_call_target="tpu_custom_call" | custom-call | tf_op jit(solution)/shard_map/attend/pallas_call | solution.py:1185
  97.0 0.7 copy.28.valid_ref
  97.8 172.4 %middle.1 = (bf16[128,2048]{1,0:T(8,128)(2,1)}, f32[128,1]{1,0:T(8,128)}, f32[128,2048]{1,0:T(8,128)}, bf16[1024,256]{1,0:T(8,128)(2,1)}, bf16[8,128,2048]{2,1,0...) custom-call(bf16[1024,256]{1,0:T(8,128)(2,1)} %get-tuple-element.55.a_ref, ...), custom_call_target="tpu_custom_call" | custom-call | tf_op jit(solution)/shard_map/middle/pallas_call | solution.py:513
  270.1 60.1 %attend_back.1 = (bf16[1024,384]{1,0:T(8,128)(2,1)}, bf16[176,1024]{1,0:T(8,128)(2,1)}) custom-call(bf16[8,512,128]{2,1,0:T(8,128)(2,1)} %get-tuple-element.61.qp_ref, bf16[2,4,8,128,128]{4,3,2,1,0:T(8,128)(2,1)} %get-tuple-element.62.kv_ref, f32[8,8,512]{2,1,0:T(8,128)} %get-tuple-element.63.lse_ref, s32[8,16,128]{2,1,0:T(8,128)} %get-tuple-element.53.meta_ref, ...), custom_call_target="tpu_custom_call" | custom-call | tf_op jit(solution)/shard_map/attend_back/pallas_call | solution.py:1301
  330.2 54.7 %last.1 = (f32[128,2048]{1,0:T(8,128)}, bf16[352,2048]{1,0:T(8,128)(2,1)}, bf16[8,176,128]{2,1,0:T(8,128)(2,1)}, bf16[48,1024]{1,0:T(8,128)(2,1)}, bf16[2,128,128]{2,1,0:T(8,128)(2,1)}) custom-call(bf16[1024,384]{1,0:T(8,128)(2,1)} %get-tuple-element.66.dqkv_ref, bf16[384,2048]{1,0:T(8,128)(2,1)} %get-tuple-element.52.wqkv_ref, ...), custom_call_target="tpu_custom_call" | custom-call | tf_op jit(solution)/shard_map/last/pallas_call | solution.py:923
  384.9 0.1 reduce.2
  385.0 0.1 pad.5.clone
  385.1 0.7 maximum_maximum_fusion.stats_ref
  385.8 49.2 %return_grads.1 = (f32[8,128]{1,0:T(8,128)}, bf16[2,5632,128]{2,1,0:T(8,128)(2,1)}, bf16[8,8,48,128]{3,2,1,0:T(8,128)(2,1)}, bf16[128,2048]{1,0:T(8,128)(2,1)}) custom-call(f32[8,128]{1,0:T(8,128)} %maximum_maximum_fusion.stats_ref, bf16[8,176,128]{2,1,0:T(8,128)(2,1)} %get-tuple-element.71.got_gu, bf16[48,1024]{1,0:T(8,128)(2,1)} %get-tuple-element.72.qkv_ref, ...), custom_call_target="tpu_custom_call" | custom-call | tf_op jit(solution)/shard_map/return_grads/pallas_call | solution.py:1405
  435.0 0.7 copy.30.gain_ref
  435.8 11.6 %turn_back.1 = (f32[128,5632]{1,0:T(8,128)}, f32[128,5632]{1,0:T(8,128)}, f32[352,2048]{1,0:T(8,128)}, f32[128,1]{1,0:T(8,128)}) custom-call(f32[8,128]{1,0:T(8,128)} %get-tuple-element.74.info_ref, bf16[2,5632,128]{2,1,0:T(8,128)(2,1)} %get-tuple-element.84.all_ref, f32[128,1]{1,0:T(8,128)} %copy.30.gain_ref, bf16[128,5632]{1,0:T(8,128)(2,1)} %wg_ref.3, ...), custom_call_target="tpu_custom_call" | custom-call | tf_op jit(solution)/shard_map/turn_back/pallas_call | solution.py:1448
  447.4 1.5 reduce.4
  448.9 0.7 copy.29.gain_ref
  449.6 4.0 turn_back_qkv.1
  453.6 1.5 reduce.3
  455.1 1.2 slice.19
  456.3 0.8 copy.37
  (16 shorter events, 0.1 us)
Async XLA Ops:
  1.5 44.4 %copy-start = (f32[6,128,128]{2,1,0:T(8,128)}, f32[6,128,128]{2,1,0:T(8,128)S(1)}, u32[]{:S(2)}) copy-start(f32[6,128,128]{2,1,0:T(8,128)S(1)} %bitcast_dynamic-update-slice_fusion.tab_ref) | copy-start | bytes 1179652
  45.9 51.1 %copy-start.3 = (s32[128]{0:T(128)S(1)}, s32[128]{0:T(128)}, u32[]{:S(2)}) copy-start(s32[128]{0:T(128)} %param.16) | copy-start | bytes 1540
  330.2 54.7 %copy-start.2 = (f32[128,1]{1,0:T(8,128)S(1)}, f32[128,1]{1,0:T(8,128)}, u32[]{:S(2)}) copy-start(f32[128,1]{1,0:T(8,128)} %get-tuple-element.60) | copy-start | bytes 1540
  447.4 8.9 %copy-start.1 = (bf16[128,2048]{1,0:T(8,128)(2,1)S(1)}, bf16[128,2048]{1,0:T(8,128)(2,1)}, u32[]{:S(2)}) copy-start(bf16[128,2048]{1,0:T(8,128)(2,1)} %get-tuple-element.117) | copy-start | bytes 1572868

commit v5 on v4

v5 whole, which is shorter than its diff:
```python
import functools

import jax
import jax.numpy as jnp
from jax import lax
from jax.experimental import pallas as pl
from jax.experimental.pallas import tpu as pltpu
from jax.sharding import Mesh, PartitionSpec as P

D = 2048
HEADS = 32
KV_HEADS = 4
HD = 64
FF = 5632
KVD = 256
EPSILON = 1e-05
THETA = 10000.0
NEGATIVE = -1e30
AXES = ("y_hi", "z", "x", "y_lo", "core")
BF = jnp.bfloat16
F32 = jnp.float32


def dot(a, b, ca, cb):
    return lax.dot_general(a, b, (((ca,), (cb,)), ((), ())), preferred_element_type=F32)


def tables(positions):
    indices = jnp.arange(HD // 2, dtype=jnp.int32).astype(F32)
    frequency = THETA ** (-(indices * 2.0 / HD))
    angles = positions.astype(F32)[:, None] * frequency[None, :]
    angles = jnp.concatenate([angles, angles], axis=1)
    return jnp.cos(angles), jnp.sin(angles)


def positions_of(c):
    t = jnp.arange(64, dtype=jnp.int32)
    return jnp.concatenate([c * 64 + t, (15 - c) * 64 + t])


MESH = pl.DeviceIdType.MESH
HALVES = (pl.ds(0, 64), pl.ds(64, 64))
VM = pl.BlockSpec(memory_space=pltpu.VMEM)
HB = pl.BlockSpec(memory_space=pl.ANY)


def params(number):
    return pltpu.CompilerParams(collective_id=number, has_side_effects=True, vmem_limit_bytes=56 * 2**20)


def send(src, dst, sems, i, device):
    copy = pltpu.make_async_remote_copy(
        src_ref=src, dst_ref=dst, send_sem=sems[0].at[i], recv_sem=sems[1].at[i], device_id=device, device_id_type=MESH
    )
    copy.start()
    return copy


def meet(devices):
    barrier = pltpu.get_barrier_semaphore()
    for device in devices:
        pl.semaphore_signal(barrier, inc=1, device_id=device, device_id_type=MESH)
    pl.semaphore_wait(barrier, len(devices))


class Ring:
    def __init__(self):
        x, core = lax.axis_index("x"), lax.axis_index("core")
        self.x, self.core = x, core
        self.right_x, self.left_x, self.far_x = lax.rem(x + 1, 4), lax.rem(x + 3, 4), lax.rem(x + 2, 4)
        self.right, self.left, self.sibling = {"x": self.right_x}, {"x": self.left_x}, {"core": 1 - core}


def norm_scale(v):
    return lax.rsqrt(jnp.mean(v * v, axis=1, keepdims=True) + EPSILON)


class Side:
    in_place = False

    def middle(self):
        pass


class Torus:
    def __init__(self):
        self.y_hi, self.y_lo, self.z = lax.axis_index("y_hi"), lax.axis_index("y_lo"), lax.axis_index("z")
        self.y = self.y_hi * 2 + self.y_lo
        self.ys = [(dy, lax.rem(self.y + dy, 4)) for dy in (1, 3, 2)]
        self.zs = [(dz, lax.rem(self.z + dz, 4)) for dz in (1, 3, 2)]
        self.peers = [self.y_device(y) for _, y in self.ys] + [{"z": z} for _, z in self.zs]

    def y_device(self, y):
        return {"y_hi": y // 2, "y_lo": lax.rem(y, 2)}


def lanes_at(start, size):
    return pl.ds(pl.multiple_of(start, 128), size)


def add_up(out, terms, lead, rows):
    steps = rows // 16

    def body(k, _):
        i, r = k // steps, pl.ds(pl.multiple_of(lax.rem(k, steps) * 16, 16), 16)
        total = None
        for at in terms:
            term = at(i, r).astype(F32)
            total = term if total is None else total + term
        out(i, r, total.astype(BF))
        return 0

    lax.fori_loop(0, lead * steps, body, 0)


class Ag:
    def __init__(self, ring, buf, sems):
        r = self.r = ring
        self.buf, self.sems = buf, sems
        self.plan = (
            (r.x, 0, r.right), (r.x, 1, r.right), (r.x, 1, r.left), (r.x, 0, r.left),
            (r.left_x, 0, r.right), (r.right_x, 1, r.left),
            (r.x, 0, r.sibling), (r.x, 1, r.sibling),
            (r.left_x, 0, r.sibling), (r.left_x, 1, r.sibling), (r.right_x, 0, r.sibling), (r.right_x, 1, r.sibling),
            (r.far_x, 0, r.sibling), (r.far_x, 1, r.sibling),
        )

    def copy(self, i):
        x, half, device = self.plan[i]
        block = self.buf.at[x * 2 + self.r.core, HALVES[half]]
        return pltpu.make_async_remote_copy(
            src_ref=block, dst_ref=block, send_sem=self.sems[0].at[i], recv_sem=self.sems[1].at[i],
            device_id=device, device_id_type=MESH,
        )

    def begin(self, half):
        for i in ((0, 3, 6), (2, 1, 7))[half]:
            self.copy(i).start()

    def near(self):
        for got, onward in ((0, (4, 8)), (2, (5, 11)), (1, (9,)), (3, (10,))):
            self.copy(got).wait_recv()
            for i in onward:
                self.copy(i).start()

    def far(self):
        for got, onward in ((4, 12), (5, 13)):
            self.copy(got).wait_recv()
            self.copy(onward).start()

    def have(self, *which):
        for i in which:
            self.copy(i).wait_recv()

    def drain(self):
        for i in range(14):
            self.copy(i).wait_send()


class Rs:
    def __init__(self, ring, parts, held, got, sems):
        r = self.r = ring
        self.parts, self.held, self.got, self.sems = parts, held, got, sems
        self.blocks = (r.far_x, r.right_x, r.left_x, r.x)
        a, b = HALVES
        self.plan = {
            4: (held.at[0, a], got.at[4, a], r.right), 5: (held.at[0, b], got.at[4, b], r.left),
            6: (held.at[1, b], got.at[5, b], r.right), 7: (held.at[2, a], got.at[5, a], r.left),
            8: (held.at[1, a], got.at[6, a], r.right), 9: (held.at[2, b], got.at[6, b], r.left),
        }

    def swap(self, i, x):
        return pltpu.make_async_remote_copy(
            src_ref=self.parts.at[x * 2 + 1 - self.r.core], dst_ref=self.got.at[i], send_sem=self.sems[0].at[i],
            recv_sem=self.sems[1].at[i], device_id=self.r.sibling, device_id_type=MESH,
        )

    def copy(self, i):
        if i < 4:
            return self.swap(i, self.blocks[i])
        src, dst, device = self.plan[i]
        return pltpu.make_async_remote_copy(
            src_ref=src, dst_ref=dst, send_sem=self.sems[0].at[i], recv_sem=self.sems[1].at[i],
            device_id=device, device_id_type=MESH,
        )

    def pair(self, i, half):
        x = self.blocks[i]

        def body(k, _):
            rows = pl.ds(half * 64 + k * 16, 16)
            total = self.parts[x * 2 + self.r.core, rows, :].astype(F32) + self.got[i, rows, :].astype(F32)
            self.held[i, rows, :] = total.astype(BF)
            return 0

        lax.fori_loop(0, 4, body, 0)

    def onward(self, i, half):
        def body(k, _):
            rows = pl.ds(half * 64 + k * 16, 16)
            total = self.held[i, rows, :].astype(F32) + self.got[4, rows, :].astype(F32)
            self.held[i, rows, :] = total.astype(BF)
            return 0

        lax.fori_loop(0, 4, body, 0)

    def send_left(self):
        self.copy(2).wait_recv()
        self.pair(2, 0)
        self.copy(7).start()

    def send_right(self):
        self.copy(1).wait_recv()
        self.pair(1, 1)
        self.copy(6).start()

    def send_far(self):
        self.copy(0).wait_recv()
        self.pair(0, 0)
        self.copy(4).start()
        self.pair(0, 1)
        self.copy(5).start()

    def relay(self):
        self.pair(1, 0)
        self.pair(2, 1)
        self.copy(4).wait_recv()
        self.onward(1, 0)
        self.copy(8).start()
        self.copy(5).wait_recv()
        self.onward(2, 1)
        self.copy(9).start()
        self.copy(3).wait_recv()

    def ready(self, half):
        for i in ((7, 8), (6, 9))[half]:
            self.copy(i).wait_recv()

    def total(self, rows):
        r = self.r
        return (
            self.parts[r.x * 2 + r.core, rows, :].astype(F32)
            + self.got[3, rows, :].astype(F32)
            + self.got[5, rows, :].astype(F32)
            + self.got[6, rows, :].astype(F32)
        )

    def drain(self):
        for i in range(10):
            self.copy(i).wait_send()


def middle_kernel(
    down_side, gu_side, a_ref, wo_ref, x_ref, valid_ref, wd_ref, teacher_hbm, half_w_ref,
    out_ref, loss_ref, dy1_ref, da_ref, gout_ref, ggu_ref, piece_ref, gu_piece_ref,
    w, n2, dyg, dag, parts, held, got, y1, gate, up, mid, mid_t, dup, dgu1, dgu2, gd, gu1, dmid,
    rs1_s, rs1_r, ag1_s, ag1_r, rs2_s, rs2_r, ag2_s, ag2_r, rs3_s, rs3_r, ag3_s, ag3_r, w_s, w_r, loc, *side_scratch,
):
    ring = Ring()
    y_lo = lax.axis_index("y_lo")
    near, other = y_partners()
    down_side.bind(ring, (gd,), (piece_ref,), side_scratch[: len(down_side.scratch)])
    gu_side.bind(ring, (gu1,), (gu_piece_ref,), side_scratch[len(down_side.scratch) :])
    meet([ring.right, ring.left, ring.sibling] + Torus().peers)
    here = ring.x * 2 + ring.core
    dy, dgate = dy1_ref, mid
    teacher = dag.at[here]
    teacher_copy = pltpu.make_async_copy(teacher_hbm, teacher, loc.at[4])
    teacher_copy.start()

    wcopies = []
    for dx in range(4):
        lanes = group_lanes(lax.rem(ring.x + 4 - dx, 4), y_lo)
        src, dst = half_w_ref.at[:, :, :, lanes], w.at[:, :, :, lanes]
        wcopies.append(send(src, dst, (w_s, w_r), dx, (near, other)[dx // 2]))
        copy = pltpu.make_async_copy(src, dst, loc.at[dx])
        copy.start()
        wcopies.append(copy)

    def rows_of(x):
        return pl.ds(pl.multiple_of(x * 256, 256), 256)

    def block(buf, x):
        return buf[pl.ds(x * 2, 2)].reshape(256, D)

    def put(x, product):
        def body(k, _):
            lanes = lanes_at(k * 512, 512)
            parts[pl.ds(x * 2, 2), :, lanes] = product(lanes).astype(BF).reshape(2, 128, 512)
            return 0

        lax.fori_loop(0, 4, body, 0)

    def reduced(rs, op, ag, buf):
        for half in range(2):
            rs.ready(half)

            def body(k, _, half=half):
                rows = pl.ds(half * 64 + k * 16, 16)
                buf[here, rows, :] = op(rows, rs.total(rows)).astype(BF)
                return 0

            lax.fori_loop(0, 4, body, 0)
            ag.begin(half)

    def over_blocks(ag, rs, work):
        def step(i, _):
            at = functools.partial(jnp.equal, i)

            @pl.when(at(0))
            def _():
                ag.have(6, 7)

            @pl.when(at(1))
            def _():
                ag.near()
                ag.have(8, 9)

            @pl.when(at(2))
            def _():
                ag.have(10, 11)
                if rs is not None:
                    rs.send_left()

            @pl.when(at(3))
            def _():
                if rs is not None:
                    rs.send_right()
                ag.far()
                ag.have(12, 13)

            x = lax.rem(ring.x + jnp.where(at(1), 3, jnp.where(at(2), 1, jnp.where(at(3), 2, 0))), 4)
            work(x)
            if rs is not None:
                rs.swap(3 - i, x).start()
            return 0

        lax.fori_loop(0, 4, step, 0)

    rs = Rs(ring, parts, held, got, (rs1_s, rs1_r))
    ag = Ag(ring, n2, (ag1_s, ag1_r))
    for i in range(4):
        x = rs.blocks[i]
        put(x, lambda lanes, x=x: nn(a_ref[rows_of(x), :], wo_ref[:, lanes]))
        rs.copy(i).start()
        if i == 1:
            rs.send_far()
        elif i == 2:
            rs.send_right()
        elif i == 3:
            rs.send_left()
    rs.relay()

    def op1(rows, total):
        v = x_ref[rows, :].astype(F32) + total
        y1[rows, :] = v
        return v * norm_scale(v)

    reduced(rs, op1, ag, n2)
    rs.drain()
    for copy in wcopies:
        copy.wait()
    teacher_copy.wait()

    rs = Rs(ring, parts, held, got, (rs2_s, rs2_r))

    def forward(x):
        rows = rows_of(x)
        gate[rows, :] = nt(block(n2, x), w[0].reshape(704, D))
        up[rows, :] = nt(block(n2, x), w[1].reshape(704, D))

        def body(k, _):
            r = pl.ds(pl.multiple_of(x * 256 + k * 32, 32), 32)
            g = gate[r, :]
            mid[pl.ds(pl.multiple_of(k * 32, 32), 32), :] = (g * jax.nn.sigmoid(g) * up[r, :]).astype(BF)
            return 0

        lax.fori_loop(0, 8, body, 0)
        put(x, lambda lanes: nn(mid[...], wd_ref[:, lanes]))
        mid_t[:, rows] = mid[...].T

    over_blocks(ag, rs, forward)
    rs.send_far()
    rs.relay()
    ag.drain()

    def op2(rows, total):
        v = y1[rows, :] + total
        out_ref[rows, :] = v.astype(BF)
        miss = v - dag[here, rows, :].astype(F32)
        valid = valid_ref[rows, :]
        loss_ref[rows, :] = valid * jnp.mean(miss * miss, axis=1, keepdims=True)
        dy[rows, :] = valid * miss
        return valid * miss

    ag = Ag(ring, dyg, (ag2_s, ag2_r))
    reduced(rs, op2, ag, dyg)
    rs.drain()

    rs = Rs(ring, parts, held, got, (rs3_s, rs3_r))

    def backward(x):
        rows = rows_of(x)
        dgate_mid = nt(block(dyg, x), wd_ref[...])
        dmid[...] = dgate_mid

        def body(k, _):
            r = pl.ds(pl.multiple_of(x * 256 + k * 32, 32), 32)
            q = pl.ds(pl.multiple_of(k * 32, 32), 32)
            g, dm = gate[r, :], dmid[q, :]
            sg = jax.nn.sigmoid(g)
            dgate[q, :] = (dm * up[r, :] * sg * (1.0 + g * (1.0 - sg))).astype(BF)
            dup[q, :] = (dm * (g * sg)).astype(BF)
            return 0

        lax.fori_loop(0, 8, body, 0)
        put(x, lambda lanes: nn(dgate[...], w[0, :, :, lanes].reshape(704, 512)) + nn(dup[...], w[1, :, :, lanes].reshape(704, 512)))
        for i, ref in enumerate((dgate, dup)):
            turned = ref[...].T
            for c in range(4):
                dgu1[pl.ds((4 * i + c) * 96, 96), rows] = turned[176 * c : 176 * c + 96]
                dgu2[pl.ds((4 * i + c) * 80, 80), rows] = turned[176 * c + 96 : 176 * c + 176]

    over_blocks(ag, rs, backward)
    rs.send_far()

    def grad_down(k, _):
        lanes = lanes_at(k * 512, 512)
        gd[:, :, lanes] = nn(mid_t[...], dyg[:, :, lanes].reshape(1024, 512)).astype(BF).reshape(2, 352, 512)
        return 0

    lax.fori_loop(0, 4, grad_down, 0)
    down_side.start()
    rs.relay()

    def grad_gu(rows, lhs, out, k):
        lanes = lanes_at(k * 512, 512)
        out[:, :, :, lanes] = nn(lhs[...], n2[:, :, lanes].reshape(1024, 512)).astype(BF).reshape(2, 4, rows, 512)

    def grad_gu1(k, _):
        grad_gu(96, dgu1, gu1, k)
        return 0

    lax.fori_loop(0, 4, grad_gu1, 0)
    gu_side.start()
    ag.drain()

    def op3(rows, total):
        v = back_norm(y1[rows, :], dy[rows, :], total)
        dy1_ref[rows, :] = v
        return v

    ag = Ag(ring, dag, (ag3_s, ag3_r))
    reduced(rs, op3, ag, dag)
    rs.drain()

    def to_attention(x):
        rows = rows_of(x)
        da_ref[rows, :] = nt(block(dag, x), wo_ref[...]).astype(BF)
        mid_t[0:256, rows] = a_ref[rows, :].T
        grad_gu(80, dgu2, ggu_ref, x)

    over_blocks(ag, None, to_attention)
    down_side.middle()
    gu_side.middle()

    def grad_out(k, _):
        lanes = lanes_at(k * 512, 512)
        gout_ref[:, :, lanes] = nn(mid_t[0:256, :], dag[:, :, lanes].reshape(1024, 512)).astype(BF).reshape(2, 128, 512)
        return 0

    lax.fori_loop(0, 4, grad_out, 0)
    ag.drain()
    down_side.finish()
    gu_side.finish()


def middle(a, wo, x, teacher, valid, half_w, wd):
    dma = pltpu.SemaphoreType.DMA
    pair = lambda n: [dma((n,)), dma((n,))]
    big = pltpu.VMEM((8, 128, D), BF)
    sides = [SumRows(jax.ShapeDtypeStruct((2, 352, D), BF), True), SumColumns(jax.ShapeDtypeStruct((2, 4, 96, D), BF), True)]
    return pl.pallas_call(
        functools.partial(middle_kernel, *sides),
        out_shape=[
            jax.ShapeDtypeStruct((128, D), BF), jax.ShapeDtypeStruct((128, 1), F32), jax.ShapeDtypeStruct((128, D), F32),
            jax.ShapeDtypeStruct((1024, 256), BF), jax.ShapeDtypeStruct((2, 128, D), BF), jax.ShapeDtypeStruct((2, 4, 80, D), BF),
            *[s for side in sides for s in side.shapes],
        ],
        in_specs=[VM] * 5 + [HB, HB],
        out_specs=[VM] * 8,
        scratch_shapes=[
            pltpu.VMEM((2, 2, 352, D), BF), big, big, big, big, pltpu.VMEM((3, 128, D), BF), pltpu.VMEM((7, 128, D), BF),
            pltpu.VMEM((128, D), F32),
            pltpu.VMEM((1024, 704), F32), pltpu.VMEM((1024, 704), F32),
            pltpu.VMEM((256, 704), BF), pltpu.VMEM((704, 1024), BF), pltpu.VMEM((256, 704), BF),
            pltpu.VMEM((768, 1024), BF), pltpu.VMEM((640, 1024), BF), pltpu.VMEM((2, 352, D), BF), pltpu.VMEM((2, 4, 96, D), BF),
            pltpu.VMEM((256, 704), F32),
            *pair(10), *pair(14), *pair(10), *pair(14), *pair(10), *pair(14), *pair(4), dma((5,)),
            *[s for side in sides for s in side.scratch],
        ],
        compiler_params=pltpu.CompilerParams(collective_id=1, has_side_effects=True, vmem_limit_bytes=63 * 2**20),
        name="middle",
    )(a, wo, x, valid, wd, teacher, half_w)


class SumColumns(Side):
    def __init__(self, grads, in_vmem=False):
        r = self.rows = grads.shape[2]
        dma = pltpu.SemaphoreType.DMA
        self.first = 0 if in_vmem else 1
        n = 3 + self.first
        self.operands = [grads]
        self.shapes = [jax.ShapeDtypeStruct((r, 1024), BF)]
        self.scratch = [
            pltpu.VMEM((n, 4, r, 512), BF), pltpu.VMEM((n, 2, 2, r, 512), BF),
            pltpu.VMEM((3, r, 512), BF), pltpu.VMEM((3, r, 512), BF),
            dma((9,)), dma((9,)), dma((6,)), dma((6,)), dma((3,)),
        ]

    def bind(self, ring, ins, outs, scratch):
        (self.g,), (self.out,) = ins, outs
        self.by, self.bz, self.by2, self.bz2, s1, r1, s2, r2, self.loc = scratch
        self.one, self.two = (s1, r1), (s2, r2)
        self.t = Torus()
        self.peers = self.t.peers

    def start(self):
        t, g = self.t, self.g
        self.c = []
        for i, (dy, y) in enumerate(t.ys):
            src = g.at[y // 2, :, :, lanes_at(lax.rem(y, 2) * 1024, 512)]
            self.c.append(send(src, self.by.at[dy - 1 + self.first], self.one, i, t.y_device(y)))
        for i, (dz, z) in enumerate(t.zs):
            for yl in range(2):
                src = g.at[:, z, :, pl.ds(yl * 1024 + 512, 512)]
                self.c.append(send(src, self.bz.at[dz - 1 + self.first, yl], self.one, 3 + 2 * i + yl, {"z": z}))
        self.l = []
        if not self.first:
            return
        self.l.append(pltpu.make_async_copy(g.at[t.y_hi, :, :, lanes_at(t.y_lo * 1024, 512)], self.by.at[0], self.loc.at[0]))
        for yl in range(2):
            self.l.append(
                pltpu.make_async_copy(g.at[:, t.z, :, pl.ds(yl * 1024 + 512, 512)], self.bz.at[0, yl], self.loc.at[1 + yl])
            )
        for copy in self.l:
            copy.start()

    def middle(self):
        t, by, bz = self.t, self.by, self.bz
        for copy in self.l:
            copy.wait()
        for copy in self.c:
            copy.wait_recv()

        def put_y(i, r, v):
            by[0, i, r, :] = v

        def put_z(i, r, v):
            bz[0, i // 2, lax.rem(i, 2), r, :] = v

        own_y = [lambda i, r: self.g[t.y_hi, i, r, lanes_at(t.y_lo * 1024, 512)]]
        own_z = [lambda i, r: self.g[lax.rem(i, 2), t.z, r, lanes_at((i // 2) * 1024 + 512, 512)]]
        if self.first:
            own_y, own_z = [], []
        n = 3 + self.first
        add_up(put_y, own_y + [lambda i, r, k=k: by[k, i, r, :] for k in range(n)], 4, self.rows)
        add_up(put_z, own_z + [lambda i, r, k=k: bz[k, i // 2, lax.rem(i, 2), r, :] for k in range(n)], 4, self.rows)
        self.c2 = []
        for i, (dz, z) in enumerate(t.zs):
            self.c2.append(send(by.at[0, z], self.by2.at[dz - 1], self.two, i, {"z": z}))
        for i, (dy, y) in enumerate(t.ys):
            self.c2.append(send(bz.at[0, lax.rem(y, 2), y // 2], self.bz2.at[dy - 1], self.two, 3 + i, t.y_device(y)))

    def finish(self):
        t, by, bz, by2, bz2, out = self.t, self.by, self.bz, self.by2, self.bz2, self.out
        for copy in self.c2:
            copy.wait_recv()

        def put_a(i, r, v):
            out[r, 0:512] = v

        def put_b(i, r, v):
            out[r, 512:1024] = v

        add_up(put_a, [lambda i, r: by[0, t.z, r, :]] + [lambda i, r, k=k: by2[k, r, :] for k in range(3)], 1, self.rows)
        add_up(put_b, [lambda i, r: bz[0, t.y_lo, t.y_hi, r, :]] + [lambda i, r, k=k: bz2[k, r, :] for k in range(3)], 1, self.rows)
        for copy in self.c + self.c2:
            copy.wait_send()


class SumRows(Side):
    def __init__(self, grads, in_vmem=False):
        r = self.rows = grads.shape[1]
        dma = pltpu.SemaphoreType.DMA
        self.first = 0 if in_vmem else 1
        n = 3 + self.first
        self.operands = [grads]
        self.shapes = [jax.ShapeDtypeStruct((2, r, 128), BF)]
        self.scratch = [
            pltpu.VMEM((n, r, 512), BF), pltpu.VMEM((n, 2, 2, r, 128), BF),
            pltpu.VMEM((3, r, 128), BF), pltpu.VMEM((3, r, 128), BF),
            dma((9,)), dma((9,)), dma((6,)), dma((6,)), dma((3,)),
        ]

    def bind(self, ring, ins, outs, scratch):
        (self.g,), (self.out,) = ins, outs
        self.by, self.bz, self.by2, self.bz2, s1, r1, s2, r2, self.loc = scratch
        self.one, self.two = (s1, r1), (s2, r2)
        self.t = Torus()
        self.peers = self.t.peers

    def start(self):
        t, g = self.t, self.g
        self.c = []
        for i, (dy, y) in enumerate(t.ys):
            src = g.at[lax.rem(y, 2), :, lanes_at((y // 2) * 1024, 512)]
            self.c.append(send(src, self.by.at[dy - 1 + self.first], self.one, i, t.y_device(y)))
        for i, (dz, z) in enumerate(t.zs):
            for yh in range(2):
                src = g.at[:, :, lanes_at(yh * 1024 + 512 + z * 128, 128)]
                self.c.append(send(src, self.bz.at[dz - 1 + self.first, yh], self.one, 3 + 2 * i + yh, {"z": z}))
        self.l = []
        if not self.first:
            return
        self.l.append(pltpu.make_async_copy(g.at[t.y_lo, :, lanes_at(t.y_hi * 1024, 512)], self.by.at[0], self.loc.at[0]))
        for yh in range(2):
            self.l.append(
                pltpu.make_async_copy(g.at[:, :, lanes_at(yh * 1024 + 512 + t.z * 128, 128)], self.bz.at[0, yh], self.loc.at[1 + yh])
            )
        for copy in self.l:
            copy.start()

    def middle(self):
        t, by, bz = self.t, self.by, self.bz
        for copy in self.l:
            copy.wait()
        for copy in self.c:
            copy.wait_recv()

        def put_y(i, r, v):
            by[0, r, :] = v

        def put_z(i, r, v):
            bz[0, i // 2, lax.rem(i, 2), r, :] = v

        own_y = [lambda i, r: self.g[t.y_lo, r, lanes_at(t.y_hi * 1024, 512)]]
        own_z = [lambda i, r: self.g[lax.rem(i, 2), r, lanes_at((i // 2) * 1024 + 512 + t.z * 128, 128)]]
        if self.first:
            own_y, own_z = [], []
        n = 3 + self.first
        add_up(put_y, own_y + [lambda i, r, k=k: by[k, r, :] for k in range(n)], 1, self.rows)
        add_up(put_z, own_z + [lambda i, r, k=k: bz[k, i // 2, lax.rem(i, 2), r, :] for k in range(n)], 4, self.rows)
        self.c2 = []
        for i, (dz, z) in enumerate(t.zs):
            self.c2.append(send(by.at[0, :, lanes_at(z * 128, 128)], self.by2.at[dz - 1], self.two, i, {"z": z}))
        for i, (dy, y) in enumerate(t.ys):
            self.c2.append(send(bz.at[0, y // 2, lax.rem(y, 2)], self.bz2.at[dy - 1], self.two, 3 + i, t.y_device(y)))

    def finish(self):
        t, by, bz, by2, bz2, out = self.t, self.by, self.bz, self.by2, self.bz2, self.out
        for copy in self.c2:
            copy.wait_recv()

        def put_a(i, r, v):
            out[0, r, :] = v

        def put_b(i, r, v):
            out[1, r, :] = v

        own = lanes_at(t.z * 128, 128)
        add_up(put_a, [lambda i, r: by[0, r, own]] + [lambda i, r, k=k: by2[k, r, :] for k in range(3)], 1, self.rows)
        add_up(put_b, [lambda i, r: bz[0, t.y_hi, t.y_lo, r, :]] + [lambda i, r, k=k: bz2[k, r, :] for k in range(3)], 1, self.rows)
        for copy in self.c + self.c2:
            copy.wait_send()


def piece_lanes(c, part):
    return lanes_at((c // 4) * 1024 + part * 512 + lax.rem(c, 4) * 128, 128)


def ctx_at(k):
    y_hi, z = lax.axis_index("y_hi"), lax.axis_index("z")
    y, zz = (1 - y_hi if k // 4 else y_hi), lax.rem(z + k % 4, 4)
    return y * 4 + zz, {"y_hi": y, "z": zz}


class Spread:
    def __init__(self, piece, slot, sems, base, y_first, local):
        self.piece, self.slot, self.sems, self.base, self.y_first, self.local = piece, slot, sems, base, y_first, local

    def copy(self, k, src, c, device):
        return pltpu.make_async_remote_copy(
            src_ref=src, dst_ref=self.slot(c), send_sem=self.sems[0].at[self.base + k - 1],
            recv_sem=self.sems[1].at[self.base + k - 1], device_id=device, device_id_type=MESH,
        )

    def first(self, k):
        here, _ = ctx_at(0)
        return self.copy(k, self.piece, here, ctx_at(k)[1])

    def second(self, dz):
        if self.y_first:
            c, _ = ctx_at(4)
            return self.copy(4 + dz, self.slot(c), c, ctx_at(dz)[1])
        c, _ = ctx_at(4 - dz)
        return self.copy(4 + dz, self.slot(c), c, ctx_at(4)[1])

    def own(self):
        return pltpu.make_async_copy(self.piece, self.slot(ctx_at(0)[0]), self.local)

    def start(self):
        for k in (4, 1, 3, 2) if self.y_first else (1, 3, 2, 4):
            self.first(k).start()
        if self.local is not None:
            self.own().start()

    def relay(self):
        if self.y_first:
            self.first(4).wait_recv()
            for dz in (1, 3, 2):
                self.second(dz).start()
        else:
            for dz in (1, 3, 2):
                self.first(dz).wait_recv()
                self.second(dz).start()

    def finish(self):
        if self.y_first:
            for dz in (1, 3, 2):
                self.first(dz).wait_recv()
        else:
            self.first(4).wait_recv()
        for dz in (1, 3, 2):
            self.second(dz).wait_recv()
            self.second(dz).wait_send()
        for k in (1, 2, 3, 4):
            self.first(k).wait_send()
        self.own().wait()


class SpreadRows(Side):
    def __init__(self, pieces):
        r = pieces.shape[1]
        dma = pltpu.SemaphoreType.DMA
        self.operands = [pieces]
        self.shapes = [jax.ShapeDtypeStruct((r, D), BF)]
        self.scratch = [dma((14,)), dma((14,)), dma((2,))]

    def bind(self, ring, ins, outs, scratch):
        (p,), (out,) = ins, outs
        self.peers = [ctx_at(k)[1] for k in range(1, 8)]
        self.s = [
            Spread(
                p.at[part], lambda c, part=part: out.at[:, piece_lanes(c, part)], scratch[:2], part * 7, part == 0,
                scratch[2].at[part],
            )
            for part in range(2)
        ]

    def start(self):
        for s in self.s:
            s.start()

    def middle(self):
        for s in self.s:
            s.relay()

    def finish(self):
        for s in self.s:
            s.finish()


class Move(Side):
    def __init__(self, pieces):
        dma = pltpu.SemaphoreType.DMA
        self.operands = [pieces]
        self.shapes = [jax.ShapeDtypeStruct((8, pieces.shape[0], 128), BF)]
        self.scratch = [dma((8,)), dma((8,))]

    def bind(self, ring, ins, outs, scratch):
        (self.p,), (self.out,), self.sems = ins, outs, scratch
        x, self.y_lo, core = lax.axis_index("x"), lax.axis_index("y_lo"), lax.axis_index("core")
        self.here16, self.here8 = x * 4 + self.y_lo * 2 + core, x * 2 + core
        self.peers = [device for _, device in group_peers()]

    def same(self, j):
        return self.here16 == self.y_lo * 8 + j

    def away(self, j):
        return pltpu.make_async_remote_copy(
            src_ref=self.p.at[:, pl.ds(j * 128, 128)], dst_ref=self.out.at[self.here8], send_sem=self.sems[0].at[j],
            recv_sem=self.sems[1].at[self.here8], device_id={"x": self.y_lo * 2 + j // 4, "y_lo": j // 2 % 2, "core": j % 2},
            device_id_type=MESH,
        )

    def stay(self, j):
        return pltpu.make_async_copy(self.p.at[:, pl.ds(j * 128, 128)], self.out.at[self.here8], self.sems[1].at[self.here8])

    def start(self):
        for j in range(8):

            @pl.when(self.same(j))
            def _():
                self.stay(j).start()

            @pl.when(jnp.logical_not(self.same(j)))
            def _():
                self.away(j).start()

    def arrive(self, s):
        pltpu.make_async_copy(self.out.at[s], self.out.at[s], self.sems[1].at[s]).wait()

    def drain(self):
        for j in range(8):

            @pl.when(jnp.logical_not(self.same(j)))
            def _():
                self.away(j).wait_send()

    def finish(self):
        for s in range(8):
            self.arrive(s)
        self.drain()


def group_peers():
    x, y_lo, core = lax.axis_index("x"), lax.axis_index("y_lo"), lax.axis_index("core")
    found = []
    for k in range(1, 16):
        dx, dy, dc = k // 4, k // 2 % 2, k % 2
        found.append((k, {"x": lax.rem(x + dx, 4), "y_lo": 1 - y_lo if dy else y_lo, "core": 1 - core if dc else core}))
    return found


class SpreadGateUp(Side):
    def __init__(self, pieces, first, into=None):
        self.r, self.first = pieces.shape[1], first
        dma = pltpu.SemaphoreType.DMA
        self.operands = [pieces]
        self.shapes = [jax.ShapeDtypeStruct((2, FF, 128), BF)]
        self.scratch = [dma((56,)), dma((56,)), dma((8,))]

    def bind(self, ring, ins, outs, scratch):
        (got,), (out,) = ins, outs
        self.s = []
        for s in range(8):

            def slot(c, s=s):
                rows = ((s // 2) * 4 + lax.rem(c // 2, 2) * 2 + s % 2) * 352 + lax.rem(c, 2) * 176 + self.first
                return out.at[c // 4, pl.ds(pl.multiple_of(rows, 16), self.r)]

            self.s.append(Spread(got.at[s], slot, scratch[:2], s * 7, s % 3 == 0, scratch[2].at[s]))

    def start(self):
        for s in self.s:
            s.start()

    def middle(self):
        for s in self.s:
            if s.y_first:
                s.relay()
        for s in self.s:
            if not s.y_first:
                s.relay()

    def finish(self):
        for s in self.s:
            s.finish()


def back_norm(v, grad, u):
    r = norm_scale(v)
    n = v * r
    return grad + r * (u - n * jnp.mean(u * n, axis=1, keepdims=True))


def y_partners():
    y_hi, y_lo = lax.axis_index("y_hi"), lax.axis_index("y_lo")
    return {"y_lo": 1 - y_lo}, {"y_hi": 1 - y_hi, "y_lo": 1 - y_lo}


def group_lanes(x, y_lo):
    return pl.ds(pl.multiple_of(x * 512 + y_lo * 256, 256), 256)


def tp_peers(ring):
    found = []
    for k in range(1, 8):
        dx, dc = k // 2, k % 2
        core = 1 - ring.core if dc else ring.core
        found.append((k, lax.rem(ring.x + dx, 4), core))
    return found


def ctx_peer(c, k):
    other = lax.rem(c + k, 8)
    return {"y_hi": other // 4, "z": lax.rem(other, 4)}


def nt(a, b):
    return dot(a, b, 1, 1)


def nn(a, b):
    return dot(a, b, 1, 0)


def key_bias(meta_ref, d, c, bias):
    docs = meta_ref[d].astype(F32)
    query_docs = meta_ref[d, pl.ds(c, 1), :].astype(F32)
    lane = lax.broadcasted_iota(jnp.int32, (128, 128), 1)
    row = lax.broadcasted_iota(jnp.int32, (128, 128), 0)

    def position(owner, i):
        return jnp.where(i < 64, owner * 64 + i, (15 - owner) * 64 + i - 64)

    query_pos = position(c, lane)
    for b in range(8):
        key_docs = jnp.broadcast_to(docs[b : b + 1, :], (128, 128)).T
        good = (query_pos >= position(b, row)) & (key_docs == query_docs)
        bias[pl.ds(b * 128, 128), :] = jnp.where(good, 0.0, NEGATIVE)


def eye():
    return (lax.broadcasted_iota(jnp.int32, (128, 128), 0) == lax.broadcasted_iota(jnp.int32, (128, 128), 1)).astype(BF)


def front_kernel(
    x_ref, meta_ref, g1_ref, g2_ref, wq_ref, wk_ref, wv_ref, wg_ref, wu_ref, wo_ref, wdn_ref, tab_ref,
    a_ref, lse_ref, metas_ref, n1_out, wqkv_out, qp_out, kv_out, wos_ref, wgu_ref, wd_ref,
    n1, wqkv, w, wt, qkv, qp, kv, bias, probs,
    ag_s, ag_r, meta_s, meta_r, w_s, w_r, y_s, y_r, gu_s, gu_r, wd_s, wd_r, kv_s, kv_r, fw_s, fw_r, loc,
):
    ring = Ring()
    y_lo = lax.axis_index("y_lo")
    c, _ = ctx_at(0)
    near, other = y_partners()
    peers = tp_peers(ring)
    meet([{"x": x, "core": core} for _, x, core in peers] + [near, other] + [ctx_at(k)[1] for k in range(1, 8)])
    here = ring.x * 2 + ring.core
    copies, local = [], []

    def copy_here(src, dst):
        copy = pltpu.make_async_copy(src, dst, loc.at[len(local)])
        copy.start()
        local.append(copy)

    ag = Ag(ring, n1, (ag_s, ag_r))

    def normed(k, _):
        rows = pl.ds(pl.multiple_of(k * 16, 16), 16)
        v = x_ref[rows, :].astype(F32)
        n1[here, rows, :] = (v * norm_scale(v)).astype(BF)
        return 0

    lax.fori_loop(0, 4, normed, 0)
    ag.begin(0)
    for k, x, core in peers:
        copies.append(send(meta_ref, metas_ref.at[here], (meta_s, meta_r), k, {"x": x, "core": core}))
    metas_ref[here] = meta_ref[...]

    one_matrix = eye()
    g1, g2 = g1_ref[...], g2_ref[...]

    def turned(ref, gain, k):
        return (nt(one_matrix, ref[:, lanes_at(k * 128, 128)]) * gain).astype(BF)

    for f in range(16):
        w[(f // 4) * 2 + f % 2, pl.ds((f // 2 % 2) * 128, 128), :] = turned(wq_ref, g1, f)
    for ref, at in ((wk_ref, 256), (wv_ref, 320)):
        for k in range(2):
            tile = turned(ref, g1, k)
            for x in (2 * k, 2 * k + 1):
                part = tile[(x % 2) * 64 : (x % 2) * 64 + 64]
                w[2 * x, pl.ds(at, 64), :] = part
                w[2 * x + 1, pl.ds(at, 64), :] = part
    lanes = lanes_at((ring.x * 4 + y_lo * 2 + ring.core) * 128, 128)
    wcopies = {}
    for k, x, core in peers:
        wcopies[k] = send(w.at[x * 2 + core], wqkv.at[:, lanes], (w_s, w_r), k, {"x": x, "core": core})
    wqkv[:, lanes] = w[here]
    lax.fori_loop(4, 8, normed, 0)
    ag.begin(1)

    copy_here(wo_ref, wos_ref.at[y_lo])
    copy_here(wdn_ref, wd_ref.at[pl.ds(pl.multiple_of(y_lo * 352, 32), 352)])
    for half, device in enumerate((near, other)):
        copies.append(send(wo_ref.at[HALVES[half]], wos_ref.at[y_lo, HALVES[half]], (y_s, y_r), 4 + half, device))

    def turn_all(ref, i):
        def body(k, _):
            wt[i, pl.ds(pl.multiple_of(k * 128, 128), 128), :] = turned(ref, g2, k)
            return 0

        lax.fori_loop(0, FF // 128, body, 0)

    turn_all(wg_ref, 0)
    for dx in range(4):
        x = lax.rem(ring.x + 4 - dx, 4)
        if dx > 0:
            wcopies[2 * dx].wait_recv()
        wcopies[2 * dx + 1].wait_recv()
        block = wqkv.at[:, group_lanes(x, y_lo)]
        copies.append(send(block, block, (y_s, y_r), dx, (near, other)[dx // 2]))
    for half, device in enumerate((near, other)):
        rows = pl.ds(pl.multiple_of(y_lo * 352 + half * 176, 16), 176)
        copies.append(send(wdn_ref.at[pl.ds(half * 176, 176)], wd_ref.at[rows], (wd_s, wd_r), half, device))
    ag.near()
    turn_all(wu_ref, 1)
    ag.far()

    for j in range(2):
        rows = pl.ds(pl.multiple_of((ring.x * 4 + 2 * j + ring.core) * 352, 32), 352)
        copy_here(wt.at[:, rows], wgu_ref.at[:, j, :, lanes])
    for k, x, core in peers:
        for j in range(2):
            rows = pl.ds(pl.multiple_of((x * 4 + 2 * j + core) * 352, 32), 352)
            copies.append(
                send(wt.at[:, rows], wgu_ref.at[:, j, :, lanes], (gu_s, gu_r), k * 2 + j, {"x": x, "core": core})
            )

    ag.have(*range(6, 14))
    for copy in copies[9:13]:
        copy.wait_recv()
    qkv[...] = nt(n1[...].reshape(1024, D), wqkv[...])
    copy_here(n1, n1_out)
    copy_here(wqkv, wqkv_out)

    lane = lax.broadcasted_iota(jnp.int32, (128, 128), 1)

    def rope(u, i):
        return u * tab_ref[i] + pltpu.roll(u, 96, 1) * tab_ref[i + 1] + pltpu.roll(u, 32, 1) * tab_ref[i + 2]

    for d in range(8):
        kv[d % 2, d // 2, c] = rope(qkv[pl.ds(d * 128, 128), 256:384], 3).astype(BF)
    spreads = [
        Spread(kv.at[ring.core, x, c], lambda i, x=x: kv.at[ring.core, x, i], (kv_s, kv_r), x * 7, x < 2, None) for x in range(4)
    ]
    for s in spreads:
        s.start()

    def turn_queries(d, _):
        for j in range(2):
            u = rope(qkv[pl.ds(pl.multiple_of(d * 128, 128), 128), pl.ds(j * 128, 128)], 0) * 0.125
            qp[d, pl.ds(j * 256, 128), :] = jnp.where(lane < 64, u, 0.0).astype(BF)
            qp[d, pl.ds(j * 256 + 128, 128), :] = jnp.where(lane < 64, pltpu.roll(u, 64, 1), 0.0).astype(BF)
        return 0

    lax.fori_loop(0, 8, turn_queries, 0)
    copy_here(qp, qp_out)

    forwards = []

    def pass_on(k):
        back = ctx_at(k if k == 4 else k // 4 * 4 + (4 - k % 4))[0]
        block = kv.at[ring.core, :, back]
        forwards.append(send(block, block, (fw_s, fw_r), k - 1, ring.sibling))

    for k in (1, 4, 3, 2):
        for s in spreads:
            s.first(k).wait_recv()
            if k < 4 and not s.y_first:
                s.second(k).start()
            if k == 4 and s.y_first:
                for dz in (1, 3, 2):
                    s.second(dz).start()
        pass_on(k)
    for dz in (1, 3, 2):
        for s in spreads:
            s.second(dz).wait_recv()
        pass_on(4 + dz)
    for copy in forwards:
        copy.wait_recv()
    copy_here(kv, kv_out)
    for copy in copies[:7]:
        copy.wait_recv()

    def one(d, _):
        key_bias(metas_ref, d, c, bias)
        keys = kv[lax.rem(d, 2), d // 2].reshape(1024, 128)
        scores = nt(keys, qp[d])
        for h in range(4):
            s = scores[:, h * 128 : (h + 1) * 128] + bias[...]
            top = jnp.max(s, axis=0, keepdims=True)
            e = jnp.exp(s - top)
            total = jnp.sum(e, axis=0, keepdims=True)
            probs[:, h * 128 : (h + 1) * 128] = (e * (1.0 / total)).astype(BF)
            lse_ref[d, :, h * 128 : (h + 1) * 128] = jnp.broadcast_to(top + jnp.log(total), (8, 128))
        mixed = nn(keys.T, probs[...])
        for j in range(2):
            two = jnp.concatenate([mixed[64:, (2 * j) * 128 : (2 * j + 1) * 128], mixed[64:, (2 * j + 1) * 128 : (2 * j + 2) * 128]], axis=0)
            a_ref[pl.ds(pl.multiple_of(d * 128, 128), 128), pl.ds(j * 128, 128)] = two.T.astype(BF)
        return 0

    lax.fori_loop(0, 8, one, 0)

    ag.drain()
    for k in range(1, 8):
        wcopies[k].wait_send()
    for s in spreads:
        for k in range(1, 5):
            s.first(k).wait_send()
        for dz in (1, 3, 2):
            s.second(dz).wait_send()
    for copy in forwards:
        copy.wait_send()
    for i, copy in enumerate(copies):
        copy.wait_send()
        if i >= 7 and not 9 <= i < 13:
            copy.wait_recv()
    for copy in local:
        copy.wait()


def front(hidden_in, meta, g1, g2, w_query, w_key, w_value, w_gate, w_up, w_out, w_down, tabs):
    dma = pltpu.SemaphoreType.DMA
    pair = lambda n: [dma((n,)), dma((n,))]
    out = lambda *shape: jax.ShapeDtypeStruct(shape, BF)
    return pl.pallas_call(
        front_kernel,
        out_shape=[
            out(1024, 256), jax.ShapeDtypeStruct((8, 8, 512), F32), jax.ShapeDtypeStruct((8, 16, 128), jnp.int32),
            out(8, 128, D), out(384, D), out(8, 512, 128), out(2, 4, 8, 128, 128), out(2, 128, D), out(2, 2, 352, D), out(704, D),
        ],
        in_specs=[VM] * 12,
        out_specs=[VM] * 3 + [HB] * 7,
        scratch_shapes=[
            pltpu.VMEM((8, 128, D), BF), pltpu.VMEM((384, D), BF), pltpu.VMEM((8, 384, 128), BF), pltpu.VMEM((2, FF, 128), BF),
            pltpu.VMEM((1024, 384), F32), pltpu.VMEM((8, 512, 128), BF), pltpu.VMEM((2, 4, 8, 128, 128), BF),
            pltpu.VMEM((1024, 128), F32), pltpu.VMEM((1024, 512), BF),
            *pair(14), *pair(8), *pair(8), *pair(6), *pair(16), *pair(2), *pair(28), *pair(7), dma((8,)),
        ],
        compiler_params=params(5),
        name="front",
    )(hidden_in, meta, g1, g2, w_query, w_key, w_value, w_gate, w_up, w_out, w_down, tabs)


def everyone():
    return [device for _, device in group_peers()] + [ctx_at(k)[1] for k in range(1, 8)] + [y_partners()[1]]


def rope_tables(c):
    cos, sin = tables(positions_of(c))
    low = jnp.arange(HD) < HD // 2
    to_low, to_high = jnp.where(low, -sin, 0.0), jnp.where(low, 0.0, sin)
    one, zero = jnp.ones_like(cos), jnp.zeros_like(cos)
    pairs = [(cos, cos), (to_low, to_low), (to_high, to_high), (cos, one), (to_low, zero), (to_high, zero)]
    return jnp.stack([jnp.concatenate(p, axis=1) for p in pairs])


def tail_kernel(
    sides, qp_ref, kv_ref, lse_ref, meta_ref, tab_ref, da_ref, x_ref, dy1_ref, stats_ref,
    wqkv_hbm, n1_hbm, ggu2_hbm, gout_hbm, piece_down_ref, piece_gu1_ref,
    grad_ref, info_ref, all_down, all_out, all_qkv, all_gu,
    bias, dap, ds, pb, mine, theirs, stage, back, dqkv, dqkv_t, parts, held, got, n1, wqkv, gq,
    piece_gu2, piece_out, piece_qkv, got_gu1, got_gu2, got_qkv, st1, st2, mid,
    co_s, co_r, kv_s, kv_r, rs_s, rs_r, st_s, st_r, st2_s, st2_r, qs_s, qs_r, loc, *side_scratch,
):
    ring = Ring()
    c, _ = ctx_at(0)
    sum_gu2, sum_out, move_gu1, down, out, spread_gu1, move_gu2, sum_qkv, move_qkv, spread_gu2 = sides
    scratch = list(side_scratch)
    places = (
        (ggu2_hbm, piece_gu2), (gout_hbm, piece_out), (piece_gu1_ref, got_gu1), (piece_down_ref, all_down), (piece_out, all_out),
        (got_gu1, all_gu), (piece_gu2, got_gu2), (gq, piece_qkv), (piece_qkv, got_qkv), (got_gu2, all_gu),
    )
    for side, (i, o) in zip(sides, places):
        side.bind(ring, (i,), (o,), scratch[: len(side.scratch)])
        del scratch[: len(side.scratch)]
    loads = [pltpu.make_async_copy(n1_hbm, n1, loc.at[0]), pltpu.make_async_copy(wqkv_hbm, wqkv, loc.at[1])]
    for load in loads:
        load.start()
    meet(everyone())
    sum_gu2.start()
    sum_out.start()
    move_gu1.start()
    group = group_peers()
    here16 = ring.x * 4 + lax.axis_index("y_lo") * 2 + ring.core
    copies = [send(stats_ref, st1.at[here16], (st_s, st_r), k, device) for k, device in group]
    st1[here16] = stats_ref[...]
    lane = lax.broadcasted_iota(jnp.int32, (128, 128), 1)

    def unrope(u, i):
        return u * tab_ref[i] - pltpu.roll(u, 96, 1) * tab_ref[i + 1] - pltpu.roll(u, 32, 1) * tab_ref[i + 2]

    def one(x, core):
        d = x * 2 + core
        rows = pl.ds(pl.multiple_of(d * 128, 128), 128)
        key_bias(meta_ref, d, c, bias)
        for j in range(2):
            tile = da_ref[rows, pl.ds(j * 128, 128)].astype(F32)
            dap[pl.ds(j * 256, 128), :] = jnp.where(lane >= 64, pltpu.roll(tile, 64, 1), 0.0).astype(BF)
            dap[pl.ds(j * 256 + 128, 128), :] = jnp.where(lane >= 64, tile, 0.0).astype(BF)
        kv = kv_ref[core, x].reshape(1024, 128)
        scores = nt(kv, qp_ref[d])
        dprobs = nt(kv, dap[...])
        for h in range(4):
            cols = slice(h * 128, (h + 1) * 128)
            p = jnp.exp(scores[:, cols] + bias[...] - lse_ref[d, 0:1, cols])
            pb[:, cols] = p.astype(BF)
            dp = dprobs[:, cols]
            centre = jnp.sum(p * dp, axis=0, keepdims=True)
            ds[:, cols] = (p * (dp - centre)).astype(BF)
        dkv = nn(ds[...], qp_ref[d]) + nn(pb[...], dap[...])
        dq = nn(kv.T, ds[...]) * 0.125
        for j in range(2):
            two = jnp.concatenate([dq[:64, (2 * j) * 128 : (2 * j + 1) * 128], dq[:64, (2 * j + 1) * 128 : (2 * j + 2) * 128]], axis=0)
            dqkv[rows, pl.ds(j * 128, 128)] = unrope(two.T, 0).astype(BF)
        return dkv

    def core_copy(x):
        return pltpu.make_async_remote_copy(
            src_ref=mine.at[x], dst_ref=theirs.at[x], send_sem=co_s.at[x], recv_sem=co_r.at[x],
            device_id=ring.sibling, device_id_type=MESH,
        )

    def kv_copy(x, k):
        other, device = ctx_at(k)
        return pltpu.make_async_remote_copy(
            src_ref=stage.at[x, other], dst_ref=back.at[x, k - 1], send_sem=kv_s.at[x * 7 + k - 1],
            recv_sem=kv_r.at[x * 7 + k - 1], device_id=device, device_id_type=MESH,
        )

    def to_sibling(x, _):
        mine[x] = one(x, 1 - ring.core).astype(BF).reshape(8, 128, 128)
        core_copy(x).start()
        dqkv[pl.ds(pl.multiple_of((x * 2 + 1 - ring.core) * 128, 128), 128), 256:384] = jnp.zeros((128, 128), BF)
        return 0

    lax.fori_loop(0, 4, to_sibling, 0)
    down.start()
    for copy in copies:
        copy.wait_recv()
    total = st1[0]
    for i in range(1, 16):
        total += st1[i]
    mid[...] = total
    st2[c] = total
    copies2 = [send(mid, st2.at[c], (st2_s, st2_r), k - 1, ctx_at(k)[1]) for k in range(1, 8)]

    def to_owners(x, _):
        dkv = one(x, ring.core)
        core_copy(x).wait_recv()
        stage[x] = (dkv + theirs[x].reshape(1024, 128).astype(F32)).astype(BF).reshape(8, 128, 128)
        for k in range(1, 8):
            kv_copy(x, k).start()
        return 0

    lax.fori_loop(0, 4, to_owners, 0)
    sum_gu2.middle()
    sum_out.middle()
    move_gu1.finish()
    down.middle()

    def gather_up(x, _):
        total = stage[x, c].astype(F32)
        for k in range(1, 8):
            kv_copy(x, k).wait_recv()
            total += back[x, k - 1].astype(F32)
        rows = pl.ds(pl.multiple_of((x * 2 + ring.core) * 128, 128), 128)
        dqkv[rows, 256:384] = unrope(total, 3).astype(BF)
        return 0

    lax.fori_loop(0, 4, gather_up, 0)
    spread_gu1.start()
    for load in loads:
        load.wait()

    rs = Rs(ring, parts, held, got, (rs_s, rs_r))
    for i in range(4):
        x = rs.blocks[i]

        def body(k, _, x=x):
            lanes = lanes_at(k * 512, 512)
            block = nn(dqkv[pl.ds(pl.multiple_of(x * 256, 256), 256), :], wqkv[:, lanes])
            parts[pl.ds(x * 2, 2), :, lanes] = block.astype(BF).reshape(2, 128, 512)
            return 0

        lax.fori_loop(0, 4, body, 0)
        rs.copy(i).start()
        if i == 1:
            rs.send_far()
        elif i == 2:
            rs.send_right()
        elif i == 3:
            rs.send_left()
    dqkv_t[...] = dqkv[...].T

    def grads(k, _):
        lanes = lanes_at(k * 512, 512)
        product = nn(dqkv_t[...], n1[:, :, lanes].reshape(1024, 512))
        gq[:, :, :, lanes] = product.astype(BF).reshape(2, 4, 48, 512)
        return 0

    lax.fori_loop(0, 4, grads, 0)
    sum_qkv.start()
    rs.relay()
    sum_gu2.finish()
    move_gu2.start()
    sum_out.finish()
    out.start()
    spread_gu1.middle()
    for half in range(2):
        rs.ready(half)

        def body(k, _, half=half):
            rows = pl.ds(half * 64 + k * 16, 16)
            grad_ref[rows, :] = back_norm(x_ref[rows, :].astype(F32), dy1_ref[rows, :], rs.total(rows))
            return 0

        lax.fori_loop(0, 4, body, 0)
    move_gu2.finish()
    spread_gu2.start()
    out.middle()
    sum_qkv.middle()
    sum_qkv.finish()
    move_qkv.start()
    spread_gu2.middle()
    move_qkv.finish()
    spread_qkv = Spread(got_qkv, lambda c: all_qkv.at[:, c], (qs_s, qs_r), 0, False, loc.at[2])
    spread_qkv.start()

    for copy in copies2:
        copy.wait_recv()
    total = st2[0]
    for i in range(1, 8):
        total += st2[i]
    sums = jnp.sum(total, axis=1, keepdims=True)
    squares, count = sums[0:1], sums[1:2]
    scale = 2.0 / (D * count)
    info_ref[...] = jnp.concatenate([squares / count, scale, jnp.zeros((6, 1), F32)], axis=0) + jnp.zeros((8, 128), F32)

    spread_qkv.relay()
    rs.drain()
    for copy in copies + copies2:
        copy.wait_send()

    def drain(x, _):
        core_copy(x).wait_send()
        for k in range(1, 8):
            kv_copy(x, k).wait_send()
        return 0

    lax.fori_loop(0, 4, drain, 0)
    down.finish()
    out.finish()
    spread_gu1.finish()
    spread_gu2.finish()
    spread_qkv.finish()


def tail(qp, kv, lse, metas, tabs, da, hidden_in, dy1, stats, wqkv, n1, grad_gu2, grad_out, piece_down, piece_gu1):
    dma = pltpu.SemaphoreType.DMA
    pair = lambda n: [dma((n,)), dma((n,))]
    bf = lambda *shape: jax.ShapeDtypeStruct(shape, BF)
    vm = lambda *shape: pltpu.VMEM(shape, BF)
    sides = [
        SumColumns(grad_gu2), SumRows(grad_out), Move(piece_gu1), SpreadRows(piece_down), SpreadRows(bf(2, 128, 128)),
        SpreadGateUp(bf(8, 96, 128), 0), Move(bf(80, 1024)), SumColumns(bf(2, 4, 48, D), True), Move(bf(48, 1024)),
        SpreadGateUp(bf(8, 80, 128), 96),
    ]
    return pl.pallas_call(
        functools.partial(tail_kernel, sides),
        out_shape=[
            jax.ShapeDtypeStruct((128, D), F32), jax.ShapeDtypeStruct((8, 128), F32),
            bf(352, D), bf(128, D), bf(8, 8, 48, 128), bf(2, FF, 128),
        ],
        in_specs=[VM] * 9 + [HB] * 4 + [VM] * 2,
        out_specs=[VM] * 5 + [HB],
        scratch_shapes=[
            pltpu.VMEM((1024, 128), F32), vm(512, 128), vm(1024, 512), vm(1024, 512),
            vm(4, 8, 128, 128), vm(4, 8, 128, 128), vm(4, 8, 128, 128), vm(4, 7, 128, 128),
            vm(1024, 384), vm(384, 1024), vm(8, 128, D), vm(3, 128, D), vm(7, 128, D), vm(8, 128, D), vm(384, D), vm(2, 4, 48, D),
            vm(80, 1024), vm(2, 128, 128), vm(48, 1024), vm(8, 96, 128), vm(8, 80, 128), vm(8, 48, 128),
            pltpu.VMEM((16, 8, 128), F32), pltpu.VMEM((8, 8, 128), F32), pltpu.VMEM((8, 128), F32),
            *pair(4), *pair(28), *pair(10), *pair(16), *pair(7), *pair(7), dma((3,)),
            *[s for side in sides for s in side.scratch],
        ],
        compiler_params=params(7),
        name="tail",
    )(qp, kv, lse, metas, tabs, da, hidden_in, dy1, stats, wqkv, n1, grad_gu2, grad_out, piece_down, piece_gu1)


def finish_kernel(
    info_ref, gu_ref, g1_ref, g2_ref, wg_ref, wu_ref, down_ref, qkv_ref, wq_ref, wk_ref, wv_ref, out_ref, gin_ref,
    gate_ref, up_ref, down_out, q_ref, k_ref, v_ref, o_ref, input_ref, gain1_ref, gain2_ref,
    total2,
):
    scale = info_ref[1:2, 0:1]
    s1, s2 = g1_ref[...] * scale, g2_ref[...] * scale
    one_matrix = eye()
    step = pl.program_id(0)

    @pl.when(step == 0)
    def _():
        total2[...] = jnp.zeros_like(total2)
        total = jnp.zeros((128, 128), F32)
        for s in range(8):
            for j in range(2):
                f = (s // 2) * 4 + j * 2 + s % 2
                part = nt(one_matrix, qkv_ref[s, j * 128 : (j + 1) * 128])
                total += part * wq_ref[:, f * 128 : (f + 1) * 128].astype(F32)
                q_ref[:, f * 128 : (f + 1) * 128] = part * s1
        for i in range(2):
            both = [qkv_ref[2 * x, 256:].astype(F32) + qkv_ref[2 * x + 1, 256:].astype(F32) for x in (2 * i, 2 * i + 1)]
            for at, w_ref, g_ref in ((0, wk_ref, k_ref), (64, wv_ref, v_ref)):
                part = jnp.concatenate([both[0][at : at + 64], both[1][at : at + 64]], axis=0).T
                total += part * w_ref[:, i * 128 : (i + 1) * 128].astype(F32)
                g_ref[:, i * 128 : (i + 1) * 128] = part * s1
        gain1_ref[...] = jnp.sum(total.T, axis=0, keepdims=True) * scale
        o_ref[...] = out_ref[...].astype(F32) * scale
        input_ref[...] = gin_ref[...] * scale

    total = total2[...]
    for i, w_ref, g_ref in ((0, wg_ref, gate_ref), (1, wu_ref, up_ref)):
        turned = nt(one_matrix, gu_ref[i])
        g_ref[...] = turned * s2
        weighed = turned * w_ref[...].astype(F32)
        for k in range(4):
            total += weighed[:, k * 128 : (k + 1) * 128]
    total2[...] = total
    down_out[...] = down_ref[...].astype(F32) * scale

    @pl.when(step == pl.num_programs(0) - 1)
    def _():
        gain2_ref[...] = jnp.sum(total2[...].T, axis=0, keepdims=True) * scale


def finish(info, all_gu, g1, g2, w_gate, w_up, down, all_qkv, w_query, w_key, w_value, out, grad_in):
    wide = pl.BlockSpec((128, 512), lambda i: (0, i))
    rows = pl.BlockSpec((32, D), lambda i: (i, 0))
    whole = lambda *shape: pl.BlockSpec(shape, lambda i: (0,) * len(shape))
    f32 = lambda *shape: jax.ShapeDtypeStruct(shape, F32)
    return pl.pallas_call(
        finish_kernel,
        grid=(11,),
        out_shape=[
            f32(128, FF), f32(128, FF), f32(352, D), f32(128, D), f32(128, KVD), f32(128, KVD), f32(128, D), f32(128, D),
            f32(1, 128), f32(1, 128),
        ],
        in_specs=[
            whole(8, 128), pl.BlockSpec((2, 512, 128), lambda i: (0, i, 0)), whole(128, 1), whole(128, 1), wide, wide, rows,
            whole(8, 384, 128), whole(128, D), whole(128, KVD), whole(128, KVD), whole(128, D), whole(128, D),
        ],
        out_specs=[
            wide, wide, rows, whole(128, D), whole(128, KVD), whole(128, KVD), whole(128, D), whole(128, D),
            whole(1, 128), whole(1, 128),
        ],
        scratch_shapes=[pltpu.VMEM((128, 128), F32)],
        compiler_params=pltpu.CompilerParams(vmem_limit_bytes=48 * 2**20),
        name="finish",
    )(info, all_gu, g1, g2, w_gate, w_up, down, all_qkv, w_query, w_key, w_value, out, grad_in)


def local(hidden_in, teacher, doc_ids, valid_mask, norm1_gain, w_query, w_key, w_value, w_out, norm2_gain, w_gate, w_up, w_down):
    c = lax.axis_index(("y_hi", "z"))
    g1 = norm1_gain.astype(F32)
    g2 = norm2_gain.astype(F32)
    valid = valid_mask.astype(F32)
    tabs = rope_tables(c)
    blocks = doc_ids.reshape(16, 64)
    key_docs = jnp.concatenate([blocks[:8], blocks[:7:-1]], axis=1)
    meta = jnp.concatenate([key_docs, valid_mask[None], jnp.zeros((7, 128), jnp.int32)], axis=0)

    a, lse, metas, n1, wqkv, qp, kv, wo, wgu, wd = front(
        hidden_in, meta, g1[None], g2[None], w_query, w_key, w_value, w_gate, w_up, w_out, w_down, tabs
    )
    wo = wo.reshape(256, D)
    layer_out, loss_rows, dy1, da, grad_out, grad_gu2, piece_down, piece_gu1 = middle(
        a, wo, hidden_in, teacher, valid[:, None], wgu, wd
    )
    stats = jnp.concatenate([loss_rows.reshape(1, 128), valid[None], jnp.zeros((6, 128), F32)], axis=0)
    grad_in, info, all_down, all_out, all_qkv, all_gu = tail(
        qp, kv, lse, metas, tabs, da, hidden_in, dy1, stats, wqkv, n1, grad_gu2, grad_out, piece_down, piece_gu1
    )
    gg, gp, gd, gq, gk, gv, go, input_grad, gain1, gain2 = finish(
        info, all_gu, g1[:, None], g2[:, None], w_gate, w_up, all_down, all_qkv.reshape(8, 384, 128),
        w_query, w_key, w_value, all_out, grad_in,
    )
    return (layer_out, info[0, 0], input_grad, gain1[0], gq, gk, gv, go, gain2[0], gg, gp, gd)


def solution(mesh):
    fine = Mesh(mesh.devices.reshape(2, 4, 4, 2, 2), AXES)
    rows = ("y_hi", "z", "x", "y_lo", "core")
    fs = ("x", "y_lo", "core")
    token, shard = P(rows, None), P(fs, None)
    return jax.shard_map(
        local,
        mesh=fine,
        in_specs=(token, token, shard, P(rows), P(fs), shard, shard, shard, shard, P(fs), shard, shard, shard),
        out_specs=(token, P(), token, P(fs), shard, shard, shard, shard, P(fs), shard, shard, shard),
        check_vma=False,
    )
```

time: 458 us -> 393 us (0.86)
  Pallas kernels: 444 us -> 376 us
  local copies, waits for them, and re-layouts: 5.29 us -> 10.4 us
    pallas_call x8 -> x4, Pallas kernels: 444 us -> 376 us  [the longest x1 168 us: middle(): pl.pallas_call(functools.partial(middle_kernel, *sides), out_shape=[jax.S...]
    unnamed x11 -> x31, local copies, waits for them, and re-layouts: 0.83 us -> 6.59 us
where the time goes in v5:
time: 393 us; the launch traced here: 392 us
  Pallas kernels  376 us (96%)
  local copies, waits for them, and re-layouts  10.4 us (3%)
  other arithmetic  4.95 us (1%)
    pallas_call x1, Pallas kernels, middle(): pl.pallas_call(functools.partial(middle_kernel, *sides), out_shape=[jax.S...  168 us
    pallas_call x1, Pallas kernels, tail(): pl.pallas_call(functools.partial(tail_kernel, sides), out_shape=[jax.Shap...  119 us
    pallas_call x1, Pallas kernels, front(): pl.pallas_call(front_kernel, out_shape=[out(1024, 256), jax.ShapeDtypeStr...  76.2 us
    pallas_call x1, Pallas kernels, finish(): pl.pallas_call(finish_kernel, grid=(11,), out_shape=[f32(128, FF), f32(12...  12.2 us

profile of v5, /device:TPU:1, one launch (start us, length us, event | category | flops | bytes accessed | tf_op | source)
XLA Modules:
  0.0 391.8 jit_solution(5702142367955966538)
XLA Ops:
  0.7 0.1 add_convert_fusion
  0.7 0.1 broadcast_multiply_fusion
  0.9 0.3 fusion.5
  1.2 0.1 fusion
  1.3 0.1 fusion.1
  1.4 0.1 fusion.2
  1.5 0.0 copy-start.11
  1.5 1.3 convert_bitcast_fusion.2
  2.8 0.7 slice_reduce_fusion.1
  3.5 0.1 slice.18
  3.6 0.1 slice.16
  3.7 0.1 pad.19.clone
  3.7 1.3 add_add_fusion.meta_ref
  5.1 76.2 %front.1 = (bf16[1024,256]{1,0:T(8,128)(2,1)}, f32[8,8,512]{2,1,0:T(8,128)}, s32[8,16,128]{2,1,0:T(8,128)}, bf16[8,128,2048]{2,1,0:T(8,128)(2,1)}, bf16[384,2048...) custom-call(bf16[128,2048]{1,0:T(8,128)(2,1)} %x_ref.5, ...), custom_call_target="tpu_custom_call" | custom-call | tf_op jit(solution)/shard_map/front/pallas_call | solution.py:1120
  81.3 0.7 copy.28.valid_ref
  82.0 168.3 %middle.1 = (bf16[128,2048]{1,0:T(8,128)(2,1)}, f32[128,1]{1,0:T(8,128)}, f32[128,2048]{1,0:T(8,128)}, bf16[1024,256]{1,0:T(8,128)(2,1)}, bf16[2,128,2048]{2,1,0...) custom-call(bf16[1024,256]{1,0:T(8,128)(2,1)} %get-tuple-element.46.a_ref, ...), custom_call_target="tpu_custom_call" | custom-call | tf_op jit(solution)/shard_map/middle/pallas_call | solution.py:483
  250.4 0.9 reduce.2
  251.3 0.1 pad.5.clone
  251.4 0.7 maximum_maximum_fusion.stats_ref
  252.1 0.0 copy-start.7
  252.1 119.0 %tail.1 = (f32[128,2048]{1,0:T(8,128)}, f32[8,128]{1,0:T(8,128)}, bf16[352,2048]{1,0:T(8,128)(2,1)}, bf16[128,2048]{1,0:T(8,128)(2,1)}, bf16[8,8,48,128]{3,2,1,0:T(8,128)(2,1)}, /*index=5*/bf16[2,5632,128]{2,1,0:T(8,128)(2,1)}) custom-call(bf16[8,512,128]{2,1,0:T(8,128)(2,1)} %get-tuple-element.51.qp_ref, ...), custom_call_target="tpu_custom_call" | custom-call | tf_op jit(solution)/shard_map/tail/pallas_call | solution.py:1363
  371.1 0.7 copy.29.g1_ref
  371.8 0.7 copy.30.g2_ref
  372.6 1.2 copy-done.3
  373.8 1.1 copy-done.4
  375.0 1.0 copy-done.5
  376.0 0.8 copy-done.8
  376.8 0.8 copy-done.9
  377.7 0.7 copy-done.10
  378.4 12.2 %finish.1 = (f32[128,5632]{1,0:T(8,128)}, f32[128,5632]{1,0:T(8,128)}, f32[352,2048]{1,0:T(8,128)}, f32[128,2048]{1,0:T(8,128)}, f32[128,256]{1,0:T(8,128)}, /*i...) custom-call(f32[8,128]{1,0:T(8,128)S(1)} %copy-done.10, ...), custom_call_target="tpu_custom_call" | custom-call | tf_op jit(solution)/shard_map/finish/pallas_call | solution.py:1435
  390.5 0.5 slice.19
  391.0 0.8 copy.37
  (30 shorter events, 0.1 us)
Async XLA Ops:
  1.5 3.6 copy-start.11
  5.1 76.2 %copy-start.13 = (s32[128]{0:T(128)S(1)}, s32[128]{0:T(128)}, u32[]{:S(2)}) copy-start(s32[128]{0:T(128)} %param.16) | copy-start | bytes 1540
  252.1 120.5 %copy-start = (bf16[128,5632]{1,0:T(8,128)(2,1)S(1)}, bf16[128,5632]{1,0:T(8,128)(2,1)}, u32[]{:S(2)}) copy-start(bf16[128,5632]{1,0:T(8,128)(2,1)} %wg_ref.3) | copy-start | bytes 4325380
  252.1 120.5 %copy-start.1 = (bf16[128,5632]{1,0:T(8,128)(2,1)S(1)}, bf16[128,5632]{1,0:T(8,128)(2,1)}, u32[]{:S(2)}) copy-start(bf16[128,5632]{1,0:T(8,128)(2,1)} %wu_ref.3) | copy-start | bytes 4325380
  252.1 120.5 %copy-start.2 = (bf16[128,2048]{1,0:T(8,128)(2,1)S(1)}, bf16[128,2048]{1,0:T(8,128)(2,1)}, u32[]{:S(2)}) copy-start(bf16[128,2048]{1,0:T(8,128)(2,1)} %wq_ref.3) | copy-start | bytes 1572868
  252.1 120.5 %copy-start.6 = (bf16[128,256]{1,0:T(8,128)(2,1)S(1)}, bf16[128,256]{1,0:T(8,128)(2,1)}, u32[]{:S(2)}) copy-start(bf16[128,256]{1,0:T(8,128)(2,1)} %wk_ref.3) | copy-start | bytes 196612
  252.1 120.5 %copy-start.7 = (bf16[128,256]{1,0:T(8,128)(2,1)S(1)}, bf16[128,256]{1,0:T(8,128)(2,1)}, u32[]{:S(2)}) copy-start(bf16[128,256]{1,0:T(8,128)(2,1)} %wv_ref.3) | copy-start | bytes 196612
  372.6 1.2 copy-start.3
  373.8 1.1 copy-start.4
  375.0 1.0 copy-start.5
  376.0 0.8 copy-start.8
  376.8 0.8 copy-start.9
  377.7 0.7 copy-start.10
  378.3 12.7 %copy-start.12 = (bf16[128,2048]{1,0:T(8,128)(2,1)S(1)}, bf16[128,2048]{1,0:T(8,128)(2,1)}, u32[]{:S(2)}) copy-start(bf16[128,2048]{1,0:T(8,128)(2,1)} %get-tuple-element.107) | copy-start | bytes 1572868

commit v6 on v5

--- a/solution.py
+++ b/solution.py
@@ -2,6 +2,7 @@
 
 import jax
 import jax.numpy as jnp
+import numpy as np
 from jax import lax
 from jax.experimental import pallas as pl
 from jax.experimental.pallas import tpu as pltpu
@@ -25,17 +26,28 @@
     return lax.dot_general(a, b, (((ca,), (cb,)), ((), ())), preferred_element_type=F32)
 
 
-def tables(positions):
-    indices = jnp.arange(HD // 2, dtype=jnp.int32).astype(F32)
-    frequency = THETA ** (-(indices * 2.0 / HD))
-    angles = positions.astype(F32)[:, None] * frequency[None, :]
-    angles = jnp.concatenate([angles, angles], axis=1)
-    return jnp.cos(angles), jnp.sin(angles)
-
-
-def positions_of(c):
-    t = jnp.arange(64, dtype=jnp.int32)
-    return jnp.concatenate([c * 64 + t, (15 - c) * 64 + t])
+def rope_angles():
+    frequency = np.float32(THETA) ** (-(np.arange(HD // 2, dtype=np.float32) * np.float32(2.0) / np.float32(HD)))
+    c, t = np.arange(8)[:, None], np.arange(64)[None]
+    positions = np.concatenate([c * 64 + t, (15 - c) * 64 + t], axis=1).astype(np.float32)
+    angles = (positions[:, :, None] * frequency).astype(np.float32).astype(np.float64)
+    angles = np.concatenate([angles] * 4, axis=2)
+    return np.stack([np.cos(angles), np.sin(angles)], axis=1).astype(np.float32)
+
+
+def fill_tables(angles, tab):
+    cos, sin = angles[0], angles[1]
+    lane = lax.broadcasted_iota(jnp.int32, (128, 128), 1)
+    low = lax.rem(lane, 64) < 32
+    to_low, to_high = jnp.where(low, -sin, 0.0), jnp.where(low, 0.0, sin)
+    tab[0], tab[1], tab[2] = cos, to_low, to_high
+    tab[3] = jnp.where(lane < 64, cos, 1.0)
+    tab[4] = jnp.where(lane < 64, to_low, 0.0)
+    tab[5] = jnp.where(lane < 64, to_high, 0.0)
+
+
+def column(row):
+    return jnp.broadcast_to(row, (128, 128)).T
 
 
 MESH = pl.DeviceIdType.MESH
@@ -82,35 +94,212 @@
         pass
 
 
-class Torus:
-    def __init__(self):
-        self.y_hi, self.y_lo, self.z = lax.axis_index("y_hi"), lax.axis_index("y_lo"), lax.axis_index("z")
-        self.y = self.y_hi * 2 + self.y_lo
-        self.ys = [(dy, lax.rem(self.y + dy, 4)) for dy in (1, 3, 2)]
-        self.zs = [(dz, lax.rem(self.z + dz, 4)) for dz in (1, 3, 2)]
-        self.peers = [self.y_device(y) for _, y in self.ys] + [{"z": z} for _, z in self.zs]
-
-    def y_device(self, y):
-        return {"y_hi": y // 2, "y_lo": lax.rem(y, 2)}
-
-
 def lanes_at(start, size):
     return pl.ds(pl.multiple_of(start, 128), size)
 
 
-def add_up(out, terms, lead, rows):
-    steps = rows // 16
-
-    def body(k, _):
-        i, r = k // steps, pl.ds(pl.multiple_of(lax.rem(k, steps) * 16, 16), 16)
-        total = None
-        for at in terms:
-            term = at(i, r).astype(F32)
-            total = term if total is None else total + term
-        out(i, r, total.astype(BF))
-        return 0
-
-    lax.fori_loop(0, lead * steps, body, 0)
+def other_of_pair(i):
+    return i + 1 - 2 * lax.rem(i, 2)
+
+
+class Stream:
+    def __init__(self, y_first, mirror, y_index, r, first, own, bufs, sems, base):
+        y_hi, y_lo, z = lax.axis_index("y_hi"), lax.axis_index("y_lo"), lax.axis_index("z")
+        y = y_hi * 2 + y_lo
+        self.r, self.own, self.sems, self.base = r, own, sems, base
+        self.b1, self.b2, self.b3, self.b4 = bufs
+        axes = []
+        for is_y, i in ((True, y), (False, z)) if y_first else ((False, z), (True, y)):
+            p, q = (other_of_pair(i), 3 - i) if mirror == 0 else (3 - i, other_of_pair(i))
+            beyond = 3 - p if mirror == 0 else other_of_pair(p)
+            devices = [{"y_hi": d // 2, "y_lo": lax.rem(d, 2)} if is_y else {"z": d} for d in (p, q)]
+            axes.append((i, p, q, beyond, devices))
+        (self.i, p, self.q, beyond, self.dev1), (i2, p2, q2, beyond2, self.dev2) = axes
+        index = (lambda v: v) if y_first else y_index
+        self.at_i, self.at_p, self.at_q, self.at_beyond = index(i2), index(p2), index(q2), index(beyond2)
+        self.views = [(view, (slot, *at)) for slot, d in ((1, beyond), (0, p)) for view, at in first(d)]
+
+    def copy(self, k, src, dst, device):
+        return pltpu.make_async_remote_copy(
+            src_ref=src, dst_ref=dst, send_sem=self.sems[0].at[self.base + k], recv_sem=self.sems[1].at[self.base + k],
+            device_id=device, device_id_type=MESH,
+        )
+
+    def copies(self, step):
+        if step == 1:
+            return [self.copy(k, view, self.b1.at[at], self.dev1[0]) for k, (view, at) in enumerate(self.views)]
+        if step == 2:
+            return [self.copy(8, self.b1.at[1], self.b2, self.dev1[1])]
+        if step == 3:
+            places = ((1, self.at_beyond), (0, self.at_p))
+            return [self.copy(9 + slot, self.b2.at[at], self.b3.at[slot], self.dev2[0]) for slot, at in places]
+        return [self.copy(11, self.b3.at[1], self.b4, self.dev2[1])]
+
+    def go(self, step):
+        for copy in self.copies(step):
+            copy.start()
+
+    def arrived(self, step):
+        for copy in self.copies(step):
+            copy.wait_recv()
+
+    def add(self, out, terms, lead):
+        def body(i, _):
+            total = None
+            for term in terms:
+                v = term(i).astype(F32)
+                total = v if total is None else total + v
+            out(i, total.astype(BF))
+            return 0
+
+        lax.fori_loop(0, lead, body, 0)
+
+    def step2(self):
+        self.arrived(1)
+        b1 = self.b1
+        for slot, d in ((1, self.q), (0, self.i)):
+
+            def put(j, v, slot=slot):
+                b1[slot, j, :, :] = v
+
+            self.add(put, [lambda j, d=d: self.own(d, j), lambda j, slot=slot: b1[slot, j, :, :]], 4)
+            if slot == 1:
+                self.go(2)
+
+    def step3(self):
+        self.arrived(2)
+        b1, b2 = self.b1, self.b2
+
+        def put(j, v):
+            b2[j, :, :] = v
+
+        self.add(put, [lambda j: b1[0, j, :, :], lambda j: b2[j, :, :]], 4)
+        self.go(3)
+
+    def step4(self):
+        self.arrived(3)
+        b2, b3 = self.b2, self.b3
+        for slot, place in ((1, self.at_q), (0, self.at_i)):
+
+            def put(j, v, slot=slot):
+                b3[slot, :, :] = v
+
+            self.add(
+                put,
+                [lambda j, p=place: b2[p, :, :], lambda j, slot=slot: b3[slot, :, :]],
+                1,
+            )
+            if slot == 1:
+                self.go(4)
+
+    def finish(self, out):
+        self.arrived(4)
+        b3, b4 = self.b3, self.b4
+        self.add(out, [lambda j: b3[0, :, :], lambda j: b4[:, :]], 1)
+        for step in (1, 2, 3, 4):
+            for copy in self.copies(step):
+                copy.wait_send()
+
+
+class TorusSum(Side):
+    def start(self):
+        for s in self.s:
+            s.go(1)
+
+    def step2(self):
+        for s in self.s:
+            s.step2()
+
+    def step3(self):
+        for s in self.s:
+            s.step3()
+
+    def step4(self):
+        for s in self.s:
+            s.step4()
+
+    def finish(self):
+        for s, out in zip(self.s, self.outs):
+            s.finish(out)
+
+    def bufs(self, scratch, i):
+        return [ref.at[i] for ref in scratch[:4]]
+
+
+class SumColumns(TorusSum):
+    def __init__(self, grads):
+        r = self.rows = grads.shape[2]
+        dma = pltpu.SemaphoreType.DMA
+        self.operands = [grads]
+        self.shapes = [jax.ShapeDtypeStruct((r, 1024), BF)]
+        self.scratch = [
+            pltpu.VMEM((4, 2, 4, r, 256), BF), pltpu.VMEM((4, 4, r, 256), BF), pltpu.VMEM((4, 2, r, 256), BF), pltpu.VMEM((4, r, 256), BF),
+            dma((48,)), dma((48,)),
+        ]
+
+    def bind(self, ring, ins, outs, scratch):
+        (g,), (out,) = ins, outs
+        self.s, self.outs = [], []
+        for i in range(4):
+            y_first, lane = i < 2, i * 256
+
+            def first(d, y_first=y_first, lane=lane):
+                if y_first:
+                    return [(g.at[d // 2, :, :, lanes_at(lax.rem(d, 2) * 1024 + lane, 256)], ())]
+                return [(g.at[:, d, :, pl.ds(yl * 1024 + lane, 256)], (pl.ds(yl * 2, 2),)) for yl in range(2)]
+
+            def own(d, j, y_first=y_first, lane=lane):
+                rows = slice(None)
+                if y_first:
+                    return g[d // 2, j, rows, lanes_at(lax.rem(d, 2) * 1024 + lane, 256)]
+                return g[lax.rem(j, 2), d, rows, lanes_at((j // 2) * 1024 + lane, 256)]
+
+            def put(j, v, lane=lane):
+                out[:, pl.ds(lane, 256)] = v
+
+            y_index = lambda y: lax.rem(y, 2) * 2 + y // 2
+            self.s.append(Stream(y_first, i % 2, y_index, self.rows, first, own, self.bufs(scratch, i), scratch[4:], i * 12))
+            self.outs.append(put)
+
+
+class SumRows(TorusSum):
+    def __init__(self, grads):
+        r = self.rows = grads.shape[1]
+        dma = pltpu.SemaphoreType.DMA
+        self.operands = [grads]
+        self.shapes = [jax.ShapeDtypeStruct((2, r, 128), BF)]
+        h = r // 2
+        self.scratch = [
+            pltpu.VMEM((4, 2, 4, h, 128), BF), pltpu.VMEM((4, 4, h, 128), BF), pltpu.VMEM((4, 2, h, 128), BF), pltpu.VMEM((4, h, 128), BF),
+            dma((48,)), dma((48,)),
+        ]
+
+    def bind(self, ring, ins, outs, scratch):
+        (g,), (out,) = ins, outs
+        self.s, self.outs = [], []
+        h = self.rows // 2
+        for i in range(4):
+            y_first, lane, row = i < 2, (i // 2) * 512, (i % 2) * h
+
+            def first(d, y_first=y_first, lane=lane, row=row):
+                half = pl.ds(row, h)
+                if y_first:
+                    return [
+                        (g.at[lax.rem(d, 2), half, lanes_at((d // 2) * 1024 + lane + z * 128, 128)], (z,)) for z in range(4)
+                    ]
+                return [(g.at[:, half, lanes_at(yh * 1024 + lane + d * 128, 128)], (pl.ds(yh * 2, 2),)) for yh in range(2)]
+
+            def own(d, j, y_first=y_first, lane=lane, row=row):
+                rows = pl.ds(row, h)
+                if y_first:
+                    return g[lax.rem(d, 2), rows, lanes_at((d // 2) * 1024 + lane + j * 128, 128)]
+                return g[lax.rem(j, 2), rows, lanes_at((j // 2) * 1024 + lane + d * 128, 128)]
+
+            def put(j, v, i=i, row=row):
+                out[i // 2, pl.ds(row, h), :] = v
+
+            self.s.append(Stream(y_first, i % 2, lambda y: y, h, first, own, self.bufs(scratch, i), scratch[4:], i * 12))
+            self.outs.append(put)
 
 
 class Ag:
@@ -137,8 +326,8 @@
         for i in ((0, 3, 6), (2, 1, 7))[half]:
             self.copy(i).start()
 
-    def near(self):
-        for got, onward in ((0, (4, 8)), (2, (5, 11)), (1, (9,)), (3, (10,))):
+    def near(self, steps=slice(None)):
+        for got, onward in ((0, (4, 8)), (2, (5, 11)), (1, (9,)), (3, (10,)))[steps]:
             self.copy(got).wait_recv()
             for i in onward:
                 self.copy(i).start()
@@ -252,8 +441,8 @@
 
 def middle_kernel(
     down_side, gu_side, a_ref, wo_ref, x_ref, valid_ref, wd_ref, teacher_hbm, half_w_ref,
-    out_ref, loss_ref, dy1_ref, da_ref, gout_ref, ggu_ref, piece_ref, gu_piece_ref,
-    w, n2, dyg, dag, parts, held, got, y1, gate, up, mid, mid_t, dup, dgu1, dgu2, gd, gu1, dmid,
+    out_ref, stats_ref, dy1_ref, da_ref, gout_ref, ggu_ref, piece_ref, gu_piece_ref,
+    w, n2, dyg, dag, parts, held, got, y1, gate, up, mid, mid_t, dup, dgu1, dgu2, gd, gu1, dmid, valid_col, loss_col,
     rs1_s, rs1_r, ag1_s, ag1_r, rs2_s, rs2_r, ag2_s, ag2_r, rs3_s, rs3_r, ag3_s, ag3_r, w_s, w_r, loc, *side_scratch,
 ):
     ring = Ring()
@@ -261,12 +450,13 @@
     near, other = y_partners()
     down_side.bind(ring, (gd,), (piece_ref,), side_scratch[: len(down_side.scratch)])
     gu_side.bind(ring, (gu1,), (gu_piece_ref,), side_scratch[len(down_side.scratch) :])
-    meet([ring.right, ring.left, ring.sibling] + Torus().peers)
+    meet([ring.right, ring.left, ring.sibling, near, other] + [{"z": p} for p in (other_of_pair(lax.axis_index("z")), 3 - lax.axis_index("z"))])
     here = ring.x * 2 + ring.core
     dy, dgate = dy1_ref, mid
     teacher = dag.at[here]
     teacher_copy = pltpu.make_async_copy(teacher_hbm, teacher, loc.at[4])
     teacher_copy.start()
+    valid_col[...] = column(valid_ref[...].astype(F32))
 
     wcopies = []
     for dx in range(4):
@@ -303,17 +493,20 @@
             lax.fori_loop(0, 4, body, 0)
             ag.begin(half)
 
-    def over_blocks(ag, rs, work):
+    def over_blocks(ag, rs, work, first=None, after=()):
         def step(i, _):
             at = functools.partial(jnp.equal, i)
 
             @pl.when(at(0))
             def _():
                 ag.have(6, 7)
+                if first is not None:
+                    ag.near(slice(2))
+                    first()
 
             @pl.when(at(1))
             def _():
-                ag.near()
+                ag.near(slice(2 if first is not None else 0, 4))
                 ag.have(8, 9)
 
             @pl.when(at(2))
@@ -333,6 +526,8 @@
             work(x)
             if rs is not None:
                 rs.swap(3 - i, x).start()
+            for k, then in enumerate(after):
+                pl.when(at(k + 1))(then)
             return 0
 
         lax.fori_loop(0, 4, step, 0)
@@ -358,8 +553,6 @@
 
     reduced(rs, op1, ag, n2)
     rs.drain()
-    for copy in wcopies:
-        copy.wait()
     teacher_copy.wait()
 
     rs = Rs(ring, parts, held, got, (rs2_s, rs2_r))
@@ -379,7 +572,11 @@
         put(x, lambda lanes: nn(mid[...], wd_ref[:, lanes]))
         mid_t[:, rows] = mid[...].T
 
-    over_blocks(ag, rs, forward)
+    def weights_here():
+        for copy in wcopies:
+            copy.wait()
+
+    over_blocks(ag, rs, forward, weights_here)
     rs.send_far()
     rs.relay()
     ag.drain()
@@ -388,14 +585,15 @@
         v = y1[rows, :] + total
         out_ref[rows, :] = v.astype(BF)
         miss = v - dag[here, rows, :].astype(F32)
-        valid = valid_ref[rows, :]
-        loss_ref[rows, :] = valid * jnp.mean(miss * miss, axis=1, keepdims=True)
+        valid = valid_col[rows, 0:1]
+        loss_col[rows, :] = jnp.broadcast_to(valid * jnp.mean(miss * miss, axis=1, keepdims=True), (16, 128))
         dy[rows, :] = valid * miss
         return valid * miss
 
     ag = Ag(ring, dyg, (ag2_s, ag2_r))
     reduced(rs, op2, ag, dyg)
     rs.drain()
+    stats_ref[...] = jnp.concatenate([loss_col[...].T[0:1], valid_ref[...].astype(F32), jnp.zeros((6, 128), F32)], axis=0)
 
     rs = Rs(ring, parts, held, got, (rs3_s, rs3_r))
 
@@ -460,9 +658,14 @@
         mid_t[0:256, rows] = a_ref[rows, :].T
         grad_gu(80, dgu2, ggu_ref, x)
 
-    over_blocks(ag, None, to_attention)
-    down_side.middle()
-    gu_side.middle()
+    def both(name):
+        def then():
+            getattr(down_side, name)()
+            getattr(gu_side, name)()
+
+        return then
+
+    over_blocks(ag, None, to_attention, after=(both("step2"), both("step3"), both("step4")))
 
     def grad_out(k, _):
         lanes = lanes_at(k * 512, 512)
@@ -479,11 +682,11 @@
     dma = pltpu.SemaphoreType.DMA
     pair = lambda n: [dma((n,)), dma((n,))]
     big = pltpu.VMEM((8, 128, D), BF)
-    sides = [SumRows(jax.ShapeDtypeStruct((2, 352, D), BF), True), SumColumns(jax.ShapeDtypeStruct((2, 4, 96, D), BF), True)]
+    sides = [SumRows(jax.ShapeDtypeStruct((2, 352, D), BF)), SumColumns(jax.ShapeDtypeStruct((2, 4, 96, D), BF))]
     return pl.pallas_call(
         functools.partial(middle_kernel, *sides),
         out_shape=[
-            jax.ShapeDtypeStruct((128, D), BF), jax.ShapeDtypeStruct((128, 1), F32), jax.ShapeDtypeStruct((128, D), F32),
+            jax.ShapeDtypeStruct((128, D), BF), jax.ShapeDtypeStruct((8, 128), F32), jax.ShapeDtypeStruct((128, D), F32),
             jax.ShapeDtypeStruct((1024, 256), BF), jax.ShapeDtypeStruct((2, 128, D), BF), jax.ShapeDtypeStruct((2, 4, 80, D), BF),
             *[s for side in sides for s in side.shapes],
         ],
@@ -495,184 +698,13 @@
             pltpu.VMEM((1024, 704), F32), pltpu.VMEM((1024, 704), F32),
             pltpu.VMEM((256, 704), BF), pltpu.VMEM((704, 1024), BF), pltpu.VMEM((256, 704), BF),
             pltpu.VMEM((768, 1024), BF), pltpu.VMEM((640, 1024), BF), pltpu.VMEM((2, 352, D), BF), pltpu.VMEM((2, 4, 96, D), BF),
-            pltpu.VMEM((256, 704), F32),
+            pltpu.VMEM((256, 704), F32), pltpu.VMEM((128, 128), F32), pltpu.VMEM((128, 128), F32),
             *pair(10), *pair(14), *pair(10), *pair(14), *pair(10), *pair(14), *pair(4), dma((5,)),
             *[s for side in sides for s in side.scratch],
         ],
         compiler_params=pltpu.CompilerParams(collective_id=1, has_side_effects=True, vmem_limit_bytes=63 * 2**20),
         name="middle",
     )(a, wo, x, valid, wd, teacher, half_w)
-
-
-class SumColumns(Side):
-    def __init__(self, grads, in_vmem=False):
-        r = self.rows = grads.shape[2]
-        dma = pltpu.SemaphoreType.DMA
-        self.first = 0 if in_vmem else 1
-        n = 3 + self.first
-        self.operands = [grads]
-        self.shapes = [jax.ShapeDtypeStruct((r, 1024), BF)]
-        self.scratch = [
-            pltpu.VMEM((n, 4, r, 512), BF), pltpu.VMEM((n, 2, 2, r, 512), BF),
-            pltpu.VMEM((3, r, 512), BF), pltpu.VMEM((3, r, 512), BF),
-            dma((9,)), dma((9,)), dma((6,)), dma((6,)), dma((3,)),
-        ]
-
-    def bind(self, ring, ins, outs, scratch):
-        (self.g,), (self.out,) = ins, outs
-        self.by, self.bz, self.by2, self.bz2, s1, r1, s2, r2, self.loc = scratch
-        self.one, self.two = (s1, r1), (s2, r2)
-        self.t = Torus()
-        self.peers = self.t.peers
-
-    def start(self):
-        t, g = self.t, self.g
-        self.c = []
-        for i, (dy, y) in enumerate(t.ys):
-            src = g.at[y // 2, :, :, lanes_at(lax.rem(y, 2) * 1024, 512)]
-            self.c.append(send(src, self.by.at[dy - 1 + self.first], self.one, i, t.y_device(y)))
-        for i, (dz, z) in enumerate(t.zs):
-            for yl in range(2):
-                src = g.at[:, z, :, pl.ds(yl * 1024 + 512, 512)]
-                self.c.append(send(src, self.bz.at[dz - 1 + self.first, yl], self.one, 3 + 2 * i + yl, {"z": z}))
-        self.l = []
-        if not self.first:
-            return
-        self.l.append(pltpu.make_async_copy(g.at[t.y_hi, :, :, lanes_at(t.y_lo * 1024, 512)], self.by.at[0], self.loc.at[0]))
-        for yl in range(2):
-            self.l.append(
-                pltpu.make_async_copy(g.at[:, t.z, :, pl.ds(yl * 1024 + 512, 512)], self.bz.at[0, yl], self.loc.at[1 + yl])
-            )
-        for copy in self.l:
-            copy.start()
-
-    def middle(self):
-        t, by, bz = self.t, self.by, self.bz
-        for copy in self.l:
-            copy.wait()
-        for copy in self.c:
-            copy.wait_recv()
-
-        def put_y(i, r, v):
-            by[0, i, r, :] = v
-
-        def put_z(i, r, v):
-            bz[0, i // 2, lax.rem(i, 2), r, :] = v
-
-        own_y = [lambda i, r: self.g[t.y_hi, i, r, lanes_at(t.y_lo * 1024, 512)]]
-        own_z = [lambda i, r: self.g[lax.rem(i, 2), t.z, r, lanes_at((i // 2) * 1024 + 512, 512)]]
-        if self.first:
-            own_y, own_z = [], []
-        n = 3 + self.first
-        add_up(put_y, own_y + [lambda i, r, k=k: by[k, i, r, :] for k in range(n)], 4, self.rows)
-        add_up(put_z, own_z + [lambda i, r, k=k: bz[k, i // 2, lax.rem(i, 2), r, :] for k in range(n)], 4, self.rows)
-        self.c2 = []
-        for i, (dz, z) in enumerate(t.zs):
-            self.c2.append(send(by.at[0, z], self.by2.at[dz - 1], self.two, i, {"z": z}))
-        for i, (dy, y) in enumerate(t.ys):
-            self.c2.append(send(bz.at[0, lax.rem(y, 2), y // 2], self.bz2.at[dy - 1], self.two, 3 + i, t.y_device(y)))
-
-    def finish(self):
-        t, by, bz, by2, bz2, out = self.t, self.by, self.bz, self.by2, self.bz2, self.out
-        for copy in self.c2:
-            copy.wait_recv()
-
-        def put_a(i, r, v):
-            out[r, 0:512] = v
-
-        def put_b(i, r, v):
-            out[r, 512:1024] = v
-
-        add_up(put_a, [lambda i, r: by[0, t.z, r, :]] + [lambda i, r, k=k: by2[k, r, :] for k in range(3)], 1, self.rows)
-        add_up(put_b, [lambda i, r: bz[0, t.y_lo, t.y_hi, r, :]] + [lambda i, r, k=k: bz2[k, r, :] for k in range(3)], 1, self.rows)
-        for copy in self.c + self.c2:
-            copy.wait_send()
-
-
-class SumRows(Side):
-    def __init__(self, grads, in_vmem=False):
-        r = self.rows = grads.shape[1]
-        dma = pltpu.SemaphoreType.DMA
-        self.first = 0 if in_vmem else 1
-        n = 3 + self.first
-        self.operands = [grads]
-        self.shapes = [jax.ShapeDtypeStruct((2, r, 128), BF)]
-        self.scratch = [
-            pltpu.VMEM((n, r, 512), BF), pltpu.VMEM((n, 2, 2, r, 128), BF),
-            pltpu.VMEM((3, r, 128), BF), pltpu.VMEM((3, r, 128), BF),
-            dma((9,)), dma((9,)), dma((6,)), dma((6,)), dma((3,)),
-        ]
-
-    def bind(self, ring, ins, outs, scratch):
-        (self.g,), (self.out,) = ins, outs
-        self.by, self.bz, self.by2, self.bz2, s1, r1, s2, r2, self.loc = scratch
-        self.one, self.two = (s1, r1), (s2, r2)
-        self.t = Torus()
-        self.peers = self.t.peers
-
-    def start(self):
-        t, g = self.t, self.g
-        self.c = []
-        for i, (dy, y) in enumerate(t.ys):
-            src = g.at[lax.rem(y, 2), :, lanes_at((y // 2) * 1024, 512)]
-            self.c.append(send(src, self.by.at[dy - 1 + self.first], self.one, i, t.y_device(y)))
-        for i, (dz, z) in enumerate(t.zs):
-            for yh in range(2):
-                src = g.at[:, :, lanes_at(yh * 1024 + 512 + z * 128, 128)]
-                self.c.append(send(src, self.bz.at[dz - 1 + self.first, yh], self.one, 3 + 2 * i + yh, {"z": z}))
-        self.l = []
-        if not self.first:
-            return
-        self.l.append(pltpu.make_async_copy(g.at[t.y_lo, :, lanes_at(t.y_hi * 1024, 512)], self.by.at[0], self.loc.at[0]))
-        for yh in range(2):
-            self.l.append(
-                pltpu.make_async_copy(g.at[:, :, lanes_at(yh * 1024 + 512 + t.z * 128, 128)], self.bz.at[0, yh], self.loc.at[1 + yh])
-            )
-        for copy in self.l:
-            copy.start()
-
-    def middle(self):
-        t, by, bz = self.t, self.by, self.bz
-        for copy in self.l:
-            copy.wait()
-        for copy in self.c:
-            copy.wait_recv()
-
-        def put_y(i, r, v):
-            by[0, r, :] = v
-
-        def put_z(i, r, v):
-            bz[0, i // 2, lax.rem(i, 2), r, :] = v
-
-        own_y = [lambda i, r: self.g[t.y_lo, r, lanes_at(t.y_hi * 1024, 512)]]
-        own_z = [lambda i, r: self.g[lax.rem(i, 2), r, lanes_at((i // 2) * 1024 + 512 + t.z * 128, 128)]]
-        if self.first:
-            own_y, own_z = [], []
-        n = 3 + self.first
-        add_up(put_y, own_y + [lambda i, r, k=k: by[k, r, :] for k in range(n)], 1, self.rows)
-        add_up(put_z, own_z + [lambda i, r, k=k: bz[k, i // 2, lax.rem(i, 2), r, :] for k in range(n)], 4, self.rows)
-        self.c2 = []
-        for i, (dz, z) in enumerate(t.zs):
-            self.c2.append(send(by.at[0, :, lanes_at(z * 128, 128)], self.by2.at[dz - 1], self.two, i, {"z": z}))
-        for i, (dy, y) in enumerate(t.ys):
-            self.c2.append(send(bz.at[0, y // 2, lax.rem(y, 2)], self.bz2.at[dy - 1], self.two, 3 + i, t.y_device(y)))
-
-    def finish(self):
-        t, by, bz, by2, bz2, out = self.t, self.by, self.bz, self.by2, self.bz2, self.out
-        for copy in self.c2:
-            copy.wait_recv()
-
-        def put_a(i, r, v):
-            out[0, r, :] = v
-
-        def put_b(i, r, v):
-            out[1, r, :] = v
-
-        own = lanes_at(t.z * 128, 128)
-        add_up(put_a, [lambda i, r: by[0, r, own]] + [lambda i, r, k=k: by2[k, r, :] for k in range(3)], 1, self.rows)
-        add_up(put_b, [lambda i, r: bz[0, t.y_hi, t.y_lo, r, :]] + [lambda i, r, k=k: bz2[k, r, :] for k in range(3)], 1, self.rows)
-        for copy in self.c + self.c2:
-            copy.wait_send()
 
 
 def piece_lanes(c, part):
@@ -927,9 +959,9 @@
 
 
 def front_kernel(
-    x_ref, meta_ref, g1_ref, g2_ref, wq_ref, wk_ref, wv_ref, wg_ref, wu_ref, wo_ref, wdn_ref, tab_ref,
+    x_ref, doc_ref, g1_ref, g2_ref, wq_ref, wk_ref, wv_ref, wg_ref, wu_ref, wo_ref, wdn_ref, angles_hbm,
     a_ref, lse_ref, metas_ref, n1_out, wqkv_out, qp_out, kv_out, wos_ref, wgu_ref, wd_ref,
-    n1, wqkv, w, wt, qkv, qp, kv, bias, probs,
+    n1, wqkv, w, wt, qkv, qp, kv, bias, probs, meta_ref, angles, tab_ref,
     ag_s, ag_r, meta_s, meta_r, w_s, w_r, y_s, y_r, gu_s, gu_r, wd_s, wd_r, kv_s, kv_r, fw_s, fw_r, loc,
 ):
     ring = Ring()
@@ -956,12 +988,21 @@
 
     lax.fori_loop(0, 4, normed, 0)
     ag.begin(0)
+    copy_here(angles_hbm.at[c], angles)
+    row = lax.broadcasted_iota(jnp.int32, (1, 128), 1)
+    tiles = [doc_ref[:, k * 128 : (k + 1) * 128] for k in range(8)]
+    meta_ref[...] = jnp.zeros_like(meta_ref)
+    for i in range(8):
+        first, second = tiles[i // 2], tiles[(15 - i) // 2]
+        if i % 2:
+            first, second = pltpu.roll(first, 64, 1), pltpu.roll(second, 64, 1)
+        meta_ref[i : i + 1, :] = jnp.where(row < 64, first, second)
     for k, x, core in peers:
         copies.append(send(meta_ref, metas_ref.at[here], (meta_s, meta_r), k, {"x": x, "core": core}))
     metas_ref[here] = meta_ref[...]
 
     one_matrix = eye()
-    g1, g2 = g1_ref[...], g2_ref[...]
+    g1, g2 = g1_ref[...].astype(F32), g2_ref[...].astype(F32)
 
     def turned(ref, gain, k):
         return (nt(one_matrix, ref[:, lanes_at(k * 128, 128)]) * gain).astype(BF)
@@ -1020,6 +1061,8 @@
                 send(wt.at[:, rows], wgu_ref.at[:, j, :, lanes], (gu_s, gu_r), k * 2 + j, {"x": x, "core": core})
             )
 
+    local[0].wait()
+    fill_tables(angles, tab_ref)
     ag.have(*range(6, 14))
     for copy in copies[9:13]:
         copy.wait_recv()
@@ -1109,11 +1152,11 @@
         copy.wait_send()
         if i >= 7 and not 9 <= i < 13:
             copy.wait_recv()
-    for copy in local:
+    for copy in local[1:]:
         copy.wait()
 
 
-def front(hidden_in, meta, g1, g2, w_query, w_key, w_value, w_gate, w_up, w_out, w_down, tabs):
+def front(hidden_in, docs, g1, g2, w_query, w_key, w_value, w_gate, w_up, w_out, w_down, angles):
     dma = pltpu.SemaphoreType.DMA
     pair = lambda n: [dma((n,)), dma((n,))]
     out = lambda *shape: jax.ShapeDtypeStruct(shape, BF)
@@ -1123,38 +1166,30 @@
             out(1024, 256), jax.ShapeDtypeStruct((8, 8, 512), F32), jax.ShapeDtypeStruct((8, 16, 128), jnp.int32),
             out(8, 128, D), out(384, D), out(8, 512, 128), out(2, 4, 8, 128, 128), out(2, 128, D), out(2, 2, 352, D), out(704, D),
         ],
-        in_specs=[VM] * 12,
+        in_specs=[VM] * 11 + [HB],
         out_specs=[VM] * 3 + [HB] * 7,
         scratch_shapes=[
             pltpu.VMEM((8, 128, D), BF), pltpu.VMEM((384, D), BF), pltpu.VMEM((8, 384, 128), BF), pltpu.VMEM((2, FF, 128), BF),
             pltpu.VMEM((1024, 384), F32), pltpu.VMEM((8, 512, 128), BF), pltpu.VMEM((2, 4, 8, 128, 128), BF),
             pltpu.VMEM((1024, 128), F32), pltpu.VMEM((1024, 512), BF),
-            *pair(14), *pair(8), *pair(8), *pair(6), *pair(16), *pair(2), *pair(28), *pair(7), dma((8,)),
+            pltpu.VMEM((16, 128), jnp.int32), pltpu.VMEM((2, 128, 128), F32), pltpu.VMEM((6, 128, 128), F32),
+            *pair(14), *pair(8), *pair(8), *pair(6), *pair(16), *pair(2), *pair(28), *pair(7), dma((9,)),
         ],
         compiler_params=params(5),
         name="front",
-    )(hidden_in, meta, g1, g2, w_query, w_key, w_value, w_gate, w_up, w_out, w_down, tabs)
+    )(hidden_in, docs, g1, g2, w_query, w_key, w_value, w_gate, w_up, w_out, w_down, angles)
 
 
 def everyone():
     return [device for _, device in group_peers()] + [ctx_at(k)[1] for k in range(1, 8)] + [y_partners()[1]]
 
 
-def rope_tables(c):
-    cos, sin = tables(positions_of(c))
-    low = jnp.arange(HD) < HD // 2
-    to_low, to_high = jnp.where(low, -sin, 0.0), jnp.where(low, 0.0, sin)
-    one, zero = jnp.ones_like(cos), jnp.zeros_like(cos)
-    pairs = [(cos, cos), (to_low, to_low), (to_high, to_high), (cos, one), (to_low, zero), (to_high, zero)]
-    return jnp.stack([jnp.concatenate(p, axis=1) for p in pairs])
-
-
 def tail_kernel(
-    sides, qp_ref, kv_ref, lse_ref, meta_ref, tab_ref, da_ref, x_ref, dy1_ref, stats_ref,
-    wqkv_hbm, n1_hbm, ggu2_hbm, gout_hbm, piece_down_ref, piece_gu1_ref,
+    sides, qp_ref, kv_ref, lse_ref, meta_ref, da_ref, x_ref, dy1_ref, stats_ref,
+    angles_hbm, wqkv_hbm, n1_hbm, ggu2_ref, gout_ref, piece_down_ref, piece_gu1_ref,
     grad_ref, info_ref, all_down, all_out, all_qkv, all_gu,
     bias, dap, ds, pb, mine, theirs, stage, back, dqkv, dqkv_t, parts, held, got, n1, wqkv, gq,
-    piece_gu2, piece_out, piece_qkv, got_gu1, got_gu2, got_qkv, st1, st2, mid,
+    piece_gu2, piece_out, piece_qkv, got_gu1, got_gu2, got_qkv, st1, st2, mid, angles, tab_ref,
     co_s, co_r, kv_s, kv_r, rs_s, rs_r, st_s, st_r, st2_s, st2_r, qs_s, qs_r, loc, *side_scratch,
 ):
     ring = Ring()
@@ -1162,14 +1197,15 @@
     sum_gu2, sum_out, move_gu1, down, out, spread_gu1, move_gu2, sum_qkv, move_qkv, spread_gu2 = sides
     scratch = list(side_scratch)
     places = (
-        (ggu2_hbm, piece_gu2), (gout_hbm, piece_out), (piece_gu1_ref, got_gu1), (piece_down_ref, all_down), (piece_out, all_out),
+        (ggu2_ref, piece_gu2), (gout_ref, piece_out), (piece_gu1_ref, got_gu1), (piece_down_ref, all_down), (piece_out, all_out),
         (got_gu1, all_gu), (piece_gu2, got_gu2), (gq, piece_qkv), (piece_qkv, got_qkv), (got_gu2, all_gu),
     )
     for side, (i, o) in zip(sides, places):
         side.bind(ring, (i,), (o,), scratch[: len(side.scratch)])
         del scratch[: len(side.scratch)]
     loads = [pltpu.make_async_copy(n1_hbm, n1, loc.at[0]), pltpu.make_async_copy(wqkv_hbm, wqkv, loc.at[1])]
-    for load in loads:
+    angles_load = pltpu.make_async_copy(angles_hbm.at[c], angles, loc.at[3])
+    for load in loads + [angles_load]:
         load.start()
     meet(everyone())
     sum_gu2.start()
@@ -1180,6 +1216,8 @@
     copies = [send(stats_ref, st1.at[here16], (st_s, st_r), k, device) for k, device in group]
     st1[here16] = stats_ref[...]
     lane = lax.broadcasted_iota(jnp.int32, (128, 128), 1)
+    angles_load.wait()
+    fill_tables(angles, tab_ref)
 
     def unrope(u, i):
         return u * tab_ref[i] - pltpu.roll(u, 96, 1) * tab_ref[i + 1] - pltpu.roll(u, 32, 1) * tab_ref[i + 2]
@@ -1222,14 +1260,32 @@
             recv_sem=kv_r.at[x * 7 + k - 1], device_id=device, device_id_type=MESH,
         )
 
-    def to_sibling(x, _):
+    def both_cores(x, _):
         mine[x] = one(x, 1 - ring.core).astype(BF).reshape(8, 128, 128)
         core_copy(x).start()
         dqkv[pl.ds(pl.multiple_of((x * 2 + 1 - ring.core) * 128, 128), 128), 256:384] = jnp.zeros((128, 128), BF)
+        dkv = one(x, ring.core)
+        core_copy(x).wait_recv()
+        stage[x] = (dkv + theirs[x].reshape(1024, 128).astype(F32)).astype(BF).reshape(8, 128, 128)
+        for k in range(1, 8):
+            kv_copy(x, k).start()
+
+        @pl.when(x == 1)
+        def _():
+            sum_gu2.step2()
+            sum_out.step2()
+            down.start()
+
+        @pl.when(x == 2)
+        def _():
+            sum_gu2.step3()
+            sum_out.step3()
+
         return 0
 
-    lax.fori_loop(0, 4, to_sibling, 0)
-    down.start()
+    lax.fori_loop(0, 4, both_cores, 0)
+    sum_gu2.step4()
+    sum_out.step4()
     for copy in copies:
         copy.wait_recv()
     total = st1[0]
@@ -1238,18 +1294,10 @@
     mid[...] = total
     st2[c] = total
     copies2 = [send(mid, st2.at[c], (st2_s, st2_r), k - 1, ctx_at(k)[1]) for k in range(1, 8)]
-
-    def to_owners(x, _):
-        dkv = one(x, ring.core)
-        core_copy(x).wait_recv()
-        stage[x] = (dkv + theirs[x].reshape(1024, 128).astype(F32)).astype(BF).reshape(8, 128, 128)
-        for k in range(1, 8):
-            kv_copy(x, k).start()
-        return 0
-
-    lax.fori_loop(0, 4, to_owners, 0)
-    sum_gu2.middle()
-    sum_out.middle()
+    sum_gu2.finish()
+    move_gu2.start()
+    sum_out.finish()
+    out.start()
     move_gu1.finish()
     down.middle()
 
@@ -1296,11 +1344,12 @@
     lax.fori_loop(0, 4, grads, 0)
     sum_qkv.start()
     rs.relay()
-    sum_gu2.finish()
-    move_gu2.start()
-    sum_out.finish()
-    out.start()
+    move_gu2.finish()
+    spread_gu2.start()
+    sum_qkv.step2()
     spread_gu1.middle()
+    out.middle()
+    sum_qkv.step3()
     for half in range(2):
         rs.ready(half)
 
@@ -1310,10 +1359,7 @@
             return 0
 
         lax.fori_loop(0, 4, body, 0)
-    move_gu2.finish()
-    spread_gu2.start()
-    out.middle()
-    sum_qkv.middle()
+    sum_qkv.step4()
     sum_qkv.finish()
     move_qkv.start()
     spread_gu2.middle()
@@ -1350,14 +1396,14 @@
     spread_qkv.finish()
 
 
-def tail(qp, kv, lse, metas, tabs, da, hidden_in, dy1, stats, wqkv, n1, grad_gu2, grad_out, piece_down, piece_gu1):
+def tail(qp, kv, lse, metas, da, hidden_in, dy1, stats, angles, wqkv, n1, grad_gu2, grad_out, piece_down, piece_gu1):
     dma = pltpu.SemaphoreType.DMA
     pair = lambda n: [dma((n,)), dma((n,))]
     bf = lambda *shape: jax.ShapeDtypeStruct(shape, BF)
     vm = lambda *shape: pltpu.VMEM(shape, BF)
     sides = [
         SumColumns(grad_gu2), SumRows(grad_out), Move(piece_gu1), SpreadRows(piece_down), SpreadRows(bf(2, 128, 128)),
-        SpreadGateUp(bf(8, 96, 128), 0), Move(bf(80, 1024)), SumColumns(bf(2, 4, 48, D), True), Move(bf(48, 1024)),
+        SpreadGateUp(bf(8, 96, 128), 0), Move(bf(80, 1024)), SumColumns(bf(2, 4, 48, D)), Move(bf(48, 1024)),
         SpreadGateUp(bf(8, 80, 128), 96),
     ]
     return pl.pallas_call(
@@ -1366,7 +1412,7 @@
             jax.ShapeDtypeStruct((128, D), F32), jax.ShapeDtypeStruct((8, 128), F32),
             bf(352, D), bf(128, D), bf(8, 8, 48, 128), bf(2, FF, 128),
         ],
-        in_specs=[VM] * 9 + [HB] * 4 + [VM] * 2,
+        in_specs=[VM] * 8 + [HB] * 3 + [VM] * 4,
         out_specs=[VM] * 5 + [HB],
         scratch_shapes=[
             pltpu.VMEM((1024, 128), F32), vm(512, 128), vm(1024, 512), vm(1024, 512),
@@ -1374,21 +1420,22 @@
             vm(1024, 384), vm(384, 1024), vm(8, 128, D), vm(3, 128, D), vm(7, 128, D), vm(8, 128, D), vm(384, D), vm(2, 4, 48, D),
             vm(80, 1024), vm(2, 128, 128), vm(48, 1024), vm(8, 96, 128), vm(8, 80, 128), vm(8, 48, 128),
             pltpu.VMEM((16, 8, 128), F32), pltpu.VMEM((8, 8, 128), F32), pltpu.VMEM((8, 128), F32),
-            *pair(4), *pair(28), *pair(10), *pair(16), *pair(7), *pair(7), dma((3,)),
+            pltpu.VMEM((2, 128, 128), F32), pltpu.VMEM((6, 128, 128), F32),
+            *pair(4), *pair(28), *pair(10), *pair(16), *pair(7), *pair(7), dma((4,)),
             *[s for side in sides for s in side.scratch],
         ],
         compiler_params=params(7),
         name="tail",
-    )(qp, kv, lse, metas, tabs, da, hidden_in, dy1, stats, wqkv, n1, grad_gu2, grad_out, piece_down, piece_gu1)
+    )(qp, kv, lse, metas, da, hidden_in, dy1, stats, angles, wqkv, n1, grad_gu2, grad_out, piece_down, piece_gu1)
 
 
 def finish_kernel(
     info_ref, gu_ref, g1_ref, g2_ref, wg_ref, wu_ref, down_ref, qkv_ref, wq_ref, wk_ref, wv_ref, out_ref, gin_ref,
-    gate_ref, up_ref, down_out, q_ref, k_ref, v_ref, o_ref, input_ref, gain1_ref, gain2_ref,
+    gate_ref, up_ref, down_out, q_ref, k_ref, v_ref, o_ref, input_ref, gain1_ref, gain2_ref, loss_ref,
     total2,
 ):
     scale = info_ref[1:2, 0:1]
-    s1, s2 = g1_ref[...] * scale, g2_ref[...] * scale
+    s1, s2 = column(g1_ref[...].astype(F32) * scale)[:, 0:1], column(g2_ref[...].astype(F32) * scale)[:, 0:1]
     one_matrix = eye()
     step = pl.program_id(0)
 
@@ -1411,13 +1458,14 @@
         gain1_ref[...] = jnp.sum(total.T, axis=0, keepdims=True) * scale
         o_ref[...] = out_ref[...].astype(F32) * scale
         input_ref[...] = gin_ref[...] * scale
+        loss_ref[...] = info_ref[0:1, 0:1]
 
     total = total2[...]
     for i, w_ref, g_ref in ((0, wg_ref, gate_ref), (1, wu_ref, up_ref)):
         turned = nt(one_matrix, gu_ref[i])
         g_ref[...] = turned * s2
         weighed = turned * w_ref[...].astype(F32)
-        for k in range(4):
+        for k in range(11):
             total += weighed[:, k * 128 : (k + 1) * 128]
     total2[...] = total
     down_out[...] = down_ref[...].astype(F32) * scale
@@ -1428,57 +1476,46 @@
 
 
 def finish(info, all_gu, g1, g2, w_gate, w_up, down, all_qkv, w_query, w_key, w_value, out, grad_in):
-    wide = pl.BlockSpec((128, 512), lambda i: (0, i))
-    rows = pl.BlockSpec((32, D), lambda i: (i, 0))
+    wide = pl.BlockSpec((128, 1408), lambda i: (0, i))
+    rows = pl.BlockSpec((88, D), lambda i: (i, 0))
     whole = lambda *shape: pl.BlockSpec(shape, lambda i: (0,) * len(shape))
     f32 = lambda *shape: jax.ShapeDtypeStruct(shape, F32)
     return pl.pallas_call(
         finish_kernel,
-        grid=(11,),
+        grid=(4,),
         out_shape=[
             f32(128, FF), f32(128, FF), f32(352, D), f32(128, D), f32(128, KVD), f32(128, KVD), f32(128, D), f32(128, D),
-            f32(1, 128), f32(1, 128),
+            f32(1, 128), f32(1, 128), f32(1, 1),
         ],
         in_specs=[
-            whole(8, 128), pl.BlockSpec((2, 512, 128), lambda i: (0, i, 0)), whole(128, 1), whole(128, 1), wide, wide, rows,
+            whole(8, 128), pl.BlockSpec((2, 1408, 128), lambda i: (0, i, 0)), whole(1, 128), whole(1, 128), wide, wide, rows,
             whole(8, 384, 128), whole(128, D), whole(128, KVD), whole(128, KVD), whole(128, D), whole(128, D),
         ],
         out_specs=[
             wide, wide, rows, whole(128, D), whole(128, KVD), whole(128, KVD), whole(128, D), whole(128, D),
-            whole(1, 128), whole(1, 128),
+            whole(1, 128), whole(1, 128), whole(1, 1),
         ],
         scratch_shapes=[pltpu.VMEM((128, 128), F32)],
-        compiler_params=pltpu.CompilerParams(vmem_limit_bytes=48 * 2**20),
+        compiler_params=pltpu.CompilerParams(vmem_limit_bytes=63 * 2**20),
         name="finish",
     )(info, all_gu, g1, g2, w_gate, w_up, down, all_qkv, w_query, w_key, w_value, out, grad_in)
 
 
 def local(hidden_in, teacher, doc_ids, valid_mask, norm1_gain, w_query, w_key, w_value, w_out, norm2_gain, w_gate, w_up, w_down):
-    c = lax.axis_index(("y_hi", "z"))
-    g1 = norm1_gain.astype(F32)
-    g2 = norm2_gain.astype(F32)
-    valid = valid_mask.astype(F32)
-    tabs = rope_tables(c)
-    blocks = doc_ids.reshape(16, 64)
-    key_docs = jnp.concatenate([blocks[:8], blocks[:7:-1]], axis=1)
-    meta = jnp.concatenate([key_docs, valid_mask[None], jnp.zeros((7, 128), jnp.int32)], axis=0)
-
+    g1, g2, valid = norm1_gain[None], norm2_gain[None], valid_mask[None]
+    angles = jnp.asarray(rope_angles())
     a, lse, metas, n1, wqkv, qp, kv, wo, wgu, wd = front(
-        hidden_in, meta, g1[None], g2[None], w_query, w_key, w_value, w_gate, w_up, w_out, w_down, tabs
+        hidden_in, doc_ids, g1, g2, w_query, w_key, w_value, w_gate, w_up, w_out, w_down, angles
     )
     wo = wo.reshape(256, D)
-    layer_out, loss_rows, dy1, da, grad_out, grad_gu2, piece_down, piece_gu1 = middle(
-        a, wo, hidden_in, teacher, valid[:, None], wgu, wd
+    layer_out, stats, dy1, da, grad_out, grad_gu2, piece_down, piece_gu1 = middle(a, wo, hidden_in, teacher, valid, wgu, wd)
+    grad_in, info, all_down, all_out, all_qkv, all_gu = tail(
+        qp, kv, lse, metas, da, hidden_in, dy1, stats, angles, wqkv, n1, grad_gu2, grad_out, piece_down, piece_gu1
     )
-    stats = jnp.concatenate([loss_rows.reshape(1, 128), valid[None], jnp.zeros((6, 128), F32)], axis=0)
-    grad_in, info, all_down, all_out, all_qkv, all_gu = tail(
-        qp, kv, lse, metas, tabs, da, hidden_in, dy1, stats, wqkv, n1, grad_gu2, grad_out, piece_down, piece_gu1
+    gg, gp, gd, gq, gk, gv, go, input_grad, gain1, gain2, loss = finish(
+        info, all_gu, g1, g2, w_gate, w_up, all_down, all_qkv.reshape(8, 384, 128), w_query, w_key, w_value, all_out, grad_in
     )
-    gg, gp, gd, gq, gk, gv, go, input_grad, gain1, gain2 = finish(
-        info, all_gu, g1[:, None], g2[:, None], w_gate, w_up, all_down, all_qkv.reshape(8, 384, 128),
-        w_query, w_key, w_value, all_out, grad_in,
-    )
-    return (layer_out, info[0, 0], input_grad, gain1[0], gq, gk, gv, go, gain2[0], gg, gp, gd)
+    return (layer_out, loss[0, 0], input_grad, gain1[0], gq, gk, gv, go, gain2[0], gg, gp, gd)
 
 
 def solution(mesh):

time: 393 us -> 375 us (0.954)
  local copies, waits for them, and re-layouts: 10.4 us -> 0.8 us
  other arithmetic: 4.95 us -> 0 us
    unnamed x31 -> x3, local copies, waits for them, and re-layouts: 6.59 us -> 0.8 us
where the time goes in v6:
time: 375 us
  Pallas kernels  374 us (100%)
    pallas_call x1, Pallas kernels, middle(): pl.pallas_call(functools.partial(middle_kernel, *sides), out_shape=[jax.S...  170 us
    pallas_call x1, Pallas kernels, tail(): pl.pallas_call(functools.partial(tail_kernel, sides), out_shape=[jax.Shap...  117 us
    pallas_call x1, Pallas kernels, front(): pl.pallas_call(front_kernel, out_shape=[out(1024, 256), jax.ShapeDtypeStr...  76.3 us
    pallas_call x1, Pallas kernels, finish(): pl.pallas_call(finish_kernel, grid=(4,), out_shape=[f32(128, FF), f32(128...  10.6 us

profile of v6, /device:TPU:1, one launch (start us, length us, event | category | flops | bytes accessed | tf_op | source)
XLA Modules:
  0.0 375.1 jit_solution(16937228560426031138)
XLA Ops:
  0.6 76.3 %front.1 = (bf16[1024,256]{1,0:T(8,128)(2,1)}, f32[8,8,512]{2,1,0:T(8,128)}, s32[8,16,128]{2,1,0:T(8,128)}, bf16[8,128,2048]{2,1,0:T(8,128)(2,1)}, bf16[384,2048...) custom-call(bf16[128,2048]{1,0:T(8,128)(2,1)} %x_ref.5, ...), custom_call_target="tpu_custom_call" | custom-call | tf_op jit(solution)/shard_map/front/pallas_call | solution.py:1163
  76.9 170.1 %middle.1 = (bf16[128,2048]{1,0:T(8,128)(2,1)}, f32[8,128]{1,0:T(8,128)}, f32[128,2048]{1,0:T(8,128)}, bf16[1024,256]{1,0:T(8,128)(2,1)}, bf16[2,128,2048]{2,1,0...) custom-call(bf16[1024,256]{1,0:T(8,128)(2,1)} %get-tuple-element.47.a_ref, ...), custom_call_target="tpu_custom_call" | custom-call | tf_op jit(solution)/shard_map/middle/pallas_call | solution.py:686
  247.0 116.7 %tail.1 = (f32[128,2048]{1,0:T(8,128)}, f32[8,128]{1,0:T(8,128)}, bf16[352,2048]{1,0:T(8,128)(2,1)}, bf16[128,2048]{1,0:T(8,128)(2,1)}, bf16[8,8,48,128]{3,2,1,0:T(8,128)(2,1)}, /*index=5*/bf16[2,5632,128]{2,1,0:T(8,128)(2,1)}) custom-call(bf16[8,512,128]{2,1,0:T(8,128)(2,1)} %get-tuple-element.52.qp_ref, ...), custom_call_target="tpu_custom_call" | custom-call | tf_op jit(solution)/shard_map/tail/pallas_call | solution.py:1409
  363.7 0.0 copy-start
  363.7 10.6 %finish.1 = (f32[128,5632]{1,0:T(8,128)}, f32[128,5632]{1,0:T(8,128)}, f32[352,2048]{1,0:T(8,128)}, f32[128,2048]{1,0:T(8,128)}, f32[128,256]{1,0:T(8,128)}, /*i...) custom-call(f32[8,128]{1,0:T(8,128)} %get-tuple-element.65.info_ref,, ...), custom_call_target="tpu_custom_call" | custom-call | tf_op jit(solution)/shard_map/finish/pallas_call | solution.py:1483
  374.3 0.0 copy-done
  374.3 0.8 copy.27
Async XLA Ops:
  363.7 10.6 %copy-start = (bf16[128,2048]{1,0:T(8,128)(2,1)S(1)}, bf16[128,2048]{1,0:T(8,128)(2,1)}, u32[]{:S(2)}) copy-start(bf16[128,2048]{1,0:T(8,128)(2,1)} %get-tuple-element.94) | copy-start | bytes 1572868

commit v7 on v6

--- a/solution.py
+++ b/solution.py
@@ -73,6 +73,29 @@
     for device in devices:
         pl.semaphore_signal(barrier, inc=1, device_id=device, device_id_type=MESH)
     pl.semaphore_wait(barrier, len(devices))
+
+
+def loading(kernel, which, n_in, n_out):
+    def wrapped(*refs):
+        ins, outs, scratch = list(refs[:n_in]), refs[n_in : n_in + n_out], list(refs[n_in + n_out :])
+        places, sems, rest = scratch[: len(which)], scratch[len(which)], scratch[len(which) + 1 :]
+        copies = []
+        for k, i in enumerate(which):
+            copies.append(pltpu.make_async_copy(ins[i], places[k], sems.at[k]))
+            copies[-1].start()
+            ins[i] = places[k]
+
+        def arrive():
+            for copy in copies:
+                copy.wait()
+
+        kernel(arrive, *ins, *outs, *rest)
+
+    return wrapped
+
+
+def places_for(inputs, which):
+    return [pltpu.VMEM(inputs[i].shape, inputs[i].dtype) for i in which] + [pltpu.SemaphoreType.DMA((len(which),))]
 
 
 class Ring:
@@ -351,11 +374,9 @@
         r = self.r = ring
         self.parts, self.held, self.got, self.sems = parts, held, got, sems
         self.blocks = (r.far_x, r.right_x, r.left_x, r.x)
-        a, b = HALVES
         self.plan = {
-            4: (held.at[0, a], got.at[4, a], r.right), 5: (held.at[0, b], got.at[4, b], r.left),
-            6: (held.at[1, b], got.at[5, b], r.right), 7: (held.at[2, a], got.at[5, a], r.left),
-            8: (held.at[1, a], got.at[6, a], r.right), 9: (held.at[2, b], got.at[6, b], r.left),
+            4: (0, 4, 0, r.right), 5: (0, 4, 1, r.left), 6: (1, 5, 1, r.right), 7: (2, 5, 0, r.left),
+            8: (1, 6, 0, r.right), 9: (2, 6, 1, r.left),
         }
 
     def swap(self, i, x):
@@ -364,66 +385,65 @@
             recv_sem=self.sems[1].at[i], device_id=self.r.sibling, device_id_type=MESH,
         )
 
-    def copy(self, i):
+    def copy(self, i, q=0):
         if i < 4:
             return self.swap(i, self.blocks[i])
-        src, dst, device = self.plan[i]
+        block, slot, half, device = self.plan[i]
+        rows, sem = pl.ds(half * 64 + q * 32, 32), 4 + (i - 4) * 2 + q
         return pltpu.make_async_remote_copy(
-            src_ref=src, dst_ref=dst, send_sem=self.sems[0].at[i], recv_sem=self.sems[1].at[i],
-            device_id=device, device_id_type=MESH,
+            src_ref=self.held.at[block, rows], dst_ref=self.got.at[slot, rows], send_sem=self.sems[0].at[sem],
+            recv_sem=self.sems[1].at[sem], device_id=device, device_id_type=MESH,
         )
 
-    def pair(self, i, half):
+    def pair(self, i, half, q):
         x = self.blocks[i]
-
-        def body(k, _):
-            rows = pl.ds(half * 64 + k * 16, 16)
+        for k in range(2):
+            rows = pl.ds(half * 64 + q * 32 + k * 16, 16)
             total = self.parts[x * 2 + self.r.core, rows, :].astype(F32) + self.got[i, rows, :].astype(F32)
             self.held[i, rows, :] = total.astype(BF)
-            return 0
-
-        lax.fori_loop(0, 4, body, 0)
-
-    def onward(self, i, half):
-        def body(k, _):
-            rows = pl.ds(half * 64 + k * 16, 16)
+
+    def onward(self, i, half, q):
+        for k in range(2):
+            rows = pl.ds(half * 64 + q * 32 + k * 16, 16)
             total = self.held[i, rows, :].astype(F32) + self.got[4, rows, :].astype(F32)
             self.held[i, rows, :] = total.astype(BF)
-            return 0
-
-        lax.fori_loop(0, 4, body, 0)
 
     def send_left(self):
         self.copy(2).wait_recv()
-        self.pair(2, 0)
-        self.copy(7).start()
+        for q in range(2):
+            self.pair(2, 0, q)
+            self.copy(7, q).start()
 
     def send_right(self):
         self.copy(1).wait_recv()
-        self.pair(1, 1)
-        self.copy(6).start()
+        for q in range(2):
+            self.pair(1, 1, q)
+            self.copy(6, q).start()
 
     def send_far(self):
         self.copy(0).wait_recv()
-        self.pair(0, 0)
-        self.copy(4).start()
-        self.pair(0, 1)
-        self.copy(5).start()
+        for q in range(2):
+            self.pair(0, 0, q)
+            self.copy(4, q).start()
+            self.pair(0, 1, q)
+            self.copy(5, q).start()
 
     def relay(self):
-        self.pair(1, 0)
-        self.pair(2, 1)
-        self.copy(4).wait_recv()
-        self.onward(1, 0)
-        self.copy(8).start()
-        self.copy(5).wait_recv()
-        self.onward(2, 1)
-        self.copy(9).start()
+        for q in range(2):
+            self.pair(1, 0, q)
+            self.pair(2, 1, q)
+        for q in range(2):
+            self.copy(4, q).wait_recv()
+            self.onward(1, 0, q)
+            self.copy(8, q).start()
+            self.copy(5, q).wait_recv()
+            self.onward(2, 1, q)
+            self.copy(9, q).start()
         self.copy(3).wait_recv()
 
-    def ready(self, half):
+    def ready(self, half, q):
         for i in ((7, 8), (6, 9))[half]:
-            self.copy(i).wait_recv()
+            self.copy(i, q).wait_recv()
 
     def total(self, rows):
         r = self.r
@@ -435,13 +455,17 @@
         )
 
     def drain(self):
-        for i in range(10):
+        for i in range(4):
             self.copy(i).wait_send()
+        for i in range(4, 10):
+            for q in range(2):
+                self.copy(i, q).wait_send()
 
 
 def middle_kernel(
-    down_side, gu_side, a_ref, wo_ref, x_ref, valid_ref, wd_ref, teacher_hbm, half_w_ref,
-    out_ref, stats_ref, dy1_ref, da_ref, gout_ref, ggu_ref, piece_ref, gu_piece_ref,
+    down_side, gu_side, arrive, a_ref, wo_ref, x_ref, valid_ref, wd_ref, teacher_hbm, half_w_ref,
+    out_hbm, stats_ref, dy1_hbm, da_ref, gout_ref, ggu_hbm, piece_ref, gu_piece_ref,
+    out_ref, dy1_ref, ggu_ref,
     w, n2, dyg, dag, parts, held, got, y1, gate, up, mid, mid_t, dup, dgu1, dgu2, gd, gu1, dmid, valid_col, loss_col,
     rs1_s, rs1_r, ag1_s, ag1_r, rs2_s, rs2_r, ag2_s, ag2_r, rs3_s, rs3_r, ag3_s, ag3_r, w_s, w_r, loc, *side_scratch,
 ):
@@ -451,6 +475,7 @@
     down_side.bind(ring, (gd,), (piece_ref,), side_scratch[: len(down_side.scratch)])
     gu_side.bind(ring, (gu1,), (gu_piece_ref,), side_scratch[len(down_side.scratch) :])
     meet([ring.right, ring.left, ring.sibling, near, other] + [{"z": p} for p in (other_of_pair(lax.axis_index("z")), 3 - lax.axis_index("z"))])
+    arrive()
     here = ring.x * 2 + ring.core
     dy, dgate = dy1_ref, mid
     teacher = dag.at[here]
@@ -482,16 +507,18 @@
         lax.fori_loop(0, 4, body, 0)
 
     def reduced(rs, op, ag, buf):
-        for half in range(2):
-            rs.ready(half)
-
-            def body(k, _, half=half):
-                rows = pl.ds(half * 64 + k * 16, 16)
-                buf[here, rows, :] = op(rows, rs.total(rows)).astype(BF)
-                return 0
-
-            lax.fori_loop(0, 4, body, 0)
-            ag.begin(half)
+        for q in range(2):
+            for half in range(2):
+                rs.ready(half, q)
+
+                def body(k, _, half=half, q=q):
+                    rows = pl.ds(pl.multiple_of(half * 64 + q * 32 + k * 16, 16), 16)
+                    buf[here, rows, :] = op(rows, rs.total(rows)).astype(BF)
+                    return 0
+
+                lax.fori_loop(0, 2, body, 0)
+                if q == 1:
+                    ag.begin(half)
 
     def over_blocks(ag, rs, work, first=None, after=()):
         def step(i, _):
@@ -666,6 +693,10 @@
         return then
 
     over_blocks(ag, None, to_attention, after=(both("step2"), both("step3"), both("step4")))
+    writes = []
+    for k, (src, dst) in enumerate(((out_ref, out_hbm), (dy1_ref, dy1_hbm), (ggu_ref, ggu_hbm))):
+        writes.append(pltpu.make_async_copy(src, dst, loc.at[5 + k]))
+        writes[-1].start()
 
     def grad_out(k, _):
         lanes = lanes_at(k * 512, 512)
@@ -676,6 +707,8 @@
     ag.drain()
     down_side.finish()
     gu_side.finish()
+    for copy in writes:
+        copy.wait()
 
 
 def middle(a, wo, x, teacher, valid, half_w, wd):
@@ -683,28 +716,32 @@
     pair = lambda n: [dma((n,)), dma((n,))]
     big = pltpu.VMEM((8, 128, D), BF)
     sides = [SumRows(jax.ShapeDtypeStruct((2, 352, D), BF)), SumColumns(jax.ShapeDtypeStruct((2, 4, 96, D), BF))]
+    inputs = (a, wo, x, valid, wd, teacher, half_w)
+    which = (0, 1, 2, 4)
     return pl.pallas_call(
-        functools.partial(middle_kernel, *sides),
+        loading(functools.partial(middle_kernel, *sides), which, 7, 8),
         out_shape=[
             jax.ShapeDtypeStruct((128, D), BF), jax.ShapeDtypeStruct((8, 128), F32), jax.ShapeDtypeStruct((128, D), F32),
             jax.ShapeDtypeStruct((1024, 256), BF), jax.ShapeDtypeStruct((2, 128, D), BF), jax.ShapeDtypeStruct((2, 4, 80, D), BF),
             *[s for side in sides for s in side.shapes],
         ],
-        in_specs=[VM] * 5 + [HB, HB],
-        out_specs=[VM] * 8,
+        in_specs=[VM if i == 3 else HB for i in range(7)],
+        out_specs=[HB, VM, HB, VM, VM, HB, VM, VM],
         scratch_shapes=[
+            *places_for(inputs, which),
+            pltpu.VMEM((128, D), BF), pltpu.VMEM((128, D), F32), pltpu.VMEM((2, 4, 80, D), BF),
             pltpu.VMEM((2, 2, 352, D), BF), big, big, big, big, pltpu.VMEM((3, 128, D), BF), pltpu.VMEM((7, 128, D), BF),
             pltpu.VMEM((128, D), F32),
             pltpu.VMEM((1024, 704), F32), pltpu.VMEM((1024, 704), F32),
             pltpu.VMEM((256, 704), BF), pltpu.VMEM((704, 1024), BF), pltpu.VMEM((256, 704), BF),
             pltpu.VMEM((768, 1024), BF), pltpu.VMEM((640, 1024), BF), pltpu.VMEM((2, 352, D), BF), pltpu.VMEM((2, 4, 96, D), BF),
             pltpu.VMEM((256, 704), F32), pltpu.VMEM((128, 128), F32), pltpu.VMEM((128, 128), F32),
-            *pair(10), *pair(14), *pair(10), *pair(14), *pair(10), *pair(14), *pair(4), dma((5,)),
+            *pair(16), *pair(14), *pair(16), *pair(14), *pair(16), *pair(14), *pair(4), dma((8,)),
             *[s for side in sides for s in side.scratch],
         ],
         compiler_params=pltpu.CompilerParams(collective_id=1, has_side_effects=True, vmem_limit_bytes=63 * 2**20),
         name="middle",
-    )(a, wo, x, valid, wd, teacher, half_w)
+    )(*inputs)
 
 
 def piece_lanes(c, part):
@@ -959,7 +996,7 @@
 
 
 def front_kernel(
-    x_ref, doc_ref, g1_ref, g2_ref, wq_ref, wk_ref, wv_ref, wg_ref, wu_ref, wo_ref, wdn_ref, angles_hbm,
+    arrive, x_ref, doc_ref, g1_ref, g2_ref, wq_ref, wk_ref, wv_ref, wg_ref, wu_ref, wo_ref, wdn_ref, angles_hbm,
     a_ref, lse_ref, metas_ref, n1_out, wqkv_out, qp_out, kv_out, wos_ref, wgu_ref, wd_ref,
     n1, wqkv, w, wt, qkv, qp, kv, bias, probs, meta_ref, angles, tab_ref,
     ag_s, ag_r, meta_s, meta_r, w_s, w_r, y_s, y_r, gu_s, gu_r, wd_s, wd_r, kv_s, kv_r, fw_s, fw_r, loc,
@@ -970,6 +1007,7 @@
     near, other = y_partners()
     peers = tp_peers(ring)
     meet([{"x": x, "core": core} for _, x, core in peers] + [near, other] + [ctx_at(k)[1] for k in range(1, 8)])
+    arrive()
     here = ring.x * 2 + ring.core
     copies, local = [], []
 
@@ -1160,15 +1198,18 @@
     dma = pltpu.SemaphoreType.DMA
     pair = lambda n: [dma((n,)), dma((n,))]
     out = lambda *shape: jax.ShapeDtypeStruct(shape, BF)
+    inputs = (hidden_in, docs, g1, g2, w_query, w_key, w_value, w_gate, w_up, w_out, w_down, angles)
+    which = (0, 4, 5, 6, 7, 8, 9, 10)
     return pl.pallas_call(
-        front_kernel,
+        loading(front_kernel, which, 12, 10),
         out_shape=[
             out(1024, 256), jax.ShapeDtypeStruct((8, 8, 512), F32), jax.ShapeDtypeStruct((8, 16, 128), jnp.int32),
             out(8, 128, D), out(384, D), out(8, 512, 128), out(2, 4, 8, 128, 128), out(2, 128, D), out(2, 2, 352, D), out(704, D),
         ],
-        in_specs=[VM] * 11 + [HB],
+        in_specs=[HB if i in which or i == 11 else VM for i in range(12)],
         out_specs=[VM] * 3 + [HB] * 7,
         scratch_shapes=[
+            *places_for(inputs, which),
             pltpu.VMEM((8, 128, D), BF), pltpu.VMEM((384, D), BF), pltpu.VMEM((8, 384, 128), BF), pltpu.VMEM((2, FF, 128), BF),
             pltpu.VMEM((1024, 384), F32), pltpu.VMEM((8, 512, 128), BF), pltpu.VMEM((2, 4, 8, 128, 128), BF),
             pltpu.VMEM((1024, 128), F32), pltpu.VMEM((1024, 512), BF),
@@ -1177,7 +1218,7 @@
         ],
         compiler_params=params(5),
         name="front",
-    )(hidden_in, docs, g1, g2, w_query, w_key, w_value, w_gate, w_up, w_out, w_down, angles)
+    )(*inputs)
 
 
 def everyone():
@@ -1185,7 +1226,7 @@
 
 
 def tail_kernel(
-    sides, qp_ref, kv_ref, lse_ref, meta_ref, da_ref, x_ref, dy1_ref, stats_ref,
+    sides, arrive, qp_ref, kv_ref, lse_ref, meta_ref, da_ref, x_ref, dy1_ref, stats_ref,
     angles_hbm, wqkv_hbm, n1_hbm, ggu2_ref, gout_ref, piece_down_ref, piece_gu1_ref,
     grad_ref, info_ref, all_down, all_out, all_qkv, all_gu,
     bias, dap, ds, pb, mine, theirs, stage, back, dqkv, dqkv_t, parts, held, got, n1, wqkv, gq,
@@ -1208,6 +1249,7 @@
     for load in loads + [angles_load]:
         load.start()
     meet(everyone())
+    arrive()
     sum_gu2.start()
     sum_out.start()
     move_gu1.start()
@@ -1350,15 +1392,16 @@
     spread_gu1.middle()
     out.middle()
     sum_qkv.step3()
-    for half in range(2):
-        rs.ready(half)
-
-        def body(k, _, half=half):
-            rows = pl.ds(half * 64 + k * 16, 16)
-            grad_ref[rows, :] = back_norm(x_ref[rows, :].astype(F32), dy1_ref[rows, :], rs.total(rows))
-            return 0
-
-        lax.fori_loop(0, 4, body, 0)
+    for q in range(2):
+        for half in range(2):
+            rs.ready(half, q)
+
+            def body(k, _, half=half, q=q):
+                rows = pl.ds(pl.multiple_of(half * 64 + q * 32 + k * 16, 16), 16)
+                grad_ref[rows, :] = back_norm(x_ref[rows, :].astype(F32), dy1_ref[rows, :], rs.total(rows))
+                return 0
+
+            lax.fori_loop(0, 2, body, 0)
     sum_qkv.step4()
     sum_qkv.finish()
     move_qkv.start()
@@ -1406,27 +1449,30 @@
         SpreadGateUp(bf(8, 96, 128), 0), Move(bf(80, 1024)), SumColumns(bf(2, 4, 48, D)), Move(bf(48, 1024)),
         SpreadGateUp(bf(8, 80, 128), 96),
     ]
+    inputs = (qp, kv, lse, metas, da, hidden_in, dy1, stats, angles, wqkv, n1, grad_gu2, grad_out, piece_down, piece_gu1)
+    which = (0, 1, 2, 4, 5, 6, 11, 12, 13, 14)
     return pl.pallas_call(
-        functools.partial(tail_kernel, sides),
+        loading(functools.partial(tail_kernel, sides), which, 15, 6),
         out_shape=[
             jax.ShapeDtypeStruct((128, D), F32), jax.ShapeDtypeStruct((8, 128), F32),
             bf(352, D), bf(128, D), bf(8, 8, 48, 128), bf(2, FF, 128),
         ],
-        in_specs=[VM] * 8 + [HB] * 3 + [VM] * 4,
+        in_specs=[HB if i in which or 8 <= i < 11 else VM for i in range(15)],
         out_specs=[VM] * 5 + [HB],
         scratch_shapes=[
+            *places_for(inputs, which),
             pltpu.VMEM((1024, 128), F32), vm(512, 128), vm(1024, 512), vm(1024, 512),
             vm(4, 8, 128, 128), vm(4, 8, 128, 128), vm(4, 8, 128, 128), vm(4, 7, 128, 128),
             vm(1024, 384), vm(384, 1024), vm(8, 128, D), vm(3, 128, D), vm(7, 128, D), vm(8, 128, D), vm(384, D), vm(2, 4, 48, D),
             vm(80, 1024), vm(2, 128, 128), vm(48, 1024), vm(8, 96, 128), vm(8, 80, 128), vm(8, 48, 128),
             pltpu.VMEM((16, 8, 128), F32), pltpu.VMEM((8, 8, 128), F32), pltpu.VMEM((8, 128), F32),
             pltpu.VMEM((2, 128, 128), F32), pltpu.VMEM((6, 128, 128), F32),
-            *pair(4), *pair(28), *pair(10), *pair(16), *pair(7), *pair(7), dma((4,)),
+            *pair(4), *pair(28), *pair(16), *pair(16), *pair(7), *pair(7), dma((4,)),
             *[s for side in sides for s in side.scratch],
         ],
         compiler_params=params(7),
         name="tail",
-    )(qp, kv, lse, metas, da, hidden_in, dy1, stats, angles, wqkv, n1, grad_gu2, grad_out, piece_down, piece_gu1)
+    )(*inputs)
 
 
 def finish_kernel(

time: 375 us -> 366 us (0.976)
  Pallas kernels: 374 us -> 364 us
    pallas_call x3, Pallas kernels: 363 us -> 353 us  [the longest x1 165 us: middle(): pl.pallas_call(loading(functools.partial(middle_kernel, *sides), which, 7...]
where the time goes in v7:
time: 366 us; the launch traced here: 365 us
  Pallas kernels  364 us (99%)
    pallas_call x1, Pallas kernels, middle(): pl.pallas_call(loading(functools.partial(middle_kernel, *sides), which, 7...  165 us
    pallas_call x1, Pallas kernels, tail(): pl.pallas_call(loading(functools.partial(tail_kernel, sides), which, 15,...  114 us
    pallas_call x1, Pallas kernels, front(): pl.pallas_call(loading(front_kernel, which, 12, 10), out_shape=[out(1024,...  74.3 us
    pallas_call x1, Pallas kernels, finish(): pl.pallas_call(finish_kernel, grid=(4,), out_shape=[f32(128, FF), f32(128...  10.6 us

profile of v7, /device:TPU:1, one launch (start us, length us, event | category | flops | bytes accessed | tf_op | source)
XLA Modules:
  0.0 365.4 jit_solution(15118810040161288864)
XLA Ops:
  0.6 74.3 %front.1 = (bf16[1024,256]{1,0:T(8,128)(2,1)}, f32[8,8,512]{2,1,0:T(8,128)}, s32[8,16,128]{2,1,0:T(8,128)}, bf16[8,128,2048]{2,1,0:T(8,128)(2,1)}, bf16[384,2048...) custom-call(bf16[128,2048]{1,0:T(8,128)(2,1)} %refs_5_.5, ...), custom_call_target="tpu_custom_call" | custom-call | tf_op jit(solution)/shard_map/front/pallas_call | solution.py:1203
  75.0 164.5 %middle.1 = (bf16[128,2048]{1,0:T(8,128)(2,1)}, f32[8,128]{1,0:T(8,128)}, f32[128,2048]{1,0:T(8,128)}, bf16[1024,256]{1,0:T(8,128)(2,1)}, bf16[2,128,2048]{2,1,0...) custom-call(bf16[1024,256]{1,0:T(8,128)(2,1)} %get-tuple-element.47.refs_0_, ...), custom_call_target="tpu_custom_call" | custom-call | tf_op jit(solution)/shard_map/middle/pallas_call | solution.py:721
  239.5 114.4 %tail.1 = (f32[128,2048]{1,0:T(8,128)}, f32[8,128]{1,0:T(8,128)}, bf16[352,2048]{1,0:T(8,128)(2,1)}, bf16[128,2048]{1,0:T(8,128)(2,1)}, bf16[8,8,48,128]{3,2,1,0:T(8,128)(2,1)}, /*index=5*/bf16[2,5632,128]{2,1,0:T(8,128)(2,1)}) custom-call(bf16[8,512,128]{2,1,0:T(8,128)(2,1)} %get-tuple-element.52.refs_0_, ...), custom_call_target="tpu_custom_call" | custom-call | tf_op jit(solution)/shard_map/tail/pallas_call | solution.py:1454
  354.0 0.0 copy-start
  354.0 10.6 %finish.1 = (f32[128,5632]{1,0:T(8,128)}, f32[128,5632]{1,0:T(8,128)}, f32[352,2048]{1,0:T(8,128)}, f32[128,2048]{1,0:T(8,128)}, f32[128,256]{1,0:T(8,128)}, /*i...) custom-call(f32[8,128]{1,0:T(8,128)} %get-tuple-element.65.info_ref,, ...), custom_call_target="tpu_custom_call" | custom-call | tf_op jit(solution)/shard_map/finish/pallas_call | solution.py:1529
  364.6 0.0 copy-done
  364.6 0.8 copy.27
Async XLA Ops:
  354.0 10.6 %copy-start = (bf16[128,2048]{1,0:T(8,128)(2,1)S(1)}, bf16[128,2048]{1,0:T(8,128)(2,1)}, u32[]{:S(2)}) copy-start(bf16[128,2048]{1,0:T(8,128)(2,1)} %get-tuple-element.94) | copy-start | bytes 1572868

commit v8 on v7

--- a/solution.py
+++ b/solution.py
@@ -17,6 +17,7 @@
 EPSILON = 1e-05
 THETA = 10000.0
 NEGATIVE = -1e30
+R1, R2 = 112, 64
 AXES = ("y_hi", "z", "x", "y_lo", "core")
 BF = jnp.bfloat16
 F32 = jnp.float32
@@ -550,9 +551,7 @@
                 ag.have(12, 13)
 
             x = lax.rem(ring.x + jnp.where(at(1), 3, jnp.where(at(2), 1, jnp.where(at(3), 2, 0))), 4)
-            work(x)
-            if rs is not None:
-                rs.swap(3 - i, x).start()
+            work(x, lambda: rs.swap(3 - i, x).start())
             for k, then in enumerate(after):
                 pl.when(at(k + 1))(then)
             return 0
@@ -584,7 +583,7 @@
 
     rs = Rs(ring, parts, held, got, (rs2_s, rs2_r))
 
-    def forward(x):
+    def forward(x, send_parts):
         rows = rows_of(x)
         gate[rows, :] = nt(block(n2, x), w[0].reshape(704, D))
         up[rows, :] = nt(block(n2, x), w[1].reshape(704, D))
@@ -597,6 +596,7 @@
 
         lax.fori_loop(0, 8, body, 0)
         put(x, lambda lanes: nn(mid[...], wd_ref[:, lanes]))
+        send_parts()
         mid_t[:, rows] = mid[...].T
 
     def weights_here():
@@ -624,7 +624,7 @@
 
     rs = Rs(ring, parts, held, got, (rs3_s, rs3_r))
 
-    def backward(x):
+    def backward(x, send_parts):
         rows = rows_of(x)
         dgate_mid = nt(block(dyg, x), wd_ref[...])
         dmid[...] = dgate_mid
@@ -640,11 +640,12 @@
 
         lax.fori_loop(0, 8, body, 0)
         put(x, lambda lanes: nn(dgate[...], w[0, :, :, lanes].reshape(704, 512)) + nn(dup[...], w[1, :, :, lanes].reshape(704, 512)))
+        send_parts()
         for i, ref in enumerate((dgate, dup)):
             turned = ref[...].T
             for c in range(4):
-                dgu1[pl.ds((4 * i + c) * 96, 96), rows] = turned[176 * c : 176 * c + 96]
-                dgu2[pl.ds((4 * i + c) * 80, 80), rows] = turned[176 * c + 96 : 176 * c + 176]
+                dgu1[pl.ds((4 * i + c) * R1, R1), rows] = turned[176 * c : 176 * c + R1]
+                dgu2[pl.ds((4 * i + c) * R2, R2), rows] = turned[176 * c + R1 : 176 * c + 176]
 
     over_blocks(ag, rs, backward)
     rs.send_far()
@@ -663,7 +664,7 @@
         out[:, :, :, lanes] = nn(lhs[...], n2[:, :, lanes].reshape(1024, 512)).astype(BF).reshape(2, 4, rows, 512)
 
     def grad_gu1(k, _):
-        grad_gu(96, dgu1, gu1, k)
+        grad_gu(R1, dgu1, gu1, k)
         return 0
 
     lax.fori_loop(0, 4, grad_gu1, 0)
@@ -679,11 +680,11 @@
     reduced(rs, op3, ag, dag)
     rs.drain()
 
-    def to_attention(x):
+    def to_attention(x, _):
         rows = rows_of(x)
         da_ref[rows, :] = nt(block(dag, x), wo_ref[...]).astype(BF)
         mid_t[0:256, rows] = a_ref[rows, :].T
-        grad_gu(80, dgu2, ggu_ref, x)
+        grad_gu(R2, dgu2, ggu_ref, x)
 
     def both(name):
         def then():
@@ -715,26 +716,26 @@
     dma = pltpu.SemaphoreType.DMA
     pair = lambda n: [dma((n,)), dma((n,))]
     big = pltpu.VMEM((8, 128, D), BF)
-    sides = [SumRows(jax.ShapeDtypeStruct((2, 352, D), BF)), SumColumns(jax.ShapeDtypeStruct((2, 4, 96, D), BF))]
+    sides = [SumRows(jax.ShapeDtypeStruct((2, 352, D), BF)), SumColumns(jax.ShapeDtypeStruct((2, 4, R1, D), BF))]
     inputs = (a, wo, x, valid, wd, teacher, half_w)
     which = (0, 1, 2, 4)
     return pl.pallas_call(
         loading(functools.partial(middle_kernel, *sides), which, 7, 8),
         out_shape=[
             jax.ShapeDtypeStruct((128, D), BF), jax.ShapeDtypeStruct((8, 128), F32), jax.ShapeDtypeStruct((128, D), F32),
-            jax.ShapeDtypeStruct((1024, 256), BF), jax.ShapeDtypeStruct((2, 128, D), BF), jax.ShapeDtypeStruct((2, 4, 80, D), BF),
+            jax.ShapeDtypeStruct((1024, 256), BF), jax.ShapeDtypeStruct((2, 128, D), BF), jax.ShapeDtypeStruct((2, 4, R2, D), BF),
             *[s for side in sides for s in side.shapes],
         ],
         in_specs=[VM if i == 3 else HB for i in range(7)],
         out_specs=[HB, VM, HB, VM, VM, HB, VM, VM],
         scratch_shapes=[
             *places_for(inputs, which),
-            pltpu.VMEM((128, D), BF), pltpu.VMEM((128, D), F32), pltpu.VMEM((2, 4, 80, D), BF),
+            pltpu.VMEM((128, D), BF), pltpu.VMEM((128, D), F32), pltpu.VMEM((2, 4, R2, D), BF),
             pltpu.VMEM((2, 2, 352, D), BF), big, big, big, big, pltpu.VMEM((3, 128, D), BF), pltpu.VMEM((7, 128, D), BF),
             pltpu.VMEM((128, D), F32),
             pltpu.VMEM((1024, 704), F32), pltpu.VMEM((1024, 704), F32),
             pltpu.VMEM((256, 704), BF), pltpu.VMEM((704, 1024), BF), pltpu.VMEM((256, 704), BF),
-            pltpu.VMEM((768, 1024), BF), pltpu.VMEM((640, 1024), BF), pltpu.VMEM((2, 352, D), BF), pltpu.VMEM((2, 4, 96, D), BF),
+            pltpu.VMEM((8 * R1, 1024), BF), pltpu.VMEM((8 * R2, 1024), BF), pltpu.VMEM((2, 352, D), BF), pltpu.VMEM((2, 4, R1, D), BF),
             pltpu.VMEM((256, 704), F32), pltpu.VMEM((128, 128), F32), pltpu.VMEM((128, 128), F32),
             *pair(16), *pair(14), *pair(16), *pair(14), *pair(16), *pair(14), *pair(4), dma((8,)),
             *[s for side in sides for s in side.scratch],
@@ -1446,8 +1447,8 @@
     vm = lambda *shape: pltpu.VMEM(shape, BF)
     sides = [
         SumColumns(grad_gu2), SumRows(grad_out), Move(piece_gu1), SpreadRows(piece_down), SpreadRows(bf(2, 128, 128)),
-        SpreadGateUp(bf(8, 96, 128), 0), Move(bf(80, 1024)), SumColumns(bf(2, 4, 48, D)), Move(bf(48, 1024)),
-        SpreadGateUp(bf(8, 80, 128), 96),
+        SpreadGateUp(bf(8, R1, 128), 0), Move(bf(R2, 1024)), SumColumns(bf(2, 4, 48, D)), Move(bf(48, 1024)),
+        SpreadGateUp(bf(8, R2, 128), R1),
     ]
     inputs = (qp, kv, lse, metas, da, hidden_in, dy1, stats, angles, wqkv, n1, grad_gu2, grad_out, piece_down, piece_gu1)
     which = (0, 1, 2, 4, 5, 6, 11, 12, 13, 14)
@@ -1464,7 +1465,7 @@
             pltpu.VMEM((1024, 128), F32), vm(512, 128), vm(1024, 512), vm(1024, 512),
             vm(4, 8, 128, 128), vm(4, 8, 128, 128), vm(4, 8, 128, 128), vm(4, 7, 128, 128),
             vm(1024, 384), vm(384, 1024), vm(8, 128, D), vm(3, 128, D), vm(7, 128, D), vm(8, 128, D), vm(384, D), vm(2, 4, 48, D),
-            vm(80, 1024), vm(2, 128, 128), vm(48, 1024), vm(8, 96, 128), vm(8, 80, 128), vm(8, 48, 128),
+            vm(R2, 1024), vm(2, 128, 128), vm(48, 1024), vm(8, R1, 128), vm(8, R2, 128), vm(8, 48, 128),
             pltpu.VMEM((16, 8, 128), F32), pltpu.VMEM((8, 8, 128), F32), pltpu.VMEM((8, 128), F32),
             pltpu.VMEM((2, 128, 128), F32), pltpu.VMEM((6, 128, 128), F32),
             *pair(4), *pair(28), *pair(16), *pair(16), *pair(7), *pair(7), dma((4,)),
@@ -1511,7 +1512,7 @@
         turned = nt(one_matrix, gu_ref[i])
         g_ref[...] = turned * s2
         weighed = turned * w_ref[...].astype(F32)
-        for k in range(11):
+        for k in range(22):
             total += weighed[:, k * 128 : (k + 1) * 128]
     total2[...] = total
     down_out[...] = down_ref[...].astype(F32) * scale
@@ -1522,19 +1523,19 @@
 
 
 def finish(info, all_gu, g1, g2, w_gate, w_up, down, all_qkv, w_query, w_key, w_value, out, grad_in):
-    wide = pl.BlockSpec((128, 1408), lambda i: (0, i))
-    rows = pl.BlockSpec((88, D), lambda i: (i, 0))
+    wide = pl.BlockSpec((128, 2816), lambda i: (0, i))
+    rows = pl.BlockSpec((176, D), lambda i: (i, 0))
     whole = lambda *shape: pl.BlockSpec(shape, lambda i: (0,) * len(shape))
     f32 = lambda *shape: jax.ShapeDtypeStruct(shape, F32)
     return pl.pallas_call(
         finish_kernel,
-        grid=(4,),
+        grid=(2,),
         out_shape=[
             f32(128, FF), f32(128, FF), f32(352, D), f32(128, D), f32(128, KVD), f32(128, KVD), f32(128, D), f32(128, D),
             f32(1, 128), f32(1, 128), f32(1, 1),
         ],
         in_specs=[
-            whole(8, 128), pl.BlockSpec((2, 1408, 128), lambda i: (0, i, 0)), whole(1, 128), whole(1, 128), wide, wide, rows,
+            whole(8, 128), pl.BlockSpec((2, 2816, 128), lambda i: (0, i, 0)), whole(1, 128), whole(1, 128), wide, wide, rows,
             whole(8, 384, 128), whole(128, D), whole(128, KVD), whole(128, KVD), whole(128, D), whole(128, D),
         ],
         out_specs=[

time: 366 us -> 364 us (level)
  Pallas kernels: 364 us -> 360 us
where the time goes in v8:
time: 364 us; the launch traced here: 362 us
  Pallas kernels  360 us (99%)
    pallas_call x1, Pallas kernels, middle(): pl.pallas_call(loading(functools.partial(middle_kernel, *sides), which, 7...  164 us
    pallas_call x1, Pallas kernels, tail(): pl.pallas_call(loading(functools.partial(tail_kernel, sides), which, 15,...  113 us
    pallas_call x1, Pallas kernels, front(): pl.pallas_call(loading(front_kernel, which, 12, 10), out_shape=[out(1024,...  74.3 us
    pallas_call x1, Pallas kernels, finish(): pl.pallas_call(finish_kernel, grid=(2,), out_shape=[f32(128, FF), f32(128...  9.06 us

profile of v8, /device:TPU:1, one launch (start us, length us, event | category | flops | bytes accessed | tf_op | source)
XLA Modules:
  0.0 361.8 jit_solution(4452766280281167504)
XLA Ops:
  0.6 74.3 %front.1 = (bf16[1024,256]{1,0:T(8,128)(2,1)}, f32[8,8,512]{2,1,0:T(8,128)}, s32[8,16,128]{2,1,0:T(8,128)}, bf16[8,128,2048]{2,1,0:T(8,128)(2,1)}, bf16[384,2048...) custom-call(bf16[128,2048]{1,0:T(8,128)(2,1)} %refs_5_.5, ...), custom_call_target="tpu_custom_call" | custom-call | tf_op jit(solution)/shard_map/front/pallas_call | solution.py:1204
  75.0 164.3 %middle.1 = (bf16[128,2048]{1,0:T(8,128)(2,1)}, f32[8,128]{1,0:T(8,128)}, f32[128,2048]{1,0:T(8,128)}, bf16[1024,256]{1,0:T(8,128)(2,1)}, bf16[2,128,2048]{2,1,0...) custom-call(bf16[1024,256]{1,0:T(8,128)(2,1)} %get-tuple-element.47.refs_0, ...), custom_call_target="tpu_custom_call" | custom-call | tf_op jit(solution)/shard_map/middle/pallas_call | solution.py:722
  239.3 112.7 %tail.1 = (f32[128,2048]{1,0:T(8,128)}, f32[8,128]{1,0:T(8,128)}, bf16[352,2048]{1,0:T(8,128)(2,1)}, bf16[128,2048]{1,0:T(8,128)(2,1)}, bf16[8,8,48,128]{3,2,1,0:T(8,128)(2,1)}, /*index=5*/bf16[2,5632,128]{2,1,0:T(8,128)(2,1)}) custom-call(bf16[8,512,128]{2,1,0:T(8,128)(2,1)} %get-tuple-element.52.refs_0_, ...), custom_call_target="tpu_custom_call" | custom-call | tf_op jit(solution)/shard_map/tail/pallas_call | solution.py:1455
  352.0 0.0 copy-start
  352.0 9.1 %finish.1 = (f32[128,5632]{1,0:T(8,128)}, f32[128,5632]{1,0:T(8,128)}, f32[352,2048]{1,0:T(8,128)}, f32[128,2048]{1,0:T(8,128)}, f32[128,256]{1,0:T(8,128)}, /*i...) custom-call(f32[8,128]{1,0:T(8,128)} %get-tuple-element.65.info_ref,, ...), custom_call_target="tpu_custom_call" | custom-call | tf_op jit(solution)/shard_map/finish/pallas_call | solution.py:1530
  361.0 0.0 copy-done
  361.0 0.8 copy.27
Async XLA Ops:
  352.0 9.1 %copy-start = (bf16[128,2048]{1,0:T(8,128)(2,1)S(1)}, bf16[128,2048]{1,0:T(8,128)(2,1)}, u32[]{:S(2)}) copy-start(bf16[128,2048]{1,0:T(8,128)(2,1)} %get-tuple-element.94) | copy-start | bytes 1572868
